TPU v7x, 32 devices: a whole 2x2x4 slice. The times are simulated.
32 devices in a mesh: group: 4 (over z), sub: 8 (over y, x, core).
Axes of the slice: x: 2, y: 2, z: 4, core: 2. Of those that a mesh axis runs over, the one named last changes fastest.
Arguments:
- points: float32 [3, 65536], P(None, ('group', 'sub')), may hold values from 0 to 1
- leaf_basis: bfloat16 [65536, 64], P(('group', 'sub')), as said below
- inner_transfer: bfloat16 [61440, 64], P(('group', 'sub'))
- device_transfer: float32 [2048, 64], P(('group', 'sub'))
- vectors: bfloat16 [65536, 384], P(('group', 'sub')), may hold values from -0.75 to 0.75
- near_index: int32 [1024, 12], P(('group', 'sub')), may hold values from 0 to 1023, as said below
- near_count: int32 [1024], P(('group', 'sub')), may hold values from 6 to 12, as said below
- far_index: int32 [1024, 3], P(('group', 'sub')), may hold values from 0 to 1023, as said below
Outputs:
- near_product: bfloat16 [65536, 384], P(('group', 'sub'))
- coupling: bfloat16 [196608, 64], P(('group', 'sub'))
- device_factor: float32 [2048, 64], P(('group', 'sub'))
- group_factor: float32 [2048, 64], P(('group', 'sub'))
- root_factor: float32 [2048, 64], P(('group', 'sub'))
Inputs may be any that keep to these rules, and one draw needn't show every extreme that they name: Slot 0 of near_index[t] is t; the first near_count[t] slots name distinct leaves of layers t // 4 - 1 to t // 4 + 1, all within 7 of t; the remaining slots hold t. far_index[t] names 3 distinct leaves of the window of 15 consecutive leaves centred on t (moved to lie inside 0 to 1023) whose layers differ from t's by two or more. near_count[t] is at most the number of leaves in layers t // 4 - 1 to t // 4 + 1. `leaf_basis`: each leaf's block has full column rank.
All inputs are finite; a program needn't handle non-finite values.
Results may differ from a plain program's by a relative error of at most 0.005.
Values may be sent and summed in bfloat16 or wider, within the bound.
No kernel may reach another device: no remote copies, remote signals or barrier semaphores. Data moves between devices by JAX's collectives and lax.ppermute only.
A program may use at most 64 MiB of HBM per device.

v0:
```python
import math

import jax
import jax.numpy as jnp
from jax import lax
from jax.experimental import pallas as pl
from jax.experimental.pallas import tpu as pltpu
from jax.sharding import PartitionSpec as P

LAYER = 4
PAD = 8
LONG_SQ = 2.25
RATIO = 25.0
SCALE = 0.5 / LONG_SQ / math.log(2.0)
OFF = -16384.0
AXES = ("group", "sub")
F32 = jnp.float32
BF16 = jnp.bfloat16
BIG = pltpu.CompilerParams(vmem_limit_bytes=56 * 1024 * 1024)


def split2(value):
    high = value.astype(BF16)
    return high, (value - high.astype(F32)).astype(BF16)


def split3(value):
    high = value.astype(BF16)
    rest = value - high.astype(F32)
    middle = rest.astype(BF16)
    return high, middle, (rest - middle.astype(F32)).astype(BF16)


def mm(left, right):
    return jnp.dot(left, right, preferred_element_type=F32)


def mm_nt(left, right):
    return lax.dot_general(left, right, (((1,), (1,)), ((), ())), preferred_element_type=F32)


def exact(left, right):
    return jnp.dot(left, right, precision=lax.Precision.HIGHEST, preferred_element_type=F32)


def iota(shape, dim):
    return lax.broadcasted_iota(jnp.int32, shape, dim)


def tree_kernel(basis, inner, transfer, points, vectors, hot, top, to_next, to_prev, sems):
    width = basis.shape[0]
    count = basis.shape[1] // width
    halo = LAYER * width
    rows = vectors.shape[0]
    copies = [
        pltpu.make_async_copy(
            vectors.at[pl.ds(start, halo), :], target.at[pl.ds(0, halo), :], sems.at[n]
        )
        for n, (start, target) in enumerate(((rows - halo, to_next), (0, to_prev)))
    ]
    for copy in copies:
        copy.start()

    for target, first, skip in ((to_next, count - PAD, 1), (to_prev, 0, 0)):
        block = basis[:, first * width : (first + PAD) * width]
        pieces = [
            block[:, (at + skip) * width : (at + skip + 3) * width] for at in (0, LAYER)
        ]
        target[halo : halo + width, :] = jnp.concatenate(pieces, axis=1)
        for n in range(2):
            start = (first + n * LAYER) * width
            coords = points[:, start : start + halo]
            high, low = split2(coords)
            base = halo + width + 16 * n
            target[base : base + 16, :] = jnp.zeros((16, target.shape[1]), BF16)
            target[base : base + 3, 0:halo] = high
            target[base + 8 : base + 11, 0:halo] = low

    both = 2 * width
    same = iota((both, both), 0) // width == iota((both, both), 1) // width
    half_block = jnp.where(same, 0.5, 0.0).astype(F32)

    def pair(index):
        return inner[:, index * both : (index + 1) * both]

    blocks = []
    for n in range(count // 4):
        stacked = jnp.concatenate(
            [basis[:, (2 * n + m) * both : (2 * n + m + 1) * both] for m in range(2)], axis=0
        )
        blocks.append(mm_nt(stacked, stacked) * half_block)
    offset = 0
    while True:
        nodes = len(blocks)
        xs, ts = [], []
        for n in range(nodes):
            t = pair(offset + n)
            parts = jnp.concatenate(split3(blocks[n]), axis=0)
            xs.append(mm(jnp.concatenate([t, t, t], axis=1), parts))
            ts.append(t)
        offset += nodes
        if nodes == 1:
            break
        blocks = []
        for n in range(nodes // 2):
            x = jnp.concatenate(split3(jnp.concatenate(xs[2 * n : 2 * n + 2], axis=0)), axis=1)
            t = jnp.concatenate(ts[2 * n : 2 * n + 2], axis=0)
            blocks.append(mm_nt(x, jnp.concatenate([t, t, t], axis=1)) * half_block)
    t = ts[0]
    x = jnp.concatenate(split3(xs[0]), axis=1)
    top_gram = mm_nt(x, jnp.concatenate([t, t, t], axis=1)) * 0.5
    top[...] = top_gram
    matrix = transfer[...]
    gram = exact(exact(matrix.T, top_gram), matrix)
    group = lax.axis_index("group")
    for g in range(hot.shape[0] // width):
        hot[g * width : (g + 1) * width, :] = jnp.where(group == g, gram, 0.0)
    for copy in copies:
        copy.wait()


def factor_lanes(work, width):
    panels = width // 8
    row = iota((8, 128), 0)

    def spread(value, k):
        return jnp.broadcast_to(value[k : k + 1, :], (8, 128))

    for p in range(panels):
        tiles = list(range(p, panels))
        for at in range(0, len(tiles), 3):
            group = tiles[at : at + 3]
            accs = [work[8 * p + k, 8 * i : 8 * i + 8, :] for i in group for k in range(8)]

            def step(j, accs, group=group, p=p):
                factors = [
                    jnp.broadcast_to(work[j, 8 * p + k : 8 * p + k + 1, :], (8, 128))
                    for k in range(8)
                ]
                out = []
                for n, i in enumerate(group):
                    column = work[j, 8 * i : 8 * i + 8, :]
                    out += [accs[8 * n + k] - column * factors[k] for k in range(8)]
                return out

            if p:
                accs = lax.fori_loop(0, 8 * p, step, accs, unroll=4)
                for n, i in enumerate(group):
                    for k in range(8):
                        work[8 * p + k, 8 * i : 8 * i + 8, :] = accs[8 * n + k]
        diag = [work[8 * p + k, 8 * p : 8 * p + 8, :] for k in range(8)]
        scales, mults = [], []
        for k in range(8):
            scale = lax.rsqrt(spread(diag[k], k))
            scales.append(scale)
            diag[k] = jnp.where(row >= k, diag[k] * scale, 0.0)
            mults.append([spread(diag[k], m) for m in range(k + 1, 8)])
            for m in range(k + 1, 8):
                diag[m] = diag[m] - diag[k] * mults[k][m - k - 1]
        for k in range(8):
            work[8 * p + k, 8 * p : 8 * p + 8, :] = diag[k]
            for i in range(p):
                work[8 * p + k, 8 * i : 8 * i + 8, :] = jnp.zeros((8, 128), F32)
        for i in range(p + 1, panels):
            tile = [work[8 * p + k, 8 * i : 8 * i + 8, :] for k in range(8)]
            for k in range(8):
                tile[k] = tile[k] * scales[k]
                for m in range(k + 1, 8):
                    tile[m] = tile[m] - tile[k] * mults[k][m - k - 1]
            for k in range(8):
                work[8 * p + k, 8 * i : 8 * i + 8, :] = tile[k]


def to_lanes(grams, work, width, many):
    for i in range(width):
        work[i, :, 0:many] = grams[pl.ds(i, many, stride=width), :].T


def from_lanes(work, factors, width, many):
    for j in range(width):
        column = work[j, :, 0:many]
        factors[pl.ds(j, many, stride=width), :] = jnp.concatenate([column, column], axis=0).T


def gaussians(exponent):
    return jnp.exp2(exponent) + jnp.exp2(exponent * RATIO + RATIO)


def main_kernel(
    points,
    basis,
    near_list,
    near_used,
    far_list,
    top,
    transfer,
    left,
    right,
    vectors,
    near,
    coupling,
    device_factor,
    wide,
    coords,
    first_rows,
    second_rows,
    second_cols,
    first_cols,
    switches,
    grams,
    work,
    factors,
    high,
    low,
    sem,
):
    width = basis.shape[0]
    own = basis.shape[1] // width
    total = own + 2 * PAD
    halo = LAYER * width
    rows = own * width
    both = 2 * width
    copy = pltpu.make_async_copy(vectors, wide.at[pl.ds(halo, rows), :], sem)
    copy.start()
    wide[0:halo, :] = left[0:halo, :]
    wide[halo + rows : 2 * halo + rows, :] = right[0:halo, :]

    coords[...] = jnp.zeros(coords.shape, F32)
    coords[0:3, PAD * width : PAD * width + rows] = points[...]
    for side, block in ((0, left), (PAD * width + rows, right)):
        for n in range(2):
            base = halo + width + 16 * n
            values = block[base : base + 16, 0:halo].astype(F32)
            coords[0:3, side + n * halo : side + (n + 1) * halo] = (
                values[0:3, :] + values[8:11, :]
            )
    lanes = coords.shape[1]
    sub = iota((8, lanes), 0)
    leaf = iota((8, lanes), 1) // width
    corner = jnp.where(sub == 0, leaf % 2 - 1, leaf // 2 % 2 - 1)
    corner = jnp.where(sub == 2, leaf // LAYER - total // LAYER // 2, corner)
    place = jnp.where(sub < 3, coords[...] + corner.astype(F32), 0.0)
    norm = jnp.sum(place * place, axis=0, keepdims=True) * SCALE
    first = jnp.where(sub == 3, -norm, jnp.where(sub == 4, 1.0, place))
    second = jnp.where(
        sub == 3, 1.0, jnp.where(sub == 4, -norm - 1.0, place * (2.0 * SCALE))
    )
    fh, fm, fl = [v.astype(F32) for v in split3(first)]
    sh, sm, sl = [v.astype(F32) for v in split3(second)]
    hot_row = iota((16, lanes), 0)
    hot_leaf = iota((16, lanes), 1) // width
    hot = jnp.where((hot_leaf + 16 - PAD) % 16 == hot_row, 1.0, 0.0).astype(F32)
    first_all = jnp.concatenate([fh, fh, fh, fm, fm, fl, hot], axis=0)
    second_all = jnp.concatenate([sh, sm, sl, sh, sm, sh, jnp.zeros_like(hot)], axis=0)
    first_cols[...] = first_all.astype(BF16)
    second_cols[...] = second_all[0:48, :].astype(BF16)
    first_rows[...] = first_all[:, PAD * width : PAD * width + rows].T.astype(BF16)
    second_rows[...] = jnp.concatenate([second_all, second_all], axis=0).T.astype(BF16)

    start_leaf = lax.axis_index(AXES) * own
    target = iota((1, own), 1)
    base_leaf = start_leaf + target // LAYER * LAYER - LAYER
    window = 3 * LAYER
    found = jnp.zeros((16, own), jnp.bool_)
    place_row = iota((16, own), 0)
    for n in range(near_list.shape[0]):
        spot = jnp.where(near_used[...] > n, near_list[n : n + 1, :] - base_leaf, -1)
        found = jnp.logical_or(found, place_row == spot)
    bias = jnp.where(found, 0.0, OFF).astype(F32)
    span = window * width
    expand = jnp.where(iota((16, span), 0) == iota((16, span), 1) // width, 1.0, 0.0)
    switches[...] = mm(bias.T.astype(BF16), expand.astype(BF16)).astype(BF16)

    lane = iota((width, both), 1)
    for n in range(own // 2):
        block = basis[:, n * both : (n + 1) * both]
        zero = jnp.zeros_like(block)
        stacked = jnp.concatenate(
            [jnp.where(lane < width, block, zero), jnp.where(lane < width, zero, block)], axis=0
        )
        at = (PAD + 2 * n) * width
        grams[at : at + both, :] = mm_nt(stacked, block)
    for block, spots in (
        (left, (1, 2, 3, 5, 6, 7)),
        (right, tuple(PAD + own + m for m in (0, 1, 2, 4, 5, 6))),
    ):
        for n, spot in enumerate(spots):
            piece = block[halo : halo + width, n * width : (n + 1) * width]
            grams[spot * width : (spot + 1) * width, :] = mm_nt(piece, piece)
    for spot in (0, 4, total - 5, total - 1):
        grams[spot * width : (spot + 1) * width, :] = top[...]

    to_lanes(grams, work, width, total)
    factor_lanes(work, width)
    from_lanes(work, factors, width, total)
    device_factor[...] = exact(factors[0:width, 0:width], transfer[...])
    high_part, low_part = split2(factors[...])
    high[...] = high_part
    low[...] = low_part

    copy.wait()

    def layer(index, carry):
        at = pl.multiple_of(index * halo, halo)
        around = pl.multiple_of(index * halo + halo, halo)
        group = pl.multiple_of(index // 4 * 16, 16)
        columns = jnp.concatenate(
            [second_cols[:, pl.ds(around, 3 * halo)], switches[pl.ds(group, 16), :]], axis=0
        )
        weights = gaussians(mm(first_rows[pl.ds(at, halo), :], columns)).astype(BF16)
        near[pl.ds(at, halo), :] = mm(weights, wide[pl.ds(at, 3 * halo), :]).astype(BF16)
        return carry

    lax.fori_loop(0, own // LAYER, layer, 0)

    far = far_list.shape[0]
    square = iota((both, both), 0) // width == iota((both, both), 1) // width
    lane_far = iota((width, both), 1) < width
    lane_wide = iota((far * width, both), 1) < width

    def far_pair(index, carry):
        t = 2 * index
        spots = [
            [
                pl.multiple_of((far_list[f, t + m] - start_leaf + PAD) * width, width)
                for f in range(far)
            ]
            for m in range(2)
        ]
        picked = [
            jnp.concatenate([second_rows[pl.ds(s, width), :] for s in spots[m]], axis=0)
            for m in range(2)
        ]
        sources = jnp.where(lane_wide, picked[0], picked[1])
        at = pl.multiple_of((PAD + t) * width, both)
        own_cols = first_cols[:, pl.ds(at, both)]
        zero = jnp.zeros((both, both), BF16)
        targets = jnp.where(square, jnp.concatenate([own_cols, own_cols], axis=0), zero)
        kernel_block = gaussians(mm(sources, targets))
        kh, kl = split2(kernel_block)
        rh = jnp.where(square, high[pl.ds(at, both), :], zero)
        rl = jnp.where(square, low[pl.ds(at, both), :], zero)
        half = mm_nt(
            jnp.concatenate([kh, kl, kh], axis=1), jnp.concatenate([rh, rh, rl], axis=1)
        ) * (1.0 / width)
        zh, zl = split2(half)
        outs = []
        for f in range(far):
            a = slice(f * width, (f + 1) * width)
            sh = jnp.where(
                lane_far, high[pl.ds(spots[0][f], width), :], high[pl.ds(spots[1][f], width), :]
            )
            sl = jnp.where(
                lane_far, low[pl.ds(spots[0][f], width), :], low[pl.ds(spots[1][f], width), :]
            )
            ph = jnp.where(square, jnp.concatenate([zh[a], zh[a]], axis=0), zero)
            plow = jnp.where(square, jnp.concatenate([zl[a], zl[a]], axis=0), zero)
            outs.append(
                mm(jnp.concatenate([sh, sh, sl], axis=1), jnp.concatenate([ph, plow, ph], axis=0))
            )
        line = jnp.concatenate(
            [out[:, 0:width] for out in outs] + [out[:, width:both] for out in outs], axis=1
        )
        where = pl.multiple_of(index * (2 * far * width), both)
        coupling[:, pl.ds(where, 2 * far * width)] = line.astype(BF16)
        return carry

    lax.fori_loop(0, own // 2, far_pair, 0)


def upper_kernel(sums, group_factor, root_factor, grams, work, factors):
    width = sums.shape[1]
    groups = sums.shape[0] // width
    members = lax.axis_size("sub")
    group = lax.axis_index("group")
    total = sums[0:width, :]
    for g in range(1, groups):
        total = total + sums[g * width : (g + 1) * width, :]
    mine = sums[pl.ds(pl.multiple_of(group * width, width), width), :]
    for n in range(8):
        grams[n * width : (n + 1) * width, :] = (
            mine * (1.0 / members) if n == 0 else total * (1.0 / (members * groups))
        )
    to_lanes(grams, work, width, 8)
    factor_lanes(work, width)
    from_lanes(work, factors, width, 8)
    group_factor[...] = factors[0:width, 0:width]
    root_factor[...] = factors[width : 2 * width, 0:width]


def shift(block, distance):
    devices = range(lax.axis_size(AXES))
    route = [(i - distance, i) for i in devices if i - distance in devices]
    return lax.ppermute(block, AXES, route)


def per_device(
    points, leaf_basis, inner_transfer, device_transfer, vectors, near_index, near_count, far_index
):
    own = near_index.shape[0]
    width = leaf_basis.shape[1]
    columns = vectors.shape[1]
    halo = LAYER * width
    total = own + 2 * PAD
    groups = lax.axis_size("group")
    vmem = pl.BlockSpec(memory_space=pltpu.VMEM)
    smem = pl.BlockSpec(memory_space=pltpu.SMEM)
    hbm = pl.BlockSpec(memory_space=pl.ANY)
    square = jax.ShapeDtypeStruct((width, width), F32)
    sent = jax.ShapeDtypeStruct((halo + width + 32, columns), BF16)
    basis = leaf_basis.T

    hot, top, to_next, to_prev = pl.pallas_call(
        tree_kernel,
        out_shape=(jax.ShapeDtypeStruct((groups * width, width), F32), square, sent, sent),
        in_specs=[vmem, vmem, vmem, vmem, hbm],
        out_specs=(vmem, vmem, vmem, vmem),
        scratch_shapes=[pltpu.SemaphoreType.DMA((2,))],
        compiler_params=BIG,
        name="tree",
    )(basis, inner_transfer.T, device_transfer, points, vectors)
    left = shift(to_next, 1)
    right = shift(to_prev, -1)
    sums = lax.psum(hot, AXES)

    near, coupling, device_factor = pl.pallas_call(
        main_kernel,
        out_shape=(
            jax.ShapeDtypeStruct(vectors.shape, BF16),
            jax.ShapeDtypeStruct((width, own * far_index.shape[1] * width), BF16),
            square,
        ),
        in_specs=[vmem] * 4 + [smem] + [vmem] * 4 + [hbm],
        out_specs=(vmem, vmem, vmem),
        scratch_shapes=[
            pltpu.VMEM((own * width + 2 * halo, columns), BF16),
            pltpu.VMEM((8, total * width), F32),
            pltpu.VMEM((own * width, 64), BF16),
            pltpu.VMEM((total * width, 128), BF16),
            pltpu.VMEM((48, total * width), BF16),
            pltpu.VMEM((64, total * width), BF16),
            pltpu.VMEM((own, 3 * halo), BF16),
            pltpu.VMEM((total * width, width), F32),
            pltpu.VMEM((width, width, 128), F32),
            pltpu.VMEM((total * width, 2 * width), F32),
            pltpu.VMEM((total * width, 2 * width), BF16),
            pltpu.VMEM((total * width, 2 * width), BF16),
            pltpu.SemaphoreType.DMA,
        ],
        compiler_params=BIG,
        name="leaves",
    )(
        points,
        basis,
        near_index.T,
        near_count.reshape(1, own),
        far_index.T,
        top,
        device_transfer,
        left,
        right,
        vectors,
    )

    group_factor, root_factor = pl.pallas_call(
        upper_kernel,
        out_shape=(square, square),
        in_specs=[vmem],
        out_specs=(vmem, vmem),
        scratch_shapes=[
            pltpu.VMEM((8 * width, width), F32),
            pltpu.VMEM((width, width, 128), F32),
            pltpu.VMEM((8 * width, 2 * width), F32),
        ],
        compiler_params=BIG,
        name="upper",
    )(sums)
    return near, coupling.T, device_factor, group_factor, root_factor


def solution(mesh):
    split = P(AXES, None)
    return jax.shard_map(
        per_device,
        mesh=mesh,
        in_specs=(P(None, AXES), split, split, split, split, split, P(AXES), split),
        out_specs=(split, split, split, split, split),
        check_vma=False,
    )
```

profile of v0, /device:TPU:0, one launch (start us, length us, event | category | flops | bytes accessed | tf_op | source)
XLA Modules:
  0.0 176.9 jit_solution(17255916871073028059)
XLA Ops:
  7.2 0.0 all-reduce.2.cloned.1.call-start
  7.2 3.8 %tree.1 = (f32[256,64]{1,0:T(8,128)}, f32[64,64]{1,0:T(8,128)}, bf16[352,384]{1,0:T(8,128)(2,1)}, bf16[352,384]{1,0:T(8,128)(2,1)}) custom-call(bf16[64,2048]{1,0:T(8,128)(2,1)} %bitcast.6, bf16[64,1920]{1,0:T(8,128)(2,1)} %bitcast.8, f32[64,64]{1,0:T(8,128)} %transfer.3, f32[3,2048]{1,0:T(4,128)} %points.3, bf16[2048,384]{1,0:T(8,128)(2,1)} %vectors.3), custom_call_target="tpu_custom_call" | custom-call | tf_op jit(solution)/shard_map/tree/pallas_call | solution.py:413
  11.0 2.4 %collective-permute-start = (bf16[352,384]{1,0:T(8,128)(2,1)}, bf16[352,384]{1,0:T(8,128)(2,1)S(1)}, u32[]{:S(2)}, u32[]{:S(2)}) collective-permute-start(bf16[352,384]{1,0:T(8,128)(2,1)} %get-tuple-element.15), channel_id=1, source_target_pairs={{0,1},{1,2},{2,3},{3,4},{4,5},{5,6},{6,7},{7,8},{8,9},{9,10},{10,1... | collective-permute-start | bytes 811016 | tf_op jit(solution)/shard_map/ppermute | solution.py:394
  13.4 1.3 collective-permute-start.1
  14.7 0.0 all-reduce.2.cloned.1.call-update
  14.7 127.2 %all-reduce.2.cloned.1.call-done.sums = f32[256,64]{1,0:T(8,128)} async-done(((f32[256,64]{1,0:T(8,128)}), f32[256,64]{1,0:T(8,128)}) %all-reduce.2.cloned.1.call-update) | async-done | bytes 65552 | tf_op jit(solution)/shard_map/psum | solution.py:424
  141.9 5.9 %upper.1 = (f32[64,64]{1,0:T(8,128)}, f32[64,64]{1,0:T(8,128)}) custom-call(f32[256,64]{1,0:T(8,128)} %all-reduce.2.cloned.1.call-done.sums), custom_call_target="tpu_custom_call" | custom-call | tf_op jit(solution)/shard_map/upper/pallas_call | solution.py:465
  147.8 0.0 collective-permute-done.left
  147.8 0.0 copy-start
  147.8 0.0 collective-permute-done.1.right
  147.8 0.0 copy-start.1
  147.8 0.7 copy-done
  148.5 0.1 copy-done.1
  148.6 21.4 %leaves.1 = (bf16[2048,384]{1,0:T(8,128)(2,1)}, bf16[64,6144]{1,0:T(8,128)(2,1)}, f32[64,64]{1,0:T(8,128)}) custom-call(f32[3,2048]{1,0:T(4,128)} %points.3, bf16[64,2048]{1,0:T(8,128)(2,1)} %bitcast.7, s32[12,32]{1,0:T(8,128)} %bitcast.9, s32[1,32]{1,0:T(1,128)} %bitcast.11, s32[3,32]{1,0:T(4,128)} %bitcast.10, f32[64,64]{1,0:T(8,128)} %get-tuple-element.14.top, ...), custom_call_target="tpu_custom_call" | custom-call | tf_op jit(solution)/shard_map/leaves/pallas_call | solution.py:426
Async XLA Ops:
  7.2 134.7 %all-reduce.2.cloned.1.call-start = ((), (), s32[]{:S(2)}) async-start(), calls=%async_computation | async-start | bytes 262144 | tf_op jit(solution)/shard_map/psum | solution.py:424
  11.0 136.8 %collective-permute-start = (bf16[352,384]{1,0:T(8,128)(2,1)}, bf16[352,384]{1,0:T(8,128)(2,1)S(1)}, u32[]{:S(2)}, u32[]{:S(2)}) collective-permute-start(bf16[352,384]{1,0:T(8,128)(2,1)} %get-tuple-element.15), channel_id=1, source_target_pairs={{0,1},{1,2},{2,3},{3,4},{4,5},{5,6},{6,7},{7,8},{8,9},{9,10},{10,1... | collective-permute-start | bytes 811016 | tf_op jit(solution)/shard_map/ppermute | solution.py:394
  13.4 134.4 %collective-permute-start.1 = (bf16[352,384]{1,0:T(8,128)(2,1)}, bf16[352,384]{1,0:T(8,128)(2,1)S(1)}, u32[]{:S(2)}, u32[]{:S(2)}) collective-permute-start(bf16[352,384]{1,0:T(8,128)(2,1)} %get-tuple-element.16), channel_id=1, source_target_pairs={{1,0},{2,1},{3,2},{4,3},{5,4},{6,5},{7,6},{8,7},{9,8},{10,9},{11,1... | collective-permute-start | bytes 811016 | tf_op jit(solution)/shard_map/ppermute | solution.py:394
  147.8 0.7 copy-start
  147.8 0.8 copy-start.1
Sparse Core Ops, SparseCore 0:
  14.9 127.0 all-reduce.1
where the time goes:
time: 177 us
  waiting for transfers between devices  127 us (72%)
  Pallas kernels  31.2 us (18%)
  between operations  14.1 us (8%)
  starting transfers between devices  3.71 us (2%)
    psum x1, waiting for transfers between devices, per_device(): sums = lax.psum(hot, AXES)  127 us
    pallas_call x1, Pallas kernels, per_device(): pl.pallas_call(main_kernel, out_shape=(jax.ShapeDtypeStruct(vectors.shape...  21.4 us
    pallas_call x1, Pallas kernels, per_device(): pl.pallas_call(upper_kernel, out_shape=(square, square), in_specs=[vmem],...  5.91 us
    pallas_call x1, Pallas kernels, per_device(): pl.pallas_call(tree_kernel, out_shape=(jax.ShapeDtypeStruct((groups * wid...  3.8 us
    ppermute x2, starting transfers between devices, shift(): return lax.ppermute(block, AXES, route)  3.67 us
  transfers between devices with their start and end apart: 3, of which 1 were waited for; matrix products, arithmetic and copies ran while one was open for 0% of the time, Pallas kernels for 3%

commit v1 on v0

--- a/solution.py
+++ b/solution.py
@@ -47,7 +47,7 @@
     return lax.broadcasted_iota(jnp.int32, shape, dim)
 
 
-def tree_kernel(basis, inner, transfer, points, vectors, hot, top, to_next, to_prev, sems):
+def tree_kernel(basis, inner, transfer, points, vectors, fan, top, to_next, to_prev, sems):
     width = basis.shape[0]
     count = basis.shape[1] // width
     halo = LAYER * width
@@ -112,63 +112,62 @@
     top[...] = top_gram
     matrix = transfer[...]
     gram = exact(exact(matrix.T, top_gram), matrix)
-    group = lax.axis_index("group")
-    for g in range(hot.shape[0] // width):
-        hot[g * width : (g + 1) * width, :] = jnp.where(group == g, gram, 0.0)
+    for n in range(fan.shape[0]):
+        fan[n, :, :] = jnp.concatenate([gram[: width // 2], gram[width // 2 :]], axis=1)
     for copy in copies:
         copy.wait()
 
 
-def factor_lanes(work, width):
+def factor_lanes(work, width, beside):
     panels = width // 8
     row = iota((8, 128), 0)
 
-    def spread(value, k):
-        return jnp.broadcast_to(value[k : k + 1, :], (8, 128))
+    def spread(j, i):
+        return jnp.broadcast_to(work[j, i : i + 1, :], (8, 128))
 
     for p in range(panels):
+        at = 8 * p
         tiles = list(range(p, panels))
-        for at in range(0, len(tiles), 3):
-            group = tiles[at : at + 3]
-            accs = [work[8 * p + k, 8 * i : 8 * i + 8, :] for i in group for k in range(8)]
-
-            def step(j, accs, group=group, p=p):
-                factors = [
-                    jnp.broadcast_to(work[j, 8 * p + k : 8 * p + k + 1, :], (8, 128))
-                    for k in range(8)
-                ]
-                out = []
-                for n, i in enumerate(group):
-                    column = work[j, 8 * i : 8 * i + 8, :]
-                    out += [accs[8 * n + k] - column * factors[k] for k in range(8)]
-                return out
-
-            if p:
-                accs = lax.fori_loop(0, 8 * p, step, accs, unroll=4)
+        if p:
+            for start in range(0, len(tiles), 3):
+                group = tiles[start : start + 3]
+                accs = [work[at + k, 8 * i : 8 * i + 8, :] for i in group for k in range(8)]
+
+                def step(j, accs, group=group, at=at):
+                    factors = [spread(j, at + k) for k in range(8)]
+                    out = []
+                    for n, i in enumerate(group):
+                        column = work[j, 8 * i : 8 * i + 8, :]
+                        out += [accs[8 * n + k] - column * factors[k] for k in range(8)]
+                    return out
+
+                accs = lax.fori_loop(0, at, step, accs, unroll=4)
                 for n, i in enumerate(group):
                     for k in range(8):
-                        work[8 * p + k, 8 * i : 8 * i + 8, :] = accs[8 * n + k]
-        diag = [work[8 * p + k, 8 * p : 8 * p + 8, :] for k in range(8)]
-        scales, mults = [], []
+                        work[at + k, 8 * i : 8 * i + 8, :] = accs[8 * n + k]
+        entry = {(k, m): spread(at + k, at + m) for k in range(8) for m in range(k, 8)}
+        scales = []
         for k in range(8):
-            scale = lax.rsqrt(spread(diag[k], k))
-            scales.append(scale)
-            diag[k] = jnp.where(row >= k, diag[k] * scale, 0.0)
-            mults.append([spread(diag[k], m) for m in range(k + 1, 8)])
+            scales.append(lax.rsqrt(entry[k, k]))
             for m in range(k + 1, 8):
-                diag[m] = diag[m] - diag[k] * mults[k][m - k - 1]
-        for k in range(8):
-            work[8 * p + k, 8 * p : 8 * p + 8, :] = diag[k]
-            for i in range(p):
-                work[8 * p + k, 8 * i : 8 * i + 8, :] = jnp.zeros((8, 128), F32)
-        for i in range(p + 1, panels):
-            tile = [work[8 * p + k, 8 * i : 8 * i + 8, :] for k in range(8)]
+                entry[k, m] = entry[k, m] * scales[k]
+            for m in range(k + 1, 8):
+                for q in range(m, 8):
+                    entry[m, q] = entry[m, q] - entry[k, m] * entry[k, q]
+        for i in tiles:
+            tile = [work[at + k, 8 * i : 8 * i + 8, :] for k in range(8)]
             for k in range(8):
                 tile[k] = tile[k] * scales[k]
                 for m in range(k + 1, 8):
-                    tile[m] = tile[m] - tile[k] * mults[k][m - k - 1]
+                    tile[m] = tile[m] - tile[k] * entry[k, m]
             for k in range(8):
-                work[8 * p + k, 8 * i : 8 * i + 8, :] = tile[k]
+                work[at + k, 8 * i : 8 * i + 8, :] = (
+                    jnp.where(row >= k, tile[k], 0.0) if i == p else tile[k]
+                )
+        for i in range(p):
+            for k in range(8):
+                work[at + k, 8 * i : 8 * i + 8, :] = jnp.zeros((8, 128), F32)
+        beside(p)
 
 
 def to_lanes(grams, work, width, many):
@@ -193,6 +192,7 @@
     near_used,
     far_list,
     top,
+    sums,
     transfer,
     left,
     right,
@@ -200,7 +200,10 @@
     near,
     coupling,
     device_factor,
+    group_factor,
+    root_factor,
     wide,
+    sides,
     coords,
     first_rows,
     second_rows,
@@ -212,7 +215,7 @@
     factors,
     high,
     low,
-    sem,
+    sems,
 ):
     width = basis.shape[0]
     own = basis.shape[1] // width
@@ -220,17 +223,32 @@
     halo = LAYER * width
     rows = own * width
     both = 2 * width
-    copy = pltpu.make_async_copy(vectors, wide.at[pl.ds(halo, rows), :], sem)
-    copy.start()
-    wide[0:halo, :] = left[0:halo, :]
-    wide[halo + rows : 2 * halo + rows, :] = right[0:halo, :]
+    extra = sides.shape[1]
+    side_copies = [
+        pltpu.make_async_copy(side.at[pl.ds(halo, extra), :], sides.at[n], sems.at[n])
+        for n, side in enumerate((left, right))
+    ]
+    copies = [
+        pltpu.make_async_copy(source, wide.at[pl.ds(start, many), :], sems.at[2 + n])
+        for n, (source, start, many) in enumerate(
+            (
+                (left.at[pl.ds(0, halo), :], 0, halo),
+                (right.at[pl.ds(0, halo), :], halo + rows, halo),
+                (vectors, halo, rows),
+            )
+        )
+    ]
+    for copy in side_copies + copies:
+        copy.start()
 
     coords[...] = jnp.zeros(coords.shape, F32)
     coords[0:3, PAD * width : PAD * width + rows] = points[...]
-    for side, block in ((0, left), (PAD * width + rows, right)):
+    for copy in side_copies:
+        copy.wait()
+    for block, side in enumerate((0, PAD * width + rows)):
         for n in range(2):
-            base = halo + width + 16 * n
-            values = block[base : base + 16, 0:halo].astype(F32)
+            base = width + 16 * n
+            values = sides[block, base : base + 16, 0:halo].astype(F32)
             coords[0:3, side + n * halo : side + (n + 1) * halo] = (
                 values[0:3, :] + values[8:11, :]
             )
@@ -280,38 +298,56 @@
         )
         at = (PAD + 2 * n) * width
         grams[at : at + both, :] = mm_nt(stacked, block)
-    for block, spots in (
-        (left, (1, 2, 3, 5, 6, 7)),
-        (right, tuple(PAD + own + m for m in (0, 1, 2, 4, 5, 6))),
+    for block, spots in enumerate(
+        ((1, 2, 3, 5, 6, 7), tuple(PAD + own + m for m in (0, 1, 2, 4, 5, 6)))
     ):
         for n, spot in enumerate(spots):
-            piece = block[halo : halo + width, n * width : (n + 1) * width]
+            piece = sides[block, 0:width, n * width : (n + 1) * width]
             grams[spot * width : (spot + 1) * width, :] = mm_nt(piece, piece)
-    for spot in (0, 4, total - 5, total - 1):
-        grams[spot * width : (spot + 1) * width, :] = top[...]
+    members, groups = lax.axis_size("sub"), lax.axis_size("group")
+    root = sums[0, :, :]
+    for g in range(1, groups):
+        root = root + sums[g, :, :]
+    mine = sums[lax.axis_index("group"), :, :]
+    root, mine = (
+        jnp.concatenate([v[:, :width], v[:, width:]], axis=0) for v in (root, mine)
+    )
+    spare = (0, 4, total - 5, total - 1)
+    for spot, gram in zip(
+        spare,
+        (top[...], mine * (1.0 / members), root * (1.0 / (members * groups)), top[...]),
+    ):
+        grams[spot * width : (spot + 1) * width, :] = gram
+
+    for copy in copies:
+        copy.wait()
+
+    def layer(index):
+        at = index * halo
+        around = index * halo + halo
+        group = index // 4 * 16
+        columns = jnp.concatenate(
+            [second_cols[:, pl.ds(around, 3 * halo)], switches[pl.ds(group, 16), :]], axis=0
+        )
+        weights = gaussians(mm(first_rows[pl.ds(at, halo), :], columns)).astype(BF16)
+        near[pl.ds(at, halo), :] = mm(weights, wide[pl.ds(at, 3 * halo), :]).astype(BF16)
 
     to_lanes(grams, work, width, total)
-    factor_lanes(work, width)
+    layers = own // LAYER
+    panels = width // 8
+
+    def some_layers(p):
+        for index in range(p * layers // panels, (p + 1) * layers // panels):
+            layer(index)
+
+    factor_lanes(work, width, some_layers)
     from_lanes(work, factors, width, total)
     device_factor[...] = exact(factors[0:width, 0:width], transfer[...])
+    for target, spot in ((group_factor, spare[1]), (root_factor, spare[2])):
+        target[...] = factors[spot * width : (spot + 1) * width, 0:width]
     high_part, low_part = split2(factors[...])
     high[...] = high_part
     low[...] = low_part
-
-    copy.wait()
-
-    def layer(index, carry):
-        at = pl.multiple_of(index * halo, halo)
-        around = pl.multiple_of(index * halo + halo, halo)
-        group = pl.multiple_of(index // 4 * 16, 16)
-        columns = jnp.concatenate(
-            [second_cols[:, pl.ds(around, 3 * halo)], switches[pl.ds(group, 16), :]], axis=0
-        )
-        weights = gaussians(mm(first_rows[pl.ds(at, halo), :], columns)).astype(BF16)
-        near[pl.ds(at, halo), :] = mm(weights, wide[pl.ds(at, 3 * halo), :]).astype(BF16)
-        return carry
-
-    lax.fori_loop(0, own // LAYER, layer, 0)
 
     far = far_list.shape[0]
     square = iota((both, both), 0) // width == iota((both, both), 1) // width
@@ -365,27 +401,7 @@
         coupling[:, pl.ds(where, 2 * far * width)] = line.astype(BF16)
         return carry
 
-    lax.fori_loop(0, own // 2, far_pair, 0)
-
-
-def upper_kernel(sums, group_factor, root_factor, grams, work, factors):
-    width = sums.shape[1]
-    groups = sums.shape[0] // width
-    members = lax.axis_size("sub")
-    group = lax.axis_index("group")
-    total = sums[0:width, :]
-    for g in range(1, groups):
-        total = total + sums[g * width : (g + 1) * width, :]
-    mine = sums[pl.ds(pl.multiple_of(group * width, width), width), :]
-    for n in range(8):
-        grams[n * width : (n + 1) * width, :] = (
-            mine * (1.0 / members) if n == 0 else total * (1.0 / (members * groups))
-        )
-    to_lanes(grams, work, width, 8)
-    factor_lanes(work, width)
-    from_lanes(work, factors, width, 8)
-    group_factor[...] = factors[0:width, 0:width]
-    root_factor[...] = factors[width : 2 * width, 0:width]
+    lax.fori_loop(0, own // 2, far_pair, 0, unroll=4)
 
 
 def shift(block, distance):
@@ -402,7 +418,7 @@
     columns = vectors.shape[1]
     halo = LAYER * width
     total = own + 2 * PAD
-    groups = lax.axis_size("group")
+    members, groups = lax.axis_size("sub"), lax.axis_size("group")
     vmem = pl.BlockSpec(memory_space=pltpu.VMEM)
     smem = pl.BlockSpec(memory_space=pltpu.SMEM)
     hbm = pl.BlockSpec(memory_space=pl.ANY)
@@ -410,9 +426,9 @@
     sent = jax.ShapeDtypeStruct((halo + width + 32, columns), BF16)
     basis = leaf_basis.T
 
-    hot, top, to_next, to_prev = pl.pallas_call(
+    fan, top, to_next, to_prev = pl.pallas_call(
         tree_kernel,
-        out_shape=(jax.ShapeDtypeStruct((groups * width, width), F32), square, sent, sent),
+        out_shape=(jax.ShapeDtypeStruct((members, width // 2, 2 * width), F32), square, sent, sent),
         in_specs=[vmem, vmem, vmem, vmem, hbm],
         out_specs=(vmem, vmem, vmem, vmem),
         scratch_shapes=[pltpu.SemaphoreType.DMA((2,))],
@@ -421,19 +437,24 @@
     )(basis, inner_transfer.T, device_transfer, points, vectors)
     left = shift(to_next, 1)
     right = shift(to_prev, -1)
-    sums = lax.psum(hot, AXES)
-
-    near, coupling, device_factor = pl.pallas_call(
+    fan = lax.all_to_all(fan, "sub", 0, 0, tiled=True)
+    gram = jnp.broadcast_to(jnp.sum(fan, axis=0, keepdims=True), (groups, *fan.shape[1:]))
+    sums = lax.all_to_all(gram, "group", 0, 0, tiled=True)
+
+    near, coupling, device_factor, group_factor, root_factor = pl.pallas_call(
         main_kernel,
         out_shape=(
             jax.ShapeDtypeStruct(vectors.shape, BF16),
             jax.ShapeDtypeStruct((width, own * far_index.shape[1] * width), BF16),
             square,
+            square,
+            square,
         ),
-        in_specs=[vmem] * 4 + [smem] + [vmem] * 4 + [hbm],
-        out_specs=(vmem, vmem, vmem),
+        in_specs=[vmem] * 4 + [smem] + [vmem] * 3 + [hbm] * 3,
+        out_specs=(vmem,) * 5,
         scratch_shapes=[
             pltpu.VMEM((own * width + 2 * halo, columns), BF16),
+            pltpu.VMEM((2, width + 32, columns), BF16),
             pltpu.VMEM((8, total * width), F32),
             pltpu.VMEM((own * width, 64), BF16),
             pltpu.VMEM((total * width, 128), BF16),
@@ -445,7 +466,7 @@
             pltpu.VMEM((total * width, 2 * width), F32),
             pltpu.VMEM((total * width, 2 * width), BF16),
             pltpu.VMEM((total * width, 2 * width), BF16),
-            pltpu.SemaphoreType.DMA,
+            pltpu.SemaphoreType.DMA((5,)),
         ],
         compiler_params=BIG,
         name="leaves",
@@ -456,25 +477,12 @@
         near_count.reshape(1, own),
         far_index.T,
         top,
+        sums,
         device_transfer,
         left,
         right,
         vectors,
     )
-
-    group_factor, root_factor = pl.pallas_call(
-        upper_kernel,
-        out_shape=(square, square),
-        in_specs=[vmem],
-        out_specs=(vmem, vmem),
-        scratch_shapes=[
-            pltpu.VMEM((8 * width, width), F32),
-            pltpu.VMEM((width, width, 128), F32),
-            pltpu.VMEM((8 * width, 2 * width), F32),
-        ],
-        compiler_params=BIG,
-        name="upper",
-    )(sums)
     return near, coupling.T, device_factor, group_factor, root_factor
 
 

time: 177 us -> 53 us (0.30)
  waiting for transfers between devices: 127 us -> 0.01 us
  blocking collectives: 0 us -> 24.5 us
  between operations: 14.1 us -> 0.68 us
  Pallas kernels: 31.2 us -> 23 us
    psum x1 -> x0, waiting for transfers between devices: 127 us -> none  [per_device(): sums = lax.psum(hot, AXES)]
    all_to_all x0 -> x2, blocking collectives: none -> 24.5 us  [the longest x1 12.6 us: per_device(): fan = lax.all_to_all(fan, 'sub', 0, 0, tiled=True)]
    pallas_call x2 -> x1, Pallas kernels: 9.71 us -> 3.87 us  [per_device(): pl.pallas_call(tree_kernel, out_shape=(jax.ShapeDtypeStruct((members, wid...]
    pallas_call x1, Pallas kernels: 21.4 us -> 19.2 us  [per_device(): pl.pallas_call(main_kernel, out_shape=(jax.ShapeDtypeStruct(vectors.shape...]
  transfers between devices with their start and end apart: 3 -> 2, of which waited for: 1 -> 0; matrix products, arithmetic and copies ran while one was open for 0% -> 0% of each run, Pallas kernels for 3% -> 0%
where the time goes in v1:
time: 53 us; the launch traced here: 52.7 us
  blocking collectives  24.5 us (46%)
  Pallas kernels  23 us (43%)
  starting transfers between devices  3.67 us (7%)
  local copies, waits for them, and re-layouts  0.79 us (1%)
  between operations  0.68 us (1%)
    pallas_call x1, Pallas kernels, per_device(): pl.pallas_call(main_kernel, out_shape=(jax.ShapeDtypeStruct(vectors.shape...  19.2 us
    all_to_all x1, blocking collectives, per_device(): fan = lax.all_to_all(fan, 'sub', 0, 0, tiled=True)  12.6 us
    all_to_all x1, blocking collectives, per_device(): sums = lax.all_to_all(gram, 'group', 0, 0, tiled=True)  11.9 us
    pallas_call x1, Pallas kernels, per_device(): pl.pallas_call(tree_kernel, out_shape=(jax.ShapeDtypeStruct((members, wid...  3.87 us
    ppermute x2, starting transfers between devices, shift(): return lax.ppermute(block, AXES, route)  3.67 us
  transfers between devices with their start and end apart: 2, of which 0 were waited for; matrix products, arithmetic and copies ran while one was open for 0% of the time, Pallas kernels for 0%

profile of v1, /device:TPU:0, one launch (start us, length us, event | category | flops | bytes accessed | tf_op | source)
XLA Modules:
  0.0 52.7 jit_solution(12813425541026013689)
XLA Ops:
  0.6 3.9 %tree.1 = (f32[8,32,128]{2,1,0:T(8,128)}, f32[64,64]{1,0:T(8,128)}, bf16[352,384]{1,0:T(8,128)(2,1)}, bf16[352,384]{1,0:T(8,128)(2,1)}) custom-call(bf16[64,2048]{1,0:T(8,128)(2,1)} %bitcast.6, bf16[64,1920]{1,0:T(8,128)(2,1)} %bitcast.8, f32[64,64]{1,0:T(8,128)} %transfer.3, f32[3,2048]{1,0:T(4,128)} %points.3, bf16[2048,384]{1,0:T(8,128)(2,1)} %vectors.3), custom_call_target="tpu_custom_call" | custom-call | tf_op jit(solution)/shard_map/tree/pallas_call | solution.py:429
  4.5 2.4 %collective-permute-start = (bf16[352,384]{1,0:T(8,128)(2,1)}, bf16[352,384]{1,0:T(8,128)(2,1)S(1)}, u32[]{:S(2)}, u32[]{:S(2)}) collective-permute-start(bf16[352,384]{1,0:T(8,128)(2,1)} %get-tuple-element.16), channel_id=1, source_target_pairs={{0,1},{1,2},{2,3},{3,4},{4,5},{5,6},{6,7},{7,8},{8,9},{9,10},{10,1... | collective-permute-start | bytes 811016 | tf_op jit(solution)/shard_map/ppermute | solution.py:410
  6.9 1.3 %collective-permute-start.1 = (bf16[352,384]{1,0:T(8,128)(2,1)}, bf16[352,384]{1,0:T(8,128)(2,1)S(1)}, u32[]{:S(2)}, u32[]{:S(2)}) collective-permute-start(bf16[352,384]{1,0:T(8,128)(2,1)} %get-tuple-element.17), channel_id=1, source_target_pairs={{1,0},{2,1},{3,2},{4,3},{5,4},{6,5},{7,6},{8,7},{9,8},{10,9},{11,1... | collective-permute-start | bytes 811016 | tf_op jit(solution)/shard_map/ppermute | solution.py:410
  8.2 12.6 %all_to_all.10 = f32[8,32,128]{2,1,0:T(8,128)S(1)} all-to-all(f32[8,32,128]{2,1,0:T(8,128)} %get-tuple-element.15), channel_id=1, replica_groups=mesh['group'=4,'sub'=8] {'sub'}, dimensions={0} | all-to-all | bytes 262144 | tf_op jit(solution)/shard_map/all_to_all | solution.py:440
  20.8 11.9 %all_to_all.11.sums = f32[4,32,128]{2,1,0:T(8,128)} all-to-all(f32[4,32,128]{2,1,0:T(8,128)S(1)} %broadcast_in_dim.2), channel_id=1, replica_groups=mesh['group'=4,'sub'=8] {'group'}, dimensions={0} | all-to-all | bytes 131072 | tf_op jit(solution)/shard_map/all_to_all | solution.py:442
  32.7 0.0 collective-permute-done.left
  32.7 0.0 copy-start
  32.7 0.0 collective-permute-done.1.right
  32.7 0.0 copy-start.1
  32.7 0.7 %copy-done = bf16[352,384]{1,0:T(8,128)(2,1)} copy-done((bf16[352,384]{1,0:T(8,128)(2,1)}, bf16[352,384]{1,0:T(8,128)(2,1)S(1)}, u32[]{:S(2)}) %copy-start) | copy-done | bytes 270360
  33.4 0.1 copy-done.1
  33.5 19.2 %leaves.1 = (bf16[2048,384]{1,0:T(8,128)(2,1)}, bf16[64,6144]{1,0:T(8,128)(2,1)}, f32[64,64]{1,0:T(8,128)}, f32[64,64]{1,0:T(8,128)}, f32[64,64]{1,0:T(8,128)}) custom-call(f32[3,2048]{1,0:T(4,128)} %points.3, bf16[64,2048]{1,0:T(8,128)(2,1)} %bitcast.7, s32[12,32]{1,0:T(8,128)} %bitcast.9, s32[1,32]{1,0:T(1,128)} %bitcast.11, s32[3,32]{1,0:T(4,128)} %bitcast.10, ...), custom_call_target="tpu_custom_call" | custom-call | tf_op jit(solution)/shard_map/leaves/pallas_call | solution.py:444
  (2 shorter events, 0.0 us)
Async XLA Ops:
  4.5 28.2 %collective-permute-start = (bf16[352,384]{1,0:T(8,128)(2,1)}, bf16[352,384]{1,0:T(8,128)(2,1)S(1)}, u32[]{:S(2)}, u32[]{:S(2)}) collective-permute-start(bf16[352,384]{1,0:T(8,128)(2,1)} %get-tuple-element.16), channel_id=1, source_target_pairs={{0,1},{1,2},{2,3},{3,4},{4,5},{5,6},{6,7},{7,8},{8,9},{9,10},{10,1... | collective-permute-start | bytes 811016 | tf_op jit(solution)/shard_map/ppermute | solution.py:410
  6.9 25.8 %collective-permute-start.1 = (bf16[352,384]{1,0:T(8,128)(2,1)}, bf16[352,384]{1,0:T(8,128)(2,1)S(1)}, u32[]{:S(2)}, u32[]{:S(2)}) collective-permute-start(bf16[352,384]{1,0:T(8,128)(2,1)} %get-tuple-element.17), channel_id=1, source_target_pairs={{1,0},{2,1},{3,2},{4,3},{5,4},{6,5},{7,6},{8,7},{9,8},{10,9},{11,1... | collective-permute-start | bytes 811016 | tf_op jit(solution)/shard_map/ppermute | solution.py:410
  32.7 0.7 %copy-start = (bf16[352,384]{1,0:T(8,128)(2,1)}, bf16[352,384]{1,0:T(8,128)(2,1)S(1)}, u32[]{:S(2)}) copy-start(bf16[352,384]{1,0:T(8,128)(2,1)S(1)} %collective-permute-done.left) | copy-start | bytes 811012
  32.7 0.8 %copy-start.1 = (bf16[352,384]{1,0:T(8,128)(2,1)}, bf16[352,384]{1,0:T(8,128)(2,1)S(1)}, u32[]{:S(2)}) copy-start(bf16[352,384]{1,0:T(8,128)(2,1)S(1)} %collective-permute-done.1.right) | copy-start | bytes 811012

commit v2 on v1

--- a/solution.py
+++ b/solution.py
@@ -11,12 +11,16 @@
 PAD = 8
 LONG_SQ = 2.25
 RATIO = 25.0
-SCALE = 0.5 / LONG_SQ / math.log(2.0)
+SCALE = 0.5 / LONG_SQ
+HALF = math.log(0.5)
 OFF = -16384.0
 AXES = ("group", "sub")
 F32 = jnp.float32
 BF16 = jnp.bfloat16
-BIG = pltpu.CompilerParams(vmem_limit_bytes=56 * 1024 * 1024)
+
+
+def room(megabytes):
+    return pltpu.CompilerParams(vmem_limit_bytes=megabytes * 1024 * 1024)
 
 
 def split2(value):
@@ -47,7 +51,7 @@
     return lax.broadcasted_iota(jnp.int32, shape, dim)
 
 
-def tree_kernel(basis, inner, transfer, points, vectors, fan, top, to_next, to_prev, sems):
+def tree_kernel(basis, inner, transfer, points, vectors, dense, top, to_next, to_prev, sems):
     width = basis.shape[0]
     count = basis.shape[1] // width
     halo = LAYER * width
@@ -112,8 +116,7 @@
     top[...] = top_gram
     matrix = transfer[...]
     gram = exact(exact(matrix.T, top_gram), matrix)
-    for n in range(fan.shape[0]):
-        fan[n, :, :] = jnp.concatenate([gram[: width // 2], gram[width // 2 :]], axis=1)
+    dense[...] = jnp.concatenate([gram[: width // 2], gram[width // 2 :]], axis=1)
     for copy in copies:
         copy.wait()
 
@@ -182,39 +185,34 @@
 
 
 def gaussians(exponent):
-    return jnp.exp2(exponent) + jnp.exp2(exponent * RATIO + RATIO)
-
-
-def main_kernel(
+    return jnp.exp(exponent) + jnp.exp(exponent * RATIO - RATIO * HALF)
+
+
+def leaves_kernel(
     points,
     basis,
     near_list,
     near_used,
-    far_list,
     top,
-    sums,
     transfer,
     left,
     right,
     vectors,
     near,
-    coupling,
+    high,
+    low,
+    second_rows,
+    first_cols,
     device_factor,
-    group_factor,
-    root_factor,
     wide,
     sides,
     coords,
     first_rows,
-    second_rows,
     second_cols,
-    first_cols,
     switches,
     grams,
     work,
     factors,
-    high,
-    low,
     sems,
 ):
     width = basis.shape[0]
@@ -261,7 +259,7 @@
     norm = jnp.sum(place * place, axis=0, keepdims=True) * SCALE
     first = jnp.where(sub == 3, -norm, jnp.where(sub == 4, 1.0, place))
     second = jnp.where(
-        sub == 3, 1.0, jnp.where(sub == 4, -norm - 1.0, place * (2.0 * SCALE))
+        sub == 3, 1.0, jnp.where(sub == 4, HALF - norm, place * (2.0 * SCALE))
     )
     fh, fm, fl = [v.astype(F32) for v in split3(first)]
     sh, sm, sl = [v.astype(F32) for v in split3(second)]
@@ -304,20 +302,8 @@
         for n, spot in enumerate(spots):
             piece = sides[block, 0:width, n * width : (n + 1) * width]
             grams[spot * width : (spot + 1) * width, :] = mm_nt(piece, piece)
-    members, groups = lax.axis_size("sub"), lax.axis_size("group")
-    root = sums[0, :, :]
-    for g in range(1, groups):
-        root = root + sums[g, :, :]
-    mine = sums[lax.axis_index("group"), :, :]
-    root, mine = (
-        jnp.concatenate([v[:, :width], v[:, width:]], axis=0) for v in (root, mine)
-    )
-    spare = (0, 4, total - 5, total - 1)
-    for spot, gram in zip(
-        spare,
-        (top[...], mine * (1.0 / members), root * (1.0 / (members * groups)), top[...]),
-    ):
-        grams[spot * width : (spot + 1) * width, :] = gram
+    for spot in (0, LAYER, total - LAYER - 1, total - 1):
+        grams[spot * width : (spot + 1) * width, :] = top[...]
 
     for copy in copies:
         copy.wait()
@@ -343,18 +329,50 @@
     factor_lanes(work, width, some_layers)
     from_lanes(work, factors, width, total)
     device_factor[...] = exact(factors[0:width, 0:width], transfer[...])
-    for target, spot in ((group_factor, spare[1]), (root_factor, spare[2])):
-        target[...] = factors[spot * width : (spot + 1) * width, 0:width]
     high_part, low_part = split2(factors[...])
     high[...] = high_part
     low[...] = low_part
 
-    far = far_list.shape[0]
+
+def far_kernel(
+    far_list,
+    all_grams,
+    high,
+    low,
+    second_rows,
+    first_cols,
+    coupling,
+    group_factor,
+    root_factor,
+    grams,
+    work,
+    factors,
+):
+    width = group_factor.shape[0]
+    far, own = far_list.shape
+    both = 2 * width
+    start_leaf = lax.axis_index(AXES) * own
+    members, groups = lax.axis_size("sub"), lax.axis_size("group")
+
+    group = lax.axis_index("group")
+    mine = all_grams[group * members, :, :]
+    for m in range(1, members):
+        mine = mine + all_grams[group * members + m, :, :]
+    everyone = all_grams[0, :, :]
+    for m in range(1, members * groups):
+        everyone = everyone + all_grams[m, :, :]
+    for n in range(8):
+        value = everyone * (1.0 / (members * groups)) if n else mine * (1.0 / members)
+        grams[n * width : (n + 1) * width, :] = jnp.concatenate(
+            [value[:, :width], value[:, width:]], axis=0
+        )
+    to_lanes(grams, work, width, 8)
+
     square = iota((both, both), 0) // width == iota((both, both), 1) // width
     lane_far = iota((width, both), 1) < width
     lane_wide = iota((far * width, both), 1) < width
 
-    def far_pair(index, carry):
+    def far_pair(index):
         t = 2 * index
         spots = [
             [
@@ -368,7 +386,7 @@
             for m in range(2)
         ]
         sources = jnp.where(lane_wide, picked[0], picked[1])
-        at = pl.multiple_of((PAD + t) * width, both)
+        at = (PAD + t) * width
         own_cols = first_cols[:, pl.ds(at, both)]
         zero = jnp.zeros((both, both), BF16)
         targets = jnp.where(square, jnp.concatenate([own_cols, own_cols], axis=0), zero)
@@ -397,11 +415,19 @@
         line = jnp.concatenate(
             [out[:, 0:width] for out in outs] + [out[:, width:both] for out in outs], axis=1
         )
-        where = pl.multiple_of(index * (2 * far * width), both)
-        coupling[:, pl.ds(where, 2 * far * width)] = line.astype(BF16)
-        return carry
-
-    lax.fori_loop(0, own // 2, far_pair, 0, unroll=4)
+        coupling[:, pl.ds(index * 2 * far * width, 2 * far * width)] = line.astype(BF16)
+
+    pairs = own // 2
+    panels = width // 8
+
+    def some_pairs(p):
+        for index in range(p * pairs // panels, (p + 1) * pairs // panels):
+            far_pair(index)
+
+    factor_lanes(work, width, some_pairs)
+    from_lanes(work, factors, width, 8)
+    group_factor[...] = factors[0:width, 0:width]
+    root_factor[...] = factors[width : 2 * width, 0:width]
 
 
 def shift(block, distance):
@@ -418,7 +444,6 @@
     columns = vectors.shape[1]
     halo = LAYER * width
     total = own + 2 * PAD
-    members, groups = lax.axis_size("sub"), lax.axis_size("group")
     vmem = pl.BlockSpec(memory_space=pltpu.VMEM)
     smem = pl.BlockSpec(memory_space=pltpu.SMEM)
     hbm = pl.BlockSpec(memory_space=pl.ANY)
@@ -426,63 +451,75 @@
     sent = jax.ShapeDtypeStruct((halo + width + 32, columns), BF16)
     basis = leaf_basis.T
 
-    fan, top, to_next, to_prev = pl.pallas_call(
+    dense, top, to_next, to_prev = pl.pallas_call(
         tree_kernel,
-        out_shape=(jax.ShapeDtypeStruct((members, width // 2, 2 * width), F32), square, sent, sent),
+        out_shape=(jax.ShapeDtypeStruct((width // 2, 2 * width), F32), square, sent, sent),
         in_specs=[vmem, vmem, vmem, vmem, hbm],
         out_specs=(vmem, vmem, vmem, vmem),
         scratch_shapes=[pltpu.SemaphoreType.DMA((2,))],
-        compiler_params=BIG,
+        compiler_params=room(8),
         name="tree",
     )(basis, inner_transfer.T, device_transfer, points, vectors)
     left = shift(to_next, 1)
     right = shift(to_prev, -1)
-    fan = lax.all_to_all(fan, "sub", 0, 0, tiled=True)
-    gram = jnp.broadcast_to(jnp.sum(fan, axis=0, keepdims=True), (groups, *fan.shape[1:]))
-    sums = lax.all_to_all(gram, "group", 0, 0, tiled=True)
-
-    near, coupling, device_factor, group_factor, root_factor = pl.pallas_call(
-        main_kernel,
+    all_grams = lax.all_gather(dense, AXES)
+
+    split_factors = jax.ShapeDtypeStruct((total * width, 2 * width), BF16)
+    near, high, low, second_rows, first_cols, device_factor = pl.pallas_call(
+        leaves_kernel,
         out_shape=(
             jax.ShapeDtypeStruct(vectors.shape, BF16),
-            jax.ShapeDtypeStruct((width, own * far_index.shape[1] * width), BF16),
-            square,
-            square,
+            split_factors,
+            split_factors,
+            split_factors,
+            jax.ShapeDtypeStruct((64, total * width), BF16),
             square,
         ),
-        in_specs=[vmem] * 4 + [smem] + [vmem] * 3 + [hbm] * 3,
-        out_specs=(vmem,) * 5,
+        in_specs=[vmem] * 6 + [hbm] * 3,
+        out_specs=(vmem,) * 6,
         scratch_shapes=[
             pltpu.VMEM((own * width + 2 * halo, columns), BF16),
             pltpu.VMEM((2, width + 32, columns), BF16),
             pltpu.VMEM((8, total * width), F32),
             pltpu.VMEM((own * width, 64), BF16),
-            pltpu.VMEM((total * width, 128), BF16),
             pltpu.VMEM((48, total * width), BF16),
-            pltpu.VMEM((64, total * width), BF16),
             pltpu.VMEM((own, 3 * halo), BF16),
             pltpu.VMEM((total * width, width), F32),
             pltpu.VMEM((width, width, 128), F32),
             pltpu.VMEM((total * width, 2 * width), F32),
-            pltpu.VMEM((total * width, 2 * width), BF16),
-            pltpu.VMEM((total * width, 2 * width), BF16),
             pltpu.SemaphoreType.DMA((5,)),
         ],
-        compiler_params=BIG,
+        compiler_params=room(28),
         name="leaves",
     )(
         points,
         basis,
         near_index.T,
         near_count.reshape(1, own),
-        far_index.T,
         top,
-        sums,
         device_transfer,
         left,
         right,
         vectors,
     )
+
+    coupling, group_factor, root_factor = pl.pallas_call(
+        far_kernel,
+        out_shape=(
+            jax.ShapeDtypeStruct((width, own * far_index.shape[1] * width), BF16),
+            square,
+            square,
+        ),
+        in_specs=[smem] + [vmem] * 5,
+        out_specs=(vmem,) * 3,
+        scratch_shapes=[
+            pltpu.VMEM((8 * width, width), F32),
+            pltpu.VMEM((width, width, 128), F32),
+            pltpu.VMEM((8 * width, 2 * width), F32),
+        ],
+        compiler_params=room(20),
+        name="far",
+    )(far_index.T, all_grams, high, low, second_rows, first_cols)
     return near, coupling.T, device_factor, group_factor, root_factor
 
 

time: 53 us -> 81.3 us (1.53)
  blocking collectives: 24.5 us -> 46.5 us
  local copies, waits for them, and re-layouts: 0.79 us -> 4.84 us
  Pallas kernels: 23 us -> 25.1 us
    all_gather x0 -> x1, blocking collectives: none -> 46.5 us  [per_device(): all_grams = lax.all_gather(dense, AXES)]
    all_to_all x2 -> x0, blocking collectives: 24.5 us -> none  [the longest x1 12.6 us: per_device(): fan = lax.all_to_all(fan, 'sub', 0, 0, tiled=True)]
    unnamed x4 -> x24, local copies, waits for them, and re-layouts: 0.79 us -> 4.84 us
    pallas_call x2 -> x3, Pallas kernels: 23 us -> 25.1 us  [the longest x1 11.6 us: per_device(): pl.pallas_call(leaves_kernel, out_shape=(jax.ShapeDtypeStruct(vectors.sha...]
where the time goes in v2:
time: 81.3 us; the launch traced here: 80.9 us
  blocking collectives  46.5 us (57%)
  Pallas kernels  25.1 us (31%)
  local copies, waits for them, and re-layouts  4.84 us (6%)
  starting transfers between devices  3.66 us (5%)
    all_gather x1, blocking collectives, per_device(): all_grams = lax.all_gather(dense, AXES)  46.5 us
    pallas_call x1, Pallas kernels, per_device(): pl.pallas_call(leaves_kernel, out_shape=(jax.ShapeDtypeStruct(vectors.sha...  11.6 us
    pallas_call x1, Pallas kernels, per_device(): pl.pallas_call(far_kernel, out_shape=(jax.ShapeDtypeStruct((width, own *...  11.1 us
    unnamed x24, local copies, waits for them, and re-layouts  4.84 us
    ppermute x2, starting transfers between devices, shift(): return lax.ppermute(block, AXES, route)  3.66 us
    pallas_call x1, Pallas kernels, per_device(): pl.pallas_call(tree_kernel, out_shape=(jax.ShapeDtypeStruct((width // 2,...  2.45 us
  transfers between devices with their start and end apart: 2, of which 0 were waited for; matrix products, arithmetic and copies ran while one was open for 0% of the time, Pallas kernels for 0%

profile of v2, /device:TPU:0, one launch (start us, length us, event | category | flops | bytes accessed | tf_op | source)
XLA Modules:
  0.0 80.9 jit_solution(2356953334817771220)
XLA Ops:
  0.6 0.0 copy-start.11
  0.6 0.0 copy-start
  0.7 1.4 %copy-done = bf16[2048,384]{1,0:T(8,128)(2,1)S(1)} copy-done((bf16[2048,384]{1,0:T(8,128)(2,1)S(1)}, bf16[2048,384]{1,0:T(8,128)(2,1)}, u32[]{:S(2)}) %copy-start) | copy-done | bytes 1572888
  2.1 0.0 copy-start.2
  2.1 0.9 %copy-done.2 = bf16[2048,64]{0,1:T(8,128)(2,1)S(1)} copy-done((bf16[2048,64]{0,1:T(8,128)(2,1)S(1)}, bf16[2048,64]{0,1:T(8,128)(2,1)}, u32[]{:S(2)}) %copy-start.2) | copy-done | bytes 262168
  3.0 0.0 copy-start.4
  3.0 0.9 %copy-done.4 = bf16[1920,64]{0,1:T(8,128)(2,1)S(1)} copy-done((bf16[1920,64]{0,1:T(8,128)(2,1)S(1)}, bf16[1920,64]{0,1:T(8,128)(2,1)}, u32[]{:S(2)}) %copy-start.4) | copy-done | bytes 245784
  4.0 0.0 copy-start.5
  4.0 0.8 copy-done.5
  4.7 0.0 copy-start.7
  4.7 0.8 copy-done.7
  5.5 0.0 copy-start.1
  5.5 0.0 copy-start.3
  5.5 0.0 copy-start.6
  5.5 0.0 copy-start.8
  5.5 0.0 copy-start.9
  5.5 2.4 %tree.1 = (f32[32,128]{1,0:T(8,128)S(1)}, f32[64,64]{1,0:T(8,128)S(1)}, bf16[352,384]{1,0:T(8,128)(2,1)S(1)}, bf16[352,384]{1,0:T(8,128)(2,1)S(1)}) custom-call(bf16[64,2048]{1,0:T(8,128)(2,1)S(1)} %bitcast.8, bf16[64,1920]{1,0:T(8,128)(2,1)S(1)} %bitcast.10, f32[64,64]{1,0:T(8,128)S(1)} %copy-done.7, f32[3,2048]{1,0:T(4,128)S(1)} %copy-done.5, ...), custom_call_target="tpu_custom_call" | custom-call | tf_op jit(solution)/shard_map/tree/pallas_call | solution.py:454
  7.9 0.0 copy-start.10
  8.0 2.4 %collective-permute-start = (bf16[352,384]{1,0:T(8,128)(2,1)S(1)}, bf16[352,384]{1,0:T(8,128)(2,1)S(1)}, u32[]{:S(2)}, u32[]{:S(2)}) collective-permute-start(bf16[352,384]{1,0:T(8,128)(2,1)S(1)} %get-tuple-element.19), channel_id=1, source_target_pairs={{0,1},{1,2},{2,3},{3,4},{4,5},{5,6},{6,7},{7,8},{8,9},{9,10},{10,1... | collective-permute-start | bytes 811016 | tf_op jit(solution)/shard_map/ppermute | solution.py:436
  10.3 1.3 %collective-permute-start.1 = (bf16[352,384]{1,0:T(8,128)(2,1)S(1)}, bf16[352,384]{1,0:T(8,128)(2,1)S(1)}, u32[]{:S(2)}, u32[]{:S(2)}) collective-permute-start(bf16[352,384]{1,0:T(8,128)(2,1)S(1)} %get-tuple-element.20), channel_id=1, source_target_pairs={{1,0},{2,1},{3,2},{4,3},{5,4},{6,5},{7,6},{8,7},{9,8},{10,9},{11,1... | collective-permute-start | bytes 811016 | tf_op jit(solution)/shard_map/ppermute | solution.py:436
  11.6 46.5 %all-gather = f32[1024,128]{1,0:T(8,128)S(1)} all-gather(f32[32,128]{1,0:T(8,128)S(1)} %get-tuple-element.22), channel_id=2, replica_groups=mesh['group'=4,'sub'=8] {'group','sub'}, dimensions={0}, use_global_device_ids=true | all-gather | bytes 540672 | tf_op jit(solution)/shard_map/all_gather | solution.py:465
  58.2 0.0 collective-permute-done.left
  58.2 0.0 collective-permute-done.1.right
  58.2 0.0 copy-done.11
  58.2 0.0 copy-done.1
  58.2 0.0 copy-done.3
  58.2 0.0 copy-done.6
  58.2 0.0 copy-done.8
  58.2 0.0 copy-done.9
  58.2 11.6 %leaves.1 = (bf16[2048,384]{1,0:T(8,128)(2,1)}, bf16[3072,128]{1,0:T(8,128)(2,1)S(1)}, bf16[3072,128]{1,0:T(8,128)(2,1)S(1)}, bf16[3072,128]{1,0:T(8,128)(2,1)S(...) custom-call(f32[3,2048]{1,0:T(4,128)S(1)} %copy-done.6, bf16[64,2048]{1,0:T(8,128)(2,1)S(1)} %bitcast.9, ...), custom_call_target="tpu_custom_call" | custom-call | tf_op jit(solution)/shard_map/leaves/pallas_call | solution.py:468
  69.8 0.0 copy-done.10
  69.8 11.1 %far.1 = (bf16[64,6144]{1,0:T(8,128)(2,1)}, f32[64,64]{1,0:T(8,128)}, f32[64,64]{1,0:T(8,128)}) custom-call(s32[3,32]{1,0:T(4,128)S(1)} %bitcast.12, f32[32,32,128]{2,1,0:T(8,128)S(1)} %bitcast.7, bf16[3072,128]{1,0:T(8,128)(2,1)S(1)} %get-tuple-element.23.high, bf16[3072,128]{1,0:T(8,128)(2,1)S(1)} %get-tuple-element.24.low, ...), custom_call_target="tpu_custom_call" | custom-call | tf_op jit(solution)/shard_map/far/pallas_call | solution.py:506
Async XLA Ops:
  0.6 57.6 %copy-start.11 = (s32[32]{0:T(128)S(1)}, s32[32]{0:T(128)}, u32[]{:S(2)}) copy-start(s32[32]{0:T(128)} %param.14) | copy-start | bytes 388
  0.6 1.4 %copy-start = (bf16[2048,384]{1,0:T(8,128)(2,1)S(1)}, bf16[2048,384]{1,0:T(8,128)(2,1)}, u32[]{:S(2)}) copy-start(bf16[2048,384]{1,0:T(8,128)(2,1)} %vectors.3) | copy-start | bytes 4718596
  2.1 0.9 %copy-start.2 = (bf16[2048,64]{0,1:T(8,128)(2,1)S(1)}, bf16[2048,64]{0,1:T(8,128)(2,1)}, u32[]{:S(2)}) copy-start(bf16[2048,64]{0,1:T(8,128)(2,1)} %param.9) | copy-start | bytes 786436
  3.0 0.9 %copy-start.4 = (bf16[1920,64]{0,1:T(8,128)(2,1)S(1)}, bf16[1920,64]{0,1:T(8,128)(2,1)}, u32[]{:S(2)}) copy-start(bf16[1920,64]{0,1:T(8,128)(2,1)} %param.10) | copy-start | bytes 737284
  4.0 0.8 copy-start.5
  4.7 0.8 copy-start.7
  5.5 52.7 %copy-start.1 = (bf16[2048,384]{1,0:T(8,128)(2,1)S(1)}, bf16[2048,384]{1,0:T(8,128)(2,1)}, u32[]{:S(2)}) copy-start(bf16[2048,384]{1,0:T(8,128)(2,1)} %vectors.3) | copy-start | bytes 4718596
  5.5 52.7 %copy-start.3 = (bf16[2048,64]{0,1:T(8,128)(2,1)S(1)}, bf16[2048,64]{0,1:T(8,128)(2,1)}, u32[]{:S(2)}) copy-start(bf16[2048,64]{0,1:T(8,128)(2,1)} %param.9) | copy-start | bytes 786436
  5.5 52.7 %copy-start.6 = (f32[3,2048]{1,0:T(4,128)S(1)}, f32[3,2048]{1,0:T(4,128)}, u32[]{:S(2)}) copy-start(f32[3,2048]{1,0:T(4,128)} %points.3) | copy-start | bytes 73732
  5.5 52.8 %copy-start.8 = (f32[64,64]{1,0:T(8,128)S(1)}, f32[64,64]{1,0:T(8,128)}, u32[]{:S(2)}) copy-start(f32[64,64]{1,0:T(8,128)} %transfer.3) | copy-start | bytes 49156
  5.5 52.8 %copy-start.9 = (s32[32,12]{0,1:T(8,128)S(1)}, s32[32,12]{0,1:T(8,128)}, u32[]{:S(2)}) copy-start(s32[32,12]{0,1:T(8,128)} %param.13) | copy-start | bytes 4612
  7.9 61.9 %copy-start.10 = (s32[32,3]{0,1:T(4,128)S(1)}, s32[32,3]{0,1:T(4,128)}, u32[]{:S(2)}) copy-start(s32[32,3]{0,1:T(4,128)} %param.15) | copy-start | bytes 1156
  8.0 50.2 %collective-permute-start = (bf16[352,384]{1,0:T(8,128)(2,1)S(1)}, bf16[352,384]{1,0:T(8,128)(2,1)S(1)}, u32[]{:S(2)}, u32[]{:S(2)}) collective-permute-start(bf16[352,384]{1,0:T(8,128)(2,1)S(1)} %get-tuple-element.19), channel_id=1, source_target_pairs={{0,1},{1,2},{2,3},{3,4},{4,5},{5,6},{6,7},{7,8},{8,9},{9,10},{10,1... | collective-permute-start | bytes 811016 | tf_op jit(solution)/shard_map/ppermute | solution.py:436
  10.3 47.9 %collective-permute-start.1 = (bf16[352,384]{1,0:T(8,128)(2,1)S(1)}, bf16[352,384]{1,0:T(8,128)(2,1)S(1)}, u32[]{:S(2)}, u32[]{:S(2)}) collective-permute-start(bf16[352,384]{1,0:T(8,128)(2,1)S(1)} %get-tuple-element.20), channel_id=1, source_target_pairs={{1,0},{2,1},{3,2},{4,3},{5,4},{6,5},{7,6},{8,7},{9,8},{10,9},{11,1... | collective-permute-start | bytes 811016 | tf_op jit(solution)/shard_map/ppermute | solution.py:436

commit v3 on v1

v3 whole, which is shorter than its diff:
```python
import math

import jax
import jax.numpy as jnp
from jax import lax
from jax.experimental import pallas as pl
from jax.experimental.pallas import tpu as pltpu
from jax.sharding import PartitionSpec as P

LAYER = 4
PAD = 8
LONG_SQ = 2.25
RATIO = 25.0
SCALE = 0.5 / LONG_SQ
HALF = math.log(0.5)
OFF = -16384.0
AXES = ("group", "sub")
F32 = jnp.float32
BF16 = jnp.bfloat16


def room(megabytes):
    return pltpu.CompilerParams(vmem_limit_bytes=megabytes * 1024 * 1024)


def split2(value):
    high = value.astype(BF16)
    return high, (value - high.astype(F32)).astype(BF16)


def split3(value):
    high = value.astype(BF16)
    rest = value - high.astype(F32)
    middle = rest.astype(BF16)
    return high, middle, (rest - middle.astype(F32)).astype(BF16)


def mm(left, right):
    return jnp.dot(left, right, preferred_element_type=F32)


def mm_nt(left, right):
    return lax.dot_general(left, right, (((1,), (1,)), ((), ())), preferred_element_type=F32)


def exact(left, right):
    return jnp.dot(left, right, precision=lax.Precision.HIGHEST, preferred_element_type=F32)


def iota(shape, dim):
    return lax.broadcasted_iota(jnp.int32, shape, dim)


def tree_kernel(basis, inner, transfer, points, vectors, dense, top, to_next, to_prev, sems):
    width = basis.shape[0]
    count = basis.shape[1] // width
    halo = LAYER * width
    rows = vectors.shape[0]
    copies = [
        pltpu.make_async_copy(
            vectors.at[pl.ds(start, halo), :], target.at[pl.ds(0, halo), :], sems.at[n]
        )
        for n, (start, target) in enumerate(((rows - halo, to_next), (0, to_prev)))
    ]
    for copy in copies:
        copy.start()

    for target, first, skip in ((to_next, count - PAD, 1), (to_prev, 0, 0)):
        block = basis[:, first * width : (first + PAD) * width]
        pieces = [
            block[:, (at + skip) * width : (at + skip + 3) * width] for at in (0, LAYER)
        ]
        target[halo : halo + width, :] = jnp.concatenate(pieces, axis=1)
        for n in range(2):
            start = (first + n * LAYER) * width
            coords = points[:, start : start + halo]
            high, low = split2(coords)
            base = halo + width + 16 * n
            target[base : base + 16, :] = jnp.zeros((16, target.shape[1]), BF16)
            target[base : base + 3, 0:halo] = high
            target[base + 8 : base + 11, 0:halo] = low

    both = 2 * width
    same = iota((both, both), 0) // width == iota((both, both), 1) // width
    half_block = jnp.where(same, 0.5, 0.0).astype(F32)

    def pair(index):
        return inner[:, index * both : (index + 1) * both]

    blocks = []
    for n in range(count // 4):
        stacked = jnp.concatenate(
            [basis[:, (2 * n + m) * both : (2 * n + m + 1) * both] for m in range(2)], axis=0
        )
        blocks.append(mm_nt(stacked, stacked) * half_block)
    offset = 0
    while True:
        nodes = len(blocks)
        xs, ts = [], []
        for n in range(nodes):
            t = pair(offset + n)
            parts = jnp.concatenate(split3(blocks[n]), axis=0)
            xs.append(mm(jnp.concatenate([t, t, t], axis=1), parts))
            ts.append(t)
        offset += nodes
        if nodes == 1:
            break
        blocks = []
        for n in range(nodes // 2):
            x = jnp.concatenate(split3(jnp.concatenate(xs[2 * n : 2 * n + 2], axis=0)), axis=1)
            t = jnp.concatenate(ts[2 * n : 2 * n + 2], axis=0)
            blocks.append(mm_nt(x, jnp.concatenate([t, t, t], axis=1)) * half_block)
    t = ts[0]
    x = jnp.concatenate(split3(xs[0]), axis=1)
    top_gram = mm_nt(x, jnp.concatenate([t, t, t], axis=1)) * 0.5
    top[...] = top_gram
    matrix = transfer[...]
    gram = exact(exact(matrix.T, top_gram), matrix)
    halves = jnp.concatenate([gram[: width // 2], gram[width // 2 :]], axis=1)
    dense[...] = halves
    parts = jnp.concatenate(split3(halves), axis=1)
    for target in (to_next, to_prev):
        target[halo + width + 32 :, :] = parts
    for copy in copies:
        copy.wait()


def factor_lanes(work, width, beside):
    panels = width // 8
    row = iota((8, 128), 0)

    def spread(j, i):
        return jnp.broadcast_to(work[j, i : i + 1, :], (8, 128))

    for p in range(panels):
        at = 8 * p
        tiles = list(range(p, panels))
        if p:
            for start in range(0, len(tiles), 3):
                group = tiles[start : start + 3]
                accs = [work[at + k, 8 * i : 8 * i + 8, :] for i in group for k in range(8)]

                def step(j, accs, group=group, at=at):
                    factors = [spread(j, at + k) for k in range(8)]
                    out = []
                    for n, i in enumerate(group):
                        column = work[j, 8 * i : 8 * i + 8, :]
                        out += [accs[8 * n + k] - column * factors[k] for k in range(8)]
                    return out

                accs = lax.fori_loop(0, at, step, accs, unroll=4)
                for n, i in enumerate(group):
                    for k in range(8):
                        work[at + k, 8 * i : 8 * i + 8, :] = accs[8 * n + k]
        entry = {(k, m): spread(at + k, at + m) for k in range(8) for m in range(k, 8)}
        scales = []
        for k in range(8):
            scales.append(lax.rsqrt(entry[k, k]))
            for m in range(k + 1, 8):
                entry[k, m] = entry[k, m] * scales[k]
            for m in range(k + 1, 8):
                for q in range(m, 8):
                    entry[m, q] = entry[m, q] - entry[k, m] * entry[k, q]
        for i in tiles:
            tile = [work[at + k, 8 * i : 8 * i + 8, :] for k in range(8)]
            for k in range(8):
                tile[k] = tile[k] * scales[k]
                for m in range(k + 1, 8):
                    tile[m] = tile[m] - tile[k] * entry[k, m]
            for k in range(8):
                work[at + k, 8 * i : 8 * i + 8, :] = (
                    jnp.where(row >= k, tile[k], 0.0) if i == p else tile[k]
                )
        for i in range(p):
            for k in range(8):
                work[at + k, 8 * i : 8 * i + 8, :] = jnp.zeros((8, 128), F32)
        beside(p)


def to_lanes(grams, work, width, many):
    for i in range(width):
        work[i, :, 0:many] = grams[pl.ds(i, many, stride=width), :].T


def from_lanes(work, factors, width, many):
    for j in range(width):
        column = work[j, :, 0:many]
        factors[pl.ds(j, many, stride=width), :] = jnp.concatenate([column, column], axis=0).T


def gaussians(exponent):
    return jnp.exp(exponent) + jnp.exp(exponent * RATIO - RATIO * HALF)


def features(place, leaf, center):
    sub = iota(place.shape, 0)
    corner = jnp.where(sub == 0, leaf % 2 - 1, leaf // 2 % 2 - 1)
    corner = jnp.where(sub == 2, leaf // LAYER - center, corner)
    place = jnp.where(sub < 3, place + corner.astype(F32), 0.0)
    norm = jnp.sum(place * place, axis=0, keepdims=True) * SCALE
    first = jnp.where(sub == 3, -norm, jnp.where(sub == 4, 1.0, place))
    second = jnp.where(
        sub == 3, 1.0, jnp.where(sub == 4, HALF - norm, place * (2.0 * SCALE))
    )
    fh, fm, fl = [v.astype(F32) for v in split3(first)]
    sh, sm, sl = [v.astype(F32) for v in split3(second)]
    return (
        jnp.concatenate([fh, fh, fh, fm, fm, fl], axis=0),
        jnp.concatenate([sh, sm, sl, sh, sm, sh], axis=0),
    )


def rows_of(second):
    blank = jnp.zeros((16, second.shape[1]), F32)
    return jnp.concatenate([second, blank, second, blank], axis=0).T.astype(BF16)


def near_weights(first_rows, second, switches, index, halo):
    group = index // 4 * 16
    columns = jnp.concatenate([second, switches[group : group + 16, :]], axis=0)
    return gaussians(mm(first_rows[index * halo : (index + 1) * halo, :], columns)).astype(BF16)


def prepare(points, near_list, near_used, first_rows, first_cols, second_cols, switches, place):
    rows = points.shape[1]
    own = near_list.shape[1]
    width = rows // own
    place[...] = jnp.zeros(place.shape, F32)
    place[0:3, :] = points[...]
    leaf = iota((8, rows), 1) // width
    first, second = features(place[...], leaf, own // LAYER // 2)
    hot_leaf = iota((16, rows), 1) // width
    hot = jnp.where(hot_leaf % 16 == iota((16, rows), 0), 1.0, 0.0).astype(F32)
    first = jnp.concatenate([first, hot], axis=0)
    first_cols[...] = first.astype(BF16)
    second_cols[...] = second.astype(BF16)
    first_rows[...] = first.T.astype(BF16)

    start_leaf = lax.axis_index(AXES) * own
    target = iota((1, own), 1)
    base_leaf = start_leaf + target // LAYER * LAYER - LAYER
    found = jnp.zeros((16, own), jnp.bool_)
    place_row = iota((16, own), 0)
    for n in range(near_list.shape[0]):
        spot = jnp.where(near_used[...] > n, near_list[n : n + 1, :] - base_leaf, -1)
        found = jnp.logical_or(found, place_row == spot)
    bias = jnp.where(found, 0.0, OFF).astype(F32)
    span = 3 * LAYER * width
    expand = jnp.where(iota((16, span), 0) == iota((16, span), 1) // width, 1.0, 0.0)
    switches[...] = mm(bias.T.astype(BF16), expand.astype(BF16)).astype(BF16)


def inner_layers(layers, vectors, first_rows, second_cols, switches, near, block, sems, halo):
    copies = []
    for n, index in enumerate(layers):
        around = slice((index - 1) * halo, (index + 2) * halo)
        weights = near_weights(first_rows, second_cols[:, around], switches, index, halo)
        block[n, :, :] = mm(weights, vectors[around, :]).astype(BF16)
        copies.append(
            pltpu.make_async_copy(block.at[n], near.at[pl.ds(index * halo, halo), :], sems.at[n])
        )
        copies[-1].start()
    for copy in copies:
        copy.wait()


def first_near_kernel(layers):
    def body(
        points, near_list, near_used, vectors,
        near, first_rows, first_cols, second_cols, switches, place, block, sems,
    ):
        prepare(
            points, near_list, near_used, first_rows, first_cols, second_cols, switches, place
        )
        halo = block.shape[1]
        inner_layers(layers, vectors, first_rows, second_cols, switches, near, block, sems, halo)

    return body


def next_near_kernel(layers):
    def body(after, old, first_rows, second_cols, switches, vectors, near, block, sems):
        halo = block.shape[1]
        inner_layers(layers, vectors, first_rows, second_cols, switches, near, block, sems, halo)

    return body


def leaves_kernel(
    old,
    basis,
    top,
    group_gram,
    root_gram,
    transfer,
    first_rows,
    second_cols,
    switches,
    left,
    right,
    vectors,
    near,
    high,
    low,
    second_rows,
    device_factor,
    group_factor,
    root_factor,
    ends,
    sides,
    place,
    halo_cols,
    block,
    grams,
    work,
    factors,
    sems,
    *,
    members,
    groups,
):
    width = basis.shape[0]
    own = basis.shape[1] // width
    total = own + 2 * PAD
    halo = LAYER * width
    layers = own // LAYER
    both = 2 * width
    extra = sides.shape[1]
    side_copies = [
        pltpu.make_async_copy(side.at[pl.ds(halo, extra), :], sides.at[n], sems.at[n])
        for n, side in enumerate((left, right))
    ]
    end_copies = [
        pltpu.make_async_copy(side.at[pl.ds(0, halo), :], ends.at[n], sems.at[2 + n])
        for n, side in enumerate((left, right))
    ]
    for copy in side_copies + end_copies:
        copy.start()

    lane = iota((width, both), 1)
    for n in range(own // 2):
        pair = basis[:, n * both : (n + 1) * both]
        zero = jnp.zeros_like(pair)
        stacked = jnp.concatenate(
            [jnp.where(lane < width, pair, zero), jnp.where(lane < width, zero, pair)], axis=0
        )
        at = (PAD + 2 * n) * width
        grams[at : at + both, :] = mm_nt(stacked, pair)
    spare = (0, LAYER, total - LAYER - 1, total - 1)
    for spot, gram in zip(
        spare,
        (
            top[...],
            group_gram[...] * (1.0 / members),
            root_gram[...] * (1.0 / (members * groups)),
            top[...],
        ),
    ):
        if gram.shape[0] < width:
            gram = jnp.concatenate([gram[:, :width], gram[:, width:]], axis=0)
        grams[spot * width : (spot + 1) * width, :] = gram
    for copy in side_copies:
        copy.wait()
    for side, spots in enumerate(
        ((1, 2, 3, 5, 6, 7), tuple(PAD + own + m for m in (0, 1, 2, 4, 5, 6)))
    ):
        for n, spot in enumerate(spots):
            piece = sides[side, 0:width, n * width : (n + 1) * width]
            grams[spot * width : (spot + 1) * width, :] = mm_nt(piece, piece)

    lanes = PAD * width
    place[...] = jnp.zeros(place.shape, F32)
    for side, first_leaf in enumerate((-PAD, own)):
        for n in range(2):
            base = width + 16 * n
            values = sides[side, base : base + 16, 0:halo].astype(F32)
            place[0:3, n * halo : (n + 1) * halo] = values[0:3, :] + values[8:11, :]
        leaf = iota((8, lanes), 1) // width + (first_leaf + PAD)
        second = features(place[...], leaf, layers // 2 + PAD // LAYER)[1]
        halo_cols[side, :, :] = second.astype(BF16)
        at = (PAD + first_leaf) * width
        second_rows[at : at + lanes, :] = rows_of(second)
    for n in range(own * width // 512):
        at = PAD * width + n * 512
        second_rows[at : at + 512, :] = rows_of(
            second_cols[:, n * 512 : (n + 1) * 512].astype(F32)
        )

    copies = [
        pltpu.make_async_copy(block.at[n], near.at[pl.ds(index * halo, halo), :], sems.at[4 + n])
        for n, index in enumerate((0, layers - 1))
    ]

    def edge(n):
        if n == 0:
            columns = [halo_cols[0, :, halo:], second_cols[:, 0 : 2 * halo]]
            index = 0
        else:
            columns = [second_cols[:, (layers - 2) * halo :], halo_cols[1, :, 0:halo]]
            index = layers - 1
        weights = near_weights(
            first_rows, jnp.concatenate(columns, axis=1), switches, index, halo
        )
        if n == 0:
            value = mm(weights[:, 0:halo], ends[0, :, :])
            value = value + mm(weights[:, halo:], vectors[0 : 2 * halo, :])
        else:
            value = mm(weights[:, 0 : 2 * halo], vectors[(layers - 2) * halo :, :])
            value = value + mm(weights[:, 2 * halo :], ends[1, :, :])
        block[n, :, :] = value.astype(BF16)
        copies[n].start()

    def beside(p):
        if p in (1, 3):
            edge(p // 2)

    to_lanes(grams, work, width, total)
    for copy in end_copies:
        copy.wait()
    factor_lanes(work, width, beside)
    from_lanes(work, factors, width, total)
    device_factor[...] = exact(factors[0:width, 0:width], transfer[...])
    for target, spot in ((group_factor, spare[1]), (root_factor, spare[2])):
        target[...] = factors[spot * width : (spot + 1) * width, 0:width]
    high_part, low_part = split2(factors[...])
    high[...] = high_part
    low[...] = low_part
    for copy in copies:
        copy.wait()


def far_kernel(far_list, high, low, second_rows, first_cols, coupling):
    width = coupling.shape[0]
    far, own = far_list.shape
    both = 2 * width
    start_leaf = lax.axis_index(AXES) * own
    square = iota((both, both), 0) // width == iota((both, both), 1) // width
    lane_far = iota((width, both), 1) < width
    lane_wide = iota((far * width, both), 1) < width

    def far_pair(index):
        t = 2 * index
        spots = [
            [
                pl.multiple_of((far_list[f, t + m] - start_leaf + PAD) * width, width)
                for f in range(far)
            ]
            for m in range(2)
        ]
        picked = [
            jnp.concatenate([second_rows[pl.ds(s, width), :] for s in spots[m]], axis=0)
            for m in range(2)
        ]
        sources = jnp.where(lane_wide, picked[0], picked[1])
        at = (PAD + t) * width
        own_cols = first_cols[:, t * width : t * width + both]
        zero = jnp.zeros((both, both), BF16)
        targets = jnp.where(square, jnp.concatenate([own_cols, own_cols], axis=0), zero)
        kernel_block = gaussians(mm(sources, targets))
        kh, kl = split2(kernel_block)
        rh = jnp.where(square, high[pl.ds(at, both), :], zero)
        rl = jnp.where(square, low[pl.ds(at, both), :], zero)
        half = mm_nt(
            jnp.concatenate([kh, kl, kh], axis=1), jnp.concatenate([rh, rh, rl], axis=1)
        ) * (1.0 / width)
        zh, zl = split2(half)
        outs = []
        for f in range(far):
            a = slice(f * width, (f + 1) * width)
            sh = jnp.where(
                lane_far, high[pl.ds(spots[0][f], width), :], high[pl.ds(spots[1][f], width), :]
            )
            sl = jnp.where(
                lane_far, low[pl.ds(spots[0][f], width), :], low[pl.ds(spots[1][f], width), :]
            )
            ph = jnp.where(square, jnp.concatenate([zh[a], zh[a]], axis=0), zero)
            plow = jnp.where(square, jnp.concatenate([zl[a], zl[a]], axis=0), zero)
            outs.append(
                mm(jnp.concatenate([sh, sh, sl], axis=1), jnp.concatenate([ph, plow, ph], axis=0))
            )
        line = jnp.concatenate(
            [out[:, 0:width] for out in outs] + [out[:, width:both] for out in outs], axis=1
        )
        coupling[:, pl.ds(index * 2 * far * width, 2 * far * width)] = line.astype(BF16)

    for index in range(own // 2):
        far_pair(index)


def shift(block, distance):
    devices = range(lax.axis_size(AXES))
    route = [(i - distance, i) for i in devices if i - distance in devices]
    return lax.ppermute(block, AXES, route)


def exchange(value, axis, bit):
    mask = 2**bit
    pairs = [(source, source ^ mask) for source in range(lax.axis_size(axis))]
    return value + lax.ppermute(value, axis, pairs)


def per_device(
    points, leaf_basis, inner_transfer, device_transfer, vectors, near_index, near_count, far_index
):
    own = near_index.shape[0]
    width = leaf_basis.shape[1]
    columns = vectors.shape[1]
    halo = LAYER * width
    half = width // 2
    layers = own // LAYER
    total = own + 2 * PAD
    members, groups = lax.axis_size("sub"), lax.axis_size("group")
    vmem = pl.BlockSpec(memory_space=pltpu.VMEM)
    smem = pl.BlockSpec(memory_space=pltpu.SMEM)
    hbm = pl.BlockSpec(memory_space=pl.ANY)
    square = jax.ShapeDtypeStruct((width, width), F32)
    sent = jax.ShapeDtypeStruct((halo + width + 32 + half, columns), BF16)
    product = jax.ShapeDtypeStruct(vectors.shape, BF16)
    basis = leaf_basis.T

    dense, top, to_next, to_prev = pl.pallas_call(
        tree_kernel,
        out_shape=(jax.ShapeDtypeStruct((half, 2 * width), F32), square, sent, sent),
        in_specs=[vmem, vmem, vmem, vmem, hbm],
        out_specs=(vmem, vmem, vmem, vmem),
        scratch_shapes=[pltpu.SemaphoreType.DMA((2,))],
        compiler_params=room(8),
        name="tree",
    )(basis, inner_transfer.T, device_transfer, points, vectors)
    left = shift(to_next, 1)
    right = shift(to_prev, -1)

    steps = [("sub", bit) for bit in range(1, members.bit_length() - 1)]
    steps += [("group", bit) for bit in range(groups.bit_length() - 1)]
    inner = list(range(1, layers - 1))
    chunks = [inner[:2]] + [[index] for index in inner[2:]]
    scratch = [
        pltpu.VMEM((2, halo, columns), BF16),
        pltpu.SemaphoreType.DMA((2,)),
    ]
    near, first_rows, first_cols, second_cols, switches = pl.pallas_call(
        first_near_kernel(chunks[0]),
        out_shape=(
            product,
            jax.ShapeDtypeStruct((own * width, 64), BF16),
            jax.ShapeDtypeStruct((64, own * width), BF16),
            jax.ShapeDtypeStruct((48, own * width), BF16),
            jax.ShapeDtypeStruct((own, 3 * halo), BF16),
        ),
        in_specs=[vmem] * 4,
        out_specs=(hbm,) + (vmem,) * 4,
        scratch_shapes=[pltpu.VMEM((8, own * width), F32)] + scratch,
        compiler_params=room(10),
        cost_estimate=pl.CostEstimate(
            flops=10**9, bytes_accessed=4 * 10**6, transcendentals=10**6
        ),
        name="near_0",
    )(points, near_index.T, near_count.reshape(1, own), vectors)

    odd = lax.axis_index("sub") % 2 == 1
    other = jnp.where(odd, left[halo + width + 32 :, :], right[halo + width + 32 :, :])
    parts = [other[:, n * 2 * width : (n + 1) * 2 * width].astype(F32) for n in range(3)]
    gram = dense + (parts[0] + (parts[1] + parts[2]))
    group_gram = gram
    for n, (axis, bit) in enumerate(steps):
        before = gram
        gram = exchange(gram, axis, bit)
        if axis == "sub":
            group_gram = gram
        if n + 1 < len(chunks):
            near = pl.pallas_call(
                next_near_kernel(chunks[n + 1]),
                out_shape=product,
                in_specs=[hbm, hbm] + [vmem] * 4,
                out_specs=hbm,
                scratch_shapes=scratch,
                input_output_aliases={1: 0},
                compiler_params=room(10),
                cost_estimate=pl.CostEstimate(
                    flops=10**9, bytes_accessed=4 * 10**6, transcendentals=10**6
                ),
                name=f"near_{n + 1}",
            )(before, near, first_rows, second_cols, switches, vectors)
            gram, near = lax.optimization_barrier((gram, near))

    split_factors = jax.ShapeDtypeStruct((total * width, 2 * width), BF16)
    near, high, low, second_rows, device_factor, group_factor, root_factor = pl.pallas_call(
        lambda *refs: leaves_kernel(*refs, members=members, groups=groups),
        out_shape=(product, split_factors, split_factors, split_factors, square, square, square),
        in_specs=[hbm] + [vmem] * 8 + [hbm] * 2 + [vmem],
        out_specs=(hbm,) + (vmem,) * 6,
        scratch_shapes=[
            pltpu.VMEM((2, halo, columns), BF16),
            pltpu.VMEM((2, width + 32, columns), BF16),
            pltpu.VMEM((8, PAD * width), F32),
            pltpu.VMEM((2, 48, PAD * width), BF16),
            pltpu.VMEM((2, halo, columns), BF16),
            pltpu.VMEM((total * width, width), F32),
            pltpu.VMEM((width, width, 128), F32),
            pltpu.VMEM((total * width, 2 * width), F32),
            pltpu.SemaphoreType.DMA((6,)),
        ],
        input_output_aliases={0: 0},
        compiler_params=room(24),
        name="leaves",
    )(
        near,
        basis,
        top,
        group_gram,
        gram,
        device_transfer,
        first_rows,
        second_cols,
        switches,
        left,
        right,
        vectors,
    )

    coupling = pl.pallas_call(
        far_kernel,
        out_shape=jax.ShapeDtypeStruct((width, own * far_index.shape[1] * width), BF16),
        in_specs=[smem] + [vmem] * 4,
        out_specs=vmem,
        compiler_params=room(16),
        name="far",
    )(far_index.T, high, low, second_rows, first_cols)
    return near, coupling.T, device_factor, group_factor, root_factor


def solution(mesh):
    split = P(AXES, None)
    return jax.shard_map(
        per_device,
        mesh=mesh,
        in_specs=(P(None, AXES), split, split, split, split, split, P(AXES), split),
        out_specs=(split, split, split, split, split),
        check_vma=False,
    )
```

time: 53 us -> 52.7 us (level)
  blocking collectives: 24.5 us -> 0 us
  starting transfers between devices: 3.67 us -> 17.6 us
  local copies, waits for them, and re-layouts: 0.79 us -> 4.84 us
  waiting for transfers between devices: 0.01 us -> 4.01 us
  Pallas kernels: 23 us -> 25 us
    all_to_all x2 -> x0, blocking collectives: 24.5 us -> none  [the longest x1 12.6 us: per_device(): fan = lax.all_to_all(fan, 'sub', 0, 0, tiled=True)]
    ppermute x0 -> x4, starting transfers between devices: none -> 13.9 us  [exchange(): return value + lax.ppermute(value, axis, pairs)]
    unnamed x4 -> x24, local copies, waits for them, and re-layouts: 0.79 us -> 4.84 us
    ppermute x2, waiting for transfers between devices: 0.01 us -> 2.26 us  [shift(): return lax.ppermute(block, AXES, route)]
    pallas_call x2 -> x8, Pallas kernels: 23 us -> 25 us  [the longest x1 8.4 us: per_device(): pl.pallas_call(lambda *refs: leaves_kernel(*refs, members=members, groups...]
    ppermute x0 -> x4, waiting for transfers between devices: none -> 1.75 us  [exchange(): return value + lax.ppermute(value, axis, pairs)]
  transfers between devices with their start and end apart: 2 -> 6, of which waited for: 0 -> 5; matrix products, arithmetic and copies ran while one was open for 0% -> 0% of each run, Pallas kernels for 0% -> 13%
where the time goes in v3:
time: 52.7 us; the launch traced here: 52.3 us
  Pallas kernels  25 us (47%)
  starting transfers between devices  17.6 us (33%)
  local copies, waits for them, and re-layouts  4.84 us (9%)
  waiting for transfers between devices  4.01 us (8%)
  between operations  0.82 us (2%)
    ppermute x4, starting transfers between devices, exchange(): return value + lax.ppermute(value, axis, pairs)  13.9 us
    pallas_call x1, Pallas kernels, per_device(): pl.pallas_call(lambda *refs: leaves_kernel(*refs, members=members, groups...  8.4 us
    pallas_call x1, Pallas kernels, per_device(): pl.pallas_call(far_kernel, out_shape=jax.ShapeDtypeStruct((width, own * f...  7.19 us
    pallas_call x4, Pallas kernels, per_device(): pl.pallas_call(next_near_kernel(chunks[n + 1]), out_shape=product, in_spe...  5.09 us
    unnamed x24, local copies, waits for them, and re-layouts  4.84 us
    ppermute x2, starting transfers between devices, shift(): return lax.ppermute(block, AXES, route)  3.67 us
    pallas_call x1, Pallas kernels, per_device(): pl.pallas_call(tree_kernel, out_shape=(jax.ShapeDtypeStruct((half, 2 * wi...  2.44 us
    ppermute x2, waiting for transfers between devices, shift(): return lax.ppermute(block, AXES, route)  2.26 us
  transfers between devices with their start and end apart: 6, of which 5 were waited for; matrix products, arithmetic and copies ran while one was open for 0% of the time, Pallas kernels for 13%

profile of v3, /device:TPU:0, one launch (start us, length us, event | category | flops | bytes accessed | tf_op | source)
XLA Modules:
  0.0 52.3 jit_solution(11930240955111958735)
XLA Ops:
  0.6 0.0 copy-start.11
  0.6 0.0 copy-start
  0.7 1.4 %copy-done = bf16[2048,384]{1,0:T(8,128)(2,1)S(1)} copy-done((bf16[2048,384]{1,0:T(8,128)(2,1)S(1)}, bf16[2048,384]{1,0:T(8,128)(2,1)}, u32[]{:S(2)}) %copy-start) | copy-done | bytes 1572888
  2.1 0.0 copy-start.2
  2.1 0.9 %copy-done.2 = bf16[2048,64]{0,1:T(8,128)(2,1)S(1)} copy-done((bf16[2048,64]{0,1:T(8,128)(2,1)S(1)}, bf16[2048,64]{0,1:T(8,128)(2,1)}, u32[]{:S(2)}) %copy-start.2) | copy-done | bytes 262168
  3.0 0.0 copy-start.4
  3.0 0.9 %copy-done.4 = bf16[1920,64]{0,1:T(8,128)(2,1)S(1)} copy-done((bf16[1920,64]{0,1:T(8,128)(2,1)S(1)}, bf16[1920,64]{0,1:T(8,128)(2,1)}, u32[]{:S(2)}) %copy-start.4) | copy-done | bytes 245784
  4.0 0.0 copy-start.5
  4.0 0.8 %copy-done.5 = f32[64,64]{1,0:T(8,128)S(1)} copy-done((f32[64,64]{1,0:T(8,128)S(1)}, f32[64,64]{1,0:T(8,128)}, u32[]{:S(2)}) %copy-start.5) | copy-done | bytes 16408
  4.7 0.0 copy-start.7
  4.7 0.8 %copy-done.7 = f32[3,2048]{1,0:T(4,128)S(1)} copy-done((f32[3,2048]{1,0:T(4,128)S(1)}, f32[3,2048]{1,0:T(4,128)}, u32[]{:S(2)}) %copy-start.7) | copy-done | bytes 24600
  5.5 0.0 copy-start.1
  5.5 0.0 copy-start.8
  5.5 0.0 copy-start.10
  5.5 2.4 %tree.1 = (f32[32,128]{1,0:T(8,128)S(1)}, f32[64,64]{1,0:T(8,128)S(1)}, bf16[384,384]{1,0:T(8,128)(2,1)S(1)}, bf16[384,384]{1,0:T(8,128)(2,1)S(1)}) custom-call(bf16[64,2048]{1,0:T(8,128)(2,1)S(1)} %bitcast.6, bf16[64,1920]{1,0:T(8,128)(2,1)S(1)} %bitcast.8, f32[64,64]{1,0:T(8,128)S(1)} %copy-done.5, f32[3,2048]{1,0:T(4,128)S(1)} %copy-done.7, ...), custom_call_target="tpu_custom_call" | custom-call | tf_op jit(solution)/shard_map/tree/pallas_call | solution.py:521
  7.9 2.4 %collective-permute-start = (bf16[384,384]{1,0:T(8,128)(2,1)S(1)}, bf16[384,384]{1,0:T(8,128)(2,1)S(1)}, u32[]{:S(2)}, u32[]{:S(2)}) collective-permute-start(bf16[384,384]{1,0:T(8,128)(2,1)S(1)} %get-tuple-element.30), channel_id=1, source_target_pairs={{0,1},{1,2},{2,3},{3,4},{4,5},{5,6},{6,7},{7,8},{8,9},{9,10},{10,1... | collective-permute-start | bytes 884744 | tf_op jit(solution)/shard_map/ppermute | solution.py:493
  10.3 1.3 %collective-permute-start.1 = (bf16[384,384]{1,0:T(8,128)(2,1)S(1)}, bf16[384,384]{1,0:T(8,128)(2,1)S(1)}, u32[]{:S(2)}, u32[]{:S(2)}) collective-permute-start(bf16[384,384]{1,0:T(8,128)(2,1)S(1)} %get-tuple-element.31), channel_id=1, source_target_pairs={{1,0},{2,1},{3,2},{4,3},{5,4},{6,5},{7,6},{8,7},{9,8},{10,9},{11,1... | collective-permute-start | bytes 884744 | tf_op jit(solution)/shard_map/ppermute | solution.py:493
  11.6 0.0 copy-done.11
  11.6 0.0 copy-done.1
  11.6 0.0 copy-done.8
  11.6 0.0 copy-done.10
  11.7 1.9 %near_0.1 = (bf16[2048,384]{1,0:T(8,128)(2,1)}, bf16[2048,64]{1,0:T(8,128)(2,1)S(1)}, bf16[64,2048]{1,0:T(8,128)(2,1)S(1)}, bf16[48,2048]{1,0:T(8,128)(2,1)S(1)}, bf16[32,768]{1,0:T(8,128)(2,1)S(1)}) custom-call(f32[3,2048]{1,0:T(4,128)S(1)} %copy-done.8, s32[12,32]{1,0:T(8,128)S(1)} %bitcast.10, s32[1,32]{1,0:T(1,128)S(1)} %bitcast.11, ...), custom_call_target="tpu_custom_call" | custom-call | flops 1000000000 | bytes 4000000 | tf_op jit(solution)/shard_map/near_0/pallas_call | solution.py:541
  13.6 0.0 collective-permute-done.refs_9_
  13.6 2.3 %collective-permute-done.1.refs_10_ = bf16[384,384]{1,0:T(8,128)(2,1)S(1)} collective-permute-done((bf16[384,384]{1,0:T(8,128)(2,1)S(1)}, bf16[384,384]{1,0:T(8,128)(2,1)S(1)}, u32[]{:S(2)}, u32[]{:S(2)}) %collective-permute-start.1) | collective-permute-done | bytes 294944 | tf_op jit(solution)/shard_map/ppermute | solution.py:493
  15.9 5.3 %collective-permute-start.2 = (f32[32,128]{1,0:T(8,128)S(1)}, f32[32,128]{1,0:T(8,128)S(1)}, u32[]{:S(2)}, u32[]{:S(2)}) collective-permute-start(f32[32,128]{1,0:T(8,128)S(1)} %add_add_fusion.after), channel_id=1, source_target_pairs={{0,2},{1,3},{2,0},{3,1},{4,6},{5,7},{6,4},{7,5},{8,10},{9,11},{10,... | collective-permute-start | bytes 49160 | tf_op jit(solution)/shard_map/ppermute | solution.py:499
  21.2 1.3 %near_1.1.old = bf16[2048,384]{1,0:T(8,128)(2,1)} custom-call(f32[32,128]{1,0:T(8,128)S(1)} %add_add_fusion.after, bf16[2048,384]{1,0:T(8,128)(2,1)} %get-tuple-element.32.old, bf16[2048,64]{1,0:T(8,128)(2,1)S(1)} %get-tuple-element.33.first_rows.refs_6_, bf16[48,2048]{1,0:T(8,128)(2,1)S(1)} %get-tuple-element.34.second_cols.refs_7_, ...), custom_call_target="tpu_custom_call", output_to_operand_aliasing={{}: (1, {})} | custom-call | flops 1000000000 | bytes 4000000 | tf_op jit(solution)/shard_map/near_1/pallas_call | solution.py:571
  22.4 0.4 collective-permute-done.2
  22.9 2.5 %collective-permute-start.3 = (f32[32,128]{1,0:T(8,128)S(1)}, f32[32,128]{1,0:T(8,128)S(1)}, u32[]{:S(2)}, u32[]{:S(2)}) collective-permute-start(f32[32,128]{1,0:T(8,128)S(1)} %add.29.after), channel_id=1, source_target_pairs={{0,4},{1,5},{2,6},{3,7},{4,0},{5,1},{6,2},{7,3},{8,12},{9,13},{10,... | collective-permute-start | bytes 49160 | tf_op jit(solution)/shard_map/ppermute | solution.py:499
  25.4 1.3 %near_2.1.old = bf16[2048,384]{1,0:T(8,128)(2,1)} custom-call(f32[32,128]{1,0:T(8,128)S(1)} %add.29.after, bf16[2048,384]{1,0:T(8,128)(2,1)} %near_1.1.old, bf16[2048,64]{1,0:T(8,128)(2,1)S(1)} %get-tuple-element.33.first_rows.refs_6_, bf16[48,2048]{1,0:T(8,128)(2,1)S(1)} %get-tuple-element.34.second_cols.refs_7_, ...), custom_call_target="tpu_custom_call", output_to_operand_aliasing={{}: (1, {})} | custom-call | flops 1000000000 | bytes 4000000 | tf_op jit(solution)/shard_map/near_2/pallas_call | solution.py:571
  26.7 0.4 collective-permute-done.3
  27.1 3.0 %collective-permute-start.4 = (f32[32,128]{1,0:T(8,128)S(1)}, f32[32,128]{1,0:T(8,128)S(1)}, u32[]{:S(2)}, u32[]{:S(2)}) collective-permute-start(f32[32,128]{1,0:T(8,128)S(1)} %add.30.after.refs_3_), channel_id=1, source_target_pairs={{0,8},{8,0},{16,24},{24,16},{1,9},{9,1},{17,25},{25,17},{2,10},{10... | collective-permute-start | bytes 49160 | tf_op jit(solution)/shard_map/ppermute | solution.py:499
  30.1 1.3 %near_3.1.old = bf16[2048,384]{1,0:T(8,128)(2,1)} custom-call(f32[32,128]{1,0:T(8,128)S(1)} %add.30.after.refs_3_, bf16[2048,384]{1,0:T(8,128)(2,1)} %near_2.1.old, bf16[2048,64]{1,0:T(8,128)(2,1)S(1)} %get-tuple-element.33.first_rows.refs_6_, bf16[48,2048]{1,0:T(8,128)(2,1)S(1)} %get-tuple-element.34.second_cols.refs_7_, ...), custom_call_target="tpu_custom_call", output_to_operand_aliasing={{}: (1, {})} | custom-call | flops 1000000000 | bytes 4000000 | tf_op jit(solution)/shard_map/near_3/pallas_call | solution.py:571
  31.4 0.4 collective-permute-done.4
  31.9 0.0 copy-start.3
  31.9 0.0 copy-start.6
  31.9 3.1 %collective-permute-start.5 = (f32[32,128]{1,0:T(8,128)S(1)}, f32[32,128]{1,0:T(8,128)S(1)}, u32[]{:S(2)}, u32[]{:S(2)}) collective-permute-start(f32[32,128]{1,0:T(8,128)S(1)} %add.31.after), channel_id=1, source_target_pairs={{0,16},{8,24},{16,0},{24,8},{1,17},{9,25},{17,1},{25,9},{2,18},{10... | collective-permute-start | bytes 49160 | tf_op jit(solution)/shard_map/ppermute | solution.py:499
  35.0 1.3 %near_4.1.refs_0_ = bf16[2048,384]{1,0:T(8,128)(2,1)} custom-call(f32[32,128]{1,0:T(8,128)S(1)} %add.31.after, bf16[2048,384]{1,0:T(8,128)(2,1)} %near_3.1.old, bf16[2048,64]{1,0:T(8,128)(2,1)S(1)} %get-tuple-element.33.first_rows.refs_6_, bf16[48,2048]{1,0:T(8,128)(2,1)S(1)} %get-tuple-element.34.second_cols.refs_7_, ...), custom_call_target="tpu_custom_call", output_to_operand_aliasing={{}: (1, {})} | custom-call | flops 1000000000 | bytes 4000000 | tf_op jit(solution)/shard_map/near_4/pallas_call | solution.py:571
  36.3 0.4 collective-permute-done.5
  36.7 0.0 copy-done.3
  36.7 0.0 copy-done.6
  36.7 0.0 copy-start.9
  36.7 8.4 %leaves.1 = (bf16[2048,384]{1,0:T(8,128)(2,1)}, bf16[3072,128]{1,0:T(8,128)(2,1)S(1)}, bf16[3072,128]{1,0:T(8,128)(2,1)S(1)}, bf16[3072,128]{1,0:T(8,128)(2,1)S(...) custom-call(bf16[2048,384]{1,0:T(8,128)(2,1)} %near_4.1.refs_0_, ...), custom_call_target="tpu_custom_call", output_to_operand_aliasing={{0}: (0, {})} | custom-call | tf_op jit(solution)/shard_map/leaves/pallas_call | solution.py:587
  45.1 0.0 copy-done.9
  45.1 7.2 %far.1 = bf16[64,6144]{1,0:T(8,128)(2,1)} custom-call(s32[3,32]{1,0:T(4,128)S(1)} %bitcast.9, bf16[3072,128]{1,0:T(8,128)(2,1)S(1)} %get-tuple-element.46.high, bf16[3072,128]{1,0:T(8,128)(2,1)S(1)} %get-tuple-element.47.low, bf16[3072,128]{1,0:T(8,128)(2,1)S(1)} %get-tuple-element.48.second_rows, bf16[64,2048]{1,0:T(8,128)(2,1)S(1)} %get-tuple-element.49.first_cols), custom_call_target="tpu_custom_call" | custom-call | tf_op jit(solution)/shard_map/far/pallas_call | solution.py:621
  (6 shorter events, 0.0 us)
Async XLA Ops:
  0.6 11.0 %copy-start.11 = (s32[32]{0:T(128)S(1)}, s32[32]{0:T(128)}, u32[]{:S(2)}) copy-start(s32[32]{0:T(128)} %param.14) | copy-start | bytes 388
  0.6 1.4 %copy-start = (bf16[2048,384]{1,0:T(8,128)(2,1)S(1)}, bf16[2048,384]{1,0:T(8,128)(2,1)}, u32[]{:S(2)}) copy-start(bf16[2048,384]{1,0:T(8,128)(2,1)} %refs_11_.1) | copy-start | bytes 4718596
  2.1 0.9 %copy-start.2 = (bf16[2048,64]{0,1:T(8,128)(2,1)S(1)}, bf16[2048,64]{0,1:T(8,128)(2,1)}, u32[]{:S(2)}) copy-start(bf16[2048,64]{0,1:T(8,128)(2,1)} %param.9) | copy-start | bytes 786436
  3.0 0.9 %copy-start.4 = (bf16[1920,64]{0,1:T(8,128)(2,1)S(1)}, bf16[1920,64]{0,1:T(8,128)(2,1)}, u32[]{:S(2)}) copy-start(bf16[1920,64]{0,1:T(8,128)(2,1)} %param.10) | copy-start | bytes 737284
  4.0 0.8 %copy-start.5 = (f32[64,64]{1,0:T(8,128)S(1)}, f32[64,64]{1,0:T(8,128)}, u32[]{:S(2)}) copy-start(f32[64,64]{1,0:T(8,128)} %refs_5_.1) | copy-start | bytes 49156
  4.7 0.8 %copy-start.7 = (f32[3,2048]{1,0:T(4,128)S(1)}, f32[3,2048]{1,0:T(4,128)}, u32[]{:S(2)}) copy-start(f32[3,2048]{1,0:T(4,128)} %points.3) | copy-start | bytes 73732
  5.5 6.2 %copy-start.1 = (bf16[2048,384]{1,0:T(8,128)(2,1)S(1)}, bf16[2048,384]{1,0:T(8,128)(2,1)}, u32[]{:S(2)}) copy-start(bf16[2048,384]{1,0:T(8,128)(2,1)} %refs_11_.1) | copy-start | bytes 4718596
  5.5 6.2 %copy-start.8 = (f32[3,2048]{1,0:T(4,128)S(1)}, f32[3,2048]{1,0:T(4,128)}, u32[]{:S(2)}) copy-start(f32[3,2048]{1,0:T(4,128)} %points.3) | copy-start | bytes 73732
  5.5 6.2 %copy-start.10 = (s32[32,12]{0,1:T(8,128)S(1)}, s32[32,12]{0,1:T(8,128)}, u32[]{:S(2)}) copy-start(s32[32,12]{0,1:T(8,128)} %param.13) | copy-start | bytes 4612
  7.9 5.7 %collective-permute-start = (bf16[384,384]{1,0:T(8,128)(2,1)S(1)}, bf16[384,384]{1,0:T(8,128)(2,1)S(1)}, u32[]{:S(2)}, u32[]{:S(2)}) collective-permute-start(bf16[384,384]{1,0:T(8,128)(2,1)S(1)} %get-tuple-element.30), channel_id=1, source_target_pairs={{0,1},{1,2},{2,3},{3,4},{4,5},{5,6},{6,7},{7,8},{8,9},{9,10},{10,1... | collective-permute-start | bytes 884744 | tf_op jit(solution)/shard_map/ppermute | solution.py:493
  10.3 5.6 %collective-permute-start.1 = (bf16[384,384]{1,0:T(8,128)(2,1)S(1)}, bf16[384,384]{1,0:T(8,128)(2,1)S(1)}, u32[]{:S(2)}, u32[]{:S(2)}) collective-permute-start(bf16[384,384]{1,0:T(8,128)(2,1)S(1)} %get-tuple-element.31), channel_id=1, source_target_pairs={{1,0},{2,1},{3,2},{4,3},{5,4},{6,5},{7,6},{8,7},{9,8},{10,9},{11,1... | collective-permute-start | bytes 884744 | tf_op jit(solution)/shard_map/ppermute | solution.py:493
  15.9 7.0 %collective-permute-start.2 = (f32[32,128]{1,0:T(8,128)S(1)}, f32[32,128]{1,0:T(8,128)S(1)}, u32[]{:S(2)}, u32[]{:S(2)}) collective-permute-start(f32[32,128]{1,0:T(8,128)S(1)} %add_add_fusion.after), channel_id=1, source_target_pairs={{0,2},{1,3},{2,0},{3,1},{4,6},{5,7},{6,4},{7,5},{8,10},{9,11},{10,... | collective-permute-start | bytes 49160 | tf_op jit(solution)/shard_map/ppermute | solution.py:499
  22.9 4.2 %collective-permute-start.3 = (f32[32,128]{1,0:T(8,128)S(1)}, f32[32,128]{1,0:T(8,128)S(1)}, u32[]{:S(2)}, u32[]{:S(2)}) collective-permute-start(f32[32,128]{1,0:T(8,128)S(1)} %add.29.after), channel_id=1, source_target_pairs={{0,4},{1,5},{2,6},{3,7},{4,0},{5,1},{6,2},{7,3},{8,12},{9,13},{10,... | collective-permute-start | bytes 49160 | tf_op jit(solution)/shard_map/ppermute | solution.py:499
  27.1 4.7 %collective-permute-start.4 = (f32[32,128]{1,0:T(8,128)S(1)}, f32[32,128]{1,0:T(8,128)S(1)}, u32[]{:S(2)}, u32[]{:S(2)}) collective-permute-start(f32[32,128]{1,0:T(8,128)S(1)} %add.30.after.refs_3_), channel_id=1, source_target_pairs={{0,8},{8,0},{16,24},{24,16},{1,9},{9,1},{17,25},{25,17},{2,10},{10... | collective-permute-start | bytes 49160 | tf_op jit(solution)/shard_map/ppermute | solution.py:499
  31.9 4.8 %copy-start.3 = (bf16[2048,64]{0,1:T(8,128)(2,1)S(1)}, bf16[2048,64]{0,1:T(8,128)(2,1)}, u32[]{:S(2)}) copy-start(bf16[2048,64]{0,1:T(8,128)(2,1)} %param.9) | copy-start | bytes 786436
  31.9 4.8 %copy-start.6 = (f32[64,64]{1,0:T(8,128)S(1)}, f32[64,64]{1,0:T(8,128)}, u32[]{:S(2)}) copy-start(f32[64,64]{1,0:T(8,128)} %refs_5_.1) | copy-start | bytes 49156
  31.9 4.8 %collective-permute-start.5 = (f32[32,128]{1,0:T(8,128)S(1)}, f32[32,128]{1,0:T(8,128)S(1)}, u32[]{:S(2)}, u32[]{:S(2)}) collective-permute-start(f32[32,128]{1,0:T(8,128)S(1)} %add.31.after), channel_id=1, source_target_pairs={{0,16},{8,24},{16,0},{24,8},{1,17},{9,25},{17,1},{25,9},{2,18},{10... | collective-permute-start | bytes 49160 | tf_op jit(solution)/shard_map/ppermute | solution.py:499
  36.7 8.4 %copy-start.9 = (s32[32,3]{0,1:T(4,128)S(1)}, s32[32,3]{0,1:T(4,128)}, u32[]{:S(2)}) copy-start(s32[32,3]{0,1:T(4,128)} %param.15) | copy-start | bytes 1156

commit v4 on v3

v4 whole, which is shorter than its diff:
```python
import functools
import math

import jax
import jax.numpy as jnp
from jax import lax
from jax.experimental import pallas as pl
from jax.experimental.pallas import tpu as pltpu
from jax.sharding import PartitionSpec as P

LAYER = 4
PAD = 8
LONG_SQ = 2.25
RATIO = 25.0
SCALE = 0.5 / LONG_SQ
HALF = math.log(0.5)
OFF = -16384.0
STRIDE = 72
AXES = ("group", "sub")
F32 = jnp.float32
BF16 = jnp.bfloat16


def room(megabytes):
    return pltpu.CompilerParams(vmem_limit_bytes=megabytes * 1024 * 1024)


def split2(value):
    high = value.astype(BF16)
    return high, (value - high.astype(F32)).astype(BF16)


def split3(value):
    high = value.astype(BF16)
    rest = value - high.astype(F32)
    middle = rest.astype(BF16)
    return high, middle, (rest - middle.astype(F32)).astype(BF16)


def mm(left, right):
    return jnp.dot(left, right, preferred_element_type=F32)


def mm_nt(left, right):
    return lax.dot_general(left, right, (((1,), (1,)), ((), ())), preferred_element_type=F32)


def exact(left, right):
    return jnp.dot(left, right, precision=lax.Precision.HIGHEST, preferred_element_type=F32)


def iota(shape, dim):
    return lax.broadcasted_iota(jnp.int32, shape, dim)


def tree_kernel(
    points_in, basis_in, inner_in, transfer_in, vectors,
    dense, top, to_next, to_prev, points, basis, inner, transfer, sems,
):
    width = basis.shape[0]
    count = basis.shape[1] // width
    halo = LAYER * width
    rows = vectors.shape[0]
    sides = ((to_next, rows - halo, (count - PAD) * width, 1), (to_prev, 0, 0, 0))
    basis_copy, inner_copy, points_copy, transfer_copy = loads = [
        pltpu.make_async_copy(source, target, sems.at[n])
        for n, (source, target) in enumerate(
            (
                (basis_in, basis),
                (inner_in, inner),
                (points_in, points),
                (transfer_in, transfer),
            )
        )
    ]
    copies = [
        pltpu.make_async_copy(
            vectors.at[pl.ds(start, halo), :], target.at[pl.ds(0, halo), :], sems.at[4 + n]
        )
        for n, (target, start, _, _) in enumerate(sides)
    ]
    for copy in loads + copies:
        copy.start()
    basis_copy.wait()
    points_copy.wait()
    transfer_copy.wait()

    for target, _, start, skip in sides:
        pieces = [
            basis[:, start + (at + skip) * width : start + (at + skip + 3) * width]
            for at in (0, LAYER)
        ]
        target[halo : halo + width, :] = jnp.concatenate(pieces, axis=1)
        for n in range(2):
            high, low = split2(points[:, start + n * halo : start + (n + 1) * halo])
            base = halo + width + 16 * n
            target[base : base + 16, :] = jnp.zeros((16, target.shape[1]), BF16)
            target[base : base + 3, 0:halo] = high
            target[base + 8 : base + 11, 0:halo] = low

    both = 2 * width
    same = iota((both, both), 0) // width == iota((both, both), 1) // width
    half_block = jnp.where(same, 0.5, 0.0).astype(F32)

    def pair(index):
        return inner[:, index * both : (index + 1) * both]

    blocks = []
    for n in range(count // 4):
        stacked = jnp.concatenate(
            [basis[:, (2 * n + m) * both : (2 * n + m + 1) * both] for m in range(2)], axis=0
        )
        blocks.append(mm_nt(stacked, stacked) * half_block)
    inner_copy.wait()
    offset = 0
    while True:
        nodes = len(blocks)
        xs, ts = [], []
        for n in range(nodes):
            t = pair(offset + n)
            parts = jnp.concatenate(split3(blocks[n]), axis=0)
            xs.append(mm(jnp.concatenate([t, t, t], axis=1), parts))
            ts.append(t)
        offset += nodes
        if nodes == 1:
            break
        blocks = []
        for n in range(nodes // 2):
            x = jnp.concatenate(split3(jnp.concatenate(xs[2 * n : 2 * n + 2], axis=0)), axis=1)
            t = jnp.concatenate(ts[2 * n : 2 * n + 2], axis=0)
            blocks.append(mm_nt(x, jnp.concatenate([t, t, t], axis=1)) * half_block)
    t = ts[0]
    x = jnp.concatenate(split3(xs[0]), axis=1)
    top_gram = mm_nt(x, jnp.concatenate([t, t, t], axis=1)) * 0.5
    top[...] = top_gram
    matrix = transfer[...]
    gram = exact(exact(matrix.T, top_gram), matrix)
    dense[...] = jnp.concatenate([gram[: width // 2], gram[width // 2 :]], axis=1)
    for copy in copies:
        copy.wait()


def factor_lanes(work, width, beside):
    panels = width // 8
    row = iota((8, 128), 0)

    def spread(j, i):
        return jnp.broadcast_to(work[j, i : i + 1, :], (8, 128))

    for p in range(panels):
        at = 8 * p
        tiles = list(range(p, panels))
        if p:
            for start in range(0, len(tiles), 3):
                group = tiles[start : start + 3]
                accs = [work[at + k, 8 * i : 8 * i + 8, :] for i in group for k in range(8)]

                def step(j, accs, group=group, at=at):
                    factors = [spread(j, at + k) for k in range(8)]
                    out = []
                    for n, i in enumerate(group):
                        column = work[j, 8 * i : 8 * i + 8, :]
                        out += [accs[8 * n + k] - column * factors[k] for k in range(8)]
                    return out

                accs = lax.fori_loop(0, at, step, accs, unroll=4)
                for n, i in enumerate(group):
                    for k in range(8):
                        work[at + k, 8 * i : 8 * i + 8, :] = accs[8 * n + k]
        entry = {(k, m): spread(at + k, at + m) for k in range(8) for m in range(k, 8)}
        scales = []
        for k in range(8):
            scales.append(lax.rsqrt(entry[k, k]))
            for m in range(k + 1, 8):
                entry[k, m] = entry[k, m] * scales[k]
            for m in range(k + 1, 8):
                for q in range(m, 8):
                    entry[m, q] = entry[m, q] - entry[k, m] * entry[k, q]
        for i in tiles:
            tile = [work[at + k, 8 * i : 8 * i + 8, :] for k in range(8)]
            for k in range(8):
                tile[k] = tile[k] * scales[k]
                for m in range(k + 1, 8):
                    tile[m] = tile[m] - tile[k] * entry[k, m]
            for k in range(8):
                work[at + k, 8 * i : 8 * i + 8, :] = (
                    jnp.where(row >= k, tile[k], 0.0) if i == p else tile[k]
                )
        for i in range(p):
            for k in range(8):
                work[at + k, 8 * i : 8 * i + 8, :] = jnp.zeros((8, 128), F32)
        beside(p)


def to_lanes(grams, work, width, many):
    for i in range(width):
        work[i, :, 0:many] = grams[pl.ds(i, many, stride=STRIDE), :].T


def from_lanes(work, factors, width, many):
    for j in range(width):
        column = work[j, :, 0:many]
        factors[pl.ds(j, many, stride=STRIDE), :] = jnp.concatenate([column, column], axis=0).T


def gaussians(exponent):
    return jnp.exp(exponent) + jnp.exp(exponent * RATIO - RATIO * HALF)


def features(place, leaf, center):
    sub = iota(place.shape, 0)
    corner = jnp.where(sub == 0, leaf % 2 - 1, leaf // 2 % 2 - 1)
    corner = jnp.where(sub == 2, leaf // LAYER - center, corner)
    place = jnp.where(sub < 3, place + corner.astype(F32), 0.0)
    norm = jnp.sum(place * place, axis=0, keepdims=True) * SCALE
    first = jnp.where(sub == 3, -norm, jnp.where(sub == 4, 1.0, place))
    second = jnp.where(
        sub == 3, 1.0, jnp.where(sub == 4, HALF - norm, place * (2.0 * SCALE))
    )
    fh, fm, fl = [v.astype(F32) for v in split3(first)]
    sh, sm, sl = [v.astype(F32) for v in split3(second)]
    return (
        jnp.concatenate([fh, fh, fh, fm, fm, fl], axis=0),
        jnp.concatenate([sh, sm, sl, sh, sm, sh], axis=0),
    )


def rows_of(second):
    blank = jnp.zeros((16, second.shape[1]), F32)
    return jnp.concatenate([second, blank, second, blank], axis=0).T.astype(BF16)


def near_weights(first_rows, second, switches, index, halo):
    group = index // 4 * 16
    columns = jnp.concatenate([second, switches[group : group + 16, :]], axis=0)
    return gaussians(mm(first_rows[index * halo : (index + 1) * halo, :], columns)).astype(BF16)


def prepare(
    points, near_list, near_used, first_rows, first_cols, second_cols, second_rows, switches, place
):
    rows = points.shape[1]
    own = near_list.shape[1]
    width = rows // own
    place[...] = jnp.zeros(place.shape, F32)
    place[0:3, :] = points[...]
    leaf = iota((8, rows), 1) // width
    first, second = features(place[...], leaf, own // LAYER // 2)
    hot_leaf = iota((16, rows), 1) // width
    hot = jnp.where(hot_leaf % 16 == iota((16, rows), 0), 1.0, 0.0).astype(F32)
    first = jnp.concatenate([first, hot], axis=0)
    first_cols[...] = first.astype(BF16)
    second_cols[...] = second.astype(BF16)
    first_rows[...] = first.T.astype(BF16)
    second_rows[...] = rows_of(second)

    start_leaf = lax.axis_index(AXES) * own
    target = iota((1, own), 1)
    base_leaf = start_leaf + target // LAYER * LAYER - LAYER
    found = jnp.zeros((16, own), jnp.bool_)
    place_row = iota((16, own), 0)
    for n in range(near_list.shape[0]):
        spot = jnp.where(near_used[...] > n, near_list[n : n + 1, :] - base_leaf, -1)
        found = jnp.logical_or(found, place_row == spot)
    bias = jnp.where(found, 0.0, OFF).astype(F32)
    span = 3 * LAYER * width
    expand = jnp.where(iota((16, span), 0) == iota((16, span), 1) // width, 1.0, 0.0)
    switches[...] = mm(bias.T.astype(BF16), expand.astype(BF16)).astype(BF16)


def inner_layers(layers, vectors, first_rows, second_cols, switches, out, halo):
    for n, index in enumerate(layers):
        around = slice((index - 1) * halo, (index + 2) * halo)
        weights = near_weights(first_rows, second_cols[:, around], switches, index, halo)
        out[n * halo : (n + 1) * halo, :] = mm(weights, vectors[around, :]).astype(BF16)


def far_blocks(pairs, far_list, second_rows, first_cols, out, width, base, places):
    far, own = far_list.shape
    both = 2 * width
    start_leaf = lax.axis_index(AXES) * own
    square = iota((both, both), 0) // width == iota((both, both), 1) // width
    lane = iota((far * width, both), 1) < width
    exponents = []
    for index in pairs:
        t = 2 * index
        picked = []
        for m in range(2):
            spots = [
                pl.multiple_of((far_list[f, t + m] - start_leaf + base) * width, width)
                for f in range(far)
            ]
            picked.append(
                jnp.concatenate([second_rows[pl.ds(spot, width), :] for spot in spots], axis=0)
            )
        cols = first_cols[:, t * width : t * width + both]
        targets = jnp.where(
            square, jnp.concatenate([cols, cols], axis=0), jnp.zeros((both, both), BF16)
        )
        exponents.append(mm(jnp.where(lane, picked[0], picked[1]), targets))
    for place, exponent in zip(places, exponents):
        high, low = split2(gaussians(exponent))
        at = place * far * width
        out[at : at + far * width, 0:both] = high
        out[at : at + far * width, both : 2 * both] = low


def first_chunk_kernel(layers):
    def body(
        points, near_list, near_used, vectors,
        out, first_rows, first_cols, second_cols, second_rows, switches, place,
    ):
        prepare(
            points,
            near_list,
            near_used,
            first_rows,
            first_cols,
            second_cols,
            second_rows,
            switches,
            place,
        )
        halo = LAYER * points.shape[1] // near_list.shape[1]
        inner_layers(layers, vectors, first_rows, second_cols, switches, out, halo)

    return body


def next_chunk_kernel(layers, pairs):
    def body(
        after, far_list, first_rows, first_cols, second_cols, second_rows, switches, vectors, *outs
    ):
        width = vectors.shape[0] // far_list.shape[1]
        if layers:
            inner_layers(
                layers, vectors, first_rows, second_cols, switches, outs[0], LAYER * width
            )
        if pairs:
            far_blocks(
                pairs, far_list, second_rows, first_cols, outs[-1], width, 0, range(len(pairs))
            )

    return body


def leaves_kernel(chunks, edge_pairs, members, groups, *refs):
    outer = len(chunks)
    inner_near = refs[:outer]
    (
        far_list,
        basis,
        top,
        group_gram,
        root_gram,
        transfer,
        first_rows,
        first_cols,
        second_cols,
        own_rows,
        switches,
        left,
        right,
        vectors,
        near,
        high,
        low,
        edge_blocks,
        device_factor,
        group_factor,
        root_factor,
        ends,
        sides,
        place,
        halo_cols,
        second_rows,
        block,
        grams,
        work,
        factors,
        sems,
    ) = refs[outer:]
    width = basis.shape[0]
    own = basis.shape[1] // width
    total = own + 2 * PAD
    halo = LAYER * width
    layers = own // LAYER
    both = 2 * width
    extra = sides.shape[1]
    side_copies = [
        pltpu.make_async_copy(side.at[pl.ds(halo, extra), :], sides.at[n], sems.at[n])
        for n, side in enumerate((left, right))
    ]
    end_copies = [
        pltpu.make_async_copy(side.at[pl.ds(0, halo), :], ends.at[n], sems.at[2 + n])
        for n, side in enumerate((left, right))
    ]
    near_copies = [
        pltpu.make_async_copy(
            part, near.at[pl.ds(chunk[0] * halo, len(chunk) * halo), :], sems.at[6 + n]
        )
        for n, (part, chunk) in enumerate(zip(inner_near, chunks))
    ]
    for copy in side_copies + end_copies + near_copies:
        copy.start()

    lane = iota((width, both), 1)
    for n in range(own // 2):
        pair = basis[:, n * both : (n + 1) * both]
        zero = jnp.zeros_like(pair)
        stacked = jnp.concatenate(
            [jnp.where(lane < width, pair, zero), jnp.where(lane < width, zero, pair)], axis=0
        )
        value = mm_nt(stacked, pair)
        for m in range(2):
            at = (PAD + 2 * n + m) * STRIDE
            grams[at : at + width, :] = value[m * width : (m + 1) * width]
    spare = (0, LAYER, total - LAYER - 1, total - 1)
    for spot, gram in zip(
        spare,
        (
            top[...],
            group_gram[...] * (1.0 / members),
            root_gram[...] * (1.0 / (members * groups)),
            top[...],
        ),
    ):
        if gram.shape[0] < width:
            gram = jnp.concatenate([gram[:, :width], gram[:, width:]], axis=0)
        grams[spot * STRIDE : spot * STRIDE + width, :] = gram
    for copy in side_copies:
        copy.wait()
    for side, spots in enumerate(
        ((1, 2, 3, 5, 6, 7), tuple(PAD + own + m for m in (0, 1, 2, 4, 5, 6)))
    ):
        for n, spot in enumerate(spots):
            piece = sides[side, 0:width, n * width : (n + 1) * width]
            grams[spot * STRIDE : spot * STRIDE + width, :] = mm_nt(piece, piece)

    lanes = PAD * width
    place[...] = jnp.zeros(place.shape, F32)
    for side, first_leaf in enumerate((-PAD, own)):
        for n in range(2):
            base = width + 16 * n
            values = sides[side, base : base + 16, 0:halo].astype(F32)
            place[0:3, n * halo : (n + 1) * halo] = values[0:3, :] + values[8:11, :]
        leaf = iota((8, lanes), 1) // width + (first_leaf + PAD)
        second = features(place[...], leaf, layers // 2 + PAD // LAYER)[1]
        halo_cols[side, :, :] = second.astype(BF16)
        at = (PAD + first_leaf) * width
        second_rows[at : at + lanes, :] = rows_of(second)
    second_rows[lanes : lanes + own * width, :] = own_rows[...]

    copies = [
        pltpu.make_async_copy(block.at[n], near.at[pl.ds(index * halo, halo), :], sems.at[4 + n])
        for n, index in enumerate((0, layers - 1))
    ]

    def edge(n):
        if n == 0:
            columns = [halo_cols[0, :, halo:], second_cols[:, 0 : 2 * halo]]
            index = 0
        else:
            columns = [second_cols[:, (layers - 2) * halo :], halo_cols[1, :, 0:halo]]
            index = layers - 1
        weights = near_weights(
            first_rows, jnp.concatenate(columns, axis=1), switches, index, halo
        )
        if n == 0:
            value = mm(weights[:, 0:halo], ends[0, :, :])
            value = value + mm(weights[:, halo:], vectors[0 : 2 * halo, :])
        else:
            value = mm(weights[:, 0 : 2 * halo], vectors[(layers - 2) * halo :, :])
            value = value + mm(weights[:, 2 * halo :], ends[1, :, :])
        block[n, :, :] = value.astype(BF16)
        copies[n].start()

    panels = width // 8

    def beside(p):
        if p in (1, 3):
            edge(p // 2)
        places = range(p * len(edge_pairs) // panels, (p + 1) * len(edge_pairs) // panels)
        far_blocks(
            [edge_pairs[n] for n in places],
            far_list,
            second_rows,
            first_cols,
            edge_blocks,
            width,
            PAD,
            places,
        )

    to_lanes(grams, work, width, total)
    for copy in end_copies:
        copy.wait()
    factor_lanes(work, width, beside)
    from_lanes(work, factors, width, total)
    device_factor[...] = exact(factors[0:width, 0:width], transfer[...])
    for target, spot in ((group_factor, spare[1]), (root_factor, spare[2])):
        target[...] = factors[spot * STRIDE : spot * STRIDE + width, 0:width]
    for spot in range(total):
        at = slice(spot * width, (spot + 1) * width)
        high[at, :], low[at, :] = split2(factors[spot * STRIDE : spot * STRIDE + width, :])
    for copy in copies + near_copies:
        copy.wait()


def far_kernel(plan, far_list, high, low, *refs):
    blocks, coupling = refs[:-1], refs[-1]
    width = coupling.shape[0]
    far, own = far_list.shape
    both = 2 * width
    start_leaf = lax.axis_index(AXES) * own
    square = iota((both, both), 0) // width == iota((both, both), 1) // width
    lane = iota((width, both), 1) < width
    zero = jnp.zeros((both, both), BF16)

    def diagonal(value):
        return jnp.where(square, value, zero)

    for start in range(0, own // 2, 4):
        indices = range(start, start + 4)
        halves = []
        for index in indices:
            source, place = plan[index]
            at = place * far * width
            kh = blocks[source][at : at + far * width, 0:both]
            kl = blocks[source][at : at + far * width, both : 2 * both]
            at = (PAD + 2 * index) * width
            rh = diagonal(high[at : at + both, :])
            rl = diagonal(low[at : at + both, :])
            halves.append(
                mm_nt(
                    jnp.concatenate([kh, kl, kh], axis=1), jnp.concatenate([rh, rh, rl], axis=1)
                )
            )
        outs = []
        for index, half in zip(indices, halves):
            zh, zl = split2(half * (1.0 / width))
            for f in range(far):
                spots = [
                    pl.multiple_of((far_list[f, 2 * index + m] - start_leaf + PAD) * width, width)
                    for m in range(2)
                ]
                sh, sl = (
                    jnp.where(lane, *(part[pl.ds(spot, width), :] for spot in spots))
                    for part in (high, low)
                )
                a = slice(f * width, (f + 1) * width)
                ph = diagonal(jnp.concatenate([zh[a], zh[a]], axis=0))
                plow = diagonal(jnp.concatenate([zl[a], zl[a]], axis=0))
                outs.append(
                    mm(
                        jnp.concatenate([sh, sh, sl], axis=1),
                        jnp.concatenate([ph, plow, ph], axis=0),
                    )
                )
        for n, index in enumerate(indices):
            three = outs[n * far : (n + 1) * far]
            line = jnp.concatenate(
                [out[:, 0:width] for out in three] + [out[:, width:both] for out in three], axis=1
            )
            at = index * 2 * far * width
            coupling[:, at : at + 2 * far * width] = line.astype(BF16)


def shift(block, distance):
    devices = range(lax.axis_size(AXES))
    route = [(i - distance, i) for i in devices if i - distance in devices]
    return lax.ppermute(block, AXES, route)


def exchange(value, axis, bit):
    mask = 2**bit
    pairs = [(source, source ^ mask) for source in range(lax.axis_size(axis))]
    return value + lax.ppermute(value, axis, pairs)


def per_device(
    points, leaf_basis, inner_transfer, device_transfer, vectors, near_index, near_count, far_index
):
    own = near_index.shape[0]
    width = leaf_basis.shape[1]
    columns = vectors.shape[1]
    halo = LAYER * width
    half = width // 2
    layers = own // LAYER
    total = own + 2 * PAD
    members, groups = lax.axis_size("sub"), lax.axis_size("group")
    vmem = pl.BlockSpec(memory_space=pltpu.VMEM)
    smem = pl.BlockSpec(memory_space=pltpu.SMEM)
    hbm = pl.BlockSpec(memory_space=pl.ANY)
    square = jax.ShapeDtypeStruct((width, width), F32)
    sent = jax.ShapeDtypeStruct((halo + width + 32, columns), BF16)
    basis = leaf_basis.T
    near_list, far_list = near_index.T, far_index.T
    cost = pl.CostEstimate(flops=10**9, bytes_accessed=4 * 10**6, transcendentals=10**6)

    dense, top, to_next, to_prev = pl.pallas_call(
        tree_kernel,
        out_shape=(jax.ShapeDtypeStruct((half, 2 * width), F32), square, sent, sent),
        in_specs=[hbm] * 5,
        out_specs=(vmem,) * 4,
        scratch_shapes=[
            pltpu.VMEM((3, own * width), F32),
            pltpu.VMEM((width, own * width), BF16),
            pltpu.VMEM((width, (own - 2) * width), BF16),
            pltpu.VMEM((width, width), F32),
            pltpu.SemaphoreType.DMA((6,)),
        ],
        compiler_params=room(60),
        name="tree",
    )(points, basis, inner_transfer.T, device_transfer, vectors)
    left = shift(to_next, 1)
    right = shift(to_prev, -1)

    steps = [("sub", bit) for bit in range(members.bit_length() - 1)]
    steps += [("group", bit) for bit in range(groups.bit_length() - 1)]
    chunks = [[1], [2, 3], [4, 5], [6], []]
    inner_pairs = list(range(PAD // 2, (own - PAD) // 2))
    few = len(inner_pairs) // 2 - 1
    pair_chunks = [[], [], [], inner_pairs[:few], inner_pairs[few:]]
    blocks, plan, parts = [], {}, []

    def part_shape(count):
        return jax.ShapeDtypeStruct((count * halo, columns), BF16)

    def block_shape(count):
        return jax.ShapeDtypeStruct((count * far_index.shape[1] * width, 4 * width), BF16)

    late_points, dense = lax.optimization_barrier((points, dense))
    part, *shared = pl.pallas_call(
        first_chunk_kernel(chunks[0]),
        out_shape=(
            part_shape(len(chunks[0])),
            jax.ShapeDtypeStruct((own * width, 64), BF16),
            jax.ShapeDtypeStruct((64, own * width), BF16),
            jax.ShapeDtypeStruct((48, own * width), BF16),
            jax.ShapeDtypeStruct((own * width, 128), BF16),
            jax.ShapeDtypeStruct((own, 3 * halo), BF16),
        ),
        in_specs=[vmem] * 4,
        out_specs=(vmem,) * 6,
        scratch_shapes=[pltpu.VMEM((8, own * width), F32)],
        compiler_params=room(10),
        cost_estimate=cost,
        name="chunk_0",
    )(late_points, near_list, near_count.reshape(1, own), vectors)
    parts.append(part)
    gram = group_gram = dense
    for n in range(max(len(steps), len(chunks))):
        before = gram
        if n < len(steps):
            axis, bit = steps[n]
            gram = exchange(gram, axis, bit)
            if axis == "sub":
                group_gram = gram
        if n == 0:
            gram, parts[0] = lax.optimization_barrier((gram, parts[0]))
        elif n < len(chunks):
            layer_chunk, pair_chunk = chunks[n], pair_chunks[n]
            shapes = [part_shape(len(layer_chunk))] * bool(layer_chunk)
            shapes += [block_shape(len(pair_chunk))] * bool(pair_chunk)
            outs = pl.pallas_call(
                next_chunk_kernel(layer_chunk, pair_chunk),
                out_shape=tuple(shapes),
                in_specs=[hbm, smem] + [vmem] * 6,
                out_specs=(vmem,) * len(shapes),
                compiler_params=room(10),
                cost_estimate=cost,
                name=f"chunk_{n}",
            )(before, far_list, *shared, vectors)
            gram, outs = lax.optimization_barrier((gram, outs))
            if layer_chunk:
                parts.append(outs[0])
            if pair_chunk:
                plan.update((index, (len(blocks), m)) for m, index in enumerate(pair_chunk))
                blocks.append(outs[-1])

    edge_pairs = [index for index in range(own // 2) if index not in plan]
    plan.update((index, (len(blocks), m)) for m, index in enumerate(edge_pairs))
    near_chunks = [chunk for chunk in chunks if chunk]
    split_factors = jax.ShapeDtypeStruct((total * width, 2 * width), BF16)
    near, high, low, edge_blocks, device_factor, group_factor, root_factor = pl.pallas_call(
        functools.partial(leaves_kernel, near_chunks, edge_pairs, members, groups),
        out_shape=(
            jax.ShapeDtypeStruct(vectors.shape, BF16),
            split_factors,
            split_factors,
            block_shape(len(edge_pairs)),
            square,
            square,
            square,
        ),
        in_specs=[hbm] * len(parts) + [smem] + [vmem] * 10 + [hbm] * 2 + [vmem],
        out_specs=(hbm,) + (vmem,) * 6,
        scratch_shapes=[
            pltpu.VMEM((2, halo, columns), BF16),
            pltpu.VMEM((2, width + 32, columns), BF16),
            pltpu.VMEM((8, PAD * width), F32),
            pltpu.VMEM((2, 48, PAD * width), BF16),
            pltpu.VMEM((total * width, 2 * width), BF16),
            pltpu.VMEM((2, halo, columns), BF16),
            pltpu.VMEM((total * STRIDE, width), F32),
            pltpu.VMEM((width, width, 128), F32),
            pltpu.VMEM((total * STRIDE, 2 * width), F32),
            pltpu.SemaphoreType.DMA((6 + len(parts),)),
        ],
        compiler_params=room(24),
        name="leaves",
    )(
        *parts,
        far_list,
        basis,
        top,
        group_gram,
        gram,
        device_transfer,
        *shared,
        left,
        right,
        vectors,
    )

    coupling = pl.pallas_call(
        functools.partial(far_kernel, plan),
        out_shape=jax.ShapeDtypeStruct((width, own * far_index.shape[1] * width), BF16),
        in_specs=[smem] + [vmem] * (3 + len(blocks)),
        out_specs=vmem,
        compiler_params=room(16),
        name="far",
    )(far_list, high, low, *blocks, edge_blocks)
    return near, coupling.T, device_factor, group_factor, root_factor


def solution(mesh):
    split = P(AXES, None)
    return jax.shard_map(
        per_device,
        mesh=mesh,
        in_specs=(P(None, AXES), split, split, split, split, split, P(AXES), split),
        out_specs=(split, split, split, split, split),
        check_vma=False,
    )
```

time: 52.7 us -> 43.3 us (0.82)
  local copies, waits for them, and re-layouts: 4.84 us -> 0.04 us
  starting transfers between devices: 17.6 us -> 14.2 us
  Pallas kernels: 25 us -> 22.5 us
  waiting for transfers between devices: 4.01 us -> 5.47 us
    unnamed x24 -> x18, local copies, waits for them, and re-layouts: 4.84 us -> 0.04 us
    pallas_call x7, Pallas kernels: 22.6 us -> 18.5 us  [the longest x1 9.15 us: per_device(): pl.pallas_call(functools.partial(leaves_kernel, near_chunks, edge_pairs,...]
    ppermute x4 -> x5, waiting for transfers between devices: 1.75 us -> 5.47 us  [exchange(): return value + lax.ppermute(value, axis, pairs)]
    ppermute x4 -> x5, starting transfers between devices: 13.9 us -> 11 us  [exchange(): return value + lax.ppermute(value, axis, pairs)]
    ppermute x2, waiting for transfers between devices: 2.26 us -> 0.01 us  [shift(): return lax.ppermute(block, AXES, route)]
    pallas_call x1, Pallas kernels: 2.44 us -> 3.98 us  [per_device(): pl.pallas_call(tree_kernel, out_shape=(jax.ShapeDtypeStruct((half, 2 * wi...]
  transfers between devices with their start and end apart: 6 -> 7, of which waited for: 5 -> 4; matrix products, arithmetic and copies ran while one was open for 0% -> 0% of each run, Pallas kernels for 13% -> 14%
where the time goes in v4:
time: 43.3 us; the launch traced here: 43.1 us
  Pallas kernels  22.5 us (52%)
  starting transfers between devices  14.2 us (33%)
  waiting for transfers between devices  5.47 us (13%)
  between operations  0.86 us (2%)
    ppermute x5, starting transfers between devices, exchange(): return value + lax.ppermute(value, axis, pairs)  11 us
    pallas_call x1, Pallas kernels, per_device(): pl.pallas_call(functools.partial(leaves_kernel, near_chunks, edge_pairs,...  9.15 us
    ppermute x5, waiting for transfers between devices, exchange(): return value + lax.ppermute(value, axis, pairs)  5.47 us
    pallas_call x4, Pallas kernels, per_device(): pl.pallas_call(next_chunk_kernel(layer_chunk, pair_chunk), out_shape=tupl...  5.17 us
    pallas_call x1, Pallas kernels, per_device(): pl.pallas_call(tree_kernel, out_shape=(jax.ShapeDtypeStruct((half, 2 * wi...  3.98 us
    pallas_call x1, Pallas kernels, per_device(): pl.pallas_call(functools.partial(far_kernel, plan), out_shape=jax.ShapeDt...  3.29 us
    ppermute x2, starting transfers between devices, shift(): return lax.ppermute(block, AXES, route)  3.26 us
    pallas_call x1, Pallas kernels, per_device(): pl.pallas_call(first_chunk_kernel(chunks[0]), out_shape=(part_shape(len(c...  0.87 us
  transfers between devices with their start and end apart: 7, of which 4 were waited for; matrix products, arithmetic and copies ran while one was open for 0% of the time, Pallas kernels for 14%

profile of v4, /device:TPU:0, one launch (start us, length us, event | category | flops | bytes accessed | tf_op | source)
XLA Modules:
  0.0 43.1 jit_solution(4187763652294263590)
XLA Ops:
  0.6 0.0 copy-start
  0.6 0.0 copy-start.3
  0.7 0.0 copy-start.7
  0.7 0.0 copy-start.6
  0.7 4.0 %tree.1 = (f32[32,128]{1,0:T(8,128)}, f32[64,64]{1,0:T(8,128)}, bf16[352,384]{1,0:T(8,128)(2,1)}, bf16[352,384]{1,0:T(8,128)(2,1)}) custom-call(f32[3,2048]{1,0:T(4,128)} %points, bf16[64,2048]{1,0:T(8,128)(2,1)} %bitcast.6, bf16[64,1920]{1,0:T(8,128)(2,1)} %bitcast.17, f32[64,64]{1,0:T(8,128)} %refs_9_.1, bf16[2048,384]{1,0:T(8,128)(2,1)} %refs_17_.1), custom_call_target="tpu_custom_call" | custom-call | tf_op jit(solution)/shard_map/tree/pallas_call | solution.py:601
  4.7 0.5 %collective-permute-start = (f32[32,128]{1,0:T(8,128)}, f32[32,128]{1,0:T(8,128)S(1)}, u32[]{:S(2)}, u32[]{:S(2)}) collective-permute-start(f32[32,128]{1,0:T(8,128)} %get-tuple-element.38), channel_id=1, source_target_pairs={{0,1},{1,0},{2,3},{3,2},{4,5},{5,4},{6,7},{7,6},{8,9},{9,8},{10,11... | collective-permute-start | bytes 49160 | tf_op jit(solution)/shard_map/ppermute | solution.py:578
  5.2 2.0 %collective-permute-start.5 = (bf16[352,384]{1,0:T(8,128)(2,1)}, bf16[352,384]{1,0:T(8,128)(2,1)S(1)}, u32[]{:S(2)}, u32[]{:S(2)}) collective-permute-start(bf16[352,384]{1,0:T(8,128)(2,1)} %get-tuple-element.58), channel_id=1, source_target_pairs={{0,1},{1,2},{2,3},{3,4},{4,5},{5,6},{6,7},{7,8},{8,9},{9,10},{10,1... | collective-permute-start | bytes 811016 | tf_op jit(solution)/shard_map/ppermute | solution.py:572
  7.1 1.3 %collective-permute-start.6 = (bf16[352,384]{1,0:T(8,128)(2,1)}, bf16[352,384]{1,0:T(8,128)(2,1)S(1)}, u32[]{:S(2)}, u32[]{:S(2)}) collective-permute-start(bf16[352,384]{1,0:T(8,128)(2,1)} %get-tuple-element.59), channel_id=1, source_target_pairs={{1,0},{2,1},{3,2},{4,3},{5,4},{6,5},{7,6},{8,7},{9,8},{10,9},{11,1... | collective-permute-start | bytes 811016 | tf_op jit(solution)/shard_map/ppermute | solution.py:572
  8.4 0.0 copy-done
  8.5 0.0 copy-done.3
  8.5 0.0 copy-done.7
  8.5 0.0 copy-done.6
  8.5 0.0 copy-start.8
  8.5 0.0 copy-start.5
  8.5 0.9 %chunk_0.1 = (bf16[256,384]{1,0:T(8,128)(2,1)S(1)}, bf16[2048,64]{1,0:T(8,128)(2,1)S(1)}, bf16[64,2048]{1,0:T(8,128)(2,1)S(1)}, bf16[48,2048]{1,0:T(8,128)(2,1)S...) custom-call(f32[3,2048]{1,0:T(4,128)S(1)} %copy-done.3, s32[12,32]{1,0:T(8,128)S(1)} %bitcast.14, ...), custom_call_target="tpu_custom_call" | custom-call | flops 1000000000 | bytes 4000000 | tf_op jit(solution)/shard_map/chunk_0/pallas_call | solution.py:634
  9.4 0.0 collective-permute-done
  9.4 0.0 copy-done.8
  9.4 4.9 %collective-permute-start.1 = (f32[32,128]{1,0:T(8,128)S(1)}, f32[32,128]{1,0:T(8,128)S(1)}, u32[]{:S(2)}, u32[]{:S(2)}) collective-permute-start(f32[32,128]{1,0:T(8,128)S(1)} %add.15.after), channel_id=1, source_target_pairs={{0,2},{1,3},{2,0},{3,1},{4,6},{5,7},{6,4},{7,5},{8,10},{9,11},{10,... | collective-permute-start | bytes 49160 | tf_op jit(solution)/shard_map/ppermute | solution.py:578
  14.3 0.0 copy-done.5
  14.3 1.5 %chunk_1.1.refs_1_ = bf16[512,384]{1,0:T(8,128)(2,1)S(1)} custom-call(f32[32,128]{1,0:T(8,128)S(1)} %add.15.after, s32[3,32]{1,0:T(4,128)S(1)} %bitcast.8, bf16[2048,64]{1,0:T(8,128)(2,1)S(1)} %get-tuple-element.43.first_rows.refs_10_, bf16[64,2048]{1,0:T(8,128)(2,1)S(1)} %get-tuple-element.44.first_cols.refs_11_, ...), custom_call_target="tpu_custom_call" | custom-call | flops 1000000000 | bytes 4000000 | tf_op jit(solution)/shard_map/chunk_1/pallas_call | solution.py:666
  15.8 2.6 %collective-permute-done.1 = f32[32,128]{1,0:T(8,128)S(1)} collective-permute-done((f32[32,128]{1,0:T(8,128)S(1)}, f32[32,128]{1,0:T(8,128)S(1)}, u32[]{:S(2)}, u32[]{:S(2)}) %collective-permute-start.1) | collective-permute-done | bytes 16416 | tf_op jit(solution)/shard_map/ppermute | solution.py:578
  18.4 1.4 %collective-permute-start.2 = (f32[32,128]{1,0:T(8,128)S(1)}, f32[32,128]{1,0:T(8,128)S(1)}, u32[]{:S(2)}, u32[]{:S(2)}) collective-permute-start(f32[32,128]{1,0:T(8,128)S(1)} %add.16.after), channel_id=1, source_target_pairs={{0,4},{1,5},{2,6},{3,7},{4,0},{5,1},{6,2},{7,3},{8,12},{9,13},{10,... | collective-permute-start | bytes 49160 | tf_op jit(solution)/shard_map/ppermute | solution.py:578
  19.7 1.5 %chunk_2.1.refs_2_ = bf16[512,384]{1,0:T(8,128)(2,1)S(1)} custom-call(f32[32,128]{1,0:T(8,128)S(1)} %add.16.after, s32[3,32]{1,0:T(4,128)S(1)} %bitcast.9, bf16[2048,64]{1,0:T(8,128)(2,1)S(1)} %get-tuple-element.43.first_rows.refs_10_, bf16[64,2048]{1,0:T(8,128)(2,1)S(1)} %get-tuple-element.44.first_cols.refs_11_, ...), custom_call_target="tpu_custom_call" | custom-call | flops 1000000000 | bytes 4000000 | tf_op jit(solution)/shard_map/chunk_2/pallas_call | solution.py:666
  21.3 0.8 %collective-permute-done.2 = f32[32,128]{1,0:T(8,128)S(1)} collective-permute-done((f32[32,128]{1,0:T(8,128)S(1)}, f32[32,128]{1,0:T(8,128)S(1)}, u32[]{:S(2)}, u32[]{:S(2)}) %collective-permute-start.2) | collective-permute-done | bytes 16416 | tf_op jit(solution)/shard_map/ppermute | solution.py:578
  22.1 1.6 %collective-permute-start.3 = (f32[32,128]{1,0:T(8,128)S(1)}, f32[32,128]{1,0:T(8,128)S(1)}, u32[]{:S(2)}, u32[]{:S(2)}) collective-permute-start(f32[32,128]{1,0:T(8,128)S(1)} %add.17.after.refs_7_), channel_id=1, source_target_pairs={{0,8},{8,0},{16,24},{24,16},{1,9},{9,1},{17,25},{25,17},{2,10},{10... | collective-permute-start | bytes 49160 | tf_op jit(solution)/shard_map/ppermute | solution.py:578
  23.7 1.2 %chunk_3.1 = (bf16[256,384]{1,0:T(8,128)(2,1)S(1)}, bf16[576,256]{1,0:T(8,128)(2,1)S(1)}) custom-call(f32[32,128]{1,0:T(8,128)S(1)} %add.17.after.refs_7_, s32[3,32]{1,0:T(4,128)S(1)} %bitcast.10, bf16[2048,64]{1,0:T(8,128)(2,1)S(1)} %get-tuple-element.43.first_rows.refs_10_, bf16[64,2048]{1,0:T(8,128)(2,1)S(1)} %get-tuple-element.44.first_cols.refs_11_, ...), custom_call_target="tpu_custom_call" | custom-call | flops 1000000000 | bytes 4000000 | tf_op jit(solution)/shard_map/chunk_3/pallas_call | solution.py:666
  24.9 0.9 %collective-permute-done.3 = f32[32,128]{1,0:T(8,128)S(1)} collective-permute-done((f32[32,128]{1,0:T(8,128)S(1)}, f32[32,128]{1,0:T(8,128)S(1)}, u32[]{:S(2)}, u32[]{:S(2)}) %collective-permute-start.3) | collective-permute-done | bytes 16416 | tf_op jit(solution)/shard_map/ppermute | solution.py:578
  25.9 0.0 copy-start.1
  25.9 0.0 copy-start.2
  25.9 0.0 copy-start.4
  25.9 2.6 %collective-permute-start.4 = (f32[32,128]{1,0:T(8,128)S(1)}, f32[32,128]{1,0:T(8,128)S(1)}, u32[]{:S(2)}, u32[]{:S(2)}) collective-permute-start(f32[32,128]{1,0:T(8,128)S(1)} %add.18.after), channel_id=1, source_target_pairs={{0,16},{8,24},{16,0},{24,8},{1,17},{9,25},{17,1},{25,9},{2,18},{10... | collective-permute-start | bytes 49160 | tf_op jit(solution)/shard_map/ppermute | solution.py:578
  28.5 0.9 %chunk_4.1.refs_1_ = bf16[960,256]{1,0:T(8,128)(2,1)S(1)} custom-call(f32[32,128]{1,0:T(8,128)S(1)} %add.18.after, s32[3,32]{1,0:T(4,128)S(1)} %bitcast.11, bf16[2048,64]{1,0:T(8,128)(2,1)S(1)} %get-tuple-element.43.first_rows.refs_10_, bf16[64,2048]{1,0:T(8,128)(2,1)S(1)} %get-tuple-element.44.first_cols.refs_11_, ...), custom_call_target="tpu_custom_call" | custom-call | flops 1000000000 | bytes 4000000 | tf_op jit(solution)/shard_map/chunk_4/pallas_call | solution.py:666
  29.5 1.1 %collective-permute-done.4 = f32[32,128]{1,0:T(8,128)S(1)} collective-permute-done((f32[32,128]{1,0:T(8,128)S(1)}, f32[32,128]{1,0:T(8,128)S(1)}, u32[]{:S(2)}, u32[]{:S(2)}) %collective-permute-start.4) | collective-permute-done | bytes 16416 | tf_op jit(solution)/shard_map/ppermute | solution.py:578
  30.6 0.0 collective-permute-done.5.refs_15_
  30.6 0.0 collective-permute-done.6.refs_16_
  30.6 0.0 copy-done.1
  30.6 0.0 copy-done.2
  30.6 0.0 copy-done.4
  30.6 9.2 %leaves.1 = (bf16[2048,384]{1,0:T(8,128)(2,1)}, bf16[3072,128]{1,0:T(8,128)(2,1)S(1)}, bf16[3072,128]{1,0:T(8,128)(2,1)S(1)}, bf16[1536,256]{1,0:T(8,128)(2,1)S(...) custom-call(bf16[256,384]{1,0:T(8,128)(2,1)S(1)} %get-tuple-element.41.refs_0_, ...), custom_call_target="tpu_custom_call" | custom-call | tf_op jit(solution)/shard_map/leaves/pallas_call | solution.py:686
  39.8 3.3 %far.1 = bf16[64,6144]{1,0:T(8,128)(2,1)} custom-call(s32[3,32]{1,0:T(4,128)S(1)} %bitcast.13, bf16[3072,128]{1,0:T(8,128)(2,1)S(1)} %get-tuple-element.61.high, bf16[3072,128]{1,0:T(8,128)(2,1)S(1)} %get-tuple-element.62.low, bf16[576,256]{1,0:T(8,128)(2,1)S(1)} %get-tuple-element.63.refs_0_, bf16[960,256]{1,0:T(8,128)(2,1)S(1)} %chunk_4.1.refs_1_, ...), custom_call_target="tpu_custom_call" | custom-call | tf_op jit(solution)/shard_map/far/pallas_call | solution.py:727
  (5 shorter events, 0.0 us)
Async XLA Ops:
  0.6 7.8 %copy-start = (bf16[2048,384]{1,0:T(8,128)(2,1)S(1)}, bf16[2048,384]{1,0:T(8,128)(2,1)}, u32[]{:S(2)}) copy-start(bf16[2048,384]{1,0:T(8,128)(2,1)} %refs_17_.1) | copy-start | bytes 4718596
  0.6 7.8 %copy-start.3 = (f32[3,2048]{1,0:T(4,128)S(1)}, f32[3,2048]{1,0:T(4,128)}, u32[]{:S(2)}) copy-start(f32[3,2048]{1,0:T(4,128)} %points) | copy-start | bytes 73732
  0.7 7.8 %copy-start.7 = (s32[32]{0:T(128)S(1)}, s32[32]{0:T(128)}, u32[]{:S(2)}) copy-start(s32[32]{0:T(128)} %param.14) | copy-start | bytes 388
  0.7 7.8 %copy-start.6 = (s32[32,12]{0,1:T(8,128)S(1)}, s32[32,12]{0,1:T(8,128)}, u32[]{:S(2)}) copy-start(s32[32,12]{0,1:T(8,128)} %param.13) | copy-start | bytes 4612
  4.7 4.7 %collective-permute-start = (f32[32,128]{1,0:T(8,128)}, f32[32,128]{1,0:T(8,128)S(1)}, u32[]{:S(2)}, u32[]{:S(2)}) collective-permute-start(f32[32,128]{1,0:T(8,128)} %get-tuple-element.38), channel_id=1, source_target_pairs={{0,1},{1,0},{2,3},{3,2},{4,5},{5,4},{6,7},{7,6},{8,9},{9,8},{10,11... | collective-permute-start | bytes 49160 | tf_op jit(solution)/shard_map/ppermute | solution.py:578
  5.2 25.4 %collective-permute-start.5 = (bf16[352,384]{1,0:T(8,128)(2,1)}, bf16[352,384]{1,0:T(8,128)(2,1)S(1)}, u32[]{:S(2)}, u32[]{:S(2)}) collective-permute-start(bf16[352,384]{1,0:T(8,128)(2,1)} %get-tuple-element.58), channel_id=1, source_target_pairs={{0,1},{1,2},{2,3},{3,4},{4,5},{5,6},{6,7},{7,8},{8,9},{9,10},{10,1... | collective-permute-start | bytes 811016 | tf_op jit(solution)/shard_map/ppermute | solution.py:572
  7.1 23.5 %collective-permute-start.6 = (bf16[352,384]{1,0:T(8,128)(2,1)}, bf16[352,384]{1,0:T(8,128)(2,1)S(1)}, u32[]{:S(2)}, u32[]{:S(2)}) collective-permute-start(bf16[352,384]{1,0:T(8,128)(2,1)} %get-tuple-element.59), channel_id=1, source_target_pairs={{1,0},{2,1},{3,2},{4,3},{5,4},{6,5},{7,6},{8,7},{9,8},{10,9},{11,1... | collective-permute-start | bytes 811016 | tf_op jit(solution)/shard_map/ppermute | solution.py:572
  8.5 0.9 %copy-start.8 = (f32[32,128]{1,0:T(8,128)S(1)}, f32[32,128]{1,0:T(8,128)}, u32[]{:S(2)}) copy-start(f32[32,128]{1,0:T(8,128)} %get-tuple-element.38) | copy-start | bytes 49156
  8.5 5.8 %copy-start.5 = (s32[32,3]{0,1:T(4,128)S(1)}, s32[32,3]{0,1:T(4,128)}, u32[]{:S(2)}) copy-start(s32[32,3]{0,1:T(4,128)} %param.15) | copy-start | bytes 1156
  9.4 8.9 %collective-permute-start.1 = (f32[32,128]{1,0:T(8,128)S(1)}, f32[32,128]{1,0:T(8,128)S(1)}, u32[]{:S(2)}, u32[]{:S(2)}) collective-permute-start(f32[32,128]{1,0:T(8,128)S(1)} %add.15.after), channel_id=1, source_target_pairs={{0,2},{1,3},{2,0},{3,1},{4,6},{5,7},{6,4},{7,5},{8,10},{9,11},{10,... | collective-permute-start | bytes 49160 | tf_op jit(solution)/shard_map/ppermute | solution.py:578
  18.4 3.7 %collective-permute-start.2 = (f32[32,128]{1,0:T(8,128)S(1)}, f32[32,128]{1,0:T(8,128)S(1)}, u32[]{:S(2)}, u32[]{:S(2)}) collective-permute-start(f32[32,128]{1,0:T(8,128)S(1)} %add.16.after), channel_id=1, source_target_pairs={{0,4},{1,5},{2,6},{3,7},{4,0},{5,1},{6,2},{7,3},{8,12},{9,13},{10,... | collective-permute-start | bytes 49160 | tf_op jit(solution)/shard_map/ppermute | solution.py:578
  22.1 3.7 %collective-permute-start.3 = (f32[32,128]{1,0:T(8,128)S(1)}, f32[32,128]{1,0:T(8,128)S(1)}, u32[]{:S(2)}, u32[]{:S(2)}) collective-permute-start(f32[32,128]{1,0:T(8,128)S(1)} %add.17.after.refs_7_), channel_id=1, source_target_pairs={{0,8},{8,0},{16,24},{24,16},{1,9},{9,1},{17,25},{25,17},{2,10},{10... | collective-permute-start | bytes 49160 | tf_op jit(solution)/shard_map/ppermute | solution.py:578
  25.9 4.7 %copy-start.1 = (bf16[2048,64]{0,1:T(8,128)(2,1)S(1)}, bf16[2048,64]{0,1:T(8,128)(2,1)}, u32[]{:S(2)}) copy-start(bf16[2048,64]{0,1:T(8,128)(2,1)} %param.9) | copy-start | bytes 786436
  25.9 4.8 %copy-start.2 = (f32[64,64]{1,0:T(8,128)S(1)}, f32[64,64]{1,0:T(8,128)}, u32[]{:S(2)}) copy-start(f32[64,64]{1,0:T(8,128)} %refs_9_.1) | copy-start | bytes 49156
  25.9 4.8 %copy-start.4 = (f32[64,64]{1,0:T(8,128)S(1)}, f32[64,64]{1,0:T(8,128)}, u32[]{:S(2)}) copy-start(f32[64,64]{1,0:T(8,128)} %get-tuple-element.55.refs_6_) | copy-start | bytes 49156
  25.9 4.7 %collective-permute-start.4 = (f32[32,128]{1,0:T(8,128)S(1)}, f32[32,128]{1,0:T(8,128)S(1)}, u32[]{:S(2)}, u32[]{:S(2)}) collective-permute-start(f32[32,128]{1,0:T(8,128)S(1)} %add.18.after), channel_id=1, source_target_pairs={{0,16},{8,24},{16,0},{24,8},{1,17},{9,25},{17,1},{25,9},{2,18},{10... | collective-permute-start | bytes 49160 | tf_op jit(solution)/shard_map/ppermute | solution.py:578

commit v5 on v4

--- a/solution.py
+++ b/solution.py
@@ -22,7 +22,7 @@
 
 
 def room(megabytes):
-    return pltpu.CompilerParams(vmem_limit_bytes=megabytes * 1024 * 1024)
+    return pltpu.CompilerParams(vmem_limit_bytes=int(megabytes * 1024 * 1024))
 
 
 def split2(value):
@@ -54,20 +54,22 @@
 
 
 def tree_kernel(
-    points_in, basis_in, inner_in, transfer_in, vectors,
-    dense, top, to_next, to_prev, points, basis, inner, transfer, sems,
+    points_in, basis_in, below_in, transfer_in, vectors,
+    dense, top, outer, inner, points, basis, below, transfer, sems,
 ):
     width = basis.shape[0]
     count = basis.shape[1] // width
     halo = LAYER * width
+    span = PAD * width
     rows = vectors.shape[0]
-    sides = ((to_next, rows - halo, (count - PAD) * width, 1), (to_prev, 0, 0, 0))
-    basis_copy, inner_copy, points_copy, transfer_copy = loads = [
+    odd = lax.axis_index("sub") % 2
+    sides = ((outer, odd), (inner, 1 - odd))
+    basis_copy, below_copy, points_copy, transfer_copy = loads = [
         pltpu.make_async_copy(source, target, sems.at[n])
         for n, (source, target) in enumerate(
             (
                 (basis_in, basis),
-                (inner_in, inner),
+                (below_in, below),
                 (points_in, points),
                 (transfer_in, transfer),
             )
@@ -75,9 +77,11 @@
     ]
     copies = [
         pltpu.make_async_copy(
-            vectors.at[pl.ds(start, halo), :], target.at[pl.ds(0, halo), :], sems.at[4 + n]
-        )
-        for n, (target, start, _, _) in enumerate(sides)
+            vectors.at[pl.ds(pl.multiple_of(last * (rows - halo), 16), halo), :],
+            target.at[pl.ds(0, halo), :],
+            sems.at[4 + n],
+        )
+        for n, (target, last) in enumerate(sides)
     ]
     for copy in loads + copies:
         copy.start()
@@ -85,15 +89,20 @@
     points_copy.wait()
     transfer_copy.wait()
 
-    for target, _, start, skip in sides:
-        pieces = [
-            basis[:, start + (at + skip) * width : start + (at + skip + 3) * width]
-            for at in (0, LAYER)
-        ]
-        target[halo : halo + width, :] = jnp.concatenate(pieces, axis=1)
-        for n in range(2):
-            high, low = split2(points[:, start + n * halo : start + (n + 1) * halo])
-            base = halo + width + 16 * n
+    for target, last in sides:
+        bases = basis[:, count * width - span :], basis[:, 0:span]
+        last_three, first_three = (
+            jnp.concatenate(
+                [block[:, (at + skip) * width : (at + skip + 3) * width] for at in (0, LAYER)],
+                axis=1,
+            )
+            for skip, block in zip((1, 0), bases)
+        )
+        target[halo : halo + width, :] = jnp.where(last == 1, last_three, first_three)
+        coords = jnp.where(last == 1, points[:, count * width - span :], points[:, 0:span])
+        for m in range(2):
+            high, low = split2(coords[:, m * halo : (m + 1) * halo])
+            base = halo + width + 16 * m
             target[base : base + 16, :] = jnp.zeros((16, target.shape[1]), BF16)
             target[base : base + 3, 0:halo] = high
             target[base + 8 : base + 11, 0:halo] = low
@@ -103,7 +112,7 @@
     half_block = jnp.where(same, 0.5, 0.0).astype(F32)
 
     def pair(index):
-        return inner[:, index * both : (index + 1) * both]
+        return below[:, index * both : (index + 1) * both]
 
     blocks = []
     for n in range(count // 4):
@@ -111,7 +120,7 @@
             [basis[:, (2 * n + m) * both : (2 * n + m + 1) * both] for m in range(2)], axis=0
         )
         blocks.append(mm_nt(stacked, stacked) * half_block)
-    inner_copy.wait()
+    below_copy.wait()
     offset = 0
     while True:
         nodes = len(blocks)
@@ -135,7 +144,9 @@
     top[...] = top_gram
     matrix = transfer[...]
     gram = exact(exact(matrix.T, top_gram), matrix)
-    dense[...] = jnp.concatenate([gram[: width // 2], gram[width // 2 :]], axis=1)
+    halves = jnp.concatenate([gram[: width // 2], gram[width // 2 :]], axis=1)
+    dense[...] = halves
+    inner[halo + width + 32 :, :] = jnp.concatenate(split3(halves), axis=1)
     for copy in copies:
         copy.wait()
 
@@ -149,24 +160,6 @@
 
     for p in range(panels):
         at = 8 * p
-        tiles = list(range(p, panels))
-        if p:
-            for start in range(0, len(tiles), 3):
-                group = tiles[start : start + 3]
-                accs = [work[at + k, 8 * i : 8 * i + 8, :] for i in group for k in range(8)]
-
-                def step(j, accs, group=group, at=at):
-                    factors = [spread(j, at + k) for k in range(8)]
-                    out = []
-                    for n, i in enumerate(group):
-                        column = work[j, 8 * i : 8 * i + 8, :]
-                        out += [accs[8 * n + k] - column * factors[k] for k in range(8)]
-                    return out
-
-                accs = lax.fori_loop(0, at, step, accs, unroll=4)
-                for n, i in enumerate(group):
-                    for k in range(8):
-                        work[at + k, 8 * i : 8 * i + 8, :] = accs[8 * n + k]
         entry = {(k, m): spread(at + k, at + m) for k in range(8) for m in range(k, 8)}
         scales = []
         for k in range(8):
@@ -176,7 +169,7 @@
             for m in range(k + 1, 8):
                 for q in range(m, 8):
                     entry[m, q] = entry[m, q] - entry[k, m] * entry[k, q]
-        for i in tiles:
+        for i in range(p, panels):
             tile = [work[at + k, 8 * i : 8 * i + 8, :] for k in range(8)]
             for k in range(8):
                 tile[k] = tile[k] * scales[k]
@@ -186,10 +179,21 @@
                 work[at + k, 8 * i : 8 * i + 8, :] = (
                     jnp.where(row >= k, tile[k], 0.0) if i == p else tile[k]
                 )
-        for i in range(p):
-            for k in range(8):
-                work[at + k, 8 * i : 8 * i + 8, :] = jnp.zeros((8, 128), F32)
         beside(p)
+        for q in range(p + 1, panels):
+            for start in range(q, panels, 2):
+                group = range(start, min(start + 2, panels))
+                accs = {
+                    (i, k): work[8 * q + k, 8 * i : 8 * i + 8, :] for i in group for k in range(8)
+                }
+                for j in range(at, at + 8):
+                    factors = [spread(j, 8 * q + k) for k in range(8)]
+                    for i in group:
+                        column = work[j, 8 * i : 8 * i + 8, :]
+                        for k in range(8):
+                            accs[i, k] = accs[i, k] - column * factors[k]
+                for (i, k), value in accs.items():
+                    work[8 * q + k, 8 * i : 8 * i + 8, :] = value
 
 
 def to_lanes(grams, work, width, many):
@@ -199,7 +203,10 @@
 
 def from_lanes(work, factors, width, many):
     for j in range(width):
-        column = work[j, :, 0:many]
+        skip = j // 8 * 8
+        column = work[j, skip:, 0:many]
+        if skip:
+            column = jnp.concatenate([jnp.zeros((skip, many), F32), column], axis=0)
         factors[pl.ds(j, many, stride=STRIDE), :] = jnp.concatenate([column, column], axis=0).T
 
 
@@ -351,16 +358,15 @@
         far_list,
         basis,
         top,
-        group_gram,
-        root_gram,
+        upper,
         transfer,
         first_rows,
         first_cols,
         second_cols,
         own_rows,
         switches,
-        left,
-        right,
+        inner,
+        outer,
         vectors,
         near,
         high,
@@ -374,7 +380,7 @@
         place,
         halo_cols,
         second_rows,
-        block,
+        results,
         grams,
         work,
         factors,
@@ -387,13 +393,15 @@
     layers = own // LAYER
     both = 2 * width
     extra = sides.shape[1]
+    odd = lax.axis_index("sub") % 2
+    arrived = ((inner, 1 - odd), (outer, odd))
     side_copies = [
-        pltpu.make_async_copy(side.at[pl.ds(halo, extra), :], sides.at[n], sems.at[n])
-        for n, side in enumerate((left, right))
+        pltpu.make_async_copy(block.at[pl.ds(halo, extra), :], sides.at[side], sems.at[n])
+        for n, (block, side) in enumerate(arrived)
     ]
     end_copies = [
-        pltpu.make_async_copy(side.at[pl.ds(0, halo), :], ends.at[n], sems.at[2 + n])
-        for n, side in enumerate((left, right))
+        pltpu.make_async_copy(block.at[pl.ds(0, halo), :], ends.at[side], sems.at[2 + n])
+        for n, (block, side) in enumerate(arrived)
     ]
     near_copies = [
         pltpu.make_async_copy(
@@ -420,8 +428,8 @@
         spare,
         (
             top[...],
-            group_gram[...] * (1.0 / members),
-            root_gram[...] * (1.0 / (members * groups)),
+            upper[0 : width // 2, :] * (1.0 / members),
+            upper[width // 2 :, :] * (1.0 / (members * groups)),
             top[...],
         ),
     ):
@@ -452,7 +460,7 @@
     second_rows[lanes : lanes + own * width, :] = own_rows[...]
 
     copies = [
-        pltpu.make_async_copy(block.at[n], near.at[pl.ds(index * halo, halo), :], sems.at[4 + n])
+        pltpu.make_async_copy(results.at[n], near.at[pl.ds(index * halo, halo), :], sems.at[4 + n])
         for n, index in enumerate((0, layers - 1))
     ]
 
@@ -472,7 +480,7 @@
         else:
             value = mm(weights[:, 0 : 2 * halo], vectors[(layers - 2) * halo :, :])
             value = value + mm(weights[:, 2 * halo :], ends[1, :, :])
-        block[n, :, :] = value.astype(BF16)
+        results[n, :, :] = value.astype(BF16)
         copies[n].start()
 
     panels = width // 8
@@ -566,10 +574,13 @@
             coupling[:, at : at + 2 * far * width] = line.astype(BF16)
 
 
-def shift(block, distance):
-    devices = range(lax.axis_size(AXES))
-    route = [(i - distance, i) for i in devices if i - distance in devices]
-    return lax.ppermute(block, AXES, route)
+def swap_inner(block):
+    return lax.ppermute(block, AXES, [(i, i ^ 1) for i in range(lax.axis_size(AXES))])
+
+
+def swap_outer(block):
+    inside = range(1, lax.axis_size(AXES) - 1)
+    return lax.ppermute(block, AXES, [(i, i + 1 if i % 2 else i - 1) for i in inside])
 
 
 def exchange(value, axis, bit):
@@ -593,14 +604,23 @@
     smem = pl.BlockSpec(memory_space=pltpu.SMEM)
     hbm = pl.BlockSpec(memory_space=pl.ANY)
     square = jax.ShapeDtypeStruct((width, width), F32)
-    sent = jax.ShapeDtypeStruct((halo + width + 32, columns), BF16)
+    extra = halo + width + 32
+
+    def block_of(rows):
+        return jax.ShapeDtypeStruct((rows, columns), BF16)
+
     basis = leaf_basis.T
     near_list, far_list = near_index.T, far_index.T
     cost = pl.CostEstimate(flops=10**9, bytes_accessed=4 * 10**6, transcendentals=10**6)
 
-    dense, top, to_next, to_prev = pl.pallas_call(
+    dense, top, to_outer, to_inner = pl.pallas_call(
         tree_kernel,
-        out_shape=(jax.ShapeDtypeStruct((half, 2 * width), F32), square, sent, sent),
+        out_shape=(
+            jax.ShapeDtypeStruct((half, 2 * width), F32),
+            square,
+            block_of(extra),
+            block_of(extra + half),
+        ),
         in_specs=[hbm] * 5,
         out_specs=(vmem,) * 4,
         scratch_shapes=[
@@ -613,15 +633,14 @@
         compiler_params=room(60),
         name="tree",
     )(points, basis, inner_transfer.T, device_transfer, vectors)
-    left = shift(to_next, 1)
-    right = shift(to_prev, -1)
-
-    steps = [("sub", bit) for bit in range(members.bit_length() - 1)]
-    steps += [("group", bit) for bit in range(groups.bit_length() - 1)]
-    chunks = [[1], [2, 3], [4, 5], [6], []]
+    from_inner = swap_inner(to_inner)
+    from_outer = swap_outer(to_outer)
+
+    steps = [("group", bit) for bit in range(groups.bit_length() - 1)]
+    steps += [("sub", bit) for bit in range(1, members.bit_length() - 1)]
+    chunks = [[1, 2, 3], [4], [5], [6], []]
     inner_pairs = list(range(PAD // 2, (own - PAD) // 2))
-    few = len(inner_pairs) // 2 - 1
-    pair_chunks = [[], [], [], inner_pairs[:few], inner_pairs[few:]]
+    pair_chunks = [[], [], inner_pairs[:2], inner_pairs[2:4], inner_pairs[4:]]
     blocks, plan, parts = [], {}, []
 
     def part_shape(count):
@@ -649,18 +668,20 @@
         name="chunk_0",
     )(late_points, near_list, near_count.reshape(1, own), vectors)
     parts.append(part)
-    gram = group_gram = dense
-    for n in range(max(len(steps), len(chunks))):
+    summands = [
+        from_inner[extra:, n * 2 * width : (n + 1) * 2 * width].astype(F32) for n in range(3)
+    ]
+    pair_gram = gram = dense + (summands[0] + (summands[1] + summands[2]))
+    gram, parts[0] = lax.optimization_barrier((gram, parts[0]))
+    for n in range(max(len(steps) + 1, len(chunks)) - 1):
         before = gram
         if n < len(steps):
             axis, bit = steps[n]
+            if n == len(steps) - (members.bit_length() - 2):
+                gram = before = jnp.concatenate([pair_gram, gram], axis=0)
             gram = exchange(gram, axis, bit)
-            if axis == "sub":
-                group_gram = gram
-        if n == 0:
-            gram, parts[0] = lax.optimization_barrier((gram, parts[0]))
-        elif n < len(chunks):
-            layer_chunk, pair_chunk = chunks[n], pair_chunks[n]
+        if n + 1 < len(chunks):
+            layer_chunk, pair_chunk = chunks[n + 1], pair_chunks[n + 1]
             shapes = [part_shape(len(layer_chunk))] * bool(layer_chunk)
             shapes += [block_shape(len(pair_chunk))] * bool(pair_chunk)
             outs = pl.pallas_call(
@@ -670,7 +691,7 @@
                 out_specs=(vmem,) * len(shapes),
                 compiler_params=room(10),
                 cost_estimate=cost,
-                name=f"chunk_{n}",
+                name=f"chunk_{n + 1}",
             )(before, far_list, *shared, vectors)
             gram, outs = lax.optimization_barrier((gram, outs))
             if layer_chunk:
@@ -694,7 +715,7 @@
             square,
             square,
         ),
-        in_specs=[hbm] * len(parts) + [smem] + [vmem] * 10 + [hbm] * 2 + [vmem],
+        in_specs=[hbm] * len(parts) + [smem] + [vmem] * 9 + [hbm] * 2 + [vmem],
         out_specs=(hbm,) + (vmem,) * 6,
         scratch_shapes=[
             pltpu.VMEM((2, halo, columns), BF16),
@@ -715,12 +736,11 @@
         far_list,
         basis,
         top,
-        group_gram,
         gram,
         device_transfer,
         *shared,
-        left,
-        right,
+        from_inner,
+        from_outer,
         vectors,
     )
 

time: 43.3 us -> 41.1 us (0.949)
  starting transfers between devices: 14.2 us -> 10.2 us
  waiting for transfers between devices: 5.47 us -> 8.38 us
  Pallas kernels: 22.5 us -> 21.4 us
    ppermute x5 -> x4, waiting for transfers between devices: 5.47 us -> 8.37 us  [exchange(): return value + lax.ppermute(value, axis, pairs)]
    ppermute x2, starting transfers between devices: 3.26 us -> 1.18 us  [the longest x1 0.67 us: swap_outer(): lax.ppermute(block, AXES, [(i, i + 1 if i % 2 else i - 1) for i in inside])]
    ppermute x5 -> x4, starting transfers between devices: 11 us -> 9.04 us  [exchange(): return value + lax.ppermute(value, axis, pairs)]
    pallas_call x1, Pallas kernels: 9.15 us -> 7.9 us  [per_device(): pl.pallas_call(functools.partial(leaves_kernel, near_chunks, edge_pairs,...]
    pallas_call x1, Pallas kernels: 0.87 us -> 1.77 us  [per_device(): pl.pallas_call(first_chunk_kernel(chunks[0]), out_shape=(part_shape(len(c...]
    pallas_call x4, Pallas kernels: 5.17 us -> 4.5 us  [per_device(): pl.pallas_call(next_chunk_kernel(layer_chunk, pair_chunk), out_shape=tupl...]
  transfers between devices with their start and end apart: 7 -> 6, of which waited for: 4 -> 4; matrix products, arithmetic and copies ran while one was open for 0% -> 0% of each run, Pallas kernels for 14% -> 15%
where the time goes in v5:
time: 41.1 us; the launch traced here: 41 us
  Pallas kernels  21.4 us (52%)
  starting transfers between devices  10.2 us (25%)
  waiting for transfers between devices  8.38 us (20%)
  between operations  0.86 us (2%)
    ppermute x4, starting transfers between devices, exchange(): return value + lax.ppermute(value, axis, pairs)  9.04 us
    ppermute x4, waiting for transfers between devices, exchange(): return value + lax.ppermute(value, axis, pairs)  8.37 us
    pallas_call x1, Pallas kernels, per_device(): pl.pallas_call(functools.partial(leaves_kernel, near_chunks, edge_pairs,...  7.9 us
    pallas_call x4, Pallas kernels, per_device(): pl.pallas_call(next_chunk_kernel(layer_chunk, pair_chunk), out_shape=tupl...  4.5 us
    pallas_call x1, Pallas kernels, per_device(): pl.pallas_call(tree_kernel, out_shape=(jax.ShapeDtypeStruct((half, 2 * wi...  3.98 us
    pallas_call x1, Pallas kernels, per_device(): pl.pallas_call(functools.partial(far_kernel, plan), out_shape=jax.ShapeDt...  3.28 us
    pallas_call x1, Pallas kernels, per_device(): pl.pallas_call(first_chunk_kernel(chunks[0]), out_shape=(part_shape(len(c...  1.77 us
  transfers between devices with their start and end apart: 6, of which 4 were waited for; matrix products, arithmetic and copies ran while one was open for 0% of the time, Pallas kernels for 15%

profile of v5, /device:TPU:0, one launch (start us, length us, event | category | flops | bytes accessed | tf_op | source)
XLA Modules:
  0.0 41.0 jit_solution(7322801992603359098)
XLA Ops:
  0.6 0.0 copy-start
  0.6 0.0 copy-start.3
  0.7 0.0 copy-start.7
  0.7 0.0 copy-start.6
  0.7 4.0 %tree.1 = (f32[32,128]{1,0:T(8,128)}, f32[64,64]{1,0:T(8,128)}, bf16[352,384]{1,0:T(8,128)(2,1)}, bf16[384,384]{1,0:T(8,128)(2,1)}) custom-call(f32[3,2048]{1,0:T(4,128)} %points, bf16[64,2048]{1,0:T(8,128)(2,1)} %bitcast.6, bf16[64,1920]{1,0:T(8,128)(2,1)} %bitcast.17, f32[64,64]{1,0:T(8,128)} %refs_8_.1, bf16[2048,384]{1,0:T(8,128)(2,1)} %refs_16_.1), custom_call_target="tpu_custom_call" | custom-call | tf_op jit(solution)/shard_map/tree/pallas_call | solution.py:616
  4.7 0.5 %collective-permute-start = (bf16[384,384]{1,0:T(8,128)(2,1)}, bf16[384,384]{1,0:T(8,128)(2,1)S(1)}, u32[]{:S(2)}, u32[]{:S(2)}) collective-permute-start(bf16[384,384]{1,0:T(8,128)(2,1)} %get-tuple-element.42), channel_id=1, source_target_pairs={{0,1},{1,0},{2,3},{3,2},{4,5},{5,4},{6,7},{7,6},{8,9},{9,8},{10,11... | collective-permute-start | bytes 884744 | tf_op jit(solution)/shard_map/ppermute | solution.py:578
  5.2 0.7 %collective-permute-start.5 = (bf16[352,384]{1,0:T(8,128)(2,1)}, bf16[352,384]{1,0:T(8,128)(2,1)S(1)}, u32[]{:S(2)}, u32[]{:S(2)}) collective-permute-start(bf16[352,384]{1,0:T(8,128)(2,1)} %get-tuple-element.64), channel_id=1, source_target_pairs={{1,2},{2,1},{3,4},{4,3},{5,6},{6,5},{7,8},{8,7},{9,10},{10,9},{11,... | collective-permute-start | bytes 811016 | tf_op jit(solution)/shard_map/ppermute | solution.py:583
  5.9 0.0 copy-done
  5.9 0.0 copy-done.3
  5.9 0.0 copy-done.7
  5.9 0.0 copy-done.6
  5.9 0.0 copy-start.8
  5.9 0.0 copy-start.5
  5.9 1.8 %chunk_0.1 = (bf16[768,384]{1,0:T(8,128)(2,1)S(1)}, bf16[2048,64]{1,0:T(8,128)(2,1)S(1)}, bf16[64,2048]{1,0:T(8,128)(2,1)S(1)}, bf16[48,2048]{1,0:T(8,128)(2,1)S...) custom-call(f32[3,2048]{1,0:T(4,128)S(1)} %copy-done.3, s32[12,32]{1,0:T(8,128)S(1)} %bitcast.14, ...), custom_call_target="tpu_custom_call" | custom-call | flops 1000000000 | bytes 4000000 | tf_op jit(solution)/shard_map/chunk_0/pallas_call | solution.py:653
  7.7 0.0 collective-permute-done.refs_14_
  7.7 0.0 copy-done.8
  7.7 6.3 %collective-permute-start.1 = (f32[32,128]{1,0:T(8,128)S(1)}, f32[32,128]{1,0:T(8,128)S(1)}, u32[]{:S(2)}, u32[]{:S(2)}) collective-permute-start(f32[32,128]{1,0:T(8,128)S(1)} %add_add_fusion.after), channel_id=1, source_target_pairs={{0,8},{8,0},{16,24},{24,16},{1,9},{9,1},{17,25},{25,17},{2,10},{10... | collective-permute-start | bytes 49160 | tf_op jit(solution)/shard_map/ppermute | solution.py:589
  14.0 0.0 copy-done.5
  14.0 1.1 %chunk_1.1.refs_1_ = bf16[256,384]{1,0:T(8,128)(2,1)S(1)} custom-call(f32[32,128]{1,0:T(8,128)S(1)} %add_add_fusion.after, s32[3,32]{1,0:T(4,128)S(1)} %bitcast.8, bf16[2048,64]{1,0:T(8,128)(2,1)S(1)} %get-tuple-element.47.first_rows.refs_9_, bf16[64,2048]{1,0:T(8,128)(2,1)S(1)} %get-tuple-element.48.first_cols.refs_10_, ...), custom_call_target="tpu_custom_call" | custom-call | flops 1000000000 | bytes 4000000 | tf_op jit(solution)/shard_map/chunk_1/pallas_call | solution.py:687
  15.2 1.9 %collective-permute-done.1 = f32[32,128]{1,0:T(8,128)S(1)} collective-permute-done((f32[32,128]{1,0:T(8,128)S(1)}, f32[32,128]{1,0:T(8,128)S(1)}, u32[]{:S(2)}, u32[]{:S(2)}) %collective-permute-start.1) | collective-permute-done | bytes 16416 | tf_op jit(solution)/shard_map/ppermute | solution.py:589
  17.1 2.6 %collective-permute-start.2 = (f32[32,128]{1,0:T(8,128)S(1)}, f32[32,128]{1,0:T(8,128)S(1)}, u32[]{:S(2)}, u32[]{:S(2)}) collective-permute-start(f32[32,128]{1,0:T(8,128)S(1)} %add.24.after), channel_id=1, source_target_pairs={{0,16},{8,24},{16,0},{24,8},{1,17},{9,25},{17,1},{25,9},{2,18},{10... | collective-permute-start | bytes 49160 | tf_op jit(solution)/shard_map/ppermute | solution.py:589
  19.7 1.2 %chunk_2.1 = (bf16[256,384]{1,0:T(8,128)(2,1)S(1)}, bf16[384,256]{1,0:T(8,128)(2,1)S(1)}) custom-call(f32[32,128]{1,0:T(8,128)S(1)} %add.24.after, s32[3,32]{1,0:T(4,128)S(1)} %bitcast.9, bf16[2048,64]{1,0:T(8,128)(2,1)S(1)} %get-tuple-element.47.first_rows.refs_9_, bf16[64,2048]{1,0:T(8,128)(2,1)S(1)} %get-tuple-element.48.first_cols.refs_10_, ...), custom_call_target="tpu_custom_call" | custom-call | flops 1000000000 | bytes 4000000 | tf_op jit(solution)/shard_map/chunk_2/pallas_call | solution.py:687
  20.9 0.8 %collective-permute-done.2 = f32[32,128]{1,0:T(8,128)S(1)} collective-permute-done((f32[32,128]{1,0:T(8,128)S(1)}, f32[32,128]{1,0:T(8,128)S(1)}, u32[]{:S(2)}, u32[]{:S(2)}) %collective-permute-start.2) | collective-permute-done | bytes 16416 | tf_op jit(solution)/shard_map/ppermute | solution.py:589
  21.7 0.1 collective-permute-start.3
  21.8 1.2 %chunk_3.1 = (bf16[256,384]{1,0:T(8,128)(2,1)S(1)}, bf16[384,256]{1,0:T(8,128)(2,1)S(1)}) custom-call(f32[64,128]{1,0:T(8,128)S(1)} %pad_maximum_fusion.after, s32[3,32]{1,0:T(4,128)S(1)} %bitcast.10, bf16[2048,64]{1,0:T(8,128)(2,1)S(1)} %get-tuple-element.47.first_rows.refs_9_, bf16[64,2048]{1,0:T(8,128)(2,1)S(1)} %get-tuple-element.48.first_cols.refs_10_, ...), custom_call_target="tpu_custom_call" | custom-call | flops 1000000000 | bytes 4000000 | tf_op jit(solution)/shard_map/chunk_3/pallas_call | solution.py:687
  23.1 2.7 %collective-permute-done.3 = f32[64,128]{1,0:T(8,128)S(1)} collective-permute-done((f32[64,128]{1,0:T(8,128)S(1)}, f32[64,128]{1,0:T(8,128)S(1)}, u32[]{:S(2)}, u32[]{:S(2)}) %collective-permute-start.3) | collective-permute-done | bytes 32800 | tf_op jit(solution)/shard_map/ppermute | solution.py:589
  25.7 0.0 copy-start.1
  25.7 0.0 copy-start.2
  25.7 0.0 copy-start.4
  25.8 0.1 collective-permute-start.4
  25.8 0.9 %chunk_4.1.refs_2_ = bf16[768,256]{1,0:T(8,128)(2,1)S(1)} custom-call(f32[64,128]{1,0:T(8,128)S(1)} %fusion.after, s32[3,32]{1,0:T(4,128)S(1)} %bitcast.11, bf16[2048,64]{1,0:T(8,128)(2,1)S(1)} %get-tuple-element.47.first_rows.refs_9_, bf16[64,2048]{1,0:T(8,128)(2,1)S(1)} %get-tuple-element.48.first_cols.refs_10_, ...), custom_call_target="tpu_custom_call" | custom-call | flops 1000000000 | bytes 4000000 | tf_op jit(solution)/shard_map/chunk_4/pallas_call | solution.py:687
  26.7 3.0 %collective-permute-done.4 = f32[64,128]{1,0:T(8,128)S(1)} collective-permute-done((f32[64,128]{1,0:T(8,128)S(1)}, f32[64,128]{1,0:T(8,128)S(1)}, u32[]{:S(2)}, u32[]{:S(2)}) %collective-permute-start.4) | collective-permute-done | bytes 32800 | tf_op jit(solution)/shard_map/ppermute | solution.py:589
  29.7 0.0 collective-permute-done.5.refs_15_
  29.7 0.0 copy-done.1
  29.8 0.0 copy-done.2
  29.8 0.0 copy-done.4
  29.8 7.9 %leaves.1 = (bf16[2048,384]{1,0:T(8,128)(2,1)}, bf16[3072,128]{1,0:T(8,128)(2,1)S(1)}, bf16[3072,128]{1,0:T(8,128)(2,1)S(1)}, bf16[1536,256]{1,0:T(8,128)(2,1)S(...) custom-call(bf16[768,384]{1,0:T(8,128)(2,1)S(1)} %get-tuple-element.45.refs_0_, ...), custom_call_target="tpu_custom_call" | custom-call | tf_op jit(solution)/shard_map/leaves/pallas_call | solution.py:707
  37.7 3.3 %far.1 = bf16[64,6144]{1,0:T(8,128)(2,1)} custom-call(s32[3,32]{1,0:T(4,128)S(1)} %bitcast.13, bf16[3072,128]{1,0:T(8,128)(2,1)S(1)} %get-tuple-element.66.high, bf16[3072,128]{1,0:T(8,128)(2,1)S(1)} %get-tuple-element.67.low, bf16[384,256]{1,0:T(8,128)(2,1)S(1)} %get-tuple-element.68.refs_0_, bf16[384,256]{1,0:T(8,128)(2,1)S(1)} %get-tuple-element.69.refs_1_, ...), custom_call_target="tpu_custom_call" | custom-call | tf_op jit(solution)/shard_map/far/pallas_call | solution.py:747
  (6 shorter events, 0.0 us)
Async XLA Ops:
  0.6 5.2 %copy-start = (bf16[2048,384]{1,0:T(8,128)(2,1)S(1)}, bf16[2048,384]{1,0:T(8,128)(2,1)}, u32[]{:S(2)}) copy-start(bf16[2048,384]{1,0:T(8,128)(2,1)} %refs_16_.1) | copy-start | bytes 4718596
  0.6 5.2 %copy-start.3 = (f32[3,2048]{1,0:T(4,128)S(1)}, f32[3,2048]{1,0:T(4,128)}, u32[]{:S(2)}) copy-start(f32[3,2048]{1,0:T(4,128)} %points) | copy-start | bytes 73732
  0.7 5.2 %copy-start.7 = (s32[32]{0:T(128)S(1)}, s32[32]{0:T(128)}, u32[]{:S(2)}) copy-start(s32[32]{0:T(128)} %param.14) | copy-start | bytes 388
  0.7 5.2 %copy-start.6 = (s32[32,12]{0,1:T(8,128)S(1)}, s32[32,12]{0,1:T(8,128)}, u32[]{:S(2)}) copy-start(s32[32,12]{0,1:T(8,128)} %param.13) | copy-start | bytes 4612
  4.7 3.0 %collective-permute-start = (bf16[384,384]{1,0:T(8,128)(2,1)}, bf16[384,384]{1,0:T(8,128)(2,1)S(1)}, u32[]{:S(2)}, u32[]{:S(2)}) collective-permute-start(bf16[384,384]{1,0:T(8,128)(2,1)} %get-tuple-element.42), channel_id=1, source_target_pairs={{0,1},{1,0},{2,3},{3,2},{4,5},{5,4},{6,7},{7,6},{8,9},{9,8},{10,11... | collective-permute-start | bytes 884744 | tf_op jit(solution)/shard_map/ppermute | solution.py:578
  5.2 24.6 %collective-permute-start.5 = (bf16[352,384]{1,0:T(8,128)(2,1)}, bf16[352,384]{1,0:T(8,128)(2,1)S(1)}, u32[]{:S(2)}, u32[]{:S(2)}) collective-permute-start(bf16[352,384]{1,0:T(8,128)(2,1)} %get-tuple-element.64), channel_id=1, source_target_pairs={{1,2},{2,1},{3,4},{4,3},{5,6},{6,5},{7,8},{8,7},{9,10},{10,9},{11,... | collective-permute-start | bytes 811016 | tf_op jit(solution)/shard_map/ppermute | solution.py:583
  5.9 1.8 %copy-start.8 = (f32[32,128]{1,0:T(8,128)S(1)}, f32[32,128]{1,0:T(8,128)}, u32[]{:S(2)}) copy-start(f32[32,128]{1,0:T(8,128)} %get-tuple-element.41) | copy-start | bytes 49156
  5.9 8.1 %copy-start.5 = (s32[32,3]{0,1:T(4,128)S(1)}, s32[32,3]{0,1:T(4,128)}, u32[]{:S(2)}) copy-start(s32[32,3]{0,1:T(4,128)} %param.15) | copy-start | bytes 1156
  7.7 9.3 %collective-permute-start.1 = (f32[32,128]{1,0:T(8,128)S(1)}, f32[32,128]{1,0:T(8,128)S(1)}, u32[]{:S(2)}, u32[]{:S(2)}) collective-permute-start(f32[32,128]{1,0:T(8,128)S(1)} %add_add_fusion.after), channel_id=1, source_target_pairs={{0,8},{8,0},{16,24},{24,16},{1,9},{9,1},{17,25},{25,17},{2,10},{10... | collective-permute-start | bytes 49160 | tf_op jit(solution)/shard_map/ppermute | solution.py:589
  17.1 4.6 %collective-permute-start.2 = (f32[32,128]{1,0:T(8,128)S(1)}, f32[32,128]{1,0:T(8,128)S(1)}, u32[]{:S(2)}, u32[]{:S(2)}) collective-permute-start(f32[32,128]{1,0:T(8,128)S(1)} %add.24.after), channel_id=1, source_target_pairs={{0,16},{8,24},{16,0},{24,8},{1,17},{9,25},{17,1},{25,9},{2,18},{10... | collective-permute-start | bytes 49160 | tf_op jit(solution)/shard_map/ppermute | solution.py:589
  21.7 4.0 %collective-permute-start.3 = (f32[64,128]{1,0:T(8,128)S(1)}, f32[64,128]{1,0:T(8,128)S(1)}, u32[]{:S(2)}, u32[]{:S(2)}) collective-permute-start(f32[64,128]{1,0:T(8,128)S(1)} %pad_maximum_fusion.after), channel_id=1, source_target_pairs={{0,2},{1,3},{2,0},{3,1},{4,6},{5,7},{6,4},{7,5},{8,10},{9,11},{10,... | collective-permute-start | bytes 98312 | tf_op jit(solution)/shard_map/ppermute | solution.py:589
  25.7 4.0 %copy-start.1 = (bf16[2048,64]{0,1:T(8,128)(2,1)S(1)}, bf16[2048,64]{0,1:T(8,128)(2,1)}, u32[]{:S(2)}) copy-start(bf16[2048,64]{0,1:T(8,128)(2,1)} %param.9) | copy-start | bytes 786436
  25.7 4.0 %copy-start.2 = (f32[64,64]{1,0:T(8,128)S(1)}, f32[64,64]{1,0:T(8,128)}, u32[]{:S(2)}) copy-start(f32[64,64]{1,0:T(8,128)} %refs_8_.1) | copy-start | bytes 49156
  25.7 4.0 %copy-start.4 = (f32[64,64]{1,0:T(8,128)S(1)}, f32[64,64]{1,0:T(8,128)}, u32[]{:S(2)}) copy-start(f32[64,64]{1,0:T(8,128)} %get-tuple-element.61.refs_6_) | copy-start | bytes 49156
  25.8 4.0 %collective-permute-start.4 = (f32[64,128]{1,0:T(8,128)S(1)}, f32[64,128]{1,0:T(8,128)S(1)}, u32[]{:S(2)}, u32[]{:S(2)}) collective-permute-start(f32[64,128]{1,0:T(8,128)S(1)} %fusion.after), channel_id=1, source_target_pairs={{0,4},{1,5},{2,6},{3,7},{4,0},{5,1},{6,2},{7,3},{8,12},{9,13},{10,... | collective-permute-start | bytes 98312 | tf_op jit(solution)/shard_map/ppermute | solution.py:589

commit v6 on v5

--- a/solution.py
+++ b/solution.py
@@ -15,7 +15,7 @@
 SCALE = 0.5 / LONG_SQ
 HALF = math.log(0.5)
 OFF = -16384.0
-STRIDE = 72
+STRIDE = 40
 AXES = ("group", "sub")
 F32 = jnp.float32
 BF16 = jnp.bfloat16
@@ -141,10 +141,10 @@
     t = ts[0]
     x = jnp.concatenate(split3(xs[0]), axis=1)
     top_gram = mm_nt(x, jnp.concatenate([t, t, t], axis=1)) * 0.5
-    top[...] = top_gram
+    top[...] = fold(top_gram)
     matrix = transfer[...]
     gram = exact(exact(matrix.T, top_gram), matrix)
-    halves = jnp.concatenate([gram[: width // 2], gram[width // 2 :]], axis=1)
+    halves = fold(gram)
     dense[...] = halves
     inner[halo + width + 32 :, :] = jnp.concatenate(split3(halves), axis=1)
     for copy in copies:
@@ -196,18 +196,30 @@
                     work[8 * q + k, 8 * i : 8 * i + 8, :] = value
 
 
+def fold(matrix):
+    half = matrix.shape[0] // 2
+    return jnp.concatenate([matrix[:half], matrix[half:]], axis=1)
+
+
+def unfold(matrix):
+    half = matrix.shape[1] // 2
+    return jnp.concatenate([matrix[:, :half], matrix[:, half:]], axis=0)
+
+
 def to_lanes(grams, work, width, many):
-    for i in range(width):
-        work[i, :, 0:many] = grams[pl.ds(i, many, stride=STRIDE), :].T
+    for i in range(width // 2):
+        both = grams[pl.ds(i, many, stride=STRIDE), :].T
+        work[i, :, 0:many] = both[0:width]
+        work[i + width // 2, :, 0:many] = both[width:]
 
 
 def from_lanes(work, factors, width, many):
-    for j in range(width):
-        skip = j // 8 * 8
-        column = work[j, skip:, 0:many]
-        if skip:
-            column = jnp.concatenate([jnp.zeros((skip, many), F32), column], axis=0)
-        factors[pl.ds(j, many, stride=STRIDE), :] = jnp.concatenate([column, column], axis=0).T
+    for i in range(width // 2):
+        both = []
+        for j in (i, i + width // 2):
+            skip = j // 8 * 8
+            both += [jnp.zeros((skip, many), F32)] * bool(skip) + [work[j, skip:, 0:many]]
+        factors[pl.ds(i, many, stride=STRIDE), :] = jnp.concatenate(both, axis=0).T
 
 
 def gaussians(exponent):
@@ -334,19 +346,16 @@
     return body
 
 
-def next_chunk_kernel(layers, pairs):
-    def body(
-        after, far_list, first_rows, first_cols, second_cols, second_rows, switches, vectors, *outs
-    ):
-        width = vectors.shape[0] // far_list.shape[1]
-        if layers:
-            inner_layers(
-                layers, vectors, first_rows, second_cols, switches, outs[0], LAYER * width
-            )
-        if pairs:
-            far_blocks(
-                pairs, far_list, second_rows, first_cols, outs[-1], width, 0, range(len(pairs))
-            )
+def layers_chunk_kernel(layers, halo):
+    def body(after, first_rows, second_cols, switches, vectors, out):
+        inner_layers(layers, vectors, first_rows, second_cols, switches, out, halo)
+
+    return body
+
+
+def pairs_chunk_kernel(pairs, width):
+    def body(after, far_list, first_cols, second_rows, out):
+        far_blocks(pairs, far_list, second_rows, first_cols, out, width, 0, range(len(pairs)))
 
     return body
 
@@ -422,7 +431,7 @@
         value = mm_nt(stacked, pair)
         for m in range(2):
             at = (PAD + 2 * n + m) * STRIDE
-            grams[at : at + width, :] = value[m * width : (m + 1) * width]
+            grams[at : at + width // 2, :] = fold(value[m * width : (m + 1) * width])
     spare = (0, LAYER, total - LAYER - 1, total - 1)
     for spot, gram in zip(
         spare,
@@ -433,9 +442,7 @@
             top[...],
         ),
     ):
-        if gram.shape[0] < width:
-            gram = jnp.concatenate([gram[:, :width], gram[:, width:]], axis=0)
-        grams[spot * STRIDE : spot * STRIDE + width, :] = gram
+        grams[spot * STRIDE : spot * STRIDE + width // 2, :] = gram
     for copy in side_copies:
         copy.wait()
     for side, spots in enumerate(
@@ -443,7 +450,7 @@
     ):
         for n, spot in enumerate(spots):
             piece = sides[side, 0:width, n * width : (n + 1) * width]
-            grams[spot * STRIDE : spot * STRIDE + width, :] = mm_nt(piece, piece)
+            grams[spot * STRIDE : spot * STRIDE + width // 2, :] = fold(mm_nt(piece, piece))
 
     lanes = PAD * width
     place[...] = jnp.zeros(place.shape, F32)
@@ -505,12 +512,18 @@
         copy.wait()
     factor_lanes(work, width, beside)
     from_lanes(work, factors, width, total)
-    device_factor[...] = exact(factors[0:width, 0:width], transfer[...])
+    device_factor[...] = exact(unfold(factors[0 : width // 2, :]), transfer[...])
     for target, spot in ((group_factor, spare[1]), (root_factor, spare[2])):
-        target[...] = factors[spot * STRIDE : spot * STRIDE + width, 0:width]
+        target[...] = unfold(factors[spot * STRIDE : spot * STRIDE + width // 2, :])
+    left_lanes = iota((width // 2, both), 1) < width
     for spot in range(total):
+        rows = factors[spot * STRIDE : spot * STRIDE + width // 2, :]
+        turned = pltpu.roll(rows, width, 1)
+        twice = jnp.concatenate(
+            [jnp.where(left_lanes, rows, turned), jnp.where(left_lanes, turned, rows)], axis=0
+        )
         at = slice(spot * width, (spot + 1) * width)
-        high[at, :], low[at, :] = split2(factors[spot * STRIDE : spot * STRIDE + width, :])
+        high[at, :], low[at, :] = split2(twice)
     for copy in copies + near_copies:
         copy.wait()
 
@@ -583,10 +596,9 @@
     return lax.ppermute(block, AXES, [(i, i + 1 if i % 2 else i - 1) for i in inside])
 
 
-def exchange(value, axis, bit):
-    mask = 2**bit
-    pairs = [(source, source ^ mask) for source in range(lax.axis_size(axis))]
-    return value + lax.ppermute(value, axis, pairs)
+def exchange(value, distance):
+    odd = range(1, lax.axis_size(AXES), 2)
+    return value + lax.ppermute(value, AXES, [(i, i ^ distance) for i in odd])
 
 
 def per_device(
@@ -617,7 +629,7 @@
         tree_kernel,
         out_shape=(
             jax.ShapeDtypeStruct((half, 2 * width), F32),
-            square,
+            jax.ShapeDtypeStruct((half, 2 * width), F32),
             block_of(extra),
             block_of(extra + half),
         ),
@@ -636,11 +648,13 @@
     from_inner = swap_inner(to_inner)
     from_outer = swap_outer(to_outer)
 
-    steps = [("group", bit) for bit in range(groups.bit_length() - 1)]
-    steps += [("sub", bit) for bit in range(1, members.bit_length() - 1)]
-    chunks = [[1, 2, 3], [4], [5], [6], []]
+    sub_bits = members.bit_length() - 1
+    steps = [members << bit for bit in range(groups.bit_length() - 1)]
+    steps += [1 << bit for bit in range(1, sub_bits)]
+    chunks = [[1, 2, 3], [4], [5], [6]]
     inner_pairs = list(range(PAD // 2, (own - PAD) // 2))
-    pair_chunks = [[], [], inner_pairs[:2], inner_pairs[2:4], inner_pairs[4:]]
+    few = len(inner_pairs) // 2
+    pair_chunks = [inner_pairs[:few], inner_pairs[few:]]
     blocks, plan, parts = [], {}, []
 
     def part_shape(count):
@@ -673,32 +687,46 @@
     ]
     pair_gram = gram = dense + (summands[0] + (summands[1] + summands[2]))
     gram, parts[0] = lax.optimization_barrier((gram, parts[0]))
-    for n in range(max(len(steps) + 1, len(chunks)) - 1):
+    work = [("layers", chunk) for chunk in chunks[1:]] + [("pairs", chunk) for chunk in pair_chunks]
+    first_rows, first_cols, second_cols, second_rows, switches = shared
+    for n in range(max(len(steps) + 1, len(work))):
         before = gram
         if n < len(steps):
-            axis, bit = steps[n]
-            if n == len(steps) - (members.bit_length() - 2):
+            if n == len(steps) - sub_bits + 1:
                 gram = before = jnp.concatenate([pair_gram, gram], axis=0)
-            gram = exchange(gram, axis, bit)
-        if n + 1 < len(chunks):
-            layer_chunk, pair_chunk = chunks[n + 1], pair_chunks[n + 1]
-            shapes = [part_shape(len(layer_chunk))] * bool(layer_chunk)
-            shapes += [block_shape(len(pair_chunk))] * bool(pair_chunk)
-            outs = pl.pallas_call(
-                next_chunk_kernel(layer_chunk, pair_chunk),
-                out_shape=tuple(shapes),
-                in_specs=[hbm, smem] + [vmem] * 6,
-                out_specs=(vmem,) * len(shapes),
-                compiler_params=room(10),
-                cost_estimate=cost,
-                name=f"chunk_{n + 1}",
-            )(before, far_list, *shared, vectors)
-            gram, outs = lax.optimization_barrier((gram, outs))
-            if layer_chunk:
-                parts.append(outs[0])
-            if pair_chunk:
-                plan.update((index, (len(blocks), m)) for m, index in enumerate(pair_chunk))
-                blocks.append(outs[-1])
+            gram = exchange(gram, steps[n])
+        elif n == len(steps):
+            handed = lax.ppermute(
+                gram, AXES, [(i, i - 1) for i in range(1, lax.axis_size(AXES), 2)]
+            )
+            gram = jnp.where(lax.axis_index("sub") % 2 == 1, gram, handed)
+        if n < len(work):
+            kind, chunk = work[n]
+            if kind == "layers":
+                out = pl.pallas_call(
+                    layers_chunk_kernel(chunk, halo),
+                    out_shape=part_shape(len(chunk)),
+                    in_specs=[hbm] + [vmem] * 4,
+                    out_specs=vmem,
+                    compiler_params=room(10),
+                    cost_estimate=cost,
+                    name=f"chunk_{n + 1}",
+                )(before, first_rows, second_cols, switches, vectors)
+                parts.append(out)
+            else:
+                out = pl.pallas_call(
+                    pairs_chunk_kernel(chunk, width),
+                    out_shape=block_shape(len(chunk)),
+                    in_specs=[hbm, smem] + [vmem] * 2,
+                    out_specs=vmem,
+                    compiler_params=room(10),
+                    cost_estimate=cost,
+                    name=f"chunk_{n + 1}",
+                )(before, far_list, first_cols, second_rows)
+                plan.update((index, (len(blocks), m)) for m, index in enumerate(chunk))
+                blocks.append(out)
+            gram, out = lax.optimization_barrier((gram, out))
+            (parts if kind == "layers" else blocks)[-1] = out
 
     edge_pairs = [index for index in range(own // 2) if index not in plan]
     plan.update((index, (len(blocks), m)) for m, index in enumerate(edge_pairs))
@@ -724,7 +752,7 @@
             pltpu.VMEM((2, 48, PAD * width), BF16),
             pltpu.VMEM((total * width, 2 * width), BF16),
             pltpu.VMEM((2, halo, columns), BF16),
-            pltpu.VMEM((total * STRIDE, width), F32),
+            pltpu.VMEM((total * STRIDE, 2 * width), F32),
             pltpu.VMEM((width, width, 128), F32),
             pltpu.VMEM((total * STRIDE, 2 * width), F32),
             pltpu.SemaphoreType.DMA((6 + len(parts),)),

time: 41.1 us -> 44.7 us (1.088)
  waiting for transfers between devices: 8.38 us -> 17.5 us
  starting transfers between devices: 10.2 us -> 5.44 us
  Pallas kernels: 21.4 us -> 20.4 us
    ppermute x4 -> x5, waiting for transfers between devices: 8.37 us -> 17.5 us  [the longest x1 17.5 us: per_device(): lax.ppermute(gram, AXES, [(i, i - 1) for i in range(1, lax.axis_size(AXES...]
    ppermute x4 -> x5, starting transfers between devices: 9.04 us -> 4.25 us  [the longest x4 2.65 us: exchange(): return value + lax.ppermute(value, AXES, [(i, i ^ distance) for i in odd])]
    pallas_call x4 -> x5, Pallas kernels: 4.5 us -> 3.46 us  [the longest x2 1.74 us: per_device(): pl.pallas_call(pairs_chunk_kernel(chunk, width), out_shape=block_shape(le...]
  transfers between devices with their start and end apart: 6 -> 7, of which waited for: 4 -> 1; matrix products, arithmetic and copies ran while one was open for 0% -> 0% of each run, Pallas kernels for 15% -> 12%
where the time goes in v6:
time: 44.7 us; the launch traced here: 44.4 us
  Pallas kernels  20.4 us (46%)
  waiting for transfers between devices  17.5 us (39%)
  starting transfers between devices  5.44 us (12%)
  between operations  0.99 us (2%)
    ppermute x1, waiting for transfers between devices, per_device(): lax.ppermute(gram, AXES, [(i, i - 1) for i in range(1, lax.axis_size(AXES...  17.5 us
    pallas_call x1, Pallas kernels, per_device(): pl.pallas_call(functools.partial(leaves_kernel, near_chunks, edge_pairs,...  7.93 us
    pallas_call x1, Pallas kernels, per_device(): pl.pallas_call(tree_kernel, out_shape=(jax.ShapeDtypeStruct((half, 2 * wi...  3.98 us
    pallas_call x1, Pallas kernels, per_device(): pl.pallas_call(functools.partial(far_kernel, plan), out_shape=jax.ShapeDt...  3.29 us
    ppermute x4, starting transfers between devices, exchange(): return value + lax.ppermute(value, AXES, [(i, i ^ distance) for i in odd])  2.65 us
    pallas_call x1, Pallas kernels, per_device(): pl.pallas_call(first_chunk_kernel(chunks[0]), out_shape=(part_shape(len(c...  1.77 us
    pallas_call x2, Pallas kernels, per_device(): pl.pallas_call(pairs_chunk_kernel(chunk, width), out_shape=block_shape(le...  1.74 us
    pallas_call x3, Pallas kernels, per_device(): pl.pallas_call(layers_chunk_kernel(chunk, halo), out_shape=part_shape(len...  1.72 us
  transfers between devices with their start and end apart: 7, of which 1 were waited for; matrix products, arithmetic and copies ran while one was open for 0% of the time, Pallas kernels for 12%

profile of v6, /device:TPU:0, one launch (start us, length us, event | category | flops | bytes accessed | tf_op | source)
XLA Modules:
  0.0 44.4 jit_solution(2855166565373224836)
XLA Ops:
  0.6 0.0 copy-start
  0.6 0.0 copy-start.3
  0.7 0.0 copy-start.7
  0.7 0.0 copy-start.6
  0.7 4.0 %tree.1 = (f32[32,128]{1,0:T(8,128)}, f32[32,128]{1,0:T(8,128)}, bf16[352,384]{1,0:T(8,128)(2,1)}, bf16[384,384]{1,0:T(8,128)(2,1)}) custom-call(f32[3,2048]{1,0:T(4,128)} %points, bf16[64,2048]{1,0:T(8,128)(2,1)} %bitcast.6, bf16[64,1920]{1,0:T(8,128)(2,1)} %bitcast.15, f32[64,64]{1,0:T(8,128)} %refs_8_.1, bf16[2048,384]{1,0:T(8,128)(2,1)} %refs_16_.1), custom_call_target="tpu_custom_call" | custom-call | tf_op jit(solution)/shard_map/tree/pallas_call | solution.py:628
  4.7 0.5 %collective-permute-start = (bf16[384,384]{1,0:T(8,128)(2,1)}, bf16[384,384]{1,0:T(8,128)(2,1)S(1)}, u32[]{:S(2)}, u32[]{:S(2)}) collective-permute-start(bf16[384,384]{1,0:T(8,128)(2,1)} %get-tuple-element.38), channel_id=1, source_target_pairs={{0,1},{1,0},{2,3},{3,2},{4,5},{5,4},{6,7},{7,6},{8,9},{9,8},{10,11... | collective-permute-start | bytes 884744 | tf_op jit(solution)/shard_map/ppermute | solution.py:591
  5.2 0.7 %collective-permute-start.6 = (bf16[352,384]{1,0:T(8,128)(2,1)}, bf16[352,384]{1,0:T(8,128)(2,1)S(1)}, u32[]{:S(2)}, u32[]{:S(2)}) collective-permute-start(bf16[352,384]{1,0:T(8,128)(2,1)} %get-tuple-element.57), channel_id=1, source_target_pairs={{1,2},{2,1},{3,4},{4,3},{5,6},{6,5},{7,8},{8,7},{9,10},{10,9},{11,... | collective-permute-start | bytes 811016 | tf_op jit(solution)/shard_map/ppermute | solution.py:596
  5.9 0.0 copy-done
  5.9 0.0 copy-done.3
  5.9 0.0 copy-done.7
  5.9 0.0 copy-done.6
  5.9 0.0 copy-start.8
  5.9 1.8 %chunk_0.1 = (bf16[768,384]{1,0:T(8,128)(2,1)S(1)}, bf16[2048,64]{1,0:T(8,128)(2,1)S(1)}, bf16[64,2048]{1,0:T(8,128)(2,1)S(1)}, bf16[48,2048]{1,0:T(8,128)(2,1)S...) custom-call(f32[3,2048]{1,0:T(4,128)S(1)} %copy-done.3, s32[12,32]{1,0:T(8,128)S(1)} %bitcast.12, ...), custom_call_target="tpu_custom_call" | custom-call | flops 1000000000 | bytes 4000000 | tf_op jit(solution)/shard_map/chunk_0/pallas_call | solution.py:667
  7.7 0.0 collective-permute-done.refs_14_
  7.7 0.0 copy-done.8
  7.7 0.7 %collective-permute-start.1 = (f32[32,128]{1,0:T(8,128)S(1)}, f32[32,128]{1,0:T(8,128)S(1)}, u32[]{:S(2)}, u32[]{:S(2)}) collective-permute-start(f32[32,128]{1,0:T(8,128)S(1)} %add_add_fusion.after), channel_id=1, source_target_pairs={{1,9},{3,11},{5,13},{7,15},{9,1},{11,3},{13,5},{15,7},{17,25},{19,... | collective-permute-start | bytes 49160 | tf_op jit(solution)/shard_map/ppermute | solution.py:601
  8.4 0.6 %chunk_1.1.refs_1_ = bf16[256,384]{1,0:T(8,128)(2,1)S(1)} custom-call(f32[32,128]{1,0:T(8,128)S(1)} %add_add_fusion.after, bf16[2048,64]{1,0:T(8,128)(2,1)S(1)} %get-tuple-element.43.first_rows.refs_9_, bf16[48,2048]{1,0:T(8,128)(2,1)S(1)} %get-tuple-element.44.second_cols.refs_11_, bf16[32,768]{1,0:T(8,128)(2,1)S(1)} %get-tuple-element.45.switches.refs_13_, ...), custom_call_target="tpu_custom_call" | custom-call | flops 1000000000 | bytes 4000000 | tf_op jit(solution)/shard_map/chunk_1/pallas_call | solution.py:706
  9.0 0.0 collective-permute-done.1
  9.0 0.7 %collective-permute-start.2 = (f32[32,128]{1,0:T(8,128)S(1)}, f32[32,128]{1,0:T(8,128)S(1)}, u32[]{:S(2)}, u32[]{:S(2)}) collective-permute-start(f32[32,128]{1,0:T(8,128)S(1)} %add.28.after), channel_id=1, source_target_pairs={{1,17},{3,19},{5,21},{7,23},{9,25},{11,27},{13,29},{15,31},{17,1},... | collective-permute-start | bytes 49160 | tf_op jit(solution)/shard_map/ppermute | solution.py:601
  9.7 0.6 %chunk_2.1.refs_2_ = bf16[256,384]{1,0:T(8,128)(2,1)S(1)} custom-call(f32[32,128]{1,0:T(8,128)S(1)} %add.28.after, bf16[2048,64]{1,0:T(8,128)(2,1)S(1)} %get-tuple-element.43.first_rows.refs_9_, bf16[48,2048]{1,0:T(8,128)(2,1)S(1)} %get-tuple-element.44.second_cols.refs_11_, bf16[32,768]{1,0:T(8,128)(2,1)S(1)} %get-tuple-element.45.switches.refs_13_, ...), custom_call_target="tpu_custom_call" | custom-call | flops 1000000000 | bytes 4000000 | tf_op jit(solution)/shard_map/chunk_2/pallas_call | solution.py:706
  10.2 0.0 collective-permute-done.2
  10.3 0.0 copy-start.5
  10.3 0.7 %collective-permute-start.3 = (f32[64,128]{1,0:T(8,128)S(1)}, f32[64,128]{1,0:T(8,128)S(1)}, u32[]{:S(2)}, u32[]{:S(2)}) collective-permute-start(f32[64,128]{1,0:T(8,128)S(1)} %pad_maximum_fusion.after), channel_id=1, source_target_pairs={{1,3},{3,1},{5,7},{7,5},{9,11},{11,9},{13,15},{15,13},{17,19},{19,... | collective-permute-start | bytes 98312 | tf_op jit(solution)/shard_map/ppermute | solution.py:601
  11.0 0.6 %chunk_3.1.refs_3_ = bf16[256,384]{1,0:T(8,128)(2,1)S(1)} custom-call(f32[64,128]{1,0:T(8,128)S(1)} %pad_maximum_fusion.after, bf16[2048,64]{1,0:T(8,128)(2,1)S(1)} %get-tuple-element.43.first_rows.refs_9_, bf16[48,2048]{1,0:T(8,128)(2,1)S(1)} %get-tuple-element.44.second_cols.refs_11_, bf16[32,768]{1,0:T(8,128)(2,1)S(1)} %get-tuple-element.45.switches.refs_13_, ...), custom_call_target="tpu_custom_call" | custom-call | flops 1000000000 | bytes 4000000 | tf_op jit(solution)/shard_map/chunk_3/pallas_call | solution.py:706
  11.6 0.0 collective-permute-done.3
  11.6 0.7 %collective-permute-start.4 = (f32[64,128]{1,0:T(8,128)S(1)}, f32[64,128]{1,0:T(8,128)S(1)}, u32[]{:S(2)}, u32[]{:S(2)}) collective-permute-start(f32[64,128]{1,0:T(8,128)S(1)} %fusion.after), channel_id=1, source_target_pairs={{1,5},{3,7},{5,1},{7,3},{9,13},{11,15},{13,9},{15,11},{17,21},{19,... | collective-permute-start | bytes 98312 | tf_op jit(solution)/shard_map/ppermute | solution.py:601
  12.2 0.0 copy-done.5
  12.3 0.9 %chunk_4.1.refs_0_ = bf16[768,256]{1,0:T(8,128)(2,1)S(1)} custom-call(f32[64,128]{1,0:T(8,128)S(1)} %fusion.after, s32[3,32]{1,0:T(4,128)S(1)} %bitcast.8, bf16[64,2048]{1,0:T(8,128)(2,1)S(1)} %get-tuple-element.53.first_cols.refs_10_, bf16[2048,128]{1,0:T(8,128)(2,1)S(1)} %get-tuple-element.54.second_rows.refs_12_), custom_call_target="tpu_custom_call" | custom-call | flops 1000000000 | bytes 4000000 | tf_op jit(solution)/shard_map/chunk_4/pallas_call | solution.py:717
  13.1 0.0 collective-permute-done.4
  13.2 0.0 copy-start.1
  13.2 0.0 copy-start.2
  13.2 0.0 copy-start.4
  13.2 1.6 %collective-permute-start.5 = (f32[64,128]{1,0:T(8,128)S(1)}, f32[64,128]{1,0:T(8,128)S(1)}, u32[]{:S(2)}, u32[]{:S(2)}) collective-permute-start(f32[64,128]{1,0:T(8,128)S(1)} %add.32.after), channel_id=1, source_target_pairs={{1,0},{3,2},{5,4},{7,6},{9,8},{11,10},{13,12},{15,14},{17,16},{19,... | collective-permute-start | bytes 98312 | tf_op jit(solution)/shard_map/ppermute | solution.py:699
  14.8 0.9 %chunk_5.1.refs_1_ = bf16[768,256]{1,0:T(8,128)(2,1)S(1)} custom-call(f32[64,128]{1,0:T(8,128)S(1)} %add.32.after, s32[3,32]{1,0:T(4,128)S(1)} %bitcast.9, bf16[64,2048]{1,0:T(8,128)(2,1)S(1)} %get-tuple-element.53.first_cols.refs_10_, bf16[2048,128]{1,0:T(8,128)(2,1)S(1)} %get-tuple-element.54.second_rows.refs_12_), custom_call_target="tpu_custom_call" | custom-call | flops 1000000000 | bytes 4000000 | tf_op jit(solution)/shard_map/chunk_5/pallas_call | solution.py:717
  15.7 17.5 %collective-permute-done.5 = f32[64,128]{1,0:T(8,128)S(1)} collective-permute-done((f32[64,128]{1,0:T(8,128)S(1)}, f32[64,128]{1,0:T(8,128)S(1)}, u32[]{:S(2)}, u32[]{:S(2)}) %collective-permute-start.5) | collective-permute-done | bytes 32800 | tf_op jit(solution)/shard_map/ppermute | solution.py:699
  33.2 0.0 collective-permute-done.6.refs_15_
  33.2 0.0 copy-done.1
  33.2 0.0 copy-done.2
  33.2 0.0 copy-done.4
  33.2 7.9 %leaves.1 = (bf16[2048,384]{1,0:T(8,128)(2,1)}, bf16[3072,128]{1,0:T(8,128)(2,1)S(1)}, bf16[3072,128]{1,0:T(8,128)(2,1)S(1)}, bf16[1536,256]{1,0:T(8,128)(2,1)S(...) custom-call(bf16[768,384]{1,0:T(8,128)(2,1)S(1)} %get-tuple-element.41.refs_0_, ...), custom_call_target="tpu_custom_call" | custom-call | tf_op jit(solution)/shard_map/leaves/pallas_call | solution.py:735
  41.1 3.3 %far.1 = bf16[64,6144]{1,0:T(8,128)(2,1)} custom-call(s32[3,32]{1,0:T(4,128)S(1)} %bitcast.11, bf16[3072,128]{1,0:T(8,128)(2,1)S(1)} %get-tuple-element.59.high, bf16[3072,128]{1,0:T(8,128)(2,1)S(1)} %get-tuple-element.60.low, bf16[768,256]{1,0:T(8,128)(2,1)S(1)} %chunk_4.1.refs_0_, bf16[768,256]{1,0:T(8,128)(2,1)S(1)} %chunk_5.1.refs_1_, ...), custom_call_target="tpu_custom_call" | custom-call | tf_op jit(solution)/shard_map/far/pallas_call | solution.py:775
  (7 shorter events, 0.0 us)
Async XLA Ops:
  0.6 5.2 %copy-start = (bf16[2048,384]{1,0:T(8,128)(2,1)S(1)}, bf16[2048,384]{1,0:T(8,128)(2,1)}, u32[]{:S(2)}) copy-start(bf16[2048,384]{1,0:T(8,128)(2,1)} %refs_16_.1) | copy-start | bytes 4718596
  0.6 5.2 %copy-start.3 = (f32[3,2048]{1,0:T(4,128)S(1)}, f32[3,2048]{1,0:T(4,128)}, u32[]{:S(2)}) copy-start(f32[3,2048]{1,0:T(4,128)} %points) | copy-start | bytes 73732
  0.7 5.2 %copy-start.7 = (s32[32]{0:T(128)S(1)}, s32[32]{0:T(128)}, u32[]{:S(2)}) copy-start(s32[32]{0:T(128)} %param.14) | copy-start | bytes 388
  0.7 5.2 %copy-start.6 = (s32[32,12]{0,1:T(8,128)S(1)}, s32[32,12]{0,1:T(8,128)}, u32[]{:S(2)}) copy-start(s32[32,12]{0,1:T(8,128)} %param.13) | copy-start | bytes 4612
  4.7 3.0 %collective-permute-start = (bf16[384,384]{1,0:T(8,128)(2,1)}, bf16[384,384]{1,0:T(8,128)(2,1)S(1)}, u32[]{:S(2)}, u32[]{:S(2)}) collective-permute-start(bf16[384,384]{1,0:T(8,128)(2,1)} %get-tuple-element.38), channel_id=1, source_target_pairs={{0,1},{1,0},{2,3},{3,2},{4,5},{5,4},{6,7},{7,6},{8,9},{9,8},{10,11... | collective-permute-start | bytes 884744 | tf_op jit(solution)/shard_map/ppermute | solution.py:591
  5.2 28.0 %collective-permute-start.6 = (bf16[352,384]{1,0:T(8,128)(2,1)}, bf16[352,384]{1,0:T(8,128)(2,1)S(1)}, u32[]{:S(2)}, u32[]{:S(2)}) collective-permute-start(bf16[352,384]{1,0:T(8,128)(2,1)} %get-tuple-element.57), channel_id=1, source_target_pairs={{1,2},{2,1},{3,4},{4,3},{5,6},{6,5},{7,8},{8,7},{9,10},{10,9},{11,... | collective-permute-start | bytes 811016 | tf_op jit(solution)/shard_map/ppermute | solution.py:596
  5.9 1.8 %copy-start.8 = (f32[32,128]{1,0:T(8,128)S(1)}, f32[32,128]{1,0:T(8,128)}, u32[]{:S(2)}) copy-start(f32[32,128]{1,0:T(8,128)} %get-tuple-element.37) | copy-start | bytes 49156
  7.7 1.2 %collective-permute-start.1 = (f32[32,128]{1,0:T(8,128)S(1)}, f32[32,128]{1,0:T(8,128)S(1)}, u32[]{:S(2)}, u32[]{:S(2)}) collective-permute-start(f32[32,128]{1,0:T(8,128)S(1)} %add_add_fusion.after), channel_id=1, source_target_pairs={{1,9},{3,11},{5,13},{7,15},{9,1},{11,3},{13,5},{15,7},{17,25},{19,... | collective-permute-start | bytes 49160 | tf_op jit(solution)/shard_map/ppermute | solution.py:601
  9.0 1.3 %collective-permute-start.2 = (f32[32,128]{1,0:T(8,128)S(1)}, f32[32,128]{1,0:T(8,128)S(1)}, u32[]{:S(2)}, u32[]{:S(2)}) collective-permute-start(f32[32,128]{1,0:T(8,128)S(1)} %add.28.after), channel_id=1, source_target_pairs={{1,17},{3,19},{5,21},{7,23},{9,25},{11,27},{13,29},{15,31},{17,1},... | collective-permute-start | bytes 49160 | tf_op jit(solution)/shard_map/ppermute | solution.py:601
  10.3 2.0 %copy-start.5 = (s32[32,3]{0,1:T(4,128)S(1)}, s32[32,3]{0,1:T(4,128)}, u32[]{:S(2)}) copy-start(s32[32,3]{0,1:T(4,128)} %param.15) | copy-start | bytes 1156
  10.3 1.3 %collective-permute-start.3 = (f32[64,128]{1,0:T(8,128)S(1)}, f32[64,128]{1,0:T(8,128)S(1)}, u32[]{:S(2)}, u32[]{:S(2)}) collective-permute-start(f32[64,128]{1,0:T(8,128)S(1)} %pad_maximum_fusion.after), channel_id=1, source_target_pairs={{1,3},{3,1},{5,7},{7,5},{9,11},{11,9},{13,15},{15,13},{17,19},{19,... | collective-permute-start | bytes 98312 | tf_op jit(solution)/shard_map/ppermute | solution.py:601
  11.6 1.6 %collective-permute-start.4 = (f32[64,128]{1,0:T(8,128)S(1)}, f32[64,128]{1,0:T(8,128)S(1)}, u32[]{:S(2)}, u32[]{:S(2)}) collective-permute-start(f32[64,128]{1,0:T(8,128)S(1)} %fusion.after), channel_id=1, source_target_pairs={{1,5},{3,7},{5,1},{7,3},{9,13},{11,15},{13,9},{15,11},{17,21},{19,... | collective-permute-start | bytes 98312 | tf_op jit(solution)/shard_map/ppermute | solution.py:601
  13.2 20.0 %copy-start.1 = (bf16[2048,64]{0,1:T(8,128)(2,1)S(1)}, bf16[2048,64]{0,1:T(8,128)(2,1)}, u32[]{:S(2)}) copy-start(bf16[2048,64]{0,1:T(8,128)(2,1)} %param.9) | copy-start | bytes 786436
  13.2 20.0 %copy-start.2 = (f32[64,64]{1,0:T(8,128)S(1)}, f32[64,64]{1,0:T(8,128)}, u32[]{:S(2)}) copy-start(f32[64,64]{1,0:T(8,128)} %refs_8_.1) | copy-start | bytes 49156
  13.2 20.0 %copy-start.4 = (f32[32,128]{1,0:T(8,128)S(1)}, f32[32,128]{1,0:T(8,128)}, u32[]{:S(2)}) copy-start(f32[32,128]{1,0:T(8,128)} %get-tuple-element.51.refs_6_) | copy-start | bytes 49156
  13.2 20.0 %collective-permute-start.5 = (f32[64,128]{1,0:T(8,128)S(1)}, f32[64,128]{1,0:T(8,128)S(1)}, u32[]{:S(2)}, u32[]{:S(2)}) collective-permute-start(f32[64,128]{1,0:T(8,128)S(1)} %add.32.after), channel_id=1, source_target_pairs={{1,0},{3,2},{5,4},{7,6},{9,8},{11,10},{13,12},{15,14},{17,16},{19,... | collective-permute-start | bytes 98312 | tf_op jit(solution)/shard_map/ppermute | solution.py:699

commit v7 on v6

--- a/solution.py
+++ b/solution.py
@@ -85,9 +85,49 @@
     ]
     for copy in loads + copies:
         copy.start()
+    both = 2 * width
+    lane = iota((width, 2 * both), 1)
+
+    def times(above, columns):
+        found = []
+        for n in range(above.shape[1] // both):
+            parts = jnp.concatenate(split3(above[:, n * both : (n + 1) * both]), axis=1)
+            block = columns(n * 2 * both)
+            zero = jnp.zeros_like(block)
+            block = jnp.concatenate(
+                [jnp.where(lane < both, block, zero), jnp.where(lane < both, zero, block)], axis=0
+            )
+            found.append(mm(parts, jnp.concatenate([block] * 3, axis=0)))
+        return jnp.concatenate(found, axis=1)
+
+    below_copy.wait()
+    transfer_copy.wait()
+    end = below.shape[1]
+    tops = below[:, end - both : end]
+    turned = jnp.concatenate(split3(transfer[...].T), axis=1)
+    above = jnp.concatenate(
+        [tops.astype(F32), mm(turned, jnp.concatenate([tops] * 3, axis=0))], axis=0
+    )
+    end -= both
+    nodes = 4
+    while nodes < count:
+        start = end - nodes * width
+        above = times(above, lambda at, start=start: below[:, start + at : start + at + 2 * both])
+        end = start
+        nodes *= 2
     basis_copy.wait()
+    values = times(above, lambda at: basis[:, at : at + 2 * both])
+    high, middle, low = split3(values)
+    total = mm_nt(
+        jnp.concatenate([high, high, high, middle, middle, low], axis=1),
+        jnp.concatenate([high, middle, low, high, middle, high], axis=1),
+    ) * (1.0 / count)
+    top[...] = fold(total[:width, :width])
+    halves = fold(total[width:, width:])
+    dense[...] = halves
+    inner[halo + width + 32 :, :] = jnp.concatenate(split3(halves), axis=1)
+
     points_copy.wait()
-    transfer_copy.wait()
 
     for target, last in sides:
         bases = basis[:, count * width - span :], basis[:, 0:span]
@@ -106,47 +146,6 @@
             target[base : base + 16, :] = jnp.zeros((16, target.shape[1]), BF16)
             target[base : base + 3, 0:halo] = high
             target[base + 8 : base + 11, 0:halo] = low
-
-    both = 2 * width
-    same = iota((both, both), 0) // width == iota((both, both), 1) // width
-    half_block = jnp.where(same, 0.5, 0.0).astype(F32)
-
-    def pair(index):
-        return below[:, index * both : (index + 1) * both]
-
-    blocks = []
-    for n in range(count // 4):
-        stacked = jnp.concatenate(
-            [basis[:, (2 * n + m) * both : (2 * n + m + 1) * both] for m in range(2)], axis=0
-        )
-        blocks.append(mm_nt(stacked, stacked) * half_block)
-    below_copy.wait()
-    offset = 0
-    while True:
-        nodes = len(blocks)
-        xs, ts = [], []
-        for n in range(nodes):
-            t = pair(offset + n)
-            parts = jnp.concatenate(split3(blocks[n]), axis=0)
-            xs.append(mm(jnp.concatenate([t, t, t], axis=1), parts))
-            ts.append(t)
-        offset += nodes
-        if nodes == 1:
-            break
-        blocks = []
-        for n in range(nodes // 2):
-            x = jnp.concatenate(split3(jnp.concatenate(xs[2 * n : 2 * n + 2], axis=0)), axis=1)
-            t = jnp.concatenate(ts[2 * n : 2 * n + 2], axis=0)
-            blocks.append(mm_nt(x, jnp.concatenate([t, t, t], axis=1)) * half_block)
-    t = ts[0]
-    x = jnp.concatenate(split3(xs[0]), axis=1)
-    top_gram = mm_nt(x, jnp.concatenate([t, t, t], axis=1)) * 0.5
-    top[...] = fold(top_gram)
-    matrix = transfer[...]
-    gram = exact(exact(matrix.T, top_gram), matrix)
-    halves = fold(gram)
-    dense[...] = halves
-    inner[halo + width + 32 :, :] = jnp.concatenate(split3(halves), axis=1)
     for copy in copies:
         copy.wait()
 
@@ -346,37 +345,92 @@
     return body
 
 
-def layers_chunk_kernel(layers, halo):
-    def body(after, first_rows, second_cols, switches, vectors, out):
-        inner_layers(layers, vectors, first_rows, second_cols, switches, out, halo)
+def chunk_kernel(layers, pairs, halo, width):
+    def body(after, far_in, *refs):
+        first_rows, second_cols, switches, vectors, first_cols, second_rows = refs[:6]
+        outs, far_list, sem = refs[6:-2], refs[-2], refs[-1]
+        if pairs:
+            copy = pltpu.make_async_copy(far_in, far_list, sem)
+            copy.start()
+        if layers:
+            inner_layers(layers, vectors, first_rows, second_cols, switches, outs[0], halo)
+        if pairs:
+            copy.wait()
+            far_blocks(
+                pairs, far_list, second_rows, first_cols, outs[-1], width, 0, range(len(pairs))
+            )
 
     return body
 
 
-def pairs_chunk_kernel(pairs, width):
-    def body(after, far_list, first_cols, second_rows, out):
-        far_blocks(pairs, far_list, second_rows, first_cols, out, width, 0, range(len(pairs)))
-
-    return body
+def edges_kernel(
+    after, inner, outer, first_rows, second_cols, switches, vectors,
+    out, halo_rows, ends, sides, place, halo_cols, sems,
+):
+    halo = ends.shape[1]
+    width = halo // LAYER
+    own = vectors.shape[0] // width
+    layers = own // LAYER
+    extra = sides.shape[1]
+    odd = lax.axis_index("sub") % 2
+    arrived = ((inner, 1 - odd), (outer, odd))
+    side_copies = [
+        pltpu.make_async_copy(
+            block.at[pl.ds(halo + width, extra), :], sides.at[side], sems.at[n]
+        )
+        for n, (block, side) in enumerate(arrived)
+    ]
+    end_copies = [
+        pltpu.make_async_copy(block.at[pl.ds(0, halo), :], ends.at[side], sems.at[2 + n])
+        for n, (block, side) in enumerate(arrived)
+    ]
+    for copy in side_copies + end_copies:
+        copy.start()
+    lanes = PAD * width
+    place[...] = jnp.zeros(place.shape, F32)
+    for copy in side_copies:
+        copy.wait()
+    for side, first_leaf in enumerate((-PAD, own)):
+        for n in range(2):
+            values = sides[side, 16 * n : 16 * n + 16, 0:halo].astype(F32)
+            place[0:3, n * halo : (n + 1) * halo] = values[0:3, :] + values[8:11, :]
+        leaf = iota((8, lanes), 1) // width + (first_leaf + PAD)
+        second = features(place[...], leaf, layers // 2 + PAD // LAYER)[1]
+        halo_cols[side, :, :] = second.astype(BF16)
+        halo_rows[side * lanes : (side + 1) * lanes, :] = rows_of(second)
+    weights = [
+        near_weights(
+            first_rows, jnp.concatenate(columns, axis=1), switches, index, halo
+        )
+        for index, columns in (
+            (0, [halo_cols[0, :, halo:], second_cols[:, 0 : 2 * halo]]),
+            (layers - 1, [second_cols[:, (layers - 2) * halo :], halo_cols[1, :, 0:halo]]),
+        )
+    ]
+    for copy in end_copies:
+        copy.wait()
+    value = mm(weights[0][:, 0:halo], ends[0, :, :])
+    value = value + mm(weights[0][:, halo:], vectors[0 : 2 * halo, :])
+    out[0:halo, :] = value.astype(BF16)
+    value = mm(weights[1][:, 0 : 2 * halo], vectors[(layers - 2) * halo :, :])
+    value = value + mm(weights[1][:, 2 * halo :], ends[1, :, :])
+    out[halo:, :] = value.astype(BF16)
 
 
 def leaves_kernel(chunks, edge_pairs, members, groups, *refs):
-    outer = len(chunks)
-    inner_near = refs[:outer]
+    outer_count = len(chunks) + 1
+    near_parts = refs[:outer_count]
     (
-        far_list,
+        far_in,
         basis,
         top,
         upper,
         transfer,
-        first_rows,
         first_cols,
-        second_cols,
         own_rows,
-        switches,
+        halo_rows,
         inner,
         outer,
-        vectors,
         near,
         high,
         low,
@@ -384,41 +438,37 @@
         device_factor,
         group_factor,
         root_factor,
-        ends,
+        far_list,
         sides,
-        place,
-        halo_cols,
         second_rows,
-        results,
         grams,
         work,
         factors,
         sems,
-    ) = refs[outer:]
+    ) = refs[outer_count:]
     width = basis.shape[0]
     own = basis.shape[1] // width
     total = own + 2 * PAD
     halo = LAYER * width
     layers = own // LAYER
     both = 2 * width
-    extra = sides.shape[1]
     odd = lax.axis_index("sub") % 2
-    arrived = ((inner, 1 - odd), (outer, odd))
     side_copies = [
-        pltpu.make_async_copy(block.at[pl.ds(halo, extra), :], sides.at[side], sems.at[n])
-        for n, (block, side) in enumerate(arrived)
+        pltpu.make_async_copy(block.at[pl.ds(halo, width), :], sides.at[side], sems.at[n])
+        for n, (block, side) in enumerate(((inner, 1 - odd), (outer, odd)))
     ]
-    end_copies = [
-        pltpu.make_async_copy(block.at[pl.ds(0, halo), :], ends.at[side], sems.at[2 + n])
-        for n, (block, side) in enumerate(arrived)
-    ]
+    list_copy = pltpu.make_async_copy(far_in, far_list, sems.at[2])
+    places = [(part, 0, chunk[0], len(chunk)) for part, chunk in zip(near_parts, chunks)]
+    places += [(near_parts[-1], n, index, 1) for n, index in enumerate((0, layers - 1))]
     near_copies = [
         pltpu.make_async_copy(
-            part, near.at[pl.ds(chunk[0] * halo, len(chunk) * halo), :], sems.at[6 + n]
-        )
-        for n, (part, chunk) in enumerate(zip(inner_near, chunks))
+            part.at[pl.ds(start * halo, many * halo), :],
+            near.at[pl.ds(index * halo, many * halo), :],
+            sems.at[3 + n],
+        )
+        for n, (part, start, index, many) in enumerate(places)
     ]
-    for copy in side_copies + end_copies + near_copies:
+    for copy in side_copies + [list_copy] + near_copies:
         copy.start()
 
     lane = iota((width, both), 1)
@@ -453,48 +503,12 @@
             grams[spot * STRIDE : spot * STRIDE + width // 2, :] = fold(mm_nt(piece, piece))
 
     lanes = PAD * width
-    place[...] = jnp.zeros(place.shape, F32)
-    for side, first_leaf in enumerate((-PAD, own)):
-        for n in range(2):
-            base = width + 16 * n
-            values = sides[side, base : base + 16, 0:halo].astype(F32)
-            place[0:3, n * halo : (n + 1) * halo] = values[0:3, :] + values[8:11, :]
-        leaf = iota((8, lanes), 1) // width + (first_leaf + PAD)
-        second = features(place[...], leaf, layers // 2 + PAD // LAYER)[1]
-        halo_cols[side, :, :] = second.astype(BF16)
-        at = (PAD + first_leaf) * width
-        second_rows[at : at + lanes, :] = rows_of(second)
+    second_rows[0:lanes, :] = halo_rows[0:lanes, :]
     second_rows[lanes : lanes + own * width, :] = own_rows[...]
-
-    copies = [
-        pltpu.make_async_copy(results.at[n], near.at[pl.ds(index * halo, halo), :], sems.at[4 + n])
-        for n, index in enumerate((0, layers - 1))
-    ]
-
-    def edge(n):
-        if n == 0:
-            columns = [halo_cols[0, :, halo:], second_cols[:, 0 : 2 * halo]]
-            index = 0
-        else:
-            columns = [second_cols[:, (layers - 2) * halo :], halo_cols[1, :, 0:halo]]
-            index = layers - 1
-        weights = near_weights(
-            first_rows, jnp.concatenate(columns, axis=1), switches, index, halo
-        )
-        if n == 0:
-            value = mm(weights[:, 0:halo], ends[0, :, :])
-            value = value + mm(weights[:, halo:], vectors[0 : 2 * halo, :])
-        else:
-            value = mm(weights[:, 0 : 2 * halo], vectors[(layers - 2) * halo :, :])
-            value = value + mm(weights[:, 2 * halo :], ends[1, :, :])
-        results[n, :, :] = value.astype(BF16)
-        copies[n].start()
-
+    second_rows[lanes + own * width :, :] = halo_rows[lanes:, :]
     panels = width // 8
 
     def beside(p):
-        if p in (1, 3):
-            edge(p // 2)
         places = range(p * len(edge_pairs) // panels, (p + 1) * len(edge_pairs) // panels)
         far_blocks(
             [edge_pairs[n] for n in places],
@@ -508,8 +522,7 @@
         )
 
     to_lanes(grams, work, width, total)
-    for copy in end_copies:
-        copy.wait()
+    list_copy.wait()
     factor_lanes(work, width, beside)
     from_lanes(work, factors, width, total)
     device_factor[...] = exact(unfold(factors[0 : width // 2, :]), transfer[...])
@@ -524,12 +537,14 @@
         )
         at = slice(spot * width, (spot + 1) * width)
         high[at, :], low[at, :] = split2(twice)
-    for copy in copies + near_copies:
+    for copy in near_copies:
         copy.wait()
 
 
-def far_kernel(plan, far_list, high, low, *refs):
-    blocks, coupling = refs[:-1], refs[-1]
+def far_kernel(plan, far_in, high, low, *refs):
+    blocks, (coupling, far_list, sem) = refs[:-3], refs[-3:]
+    copy = pltpu.make_async_copy(far_in, far_list, sem)
+    copy.start()
     width = coupling.shape[0]
     far, own = far_list.shape
     both = 2 * width
@@ -557,6 +572,8 @@
                     jnp.concatenate([kh, kl, kh], axis=1), jnp.concatenate([rh, rh, rl], axis=1)
                 )
             )
+        if start == 0:
+            copy.wait()
         outs = []
         for index, half in zip(indices, halves):
             zh, zl = split2(half * (1.0 / width))
@@ -592,13 +609,13 @@
 
 
 def swap_outer(block):
-    inside = range(1, lax.axis_size(AXES) - 1)
-    return lax.ppermute(block, AXES, [(i, i + 1 if i % 2 else i - 1) for i in inside])
+    many = lax.axis_size(AXES)
+    return lax.ppermute(block, AXES, [(i, (i + 1 if i % 2 else i - 1) % many) for i in range(many)])
 
 
 def exchange(value, distance):
-    odd = range(1, lax.axis_size(AXES), 2)
-    return value + lax.ppermute(value, AXES, [(i, i ^ distance) for i in odd])
+    pairs = [(i, i ^ distance) for i in range(lax.axis_size(AXES))]
+    return value + lax.ppermute(value, AXES, pairs)
 
 
 def per_device(
@@ -613,7 +630,6 @@
     total = own + 2 * PAD
     members, groups = lax.axis_size("sub"), lax.axis_size("group")
     vmem = pl.BlockSpec(memory_space=pltpu.VMEM)
-    smem = pl.BlockSpec(memory_space=pltpu.SMEM)
     hbm = pl.BlockSpec(memory_space=pl.ANY)
     square = jax.ShapeDtypeStruct((width, width), F32)
     extra = halo + width + 32
@@ -651,10 +667,10 @@
     sub_bits = members.bit_length() - 1
     steps = [members << bit for bit in range(groups.bit_length() - 1)]
     steps += [1 << bit for bit in range(1, sub_bits)]
-    chunks = [[1, 2, 3], [4], [5], [6]]
     inner_pairs = list(range(PAD // 2, (own - PAD) // 2))
     few = len(inner_pairs) // 2
-    pair_chunks = [inner_pairs[:few], inner_pairs[few:]]
+    chunks = [[1, 2], [3, 4], [5], [6]]
+    pair_chunks = [[], [], inner_pairs[:few], inner_pairs[few:]]
     blocks, plan, parts = [], {}, []
 
     def part_shape(count):
@@ -687,53 +703,63 @@
     ]
     pair_gram = gram = dense + (summands[0] + (summands[1] + summands[2]))
     gram, parts[0] = lax.optimization_barrier((gram, parts[0]))
-    work = [("layers", chunk) for chunk in chunks[1:]] + [("pairs", chunk) for chunk in pair_chunks]
     first_rows, first_cols, second_cols, second_rows, switches = shared
-    for n in range(max(len(steps) + 1, len(work))):
+    for n in range(max(len(steps), len(chunks))):
         before = gram
         if n < len(steps):
             if n == len(steps) - sub_bits + 1:
                 gram = before = jnp.concatenate([pair_gram, gram], axis=0)
             gram = exchange(gram, steps[n])
-        elif n == len(steps):
-            handed = lax.ppermute(
-                gram, AXES, [(i, i - 1) for i in range(1, lax.axis_size(AXES), 2)]
-            )
-            gram = jnp.where(lax.axis_index("sub") % 2 == 1, gram, handed)
-        if n < len(work):
-            kind, chunk = work[n]
-            if kind == "layers":
-                out = pl.pallas_call(
-                    layers_chunk_kernel(chunk, halo),
-                    out_shape=part_shape(len(chunk)),
-                    in_specs=[hbm] + [vmem] * 4,
-                    out_specs=vmem,
-                    compiler_params=room(10),
-                    cost_estimate=cost,
-                    name=f"chunk_{n + 1}",
-                )(before, first_rows, second_cols, switches, vectors)
-                parts.append(out)
-            else:
-                out = pl.pallas_call(
-                    pairs_chunk_kernel(chunk, width),
-                    out_shape=block_shape(len(chunk)),
-                    in_specs=[hbm, smem] + [vmem] * 2,
-                    out_specs=vmem,
-                    compiler_params=room(10),
-                    cost_estimate=cost,
-                    name=f"chunk_{n + 1}",
-                )(before, far_list, first_cols, second_rows)
-                plan.update((index, (len(blocks), m)) for m, index in enumerate(chunk))
-                blocks.append(out)
-            gram, out = lax.optimization_barrier((gram, out))
-            (parts if kind == "layers" else blocks)[-1] = out
+        if n + 1 < len(chunks):
+            layer_chunk, pair_chunk = chunks[n + 1], pair_chunks[n + 1]
+            shapes = [part_shape(len(layer_chunk))] * bool(layer_chunk)
+            shapes += [block_shape(len(pair_chunk))] * bool(pair_chunk)
+            outs = pl.pallas_call(
+                chunk_kernel(layer_chunk, pair_chunk, halo, width),
+                out_shape=tuple(shapes),
+                in_specs=[hbm] * 2 + [vmem] * 6,
+                out_specs=(vmem,) * len(shapes),
+                scratch_shapes=[
+                    pltpu.SMEM(far_list.shape, jnp.int32),
+                    pltpu.SemaphoreType.DMA,
+                ],
+                compiler_params=room(10),
+                cost_estimate=cost,
+                name=f"chunk_{n + 1}",
+            )(before, far_list, first_rows, second_cols, switches, vectors, first_cols, second_rows)
+            gram, outs = lax.optimization_barrier((gram, outs))
+            if layer_chunk:
+                parts.append(outs[0])
+            if pair_chunk:
+                plan.update((index, (len(blocks), m)) for m, index in enumerate(pair_chunk))
+                blocks.append(outs[-1])
+        elif n + 1 == len(chunks):
+            edge_part, halo_rows = pl.pallas_call(
+                edges_kernel,
+                out_shape=(
+                    part_shape(2),
+                    jax.ShapeDtypeStruct((2 * PAD * width, 2 * width), BF16),
+                ),
+                in_specs=[hbm] * 3 + [vmem] * 4,
+                out_specs=(vmem,) * 2,
+                scratch_shapes=[
+                    pltpu.VMEM((2, halo, columns), BF16),
+                    pltpu.VMEM((2, 32, columns), BF16),
+                    pltpu.VMEM((8, PAD * width), F32),
+                    pltpu.VMEM((2, 48, PAD * width), BF16),
+                    pltpu.SemaphoreType.DMA((4,)),
+                ],
+                compiler_params=room(10),
+                cost_estimate=cost,
+                name="edges",
+            )(before, from_inner, from_outer, first_rows, second_cols, switches, vectors)
+            gram, edge_part = lax.optimization_barrier((gram, edge_part))
 
     edge_pairs = [index for index in range(own // 2) if index not in plan]
     plan.update((index, (len(blocks), m)) for m, index in enumerate(edge_pairs))
-    near_chunks = [chunk for chunk in chunks if chunk]
     split_factors = jax.ShapeDtypeStruct((total * width, 2 * width), BF16)
     near, high, low, edge_blocks, device_factor, group_factor, root_factor = pl.pallas_call(
-        functools.partial(leaves_kernel, near_chunks, edge_pairs, members, groups),
+        functools.partial(leaves_kernel, chunks, edge_pairs, members, groups),
         out_shape=(
             jax.ShapeDtypeStruct(vectors.shape, BF16),
             split_factors,
@@ -743,40 +769,43 @@
             square,
             square,
         ),
-        in_specs=[hbm] * len(parts) + [smem] + [vmem] * 9 + [hbm] * 2 + [vmem],
+        in_specs=[hbm] * (len(parts) + 2) + [vmem] * 7 + [hbm] * 2,
         out_specs=(hbm,) + (vmem,) * 6,
         scratch_shapes=[
-            pltpu.VMEM((2, halo, columns), BF16),
-            pltpu.VMEM((2, width + 32, columns), BF16),
-            pltpu.VMEM((8, PAD * width), F32),
-            pltpu.VMEM((2, 48, PAD * width), BF16),
+            pltpu.SMEM(far_list.shape, jnp.int32),
+            pltpu.VMEM((2, width, columns), BF16),
             pltpu.VMEM((total * width, 2 * width), BF16),
-            pltpu.VMEM((2, halo, columns), BF16),
             pltpu.VMEM((total * STRIDE, 2 * width), F32),
             pltpu.VMEM((width, width, 128), F32),
             pltpu.VMEM((total * STRIDE, 2 * width), F32),
-            pltpu.SemaphoreType.DMA((6 + len(parts),)),
+            pltpu.SemaphoreType.DMA((5 + len(parts),)),
         ],
         compiler_params=room(24),
         name="leaves",
     )(
         *parts,
+        edge_part,
         far_list,
         basis,
         top,
         gram,
         device_transfer,
-        *shared,
+        first_cols,
+        second_rows,
+        halo_rows,
         from_inner,
         from_outer,
-        vectors,
     )
 
     coupling = pl.pallas_call(
         functools.partial(far_kernel, plan),
         out_shape=jax.ShapeDtypeStruct((width, own * far_index.shape[1] * width), BF16),
-        in_specs=[smem] + [vmem] * (3 + len(blocks)),
+        in_specs=[hbm] + [vmem] * (3 + len(blocks)),
         out_specs=vmem,
+        scratch_shapes=[
+            pltpu.SMEM(far_list.shape, jnp.int32),
+            pltpu.SemaphoreType.DMA,
+        ],
         compiler_params=room(16),
         name="far",
     )(far_list, high, low, *blocks, edge_blocks)

time: 44.7 us -> 39.9 us (0.89)
  waiting for transfers between devices: 17.5 us -> 10.4 us
  starting transfers between devices: 5.44 us -> 8.32 us
    ppermute x6 -> x5, waiting for transfers between devices: 17.5 us -> 10.4 us  [the longest x4 10.3 us: exchange(): return value + lax.ppermute(value, AXES, pairs)]
    ppermute x6 -> x5, starting transfers between devices: 4.92 us -> 7.81 us  [the longest x1 6.59 us: swap_outer(): lax.ppermute(block, AXES, [(i, (i + 1 if i % 2 else i - 1) % many) for i...]
    pallas_call x1, Pallas kernels: 3.98 us -> 5.05 us  [per_device(): pl.pallas_call(tree_kernel, out_shape=(jax.ShapeDtypeStruct((half, 2 * wi...]
    pallas_call x6 -> x5, Pallas kernels: 11.4 us -> 10.5 us  [the longest x1 5.69 us: per_device(): pl.pallas_call(functools.partial(leaves_kernel, chunks, edge_pairs, membe...]
    pallas_call x1, Pallas kernels: 1.77 us -> 1.3 us  [per_device(): pl.pallas_call(first_chunk_kernel(chunks[0]), out_shape=(part_shape(len(c...]
  transfers between devices with their start and end apart: 7 -> 6, of which waited for: 1 -> 4; matrix products, arithmetic and copies ran while one was open for 0% -> 0% of each run, Pallas kernels for 12% -> 15%
where the time goes in v7:
time: 39.9 us; the launch traced here: 39.8 us
  Pallas kernels  20 us (50%)
  waiting for transfers between devices  10.4 us (26%)
  starting transfers between devices  8.32 us (21%)
  between operations  1.01 us (3%)
    ppermute x4, waiting for transfers between devices, exchange(): return value + lax.ppermute(value, AXES, pairs)  10.3 us
    ppermute x1, starting transfers between devices, swap_outer(): lax.ppermute(block, AXES, [(i, (i + 1 if i % 2 else i - 1) % many) for i...  6.59 us
    pallas_call x1, Pallas kernels, per_device(): pl.pallas_call(functools.partial(leaves_kernel, chunks, edge_pairs, membe...  5.69 us
    pallas_call x1, Pallas kernels, per_device(): pl.pallas_call(tree_kernel, out_shape=(jax.ShapeDtypeStruct((half, 2 * wi...  5.05 us
    pallas_call x1, Pallas kernels, per_device(): pl.pallas_call(functools.partial(far_kernel, plan), out_shape=jax.ShapeDt...  3.2 us
    pallas_call x3, Pallas kernels, per_device(): pl.pallas_call(chunk_kernel(layer_chunk, pair_chunk, halo, width), out_sh...  2.78 us
    pallas_call x1, Pallas kernels, per_device(): pl.pallas_call(edges_kernel, out_shape=(part_shape(2), jax.ShapeDtypeStru...  1.98 us
    pallas_call x1, Pallas kernels, per_device(): pl.pallas_call(first_chunk_kernel(chunks[0]), out_shape=(part_shape(len(c...  1.3 us
  transfers between devices with their start and end apart: 6, of which 4 were waited for; matrix products, arithmetic and copies ran while one was open for 0% of the time, Pallas kernels for 15%

profile of v7, /device:TPU:0, one launch (start us, length us, event | category | flops | bytes accessed | tf_op | source)
XLA Modules:
  0.0 39.8 jit_solution(6369504476596125524)
XLA Ops:
  0.6 0.0 copy-start
  0.6 0.0 copy-start.3
  0.7 0.0 copy-start.7
  0.7 0.0 copy-start.6
  0.7 5.1 %tree.1 = (f32[32,128]{1,0:T(8,128)}, f32[32,128]{1,0:T(8,128)}, bf16[352,384]{1,0:T(8,128)(2,1)}, bf16[384,384]{1,0:T(8,128)(2,1)}) custom-call(f32[3,2048]{1,0:T(4,128)} %points, bf16[64,2048]{1,0:T(8,128)(2,1)} %bitcast.6, bf16[64,1920]{1,0:T(8,128)(2,1)} %bitcast.16, f32[64,64]{1,0:T(8,128)} %refs_9_.1, bf16[2048,384]{1,0:T(8,128)(2,1)} %vectors.5), custom_call_target="tpu_custom_call" | custom-call | tf_op jit(solution)/shard_map/tree/pallas_call | solution.py:644
  5.7 0.5 %collective-permute-start = (bf16[384,384]{1,0:T(8,128)(2,1)}, bf16[384,384]{1,0:T(8,128)(2,1)S(1)}, u32[]{:S(2)}, u32[]{:S(2)}) collective-permute-start(bf16[384,384]{1,0:T(8,128)(2,1)} %get-tuple-element.44), channel_id=1, source_target_pairs={{0,1},{1,0},{2,3},{3,2},{4,5},{5,4},{6,7},{7,6},{8,9},{9,8},{10,11... | collective-permute-start | bytes 884744 | tf_op jit(solution)/shard_map/ppermute | solution.py:608
  6.2 6.6 %collective-permute-start.5 = (bf16[352,384]{1,0:T(8,128)(2,1)}, bf16[352,384]{1,0:T(8,128)(2,1)S(1)}, u32[]{:S(2)}, u32[]{:S(2)}) collective-permute-start(bf16[352,384]{1,0:T(8,128)(2,1)} %get-tuple-element.64), channel_id=1, source_target_pairs={{0,31},{1,2},{2,1},{3,4},{4,3},{5,6},{6,5},{7,8},{8,7},{9,10},{10,... | collective-permute-start | bytes 811016 | tf_op jit(solution)/shard_map/ppermute | solution.py:613
  12.8 0.0 copy-done
  12.8 0.0 copy-done.3
  12.8 0.0 copy-done.7
  12.8 0.0 copy-done.6
  12.9 0.0 copy-start.8
  12.9 0.0 copy-start.5
  12.9 1.3 %chunk_0.1 = (bf16[512,384]{1,0:T(8,128)(2,1)S(1)}, bf16[2048,64]{1,0:T(8,128)(2,1)S(1)}, bf16[64,2048]{1,0:T(8,128)(2,1)S(1)}, bf16[48,2048]{1,0:T(8,128)(2,1)S...) custom-call(f32[3,2048]{1,0:T(4,128)S(1)} %copy-done.3, s32[12,32]{1,0:T(8,128)S(1)} %bitcast.13, ...), custom_call_target="tpu_custom_call" | custom-call | flops 1000000000 | bytes 4000000 | tf_op jit(solution)/shard_map/chunk_0/pallas_call | solution.py:683
  14.2 0.0 collective-permute-done.inner.refs_13_
  14.2 0.0 copy-done.8
  14.2 0.1 collective-permute-start.1
  14.3 0.0 copy-done.5
  14.3 1.0 %chunk_1.1.refs_1_ = bf16[512,384]{1,0:T(8,128)(2,1)S(1)} custom-call(f32[32,128]{1,0:T(8,128)S(1)} %add_add_fusion.after, s32[3,32]{1,0:T(4,128)S(1)} %bitcast.8, bf16[2048,64]{1,0:T(8,128)(2,1)S(1)} %get-tuple-element.49.refs_0_.first_rows, bf16[48,2048]{1,0:T(8,128)(2,1)S(1)} %get-tuple-element.50.refs_1_.second_cols, ...), custom_call_target="tpu_custom_call" | custom-call | flops 1000000000 | bytes 4000000 | tf_op jit(solution)/shard_map/chunk_1/pallas_call | solution.py:717
  15.3 2.7 %collective-permute-done.1 = f32[32,128]{1,0:T(8,128)S(1)} collective-permute-done((f32[32,128]{1,0:T(8,128)S(1)}, f32[32,128]{1,0:T(8,128)S(1)}, u32[]{:S(2)}, u32[]{:S(2)}) %collective-permute-start.1) | collective-permute-done | bytes 16416 | tf_op jit(solution)/shard_map/ppermute | solution.py:618
  18.0 1.0 %collective-permute-start.2 = (f32[32,128]{1,0:T(8,128)S(1)}, f32[32,128]{1,0:T(8,128)S(1)}, u32[]{:S(2)}, u32[]{:S(2)}) collective-permute-start(f32[32,128]{1,0:T(8,128)S(1)} %add.24.after), channel_id=1, source_target_pairs={{0,16},{1,17},{2,18},{3,19},{4,20},{5,21},{6,22},{7,23},{8,24},{9,... | collective-permute-start | bytes 49160 | tf_op jit(solution)/shard_map/ppermute | solution.py:618
  19.0 0.9 %chunk_2.1 = (bf16[256,384]{1,0:T(8,128)(2,1)S(1)}, bf16[768,256]{1,0:T(8,128)(2,1)S(1)}) custom-call(f32[32,128]{1,0:T(8,128)S(1)} %add.24.after, s32[3,32]{1,0:T(4,128)S(1)} %bitcast.9, bf16[2048,64]{1,0:T(8,128)(2,1)S(1)} %get-tuple-element.49.refs_0_.first_rows, bf16[48,2048]{1,0:T(8,128)(2,1)S(1)} %get-tuple-element.50.refs_1_.second_cols, ...), custom_call_target="tpu_custom_call" | custom-call | flops 1000000000 | bytes 4000000 | tf_op jit(solution)/shard_map/chunk_2/pallas_call | solution.py:717
  19.9 2.7 %collective-permute-done.2 = f32[32,128]{1,0:T(8,128)S(1)} collective-permute-done((f32[32,128]{1,0:T(8,128)S(1)}, f32[32,128]{1,0:T(8,128)S(1)}, u32[]{:S(2)}, u32[]{:S(2)}) %collective-permute-start.2) | collective-permute-done | bytes 16416 | tf_op jit(solution)/shard_map/ppermute | solution.py:618
  22.7 0.1 collective-permute-start.3
  22.8 0.9 %chunk_3.1 = (bf16[256,384]{1,0:T(8,128)(2,1)S(1)}, bf16[768,256]{1,0:T(8,128)(2,1)S(1)}) custom-call(f32[64,128]{1,0:T(8,128)S(1)} %pad_maximum_fusion.after, s32[3,32]{1,0:T(4,128)S(1)} %bitcast.10, bf16[2048,64]{1,0:T(8,128)(2,1)S(1)} %get-tuple-element.49.refs_0_.first_rows, bf16[48,2048]{1,0:T(8,128)(2,1)S(1)} %get-tuple-element.50.refs_1_.second_cols, ...), custom_call_target="tpu_custom_call" | custom-call | flops 1000000000 | bytes 4000000 | tf_op jit(solution)/shard_map/chunk_3/pallas_call | solution.py:717
  23.7 3.0 %collective-permute-done.3 = f32[64,128]{1,0:T(8,128)S(1)} collective-permute-done((f32[64,128]{1,0:T(8,128)S(1)}, f32[64,128]{1,0:T(8,128)S(1)}, u32[]{:S(2)}, u32[]{:S(2)}) %collective-permute-start.3) | collective-permute-done | bytes 32800 | tf_op jit(solution)/shard_map/ppermute | solution.py:618
  26.7 0.0 copy-start.1
  26.7 0.0 copy-start.2
  26.7 0.0 copy-start.4
  26.7 0.1 collective-permute-start.4
  26.8 0.0 collective-permute-done.5.outer.refs_14_
  26.8 2.0 %edges.1 = (bf16[512,384]{1,0:T(8,128)(2,1)S(1)}, bf16[1024,128]{1,0:T(8,128)(2,1)S(1)}) custom-call(f32[64,128]{1,0:T(8,128)S(1)} %fusion.after, bf16[384,384]{1,0:T(8,128)(2,1)S(1)} %collective-permute-done.inner.refs_13_, bf16[352,384]{1,0:T(8,128)(2,1)S(1)} %collective-permute-done.5.outer.refs_14_, ...), custom_call_target="tpu_custom_call" | custom-call | flops 1000000000 | bytes 4000000 | tf_op jit(solution)/shard_map/edges/pallas_call | solution.py:737
  28.8 1.9 %collective-permute-done.4 = f32[64,128]{1,0:T(8,128)S(1)} collective-permute-done((f32[64,128]{1,0:T(8,128)S(1)}, f32[64,128]{1,0:T(8,128)S(1)}, u32[]{:S(2)}, u32[]{:S(2)}) %collective-permute-start.4) | collective-permute-done | bytes 32800 | tf_op jit(solution)/shard_map/ppermute | solution.py:618
  30.7 0.0 copy-done.1
  30.7 0.0 copy-done.2
  30.7 0.0 copy-done.4
  30.7 5.7 %leaves.1 = (bf16[2048,384]{1,0:T(8,128)(2,1)}, bf16[3072,128]{1,0:T(8,128)(2,1)S(1)}, bf16[3072,128]{1,0:T(8,128)(2,1)S(1)}, bf16[1536,256]{1,0:T(8,128)(2,1)S(...) custom-call(bf16[512,384]{1,0:T(8,128)(2,1)S(1)} %get-tuple-element.47.refs_0_, ...), custom_call_target="tpu_custom_call" | custom-call | tf_op jit(solution)/shard_map/leaves/pallas_call | solution.py:761
  36.4 3.2 %far.1 = bf16[64,6144]{1,0:T(8,128)(2,1)} custom-call(s32[3,32]{1,0:T(4,128)S(1)} %bitcast.12, bf16[3072,128]{1,0:T(8,128)(2,1)S(1)} %get-tuple-element.71.high, bf16[3072,128]{1,0:T(8,128)(2,1)S(1)} %get-tuple-element.72.low, bf16[768,256]{1,0:T(8,128)(2,1)S(1)} %get-tuple-element.73.refs_0_, bf16[768,256]{1,0:T(8,128)(2,1)S(1)} %get-tuple-element.74.refs_1_, ...), custom_call_target="tpu_custom_call" | custom-call | tf_op jit(solution)/shard_map/far/pallas_call | solution.py:800
  (6 shorter events, 0.0 us)
Async XLA Ops:
  0.6 12.2 %copy-start = (bf16[2048,384]{1,0:T(8,128)(2,1)S(1)}, bf16[2048,384]{1,0:T(8,128)(2,1)}, u32[]{:S(2)}) copy-start(bf16[2048,384]{1,0:T(8,128)(2,1)} %vectors.5) | copy-start | bytes 4718596
  0.6 12.2 %copy-start.3 = (f32[3,2048]{1,0:T(4,128)S(1)}, f32[3,2048]{1,0:T(4,128)}, u32[]{:S(2)}) copy-start(f32[3,2048]{1,0:T(4,128)} %points) | copy-start | bytes 73732
  0.7 12.2 %copy-start.7 = (s32[32]{0:T(128)S(1)}, s32[32]{0:T(128)}, u32[]{:S(2)}) copy-start(s32[32]{0:T(128)} %param.14) | copy-start | bytes 388
  0.7 12.2 %copy-start.6 = (s32[32,12]{0,1:T(8,128)S(1)}, s32[32,12]{0,1:T(8,128)}, u32[]{:S(2)}) copy-start(s32[32,12]{0,1:T(8,128)} %param.13) | copy-start | bytes 4612
  5.7 8.5 %collective-permute-start = (bf16[384,384]{1,0:T(8,128)(2,1)}, bf16[384,384]{1,0:T(8,128)(2,1)S(1)}, u32[]{:S(2)}, u32[]{:S(2)}) collective-permute-start(bf16[384,384]{1,0:T(8,128)(2,1)} %get-tuple-element.44), channel_id=1, source_target_pairs={{0,1},{1,0},{2,3},{3,2},{4,5},{5,4},{6,7},{7,6},{8,9},{9,8},{10,11... | collective-permute-start | bytes 884744 | tf_op jit(solution)/shard_map/ppermute | solution.py:608
  6.2 20.5 %collective-permute-start.5 = (bf16[352,384]{1,0:T(8,128)(2,1)}, bf16[352,384]{1,0:T(8,128)(2,1)S(1)}, u32[]{:S(2)}, u32[]{:S(2)}) collective-permute-start(bf16[352,384]{1,0:T(8,128)(2,1)} %get-tuple-element.64), channel_id=1, source_target_pairs={{0,31},{1,2},{2,1},{3,4},{4,3},{5,6},{6,5},{7,8},{8,7},{9,10},{10,... | collective-permute-start | bytes 811016 | tf_op jit(solution)/shard_map/ppermute | solution.py:613
  12.9 1.3 %copy-start.8 = (f32[32,128]{1,0:T(8,128)S(1)}, f32[32,128]{1,0:T(8,128)}, u32[]{:S(2)}) copy-start(f32[32,128]{1,0:T(8,128)} %get-tuple-element.43) | copy-start | bytes 49156
  12.9 1.4 %copy-start.5 = (s32[32,3]{0,1:T(4,128)S(1)}, s32[32,3]{0,1:T(4,128)}, u32[]{:S(2)}) copy-start(s32[32,3]{0,1:T(4,128)} %param.15) | copy-start | bytes 1156
  14.2 3.8 %collective-permute-start.1 = (f32[32,128]{1,0:T(8,128)S(1)}, f32[32,128]{1,0:T(8,128)S(1)}, u32[]{:S(2)}, u32[]{:S(2)}) collective-permute-start(f32[32,128]{1,0:T(8,128)S(1)} %add_add_fusion.after), channel_id=1, source_target_pairs={{0,8},{1,9},{2,10},{3,11},{4,12},{5,13},{6,14},{7,15},{8,0},{9,1},... | collective-permute-start | bytes 49160 | tf_op jit(solution)/shard_map/ppermute | solution.py:618
  18.0 4.6 %collective-permute-start.2 = (f32[32,128]{1,0:T(8,128)S(1)}, f32[32,128]{1,0:T(8,128)S(1)}, u32[]{:S(2)}, u32[]{:S(2)}) collective-permute-start(f32[32,128]{1,0:T(8,128)S(1)} %add.24.after), channel_id=1, source_target_pairs={{0,16},{1,17},{2,18},{3,19},{4,20},{5,21},{6,22},{7,23},{8,24},{9,... | collective-permute-start | bytes 49160 | tf_op jit(solution)/shard_map/ppermute | solution.py:618
  22.7 4.0 %collective-permute-start.3 = (f32[64,128]{1,0:T(8,128)S(1)}, f32[64,128]{1,0:T(8,128)S(1)}, u32[]{:S(2)}, u32[]{:S(2)}) collective-permute-start(f32[64,128]{1,0:T(8,128)S(1)} %pad_maximum_fusion.after), channel_id=1, source_target_pairs={{0,2},{1,3},{2,0},{3,1},{4,6},{5,7},{6,4},{7,5},{8,10},{9,11},{10,... | collective-permute-start | bytes 98312 | tf_op jit(solution)/shard_map/ppermute | solution.py:618
  26.7 4.0 %copy-start.1 = (bf16[2048,64]{0,1:T(8,128)(2,1)S(1)}, bf16[2048,64]{0,1:T(8,128)(2,1)}, u32[]{:S(2)}) copy-start(bf16[2048,64]{0,1:T(8,128)(2,1)} %param.9) | copy-start | bytes 786436
  26.7 4.0 %copy-start.2 = (f32[64,64]{1,0:T(8,128)S(1)}, f32[64,64]{1,0:T(8,128)}, u32[]{:S(2)}) copy-start(f32[64,64]{1,0:T(8,128)} %refs_9_.1) | copy-start | bytes 49156
  26.7 4.0 %copy-start.4 = (f32[32,128]{1,0:T(8,128)S(1)}, f32[32,128]{1,0:T(8,128)}, u32[]{:S(2)}) copy-start(f32[32,128]{1,0:T(8,128)} %get-tuple-element.67.refs_7_) | copy-start | bytes 49156
  26.7 4.0 %collective-permute-start.4 = (f32[64,128]{1,0:T(8,128)S(1)}, f32[64,128]{1,0:T(8,128)S(1)}, u32[]{:S(2)}, u32[]{:S(2)}) collective-permute-start(f32[64,128]{1,0:T(8,128)S(1)} %fusion.after), channel_id=1, source_target_pairs={{0,4},{1,5},{2,6},{3,7},{4,0},{5,1},{6,2},{7,3},{8,12},{9,13},{10,... | collective-permute-start | bytes 98312 | tf_op jit(solution)/shard_map/ppermute | solution.py:618

commit v8 on v7

--- a/solution.py
+++ b/solution.py
@@ -100,7 +100,28 @@
             found.append(mm(parts, jnp.concatenate([block] * 3, axis=0)))
         return jnp.concatenate(found, axis=1)
 
+    same = iota((both, both), 0) // width == iota((both, both), 1) // width
+    half_block = jnp.where(same, 0.5, 0.0).astype(F32)
+    basis_copy.wait()
+    blocks = []
+    for n in range(count // 4):
+        stacked = jnp.concatenate(
+            [basis[:, (2 * n + m) * both : (2 * n + m + 1) * both] for m in range(2)], axis=0
+        )
+        blocks.append(mm_nt(stacked, stacked) * half_block)
     below_copy.wait()
+    halves = []
+    for n, block in enumerate(blocks):
+        t = below[:, n * both : (n + 1) * both]
+        half = mm(jnp.concatenate([t, t, t], axis=1), jnp.concatenate(split3(block), axis=0))
+        halves.append((half, t))
+    blocks = []
+    for n in range(0, len(halves), 2):
+        (first, t), (second, u) = halves[n : n + 2]
+        x = jnp.concatenate(split3(jnp.concatenate([first, second], axis=0)), axis=1)
+        t = jnp.concatenate([t, u], axis=0)
+        blocks.append(mm_nt(x, jnp.concatenate([t, t, t], axis=1)) * half_block)
+
     transfer_copy.wait()
     end = below.shape[1]
     tops = below[:, end - both : end]
@@ -110,18 +131,27 @@
     )
     end -= both
     nodes = 4
-    while nodes < count:
+    while nodes < count // 2:
         start = end - nodes * width
         above = times(above, lambda at, start=start: below[:, start + at : start + at + 2 * both])
         end = start
         nodes *= 2
-    basis_copy.wait()
-    values = times(above, lambda at: basis[:, at : at + 2 * both])
-    high, middle, low = split3(values)
-    total = mm_nt(
-        jnp.concatenate([high, high, high, middle, middle, low], axis=1),
-        jnp.concatenate([high, middle, low, high, middle, high], axis=1),
-    ) * (1.0 / count)
+
+    total = jnp.zeros((both, both), F32)
+    for n, block in enumerate(blocks):
+        rows = above[:, n * both : (n + 1) * both]
+        high, middle, low = split3(rows)
+        gh, gm, gl = split3(block)
+        x = mm(
+            jnp.concatenate([high, high, high, middle, middle, low], axis=1),
+            jnp.concatenate([gh, gm, gl, gh, gm, gh], axis=0),
+        )
+        xh, xm, xl = split3(x)
+        total = total + mm_nt(
+            jnp.concatenate([xh, xh, xh, xm, xm, xl], axis=1),
+            jnp.concatenate([high, middle, low, high, middle, high], axis=1),
+        )
+    total = total * (4.0 / count)
     top[...] = fold(total[:width, :width])
     halves = fold(total[width:, width:])
     dense[...] = halves
@@ -609,8 +639,9 @@
 
 
 def swap_outer(block):
-    many = lax.axis_size(AXES)
-    return lax.ppermute(block, AXES, [(i, (i + 1 if i % 2 else i - 1) % many) for i in range(many)])
+    last = lax.axis_size(AXES) - 1
+    route = [(i, min(max(i + 1 if i % 2 else i - 1, 0), last)) for i in range(last + 1)]
+    return lax.ppermute(block, AXES, route)
 
 
 def exchange(value, distance):

time: 39.9 us -> 39.1 us (0.980)
  starting transfers between devices: 8.32 us -> 10.4 us
  waiting for transfers between devices: 10.4 us -> 8.54 us
  Pallas kernels: 20 us -> 19 us
    ppermute x4, starting transfers between devices: 1.21 us -> 8.32 us  [exchange(): return value + lax.ppermute(value, AXES, pairs)]
    ppermute x1, starting transfers between devices: 6.59 us -> 1.6 us  [swap_outer(): return lax.ppermute(block, AXES, route)]
    ppermute x4, waiting for transfers between devices: 10.3 us -> 8.54 us  [exchange(): return value + lax.ppermute(value, AXES, pairs)]
    pallas_call x1, Pallas kernels: 5.05 us -> 4.25 us  [per_device(): pl.pallas_call(tree_kernel, out_shape=(jax.ShapeDtypeStruct((half, 2 * wi...]
where the time goes in v8:
time: 39.1 us; the launch traced here: 38.9 us
  Pallas kernels  19 us (49%)
  starting transfers between devices  10.4 us (27%)
  waiting for transfers between devices  8.54 us (22%)
  between operations  0.83 us (2%)
    ppermute x4, waiting for transfers between devices, exchange(): return value + lax.ppermute(value, AXES, pairs)  8.54 us
    ppermute x4, starting transfers between devices, exchange(): return value + lax.ppermute(value, AXES, pairs)  8.32 us
    pallas_call x1, Pallas kernels, per_device(): pl.pallas_call(functools.partial(leaves_kernel, chunks, edge_pairs, membe...  5.69 us
    pallas_call x1, Pallas kernels, per_device(): pl.pallas_call(tree_kernel, out_shape=(jax.ShapeDtypeStruct((half, 2 * wi...  4.25 us
    pallas_call x1, Pallas kernels, per_device(): pl.pallas_call(functools.partial(far_kernel, plan), out_shape=jax.ShapeDt...  3.2 us
    pallas_call x3, Pallas kernels, per_device(): pl.pallas_call(chunk_kernel(layer_chunk, pair_chunk, halo, width), out_sh...  2.78 us
    pallas_call x1, Pallas kernels, per_device(): pl.pallas_call(edges_kernel, out_shape=(part_shape(2), jax.ShapeDtypeStru...  1.81 us
    ppermute x1, starting transfers between devices, swap_outer(): return lax.ppermute(block, AXES, route)  1.6 us
  transfers between devices with their start and end apart: 6, of which 4 were waited for; matrix products, arithmetic and copies ran while one was open for 0% of the time, Pallas kernels for 15%

profile of v8, /device:TPU:0, one launch (start us, length us, event | category | flops | bytes accessed | tf_op | source)
XLA Modules:
  0.0 38.9 jit_solution(3328718304795899263)
XLA Ops:
  0.6 0.0 copy-start
  0.6 0.0 copy-start.3
  0.7 0.0 copy-start.7
  0.7 0.0 copy-start.6
  0.7 4.3 %tree.1 = (f32[32,128]{1,0:T(8,128)}, f32[32,128]{1,0:T(8,128)}, bf16[352,384]{1,0:T(8,128)(2,1)}, bf16[384,384]{1,0:T(8,128)(2,1)}) custom-call(f32[3,2048]{1,0:T(4,128)} %points, bf16[64,2048]{1,0:T(8,128)(2,1)} %bitcast.6, bf16[64,1920]{1,0:T(8,128)(2,1)} %bitcast.16, f32[64,64]{1,0:T(8,128)} %refs_9_.1, bf16[2048,384]{1,0:T(8,128)(2,1)} %vectors.5), custom_call_target="tpu_custom_call" | custom-call | tf_op jit(solution)/shard_map/tree/pallas_call | solution.py:675
  4.9 0.5 %collective-permute-start = (bf16[384,384]{1,0:T(8,128)(2,1)}, bf16[384,384]{1,0:T(8,128)(2,1)S(1)}, u32[]{:S(2)}, u32[]{:S(2)}) collective-permute-start(bf16[384,384]{1,0:T(8,128)(2,1)} %get-tuple-element.44), channel_id=1, source_target_pairs={{0,1},{1,0},{2,3},{3,2},{4,5},{5,4},{6,7},{7,6},{8,9},{9,8},{10,11... | collective-permute-start | bytes 884744 | tf_op jit(solution)/shard_map/ppermute | solution.py:638
  5.5 1.6 %collective-permute-start.5 = (bf16[352,384]{1,0:T(8,128)(2,1)}, bf16[352,384]{1,0:T(8,128)(2,1)S(1)}, u32[]{:S(2)}, u32[]{:S(2)}) collective-permute-start(bf16[352,384]{1,0:T(8,128)(2,1)} %get-tuple-element.64), channel_id=1, source_target_pairs={{0,0},{1,2},{2,1},{3,4},{4,3},{5,6},{6,5},{7,8},{8,7},{9,10},{10,9... | collective-permute-start | bytes 811016 | tf_op jit(solution)/shard_map/ppermute | solution.py:644
  7.1 0.0 copy-done
  7.1 0.0 copy-done.3
  7.1 0.0 copy-done.7
  7.1 0.0 copy-done.6
  7.1 0.0 copy-start.8
  7.1 0.0 copy-start.5
  7.1 1.3 %chunk_0.1 = (bf16[512,384]{1,0:T(8,128)(2,1)S(1)}, bf16[2048,64]{1,0:T(8,128)(2,1)S(1)}, bf16[64,2048]{1,0:T(8,128)(2,1)S(1)}, bf16[48,2048]{1,0:T(8,128)(2,1)S...) custom-call(f32[3,2048]{1,0:T(4,128)S(1)} %copy-done.3, s32[12,32]{1,0:T(8,128)S(1)} %bitcast.13, ...), custom_call_target="tpu_custom_call" | custom-call | flops 1000000000 | bytes 4000000 | tf_op jit(solution)/shard_map/chunk_0/pallas_call | solution.py:714
  8.4 0.0 collective-permute-done.inner.refs_13_
  8.4 0.0 copy-done.8
  8.4 5.4 %collective-permute-start.1 = (f32[32,128]{1,0:T(8,128)S(1)}, f32[32,128]{1,0:T(8,128)S(1)}, u32[]{:S(2)}, u32[]{:S(2)}) collective-permute-start(f32[32,128]{1,0:T(8,128)S(1)} %add_add_fusion.after), channel_id=1, source_target_pairs={{0,8},{1,9},{2,10},{3,11},{4,12},{5,13},{6,14},{7,15},{8,0},{9,1},... | collective-permute-start | bytes 49160 | tf_op jit(solution)/shard_map/ppermute | solution.py:649
  13.9 0.0 copy-done.5
  13.9 1.0 %chunk_1.1.refs_1_ = bf16[512,384]{1,0:T(8,128)(2,1)S(1)} custom-call(f32[32,128]{1,0:T(8,128)S(1)} %add_add_fusion.after, s32[3,32]{1,0:T(4,128)S(1)} %bitcast.8, bf16[2048,64]{1,0:T(8,128)(2,1)S(1)} %get-tuple-element.49.refs_0_.first_rows, bf16[48,2048]{1,0:T(8,128)(2,1)S(1)} %get-tuple-element.50.refs_1_.second_cols, ...), custom_call_target="tpu_custom_call" | custom-call | flops 1000000000 | bytes 4000000 | tf_op jit(solution)/shard_map/chunk_1/pallas_call | solution.py:748
  14.8 2.5 %collective-permute-done.1 = f32[32,128]{1,0:T(8,128)S(1)} collective-permute-done((f32[32,128]{1,0:T(8,128)S(1)}, f32[32,128]{1,0:T(8,128)S(1)}, u32[]{:S(2)}, u32[]{:S(2)}) %collective-permute-start.1) | collective-permute-done | bytes 16416 | tf_op jit(solution)/shard_map/ppermute | solution.py:649
  17.3 2.8 %collective-permute-start.2 = (f32[32,128]{1,0:T(8,128)S(1)}, f32[32,128]{1,0:T(8,128)S(1)}, u32[]{:S(2)}, u32[]{:S(2)}) collective-permute-start(f32[32,128]{1,0:T(8,128)S(1)} %add.24.after), channel_id=1, source_target_pairs={{0,16},{1,17},{2,18},{3,19},{4,20},{5,21},{6,22},{7,23},{8,24},{9,... | collective-permute-start | bytes 49160 | tf_op jit(solution)/shard_map/ppermute | solution.py:649
  20.1 0.9 %chunk_2.1 = (bf16[256,384]{1,0:T(8,128)(2,1)S(1)}, bf16[768,256]{1,0:T(8,128)(2,1)S(1)}) custom-call(f32[32,128]{1,0:T(8,128)S(1)} %add.24.after, s32[3,32]{1,0:T(4,128)S(1)} %bitcast.9, bf16[2048,64]{1,0:T(8,128)(2,1)S(1)} %get-tuple-element.49.refs_0_.first_rows, bf16[48,2048]{1,0:T(8,128)(2,1)S(1)} %get-tuple-element.50.refs_1_.second_cols, ...), custom_call_target="tpu_custom_call" | custom-call | flops 1000000000 | bytes 4000000 | tf_op jit(solution)/shard_map/chunk_2/pallas_call | solution.py:748
  21.0 1.0 %collective-permute-done.2 = f32[32,128]{1,0:T(8,128)S(1)} collective-permute-done((f32[32,128]{1,0:T(8,128)S(1)}, f32[32,128]{1,0:T(8,128)S(1)}, u32[]{:S(2)}, u32[]{:S(2)}) %collective-permute-start.2) | collective-permute-done | bytes 16416 | tf_op jit(solution)/shard_map/ppermute | solution.py:649
  22.0 0.1 collective-permute-start.3
  22.1 0.9 %chunk_3.1 = (bf16[256,384]{1,0:T(8,128)(2,1)S(1)}, bf16[768,256]{1,0:T(8,128)(2,1)S(1)}) custom-call(f32[64,128]{1,0:T(8,128)S(1)} %pad_maximum_fusion.after, s32[3,32]{1,0:T(4,128)S(1)} %bitcast.10, bf16[2048,64]{1,0:T(8,128)(2,1)S(1)} %get-tuple-element.49.refs_0_.first_rows, bf16[48,2048]{1,0:T(8,128)(2,1)S(1)} %get-tuple-element.50.refs_1_.second_cols, ...), custom_call_target="tpu_custom_call" | custom-call | flops 1000000000 | bytes 4000000 | tf_op jit(solution)/shard_map/chunk_3/pallas_call | solution.py:748
  23.0 3.0 %collective-permute-done.3 = f32[64,128]{1,0:T(8,128)S(1)} collective-permute-done((f32[64,128]{1,0:T(8,128)S(1)}, f32[64,128]{1,0:T(8,128)S(1)}, u32[]{:S(2)}, u32[]{:S(2)}) %collective-permute-start.3) | collective-permute-done | bytes 32800 | tf_op jit(solution)/shard_map/ppermute | solution.py:649
  26.0 0.0 copy-start.1
  26.0 0.0 copy-start.2
  26.0 0.0 copy-start.4
  26.0 0.1 collective-permute-start.4
  26.1 0.0 collective-permute-done.5.outer.refs_14_
  26.1 1.8 %edges.1 = (bf16[512,384]{1,0:T(8,128)(2,1)S(1)}, bf16[1024,128]{1,0:T(8,128)(2,1)S(1)}) custom-call(f32[64,128]{1,0:T(8,128)S(1)} %fusion.after, bf16[384,384]{1,0:T(8,128)(2,1)S(1)} %collective-permute-done.inner.refs_13_, bf16[352,384]{1,0:T(8,128)(2,1)S(1)} %collective-permute-done.5.outer.refs_14_, ...), custom_call_target="tpu_custom_call" | custom-call | flops 1000000000 | bytes 4000000 | tf_op jit(solution)/shard_map/edges/pallas_call | solution.py:768
  27.9 2.1 %collective-permute-done.4 = f32[64,128]{1,0:T(8,128)S(1)} collective-permute-done((f32[64,128]{1,0:T(8,128)S(1)}, f32[64,128]{1,0:T(8,128)S(1)}, u32[]{:S(2)}, u32[]{:S(2)}) %collective-permute-start.4) | collective-permute-done | bytes 32800 | tf_op jit(solution)/shard_map/ppermute | solution.py:649
  30.0 0.0 copy-done.1
  30.0 0.0 copy-done.2
  30.0 0.0 copy-done.4
  30.0 5.7 %leaves.1 = (bf16[2048,384]{1,0:T(8,128)(2,1)}, bf16[3072,128]{1,0:T(8,128)(2,1)S(1)}, bf16[3072,128]{1,0:T(8,128)(2,1)S(1)}, bf16[1536,256]{1,0:T(8,128)(2,1)S(...) custom-call(bf16[512,384]{1,0:T(8,128)(2,1)S(1)} %get-tuple-element.47.refs_0_, ...), custom_call_target="tpu_custom_call" | custom-call | tf_op jit(solution)/shard_map/leaves/pallas_call | solution.py:792
  35.7 3.2 %far.1 = bf16[64,6144]{1,0:T(8,128)(2,1)} custom-call(s32[3,32]{1,0:T(4,128)S(1)} %bitcast.12, bf16[3072,128]{1,0:T(8,128)(2,1)S(1)} %get-tuple-element.71.high, bf16[3072,128]{1,0:T(8,128)(2,1)S(1)} %get-tuple-element.72.low, bf16[768,256]{1,0:T(8,128)(2,1)S(1)} %get-tuple-element.73.refs_0_, bf16[768,256]{1,0:T(8,128)(2,1)S(1)} %get-tuple-element.74.refs_1_, ...), custom_call_target="tpu_custom_call" | custom-call | tf_op jit(solution)/shard_map/far/pallas_call | solution.py:831
  (6 shorter events, 0.0 us)
Async XLA Ops:
  0.6 6.4 %copy-start = (bf16[2048,384]{1,0:T(8,128)(2,1)S(1)}, bf16[2048,384]{1,0:T(8,128)(2,1)}, u32[]{:S(2)}) copy-start(bf16[2048,384]{1,0:T(8,128)(2,1)} %vectors.5) | copy-start | bytes 4718596
  0.6 6.4 %copy-start.3 = (f32[3,2048]{1,0:T(4,128)S(1)}, f32[3,2048]{1,0:T(4,128)}, u32[]{:S(2)}) copy-start(f32[3,2048]{1,0:T(4,128)} %points) | copy-start | bytes 73732
  0.7 6.4 %copy-start.7 = (s32[32]{0:T(128)S(1)}, s32[32]{0:T(128)}, u32[]{:S(2)}) copy-start(s32[32]{0:T(128)} %param.14) | copy-start | bytes 388
  0.7 6.4 %copy-start.6 = (s32[32,12]{0,1:T(8,128)S(1)}, s32[32,12]{0,1:T(8,128)}, u32[]{:S(2)}) copy-start(s32[32,12]{0,1:T(8,128)} %param.13) | copy-start | bytes 4612
  4.9 3.5 %collective-permute-start = (bf16[384,384]{1,0:T(8,128)(2,1)}, bf16[384,384]{1,0:T(8,128)(2,1)S(1)}, u32[]{:S(2)}, u32[]{:S(2)}) collective-permute-start(bf16[384,384]{1,0:T(8,128)(2,1)} %get-tuple-element.44), channel_id=1, source_target_pairs={{0,1},{1,0},{2,3},{3,2},{4,5},{5,4},{6,7},{7,6},{8,9},{9,8},{10,11... | collective-permute-start | bytes 884744 | tf_op jit(solution)/shard_map/ppermute | solution.py:638
  5.5 20.6 %collective-permute-start.5 = (bf16[352,384]{1,0:T(8,128)(2,1)}, bf16[352,384]{1,0:T(8,128)(2,1)S(1)}, u32[]{:S(2)}, u32[]{:S(2)}) collective-permute-start(bf16[352,384]{1,0:T(8,128)(2,1)} %get-tuple-element.64), channel_id=1, source_target_pairs={{0,0},{1,2},{2,1},{3,4},{4,3},{5,6},{6,5},{7,8},{8,7},{9,10},{10,9... | collective-permute-start | bytes 811016 | tf_op jit(solution)/shard_map/ppermute | solution.py:644
  7.1 1.3 %copy-start.8 = (f32[32,128]{1,0:T(8,128)S(1)}, f32[32,128]{1,0:T(8,128)}, u32[]{:S(2)}) copy-start(f32[32,128]{1,0:T(8,128)} %get-tuple-element.43) | copy-start | bytes 49156
  7.1 6.8 %copy-start.5 = (s32[32,3]{0,1:T(4,128)S(1)}, s32[32,3]{0,1:T(4,128)}, u32[]{:S(2)}) copy-start(s32[32,3]{0,1:T(4,128)} %param.15) | copy-start | bytes 1156
  8.4 8.9 %collective-permute-start.1 = (f32[32,128]{1,0:T(8,128)S(1)}, f32[32,128]{1,0:T(8,128)S(1)}, u32[]{:S(2)}, u32[]{:S(2)}) collective-permute-start(f32[32,128]{1,0:T(8,128)S(1)} %add_add_fusion.after), channel_id=1, source_target_pairs={{0,8},{1,9},{2,10},{3,11},{4,12},{5,13},{6,14},{7,15},{8,0},{9,1},... | collective-permute-start | bytes 49160 | tf_op jit(solution)/shard_map/ppermute | solution.py:649
  17.3 4.6 %collective-permute-start.2 = (f32[32,128]{1,0:T(8,128)S(1)}, f32[32,128]{1,0:T(8,128)S(1)}, u32[]{:S(2)}, u32[]{:S(2)}) collective-permute-start(f32[32,128]{1,0:T(8,128)S(1)} %add.24.after), channel_id=1, source_target_pairs={{0,16},{1,17},{2,18},{3,19},{4,20},{5,21},{6,22},{7,23},{8,24},{9,... | collective-permute-start | bytes 49160 | tf_op jit(solution)/shard_map/ppermute | solution.py:649
  22.0 4.0 %collective-permute-start.3 = (f32[64,128]{1,0:T(8,128)S(1)}, f32[64,128]{1,0:T(8,128)S(1)}, u32[]{:S(2)}, u32[]{:S(2)}) collective-permute-start(f32[64,128]{1,0:T(8,128)S(1)} %pad_maximum_fusion.after), channel_id=1, source_target_pairs={{0,2},{1,3},{2,0},{3,1},{4,6},{5,7},{6,4},{7,5},{8,10},{9,11},{10,... | collective-permute-start | bytes 98312 | tf_op jit(solution)/shard_map/ppermute | solution.py:649
  26.0 4.0 %copy-start.1 = (bf16[2048,64]{0,1:T(8,128)(2,1)S(1)}, bf16[2048,64]{0,1:T(8,128)(2,1)}, u32[]{:S(2)}) copy-start(bf16[2048,64]{0,1:T(8,128)(2,1)} %param.9) | copy-start | bytes 786436
  26.0 4.0 %copy-start.2 = (f32[64,64]{1,0:T(8,128)S(1)}, f32[64,64]{1,0:T(8,128)}, u32[]{:S(2)}) copy-start(f32[64,64]{1,0:T(8,128)} %refs_9_.1) | copy-start | bytes 49156
  26.0 4.0 %copy-start.4 = (f32[32,128]{1,0:T(8,128)S(1)}, f32[32,128]{1,0:T(8,128)}, u32[]{:S(2)}) copy-start(f32[32,128]{1,0:T(8,128)} %get-tuple-element.67.refs_7_) | copy-start | bytes 49156
  26.0 4.0 %collective-permute-start.4 = (f32[64,128]{1,0:T(8,128)S(1)}, f32[64,128]{1,0:T(8,128)S(1)}, u32[]{:S(2)}, u32[]{:S(2)}) collective-permute-start(f32[64,128]{1,0:T(8,128)S(1)} %fusion.after), channel_id=1, source_target_pairs={{0,4},{1,5},{2,6},{3,7},{4,0},{5,1},{6,2},{7,3},{8,12},{9,13},{10,... | collective-permute-start | bytes 98312 | tf_op jit(solution)/shard_map/ppermute | solution.py:649

commit v9 on v8

--- a/solution.py
+++ b/solution.py
@@ -55,7 +55,7 @@
 
 def tree_kernel(
     points_in, basis_in, below_in, transfer_in, vectors,
-    dense, top, outer, inner, points, basis, below, transfer, sems,
+    dense, top, outer, inner, points, basis, below, transfer, packed, staged, sems,
 ):
     width = basis.shape[0]
     count = basis.shape[1] // width
@@ -103,6 +103,30 @@
     same = iota((both, both), 0) // width == iota((both, both), 1) // width
     half_block = jnp.where(same, 0.5, 0.0).astype(F32)
     basis_copy.wait()
+    points_copy.wait()
+    for n, (target, last) in enumerate(sides):
+        bases = basis[:, count * width - span :], basis[:, 0:span]
+        last_three, first_three = (
+            jnp.concatenate(
+                [block[:, (at + skip) * width : (at + skip + 3) * width] for at in (0, LAYER)],
+                axis=1,
+            )
+            for skip, block in zip((1, 0), bases)
+        )
+        packed[n, 0:width, :] = jnp.where(last == 1, last_three, first_three)
+        coords = jnp.where(last == 1, points[:, count * width - span :], points[:, 0:span])
+        for m in range(2):
+            high, low = split2(coords[:, m * halo : (m + 1) * halo])
+            base = width + 16 * m
+            packed[n, base : base + 16, :] = jnp.zeros((16, target.shape[1]), BF16)
+            packed[n, base : base + 3, 0:halo] = high
+            packed[n, base + 8 : base + 11, 0:halo] = low
+        copies.append(
+            pltpu.make_async_copy(
+                packed.at[n], target.at[pl.ds(halo, width + 32), :], sems.at[6 + n]
+            )
+        )
+        copies[-1].start()
     blocks = []
     for n in range(count // 4):
         stacked = jnp.concatenate(
@@ -155,32 +179,18 @@
     top[...] = fold(total[:width, :width])
     halves = fold(total[width:, width:])
     dense[...] = halves
-    inner[halo + width + 32 :, :] = jnp.concatenate(split3(halves), axis=1)
-
-    points_copy.wait()
-
-    for target, last in sides:
-        bases = basis[:, count * width - span :], basis[:, 0:span]
-        last_three, first_three = (
-            jnp.concatenate(
-                [block[:, (at + skip) * width : (at + skip + 3) * width] for at in (0, LAYER)],
-                axis=1,
-            )
-            for skip, block in zip((1, 0), bases)
-        )
-        target[halo : halo + width, :] = jnp.where(last == 1, last_three, first_three)
-        coords = jnp.where(last == 1, points[:, count * width - span :], points[:, 0:span])
-        for m in range(2):
-            high, low = split2(coords[:, m * halo : (m + 1) * halo])
-            base = halo + width + 16 * m
-            target[base : base + 16, :] = jnp.zeros((16, target.shape[1]), BF16)
-            target[base : base + 3, 0:halo] = high
-            target[base + 8 : base + 11, 0:halo] = low
+    staged[...] = jnp.concatenate(split3(halves), axis=1)
+    copies.append(
+        pltpu.make_async_copy(
+            staged, inner.at[pl.ds(halo + width + 32, width // 2), :], sems.at[8]
+        )
+    )
+    copies[-1].start()
     for copy in copies:
         copy.wait()
 
 
-def factor_lanes(work, width, beside):
+def factor_lanes(work, width):
     panels = width // 8
     row = iota((8, 128), 0)
 
@@ -208,7 +218,6 @@
                 work[at + k, 8 * i : 8 * i + 8, :] = (
                     jnp.where(row >= k, tile[k], 0.0) if i == p else tile[k]
                 )
-        beside(p)
         for q in range(p + 1, panels):
             for start in range(q, panels, 2):
                 group = range(start, min(start + 2, panels))
@@ -233,13 +242,6 @@
 def unfold(matrix):
     half = matrix.shape[1] // 2
     return jnp.concatenate([matrix[:, :half], matrix[:, half:]], axis=0)
-
-
-def to_lanes(grams, work, width, many):
-    for i in range(width // 2):
-        both = grams[pl.ds(i, many, stride=STRIDE), :].T
-        work[i, :, 0:many] = both[0:width]
-        work[i + width // 2, :, 0:many] = both[width:]
 
 
 def from_lanes(work, factors, width, many):
@@ -447,116 +449,113 @@
     out[halo:, :] = value.astype(BF16)
 
 
-def leaves_kernel(chunks, edge_pairs, members, groups, *refs):
+def last_chunk_kernel(layers, pairs):
+    def body(
+        after, far_in, inner, outer, first_rows, second_cols, switches, vectors,
+        first_cols, own_rows, halo_rows, basis, top,
+        out, blocks, grams, far_list, sides, second_rows, sems,
+    ):
+        width = basis.shape[0]
+        own = basis.shape[1] // width
+        total = own + 2 * PAD
+        halo = LAYER * width
+        both = 2 * width
+        odd = lax.axis_index("sub") % 2
+        side_copies = [
+            pltpu.make_async_copy(block.at[pl.ds(halo, width), :], sides.at[side], sems.at[n])
+            for n, (block, side) in enumerate(((inner, 1 - odd), (outer, odd)))
+        ]
+        list_copy = pltpu.make_async_copy(far_in, far_list, sems.at[2])
+        for copy in side_copies + [list_copy]:
+            copy.start()
+        lanes = PAD * width
+        second_rows[0:lanes, :] = halo_rows[0:lanes, :]
+        second_rows[lanes : lanes + own * width, :] = own_rows[...]
+        second_rows[lanes + own * width :, :] = halo_rows[lanes:, :]
+        inner_layers(layers, vectors, first_rows, second_cols, switches, out, halo)
+
+        lane = iota((width, both), 1)
+        for n in range(own // 2):
+            pair = basis[:, n * both : (n + 1) * both]
+            zero = jnp.zeros_like(pair)
+            stacked = jnp.concatenate(
+                [jnp.where(lane < width, pair, zero), jnp.where(lane < width, zero, pair)], axis=0
+            )
+            value = mm_nt(stacked, pair)
+            for m in range(2):
+                at = (PAD + 2 * n + m) * STRIDE
+                grams[at : at + width // 2, :] = fold(value[m * width : (m + 1) * width])
+        for spot in (0, LAYER, total - LAYER - 1, total - 1):
+            grams[spot * STRIDE : spot * STRIDE + width // 2, :] = top[...]
+        for copy in side_copies + [list_copy]:
+            copy.wait()
+        for side, spots in enumerate(
+            ((1, 2, 3, 5, 6, 7), tuple(PAD + own + m for m in (0, 1, 2, 4, 5, 6)))
+        ):
+            for n, spot in enumerate(spots):
+                piece = sides[side, 0:width, n * width : (n + 1) * width]
+                at = spot * STRIDE
+                grams[at : at + width // 2, :] = fold(mm_nt(piece, piece))
+        far_blocks(
+            pairs, far_list, second_rows, first_cols, blocks, width, PAD, range(len(pairs))
+        )
+
+    return body
+
+
+def leaves_kernel(chunks, members, groups, *refs):
     outer_count = len(chunks) + 1
     near_parts = refs[:outer_count]
     (
-        far_in,
-        basis,
-        top,
+        grams,
         upper,
         transfer,
-        first_cols,
-        own_rows,
-        halo_rows,
-        inner,
-        outer,
         near,
         high,
         low,
-        edge_blocks,
         device_factor,
         group_factor,
         root_factor,
-        far_list,
-        sides,
-        second_rows,
-        grams,
         work,
         factors,
         sems,
     ) = refs[outer_count:]
-    width = basis.shape[0]
-    own = basis.shape[1] // width
-    total = own + 2 * PAD
+    width = transfer.shape[0]
+    total = high.shape[0] // width
+    own = total - 2 * PAD
     halo = LAYER * width
     layers = own // LAYER
     both = 2 * width
-    odd = lax.axis_index("sub") % 2
-    side_copies = [
-        pltpu.make_async_copy(block.at[pl.ds(halo, width), :], sides.at[side], sems.at[n])
-        for n, (block, side) in enumerate(((inner, 1 - odd), (outer, odd)))
-    ]
-    list_copy = pltpu.make_async_copy(far_in, far_list, sems.at[2])
     places = [(part, 0, chunk[0], len(chunk)) for part, chunk in zip(near_parts, chunks)]
     places += [(near_parts[-1], n, index, 1) for n, index in enumerate((0, layers - 1))]
     near_copies = [
         pltpu.make_async_copy(
             part.at[pl.ds(start * halo, many * halo), :],
             near.at[pl.ds(index * halo, many * halo), :],
-            sems.at[3 + n],
+            sems.at[n],
         )
         for n, (part, start, index, many) in enumerate(places)
     ]
-    for copy in side_copies + [list_copy] + near_copies:
+    for copy in near_copies:
         copy.start()
 
-    lane = iota((width, both), 1)
-    for n in range(own // 2):
-        pair = basis[:, n * both : (n + 1) * both]
-        zero = jnp.zeros_like(pair)
-        stacked = jnp.concatenate(
-            [jnp.where(lane < width, pair, zero), jnp.where(lane < width, zero, pair)], axis=0
-        )
-        value = mm_nt(stacked, pair)
-        for m in range(2):
-            at = (PAD + 2 * n + m) * STRIDE
-            grams[at : at + width // 2, :] = fold(value[m * width : (m + 1) * width])
-    spare = (0, LAYER, total - LAYER - 1, total - 1)
-    for spot, gram in zip(
-        spare,
-        (
-            top[...],
-            upper[0 : width // 2, :] * (1.0 / members),
-            upper[width // 2 :, :] * (1.0 / (members * groups)),
-            top[...],
-        ),
-    ):
-        grams[spot * STRIDE : spot * STRIDE + width // 2, :] = gram
-    for copy in side_copies:
-        copy.wait()
-    for side, spots in enumerate(
-        ((1, 2, 3, 5, 6, 7), tuple(PAD + own + m for m in (0, 1, 2, 4, 5, 6)))
-    ):
-        for n, spot in enumerate(spots):
-            piece = sides[side, 0:width, n * width : (n + 1) * width]
-            grams[spot * STRIDE : spot * STRIDE + width // 2, :] = fold(mm_nt(piece, piece))
-
-    lanes = PAD * width
-    second_rows[0:lanes, :] = halo_rows[0:lanes, :]
-    second_rows[lanes : lanes + own * width, :] = own_rows[...]
-    second_rows[lanes + own * width :, :] = halo_rows[lanes:, :]
-    panels = width // 8
-
-    def beside(p):
-        places = range(p * len(edge_pairs) // panels, (p + 1) * len(edge_pairs) // panels)
-        far_blocks(
-            [edge_pairs[n] for n in places],
-            far_list,
-            second_rows,
-            first_cols,
-            edge_blocks,
-            width,
-            PAD,
-            places,
-        )
-
-    to_lanes(grams, work, width, total)
-    list_copy.wait()
-    factor_lanes(work, width, beside)
+    spare = (LAYER, total - LAYER - 1)
+    means = (
+        upper[0 : width // 2, :] * (1.0 / members),
+        upper[width // 2 :, :] * (1.0 / (members * groups)),
+    )
+    spot_row = iota((total, both), 0)
+    for i in range(width // 2):
+        rows = grams[pl.ds(i, total, stride=STRIDE), :]
+        for spot, mean in zip(spare, means):
+            rows = jnp.where(spot_row == spot, mean[i : i + 1, :], rows)
+        turned = rows.T
+        work[i, :, 0:total] = turned[0:width]
+        work[i + width // 2, :, 0:total] = turned[width:]
+    factor_lanes(work, width)
     from_lanes(work, factors, width, total)
     device_factor[...] = exact(unfold(factors[0 : width // 2, :]), transfer[...])
-    for target, spot in ((group_factor, spare[1]), (root_factor, spare[2])):
+    for target, spot in zip((group_factor, root_factor), spare):
         target[...] = unfold(factors[spot * STRIDE : spot * STRIDE + width // 2, :])
     left_lanes = iota((width // 2, both), 1) < width
     for spot in range(total):
@@ -645,7 +644,7 @@
 
 
 def exchange(value, distance):
-    pairs = [(i, i ^ distance) for i in range(lax.axis_size(AXES))]
+    pairs = [(i, i ^ distance ^ 1) for i in range(lax.axis_size(AXES))]
     return value + lax.ppermute(value, AXES, pairs)
 
 
@@ -681,13 +680,15 @@
             block_of(extra + half),
         ),
         in_specs=[hbm] * 5,
-        out_specs=(vmem,) * 4,
+        out_specs=(vmem, vmem, hbm, hbm),
         scratch_shapes=[
             pltpu.VMEM((3, own * width), F32),
             pltpu.VMEM((width, own * width), BF16),
             pltpu.VMEM((width, (own - 2) * width), BF16),
             pltpu.VMEM((width, width), F32),
-            pltpu.SemaphoreType.DMA((6,)),
+            pltpu.VMEM((2, width + 32, columns), BF16),
+            pltpu.VMEM((half, columns), BF16),
+            pltpu.SemaphoreType.DMA((9,)),
         ],
         compiler_params=room(60),
         name="tree",
@@ -700,8 +701,9 @@
     steps += [1 << bit for bit in range(1, sub_bits)]
     inner_pairs = list(range(PAD // 2, (own - PAD) // 2))
     few = len(inner_pairs) // 2
+    edge_pairs = [index for index in range(own // 2) if index not in inner_pairs]
     chunks = [[1, 2], [3, 4], [5], [6]]
-    pair_chunks = [[], [], inner_pairs[:few], inner_pairs[few:]]
+    pair_chunks = [[], inner_pairs[:few], inner_pairs[few:], edge_pairs]
     blocks, plan, parts = [], {}, []
 
     def part_shape(count):
@@ -735,14 +737,16 @@
     pair_gram = gram = dense + (summands[0] + (summands[1] + summands[2]))
     gram, parts[0] = lax.optimization_barrier((gram, parts[0]))
     first_rows, first_cols, second_cols, second_rows, switches = shared
-    for n in range(max(len(steps), len(chunks))):
+    jobs = [1, 2, "edges", 3]
+    for n in range(max(len(steps), len(jobs))):
         before = gram
         if n < len(steps):
             if n == len(steps) - sub_bits + 1:
                 gram = before = jnp.concatenate([pair_gram, gram], axis=0)
             gram = exchange(gram, steps[n])
-        if n + 1 < len(chunks):
-            layer_chunk, pair_chunk = chunks[n + 1], pair_chunks[n + 1]
+        job = jobs[n] if n < len(jobs) else None
+        if job in (1, 2):
+            layer_chunk, pair_chunk = chunks[job], pair_chunks[job]
             shapes = [part_shape(len(layer_chunk))] * bool(layer_chunk)
             shapes += [block_shape(len(pair_chunk))] * bool(pair_chunk)
             outs = pl.pallas_call(
@@ -756,7 +760,7 @@
                 ],
                 compiler_params=room(10),
                 cost_estimate=cost,
-                name=f"chunk_{n + 1}",
+                name=f"chunk_{job}",
             )(before, far_list, first_rows, second_cols, switches, vectors, first_cols, second_rows)
             gram, outs = lax.optimization_barrier((gram, outs))
             if layer_chunk:
@@ -764,7 +768,7 @@
             if pair_chunk:
                 plan.update((index, (len(blocks), m)) for m, index in enumerate(pair_chunk))
                 blocks.append(outs[-1])
-        elif n + 1 == len(chunks):
+        elif job == "edges":
             edge_part, halo_rows = pl.pallas_call(
                 edges_kernel,
                 out_shape=(
@@ -785,53 +789,71 @@
                 name="edges",
             )(before, from_inner, from_outer, first_rows, second_cols, switches, vectors)
             gram, edge_part = lax.optimization_barrier((gram, edge_part))
-
-    edge_pairs = [index for index in range(own // 2) if index not in plan]
-    plan.update((index, (len(blocks), m)) for m, index in enumerate(edge_pairs))
+        elif job == 3:
+            part, edge_blocks, grams = pl.pallas_call(
+                last_chunk_kernel(chunks[3], edge_pairs),
+                out_shape=(
+                    part_shape(len(chunks[3])),
+                    block_shape(len(edge_pairs)),
+                    jax.ShapeDtypeStruct((total * STRIDE, 2 * width), F32),
+                ),
+                in_specs=[hbm] * 4 + [vmem] * 9,
+                out_specs=(vmem,) * 3,
+                scratch_shapes=[
+                    pltpu.SMEM(far_list.shape, jnp.int32),
+                    pltpu.VMEM((2, width, columns), BF16),
+                    pltpu.VMEM((total * width, 2 * width), BF16),
+                    pltpu.SemaphoreType.DMA((3,)),
+                ],
+                compiler_params=room(14),
+                cost_estimate=cost,
+                name="chunk_3",
+            )(
+                before,
+                far_list,
+                from_inner,
+                from_outer,
+                first_rows,
+                second_cols,
+                switches,
+                vectors,
+                first_cols,
+                second_rows,
+                halo_rows,
+                basis,
+                top,
+            )
+            gram, part = lax.optimization_barrier((gram, part))
+            parts.append(part)
+            plan.update((index, (len(blocks), m)) for m, index in enumerate(edge_pairs))
+            blocks.append(edge_blocks)
+
     split_factors = jax.ShapeDtypeStruct((total * width, 2 * width), BF16)
-    near, high, low, edge_blocks, device_factor, group_factor, root_factor = pl.pallas_call(
-        functools.partial(leaves_kernel, chunks, edge_pairs, members, groups),
+    near, high, low, device_factor, group_factor, root_factor = pl.pallas_call(
+        functools.partial(leaves_kernel, chunks, members, groups),
         out_shape=(
             jax.ShapeDtypeStruct(vectors.shape, BF16),
             split_factors,
             split_factors,
-            block_shape(len(edge_pairs)),
             square,
             square,
             square,
         ),
-        in_specs=[hbm] * (len(parts) + 2) + [vmem] * 7 + [hbm] * 2,
-        out_specs=(hbm,) + (vmem,) * 6,
+        in_specs=[hbm] * (len(parts) + 1) + [vmem] * 3,
+        out_specs=(hbm,) + (vmem,) * 5,
         scratch_shapes=[
-            pltpu.SMEM(far_list.shape, jnp.int32),
-            pltpu.VMEM((2, width, columns), BF16),
-            pltpu.VMEM((total * width, 2 * width), BF16),
-            pltpu.VMEM((total * STRIDE, 2 * width), F32),
             pltpu.VMEM((width, width, 128), F32),
             pltpu.VMEM((total * STRIDE, 2 * width), F32),
-            pltpu.SemaphoreType.DMA((5 + len(parts),)),
+            pltpu.SemaphoreType.DMA((2 + len(parts),)),
         ],
-        compiler_params=room(24),
+        compiler_params=room(20),
         name="leaves",
-    )(
-        *parts,
-        edge_part,
-        far_list,
-        basis,
-        top,
-        gram,
-        device_transfer,
-        first_cols,
-        second_rows,
-        halo_rows,
-        from_inner,
-        from_outer,
-    )
+    )(*parts, edge_part, grams, gram, device_transfer)
 
     coupling = pl.pallas_call(
         functools.partial(far_kernel, plan),
         out_shape=jax.ShapeDtypeStruct((width, own * far_index.shape[1] * width), BF16),
-        in_specs=[hbm] + [vmem] * (3 + len(blocks)),
+        in_specs=[hbm] + [vmem] * (2 + len(blocks)),
         out_specs=vmem,
         scratch_shapes=[
             pltpu.SMEM(far_list.shape, jnp.int32),
@@ -839,7 +861,7 @@
         ],
         compiler_params=room(16),
         name="far",
-    )(far_list, high, low, *blocks, edge_blocks)
+    )(far_list, high, low, *blocks)
     return near, coupling.T, device_factor, group_factor, root_factor
 
 

time: 39.1 us -> 45.6 us (1.17)
  Pallas kernels: 19 us -> 28.9 us
  waiting for transfers between devices: 8.54 us -> 3.9 us
  starting transfers between devices: 10.4 us -> 11.7 us
    pallas_call x1, Pallas kernels: 4.25 us -> 13.7 us  [per_device(): pl.pallas_call(tree_kernel, out_shape=(jax.ShapeDtypeStruct((half, 2 * wi...]
    ppermute x4, waiting for transfers between devices: 8.54 us -> 3.9 us  [exchange(): return value + lax.ppermute(value, AXES, pairs)]
    ppermute x4, starting transfers between devices: 8.32 us -> 9.6 us  [exchange(): return value + lax.ppermute(value, AXES, pairs)]
    pallas_call x1 -> x2, Pallas kernels: 5.69 us -> 6.63 us  [the longest x1 5.05 us: per_device(): pl.pallas_call(functools.partial(leaves_kernel, chunks, members, groups),...]
    pallas_call x3 -> x2, Pallas kernels: 2.78 us -> 2.27 us  [per_device(): pl.pallas_call(chunk_kernel(layer_chunk, pair_chunk, halo, width), out_sh...]
where the time goes in v9:
time: 45.6 us; the launch traced here: 45.4 us
  Pallas kernels  28.9 us (63%)
  starting transfers between devices  11.7 us (26%)
  waiting for transfers between devices  3.9 us (9%)
  between operations  0.84 us (2%)
    pallas_call x1, Pallas kernels, per_device(): pl.pallas_call(tree_kernel, out_shape=(jax.ShapeDtypeStruct((half, 2 * wi...  13.7 us
    ppermute x4, starting transfers between devices, exchange(): return value + lax.ppermute(value, AXES, pairs)  9.6 us
    pallas_call x1, Pallas kernels, per_device(): pl.pallas_call(functools.partial(leaves_kernel, chunks, members, groups),...  5.05 us
    ppermute x4, waiting for transfers between devices, exchange(): return value + lax.ppermute(value, AXES, pairs)  3.9 us
    pallas_call x1, Pallas kernels, per_device(): pl.pallas_call(functools.partial(far_kernel, plan), out_shape=jax.ShapeDt...  3.17 us
    pallas_call x2, Pallas kernels, per_device(): pl.pallas_call(chunk_kernel(layer_chunk, pair_chunk, halo, width), out_sh...  2.27 us
    pallas_call x1, Pallas kernels, per_device(): pl.pallas_call(edges_kernel, out_shape=(part_shape(2), jax.ShapeDtypeStru...  1.81 us
    ppermute x1, starting transfers between devices, swap_outer(): return lax.ppermute(block, AXES, route)  1.6 us
  transfers between devices with their start and end apart: 6, of which 4 were waited for; matrix products, arithmetic and copies ran while one was open for 0% of the time, Pallas kernels for 15%

profile of v9, /device:TPU:0, one launch (start us, length us, event | category | flops | bytes accessed | tf_op | source)
XLA Modules:
  0.0 45.4 jit_solution(12513280130374792498)
XLA Ops:
  0.6 0.0 copy-start
  0.6 0.0 copy-start.3
  0.7 0.0 copy-start.7
  0.7 0.0 copy-start.6
  0.7 13.7 %tree.1 = (f32[32,128]{1,0:T(8,128)}, f32[32,128]{1,0:T(8,128)}, bf16[352,384]{1,0:T(8,128)(2,1)}, bf16[384,384]{1,0:T(8,128)(2,1)}) custom-call(f32[3,2048]{1,0:T(4,128)} %points, bf16[64,2048]{1,0:T(8,128)(2,1)} %bitcast.6, bf16[64,1920]{1,0:T(8,128)(2,1)} %bitcast.15, f32[64,64]{1,0:T(8,128)} %refs_7_.1, bf16[2048,384]{1,0:T(8,128)(2,1)} %vectors.7), custom_call_target="tpu_custom_call" | custom-call | tf_op jit(solution)/shard_map/tree/pallas_call | solution.py:674
  14.4 0.5 %collective-permute-start = (bf16[384,384]{1,0:T(8,128)(2,1)}, bf16[384,384]{1,0:T(8,128)(2,1)S(1)}, u32[]{:S(2)}, u32[]{:S(2)}) collective-permute-start(bf16[384,384]{1,0:T(8,128)(2,1)} %get-tuple-element.46), channel_id=1, source_target_pairs={{0,1},{1,0},{2,3},{3,2},{4,5},{5,4},{6,7},{7,6},{8,9},{9,8},{10,11... | collective-permute-start | bytes 884744 | tf_op jit(solution)/shard_map/ppermute | solution.py:637
  14.9 1.6 %collective-permute-start.4 = (bf16[352,384]{1,0:T(8,128)(2,1)}, bf16[352,384]{1,0:T(8,128)(2,1)S(1)}, u32[]{:S(2)}, u32[]{:S(2)}) collective-permute-start(bf16[352,384]{1,0:T(8,128)(2,1)} %get-tuple-element.64), channel_id=1, source_target_pairs={{0,0},{1,2},{2,1},{3,4},{4,3},{5,6},{6,5},{7,8},{8,7},{9,10},{10,9... | collective-permute-start | bytes 811016 | tf_op jit(solution)/shard_map/ppermute | solution.py:643
  16.5 0.0 copy-done
  16.5 0.0 copy-done.3
  16.5 0.0 copy-done.7
  16.5 0.0 copy-done.6
  16.5 0.0 copy-start.8
  16.6 0.0 copy-start.5
  16.6 1.3 %chunk_0.1 = (bf16[512,384]{1,0:T(8,128)(2,1)S(1)}, bf16[2048,64]{1,0:T(8,128)(2,1)S(1)}, bf16[64,2048]{1,0:T(8,128)(2,1)S(1)}, bf16[48,2048]{1,0:T(8,128)(2,1)S...) custom-call(f32[3,2048]{1,0:T(4,128)S(1)} %copy-done.3, s32[12,32]{1,0:T(8,128)S(1)} %bitcast.12, ...), custom_call_target="tpu_custom_call" | custom-call | flops 1000000000 | bytes 4000000 | tf_op jit(solution)/shard_map/chunk_0/pallas_call | solution.py:716
  17.9 0.0 collective-permute-done.inner
  17.9 0.0 copy-done.8
  17.9 4.2 %collective-permute-start.1 = (f32[32,128]{1,0:T(8,128)S(1)}, f32[32,128]{1,0:T(8,128)S(1)}, u32[]{:S(2)}, u32[]{:S(2)}) collective-permute-start(f32[32,128]{1,0:T(8,128)S(1)} %add_add_fusion.after), channel_id=1, source_target_pairs={{0,9},{1,8},{2,11},{3,10},{4,13},{5,12},{6,15},{7,14},{8,1},{9,0},... | collective-permute-start | bytes 49160 | tf_op jit(solution)/shard_map/ppermute | solution.py:648
  22.1 0.0 copy-done.5
  22.1 1.4 %chunk_1.1 = (bf16[512,384]{1,0:T(8,128)(2,1)S(1)}, bf16[768,256]{1,0:T(8,128)(2,1)S(1)}) custom-call(f32[32,128]{1,0:T(8,128)S(1)} %add_add_fusion.after, s32[3,32]{1,0:T(4,128)S(1)} %bitcast.8, bf16[2048,64]{1,0:T(8,128)(2,1)S(1)} %get-tuple-element.51.refs_0_.first_rows, bf16[48,2048]{1,0:T(8,128)(2,1)S(1)} %get-tuple-element.52.refs_1_.second_cols, ...), custom_call_target="tpu_custom_call" | custom-call | flops 1000000000 | bytes 4000000 | tf_op jit(solution)/shard_map/chunk_1/pallas_call | solution.py:752
  23.5 0.1 collective-permute-done.1
  23.6 5.3 %collective-permute-start.2 = (f32[32,128]{1,0:T(8,128)S(1)}, f32[32,128]{1,0:T(8,128)S(1)}, u32[]{:S(2)}, u32[]{:S(2)}) collective-permute-start(f32[32,128]{1,0:T(8,128)S(1)} %add.24.after), channel_id=1, source_target_pairs={{0,17},{1,16},{2,19},{3,18},{4,21},{5,20},{6,23},{7,22},{8,25},{9,... | collective-permute-start | bytes 49160 | tf_op jit(solution)/shard_map/ppermute | solution.py:648
  28.9 0.9 %chunk_2.1 = (bf16[256,384]{1,0:T(8,128)(2,1)S(1)}, bf16[768,256]{1,0:T(8,128)(2,1)S(1)}) custom-call(f32[32,128]{1,0:T(8,128)S(1)} %add.24.after, s32[3,32]{1,0:T(4,128)S(1)} %bitcast.9, bf16[2048,64]{1,0:T(8,128)(2,1)S(1)} %get-tuple-element.51.refs_0_.first_rows, bf16[48,2048]{1,0:T(8,128)(2,1)S(1)} %get-tuple-element.52.refs_1_.second_cols, ...), custom_call_target="tpu_custom_call" | custom-call | flops 1000000000 | bytes 4000000 | tf_op jit(solution)/shard_map/chunk_2/pallas_call | solution.py:752
  29.8 0.6 %collective-permute-done.2 = f32[32,128]{1,0:T(8,128)S(1)} collective-permute-done((f32[32,128]{1,0:T(8,128)S(1)}, f32[32,128]{1,0:T(8,128)S(1)}, u32[]{:S(2)}, u32[]{:S(2)}) %collective-permute-start.2) | collective-permute-done | bytes 16416 | tf_op jit(solution)/shard_map/ppermute | solution.py:648
  30.4 0.0 copy-start.1
  30.4 0.0 copy-start.4
  30.4 0.1 collective-permute-start.3
  30.5 0.0 collective-permute-done.4.outer
  30.5 1.8 %edges.1 = (bf16[512,384]{1,0:T(8,128)(2,1)S(1)}, bf16[1024,128]{1,0:T(8,128)(2,1)S(1)}) custom-call(f32[64,128]{1,0:T(8,128)S(1)} %pad_maximum_fusion.after, bf16[384,384]{1,0:T(8,128)(2,1)S(1)} %collective-permute-done.inner, bf16[352,384]{1,0:T(8,128)(2,1)S(1)} %collective-permute-done.4.outer, bf16[2048,64]{1,0:T(8,128)(2,1)S(1)} %get-tuple-element.51.refs_0_.first_rows, ...), custom_call_target="tpu_custom_call" | custom-call | flops 1000000000 | bytes 4000000 | tf_op jit(solution)/shard_map/edges/pallas_call | solution.py:772
  32.4 1.5 %collective-permute-done.3 = f32[64,128]{1,0:T(8,128)S(1)} collective-permute-done((f32[64,128]{1,0:T(8,128)S(1)}, f32[64,128]{1,0:T(8,128)S(1)}, u32[]{:S(2)}, u32[]{:S(2)}) %collective-permute-start.3) | collective-permute-done | bytes 32800 | tf_op jit(solution)/shard_map/ppermute | solution.py:648
  33.9 0.0 collective-permute-start.5
  33.9 0.0 copy-done.1
  33.9 0.0 copy-done.4
  33.9 0.0 copy-start.2
  33.9 1.6 %chunk_3.1 = (bf16[256,384]{1,0:T(8,128)(2,1)S(1)}, bf16[1536,256]{1,0:T(8,128)(2,1)S(1)}, f32[1920,128]{1,0:T(8,128)S(1)}) custom-call(f32[64,128]{1,0:T(8,128)S(1)} %fusion.after, s32[3,32]{1,0:T(4,128)S(1)} %bitcast.10, bf16[384,384]{1,0:T(8,128)(2,1)S(1)} %collective-permute-done.inner, bf16[352,384]{1,0:T(8,128)(2,1)S(1)} %collective-permute-done.4.outer, ...), custom_call_target="tpu_custom_call" | custom-call | flops 1000000000 | bytes 4000000 | tf_op jit(solution)/shard_map/chunk_3/pallas_call | solution.py:793
  35.5 1.7 %collective-permute-done.5 = f32[64,128]{1,0:T(8,128)S(1)} collective-permute-done((f32[64,128]{1,0:T(8,128)S(1)}, f32[64,128]{1,0:T(8,128)S(1)}, u32[]{:S(2)}, u32[]{:S(2)}) %collective-permute-start.5) | collective-permute-done | bytes 32800 | tf_op jit(solution)/shard_map/ppermute | solution.py:648
  37.2 0.0 copy-done.2
  37.2 5.0 %leaves.1 = (bf16[2048,384]{1,0:T(8,128)(2,1)}, bf16[3072,128]{1,0:T(8,128)(2,1)S(1)}, bf16[3072,128]{1,0:T(8,128)(2,1)S(1)}, f32[64,64]{1,0:T(8,128)}, f32[64,64]{1,0:T(8,128)}, /*index=5*/f32[64,64]{1,0:T(8,128)}) custom-call(bf16[512,384]{1,0:T(8,128)(2,1)S(1)} %get-tuple-element.49.refs_0_, bf16[512,384]{1,0:T(8,128)(2,1)S(1)} %get-tuple-element.58.refs_1_, ...), custom_call_target="tpu_custom_call" | custom-call | tf_op jit(solution)/shard_map/leaves/pallas_call | solution.py:832
  42.3 3.2 %far.1 = bf16[64,6144]{1,0:T(8,128)(2,1)} custom-call(s32[3,32]{1,0:T(4,128)S(1)} %bitcast.11, bf16[3072,128]{1,0:T(8,128)(2,1)S(1)} %get-tuple-element.75.high, bf16[3072,128]{1,0:T(8,128)(2,1)S(1)} %get-tuple-element.76.low, bf16[768,256]{1,0:T(8,128)(2,1)S(1)} %get-tuple-element.77.refs_0_, bf16[768,256]{1,0:T(8,128)(2,1)S(1)} %get-tuple-element.78.refs_1_, ...), custom_call_target="tpu_custom_call" | custom-call | tf_op jit(solution)/shard_map/far/pallas_call | solution.py:853
  (6 shorter events, 0.0 us)
Async XLA Ops:
  0.6 15.9 %copy-start = (bf16[2048,384]{1,0:T(8,128)(2,1)S(1)}, bf16[2048,384]{1,0:T(8,128)(2,1)}, u32[]{:S(2)}) copy-start(bf16[2048,384]{1,0:T(8,128)(2,1)} %vectors.7) | copy-start | bytes 4718596
  0.6 15.9 %copy-start.3 = (f32[3,2048]{1,0:T(4,128)S(1)}, f32[3,2048]{1,0:T(4,128)}, u32[]{:S(2)}) copy-start(f32[3,2048]{1,0:T(4,128)} %points) | copy-start | bytes 73732
  0.7 15.9 %copy-start.7 = (s32[32]{0:T(128)S(1)}, s32[32]{0:T(128)}, u32[]{:S(2)}) copy-start(s32[32]{0:T(128)} %param.14) | copy-start | bytes 388
  0.7 15.9 %copy-start.6 = (s32[32,12]{0,1:T(8,128)S(1)}, s32[32,12]{0,1:T(8,128)}, u32[]{:S(2)}) copy-start(s32[32,12]{0,1:T(8,128)} %param.13) | copy-start | bytes 4612
  14.4 3.5 %collective-permute-start = (bf16[384,384]{1,0:T(8,128)(2,1)}, bf16[384,384]{1,0:T(8,128)(2,1)S(1)}, u32[]{:S(2)}, u32[]{:S(2)}) collective-permute-start(bf16[384,384]{1,0:T(8,128)(2,1)} %get-tuple-element.46), channel_id=1, source_target_pairs={{0,1},{1,0},{2,3},{3,2},{4,5},{5,4},{6,7},{7,6},{8,9},{9,8},{10,11... | collective-permute-start | bytes 884744 | tf_op jit(solution)/shard_map/ppermute | solution.py:637
  14.9 15.6 %collective-permute-start.4 = (bf16[352,384]{1,0:T(8,128)(2,1)}, bf16[352,384]{1,0:T(8,128)(2,1)S(1)}, u32[]{:S(2)}, u32[]{:S(2)}) collective-permute-start(bf16[352,384]{1,0:T(8,128)(2,1)} %get-tuple-element.64), channel_id=1, source_target_pairs={{0,0},{1,2},{2,1},{3,4},{4,3},{5,6},{6,5},{7,8},{8,7},{9,10},{10,9... | collective-permute-start | bytes 811016 | tf_op jit(solution)/shard_map/ppermute | solution.py:643
  16.5 1.3 %copy-start.8 = (f32[32,128]{1,0:T(8,128)S(1)}, f32[32,128]{1,0:T(8,128)}, u32[]{:S(2)}) copy-start(f32[32,128]{1,0:T(8,128)} %get-tuple-element.45) | copy-start | bytes 49156
  16.6 5.6 %copy-start.5 = (s32[32,3]{0,1:T(4,128)S(1)}, s32[32,3]{0,1:T(4,128)}, u32[]{:S(2)}) copy-start(s32[32,3]{0,1:T(4,128)} %param.15) | copy-start | bytes 1156
  17.9 5.6 %collective-permute-start.1 = (f32[32,128]{1,0:T(8,128)S(1)}, f32[32,128]{1,0:T(8,128)S(1)}, u32[]{:S(2)}, u32[]{:S(2)}) collective-permute-start(f32[32,128]{1,0:T(8,128)S(1)} %add_add_fusion.after), channel_id=1, source_target_pairs={{0,9},{1,8},{2,11},{3,10},{4,13},{5,12},{6,15},{7,14},{8,1},{9,0},... | collective-permute-start | bytes 49160 | tf_op jit(solution)/shard_map/ppermute | solution.py:648
  23.6 6.9 %collective-permute-start.2 = (f32[32,128]{1,0:T(8,128)S(1)}, f32[32,128]{1,0:T(8,128)S(1)}, u32[]{:S(2)}, u32[]{:S(2)}) collective-permute-start(f32[32,128]{1,0:T(8,128)S(1)} %add.24.after), channel_id=1, source_target_pairs={{0,17},{1,16},{2,19},{3,18},{4,21},{5,20},{6,23},{7,22},{8,25},{9,... | collective-permute-start | bytes 49160 | tf_op jit(solution)/shard_map/ppermute | solution.py:648
  30.4 3.4 %copy-start.1 = (bf16[2048,64]{0,1:T(8,128)(2,1)S(1)}, bf16[2048,64]{0,1:T(8,128)(2,1)}, u32[]{:S(2)}) copy-start(bf16[2048,64]{0,1:T(8,128)(2,1)} %param.9) | copy-start | bytes 786436
  30.4 3.4 %copy-start.4 = (f32[32,128]{1,0:T(8,128)S(1)}, f32[32,128]{1,0:T(8,128)}, u32[]{:S(2)}) copy-start(f32[32,128]{1,0:T(8,128)} %get-tuple-element.68.top) | copy-start | bytes 49156
  30.4 3.4 %collective-permute-start.3 = (f32[64,128]{1,0:T(8,128)S(1)}, f32[64,128]{1,0:T(8,128)S(1)}, u32[]{:S(2)}, u32[]{:S(2)}) collective-permute-start(f32[64,128]{1,0:T(8,128)S(1)} %pad_maximum_fusion.after), channel_id=1, source_target_pairs={{0,3},{1,2},{2,1},{3,0},{4,7},{5,6},{6,5},{7,4},{8,11},{9,10},{10,... | collective-permute-start | bytes 98312 | tf_op jit(solution)/shard_map/ppermute | solution.py:648
  33.9 3.3 %collective-permute-start.5 = (f32[64,128]{1,0:T(8,128)S(1)}, f32[64,128]{1,0:T(8,128)S(1)}, u32[]{:S(2)}, u32[]{:S(2)}) collective-permute-start(f32[64,128]{1,0:T(8,128)S(1)} %fusion.after), channel_id=1, source_target_pairs={{0,5},{1,4},{2,7},{3,6},{4,1},{5,0},{6,3},{7,2},{8,13},{9,12},{10,... | collective-permute-start | bytes 98312 | tf_op jit(solution)/shard_map/ppermute | solution.py:648
  33.9 3.3 %copy-start.2 = (f32[64,64]{1,0:T(8,128)S(1)}, f32[64,64]{1,0:T(8,128)}, u32[]{:S(2)}) copy-start(f32[64,64]{1,0:T(8,128)} %refs_7_.1) | copy-start | bytes 49156

commit v10 on v9

--- a/solution.py
+++ b/solution.py
@@ -55,7 +55,7 @@
 
 def tree_kernel(
     points_in, basis_in, below_in, transfer_in, vectors,
-    dense, top, outer, inner, points, basis, below, transfer, packed, staged, sems,
+    dense, top, outer, inner, points, basis, below, transfer, passing, packed, staged, sems,
 ):
     width = basis.shape[0]
     count = basis.shape[1] // width
@@ -75,16 +75,21 @@
             )
         )
     ]
-    copies = [
+    vector_loads = [
         pltpu.make_async_copy(
             vectors.at[pl.ds(pl.multiple_of(last * (rows - halo), 16), halo), :],
-            target.at[pl.ds(0, halo), :],
+            passing.at[n],
             sems.at[4 + n],
         )
-        for n, (target, last) in enumerate(sides)
+        for n, (_, last) in enumerate(sides)
     ]
-    for copy in loads + copies:
+    copies = [
+        pltpu.make_async_copy(passing.at[n], target.at[pl.ds(0, halo), :], sems.at[9 + n])
+        for n, (target, _) in enumerate(sides)
+    ]
+    for copy in loads + vector_loads:
         copy.start()
+
     both = 2 * width
     lane = iota((width, 2 * both), 1)
 
@@ -134,6 +139,9 @@
         )
         blocks.append(mm_nt(stacked, stacked) * half_block)
     below_copy.wait()
+    for load, copy in zip(vector_loads, copies[:2]):
+        load.wait()
+        copy.start()
     halves = []
     for n, block in enumerate(blocks):
         t = below[:, n * both : (n + 1) * both]
@@ -571,7 +579,7 @@
 
 
 def far_kernel(plan, far_in, high, low, *refs):
-    blocks, (coupling, far_list, sem) = refs[:-3], refs[-3:]
+    blocks, (coupling, far_list, lines, sem, sems) = refs[:-5], refs[-5:]
     copy = pltpu.make_async_copy(far_in, far_list, sem)
     copy.start()
     width = coupling.shape[0]
@@ -585,6 +593,7 @@
     def diagonal(value):
         return jnp.where(square, value, zero)
 
+    copies = []
     for start in range(0, own // 2, 4):
         indices = range(start, start + 4)
         halves = []
@@ -630,7 +639,14 @@
                 [out[:, 0:width] for out in three] + [out[:, width:both] for out in three], axis=1
             )
             at = index * 2 * far * width
-            coupling[:, at : at + 2 * far * width] = line.astype(BF16)
+            lines[:, at : at + 2 * far * width] = line.astype(BF16)
+        group = pl.ds(start * 2 * far * width, 8 * far * width)
+        copies.append(
+            pltpu.make_async_copy(lines.at[:, group], coupling.at[:, group], sems.at[start // 4])
+        )
+        copies[-1].start()
+    for copy in copies:
+        copy.wait()
 
 
 def swap_inner(block):
@@ -638,9 +654,8 @@
 
 
 def swap_outer(block):
-    last = lax.axis_size(AXES) - 1
-    route = [(i, min(max(i + 1 if i % 2 else i - 1, 0), last)) for i in range(last + 1)]
-    return lax.ppermute(block, AXES, route)
+    many = lax.axis_size(AXES)
+    return lax.ppermute(block, AXES, [(i, (i + 1 if i % 2 else i - 1) % many) for i in range(many)])
 
 
 def exchange(value, distance):
@@ -686,9 +701,10 @@
             pltpu.VMEM((width, own * width), BF16),
             pltpu.VMEM((width, (own - 2) * width), BF16),
             pltpu.VMEM((width, width), F32),
+            pltpu.VMEM((2, halo, columns), BF16),
             pltpu.VMEM((2, width + 32, columns), BF16),
             pltpu.VMEM((half, columns), BF16),
-            pltpu.SemaphoreType.DMA((9,)),
+            pltpu.SemaphoreType.DMA((11,)),
         ],
         compiler_params=room(60),
         name="tree",
@@ -854,10 +870,12 @@
         functools.partial(far_kernel, plan),
         out_shape=jax.ShapeDtypeStruct((width, own * far_index.shape[1] * width), BF16),
         in_specs=[hbm] + [vmem] * (2 + len(blocks)),
-        out_specs=vmem,
+        out_specs=hbm,
         scratch_shapes=[
             pltpu.SMEM(far_list.shape, jnp.int32),
+            pltpu.VMEM((width, own * far_index.shape[1] * width), BF16),
             pltpu.SemaphoreType.DMA,
+            pltpu.SemaphoreType.DMA((own // 8,)),
         ],
         compiler_params=room(16),
         name="far",

time: 45.6 us -> 36.2 us (0.79)
  Pallas kernels: 28.9 us -> 19.7 us
  starting transfers between devices: 11.7 us -> 8.13 us
  waiting for transfers between devices: 3.9 us -> 7.09 us
    pallas_call x1, Pallas kernels: 13.7 us -> 4.6 us  [per_device(): pl.pallas_call(tree_kernel, out_shape=(jax.ShapeDtypeStruct((half, 2 * wi...]
    ppermute x4, starting transfers between devices: 9.6 us -> 1.02 us  [exchange(): return value + lax.ppermute(value, AXES, pairs)]
    ppermute x1, starting transfers between devices: 1.6 us -> 6.59 us  [swap_outer(): lax.ppermute(block, AXES, [(i, (i + 1 if i % 2 else i - 1) % many) for i...]
    ppermute x4, waiting for transfers between devices: 3.9 us -> 7.08 us  [exchange(): return value + lax.ppermute(value, AXES, pairs)]
  transfers between devices with their start and end apart: 6 -> 6, of which waited for: 4 -> 4; matrix products, arithmetic and copies ran while one was open for 0% -> 0% of each run, Pallas kernels for 15% -> 20%
where the time goes in v10:
time: 36.2 us; the launch traced here: 36 us
  Pallas kernels  19.7 us (54%)
  starting transfers between devices  8.13 us (22%)
  waiting for transfers between devices  7.09 us (20%)
  between operations  1.01 us (3%)
    ppermute x4, waiting for transfers between devices, exchange(): return value + lax.ppermute(value, AXES, pairs)  7.08 us
    ppermute x1, starting transfers between devices, swap_outer(): lax.ppermute(block, AXES, [(i, (i + 1 if i % 2 else i - 1) % many) for i...  6.59 us
    pallas_call x1, Pallas kernels, per_device(): pl.pallas_call(functools.partial(leaves_kernel, chunks, members, groups),...  5.05 us
    pallas_call x1, Pallas kernels, per_device(): pl.pallas_call(tree_kernel, out_shape=(jax.ShapeDtypeStruct((half, 2 * wi...  4.6 us
    pallas_call x1, Pallas kernels, per_device(): pl.pallas_call(functools.partial(far_kernel, plan), out_shape=jax.ShapeDt...  2.92 us
    pallas_call x2, Pallas kernels, per_device(): pl.pallas_call(chunk_kernel(layer_chunk, pair_chunk, halo, width), out_sh...  2.26 us
    pallas_call x1, Pallas kernels, per_device(): pl.pallas_call(edges_kernel, out_shape=(part_shape(2), jax.ShapeDtypeStru...  1.99 us
    pallas_call x1, Pallas kernels, per_device(): pl.pallas_call(last_chunk_kernel(chunks[3], edge_pairs), out_shape=(part_...  1.58 us
  transfers between devices with their start and end apart: 6, of which 4 were waited for; matrix products, arithmetic and copies ran while one was open for 0% of the time, Pallas kernels for 20%

profile of v10, /device:TPU:0, one launch (start us, length us, event | category | flops | bytes accessed | tf_op | source)
XLA Modules:
  0.0 36.0 jit_solution(141659368920565553)
XLA Ops:
  0.6 0.0 copy-start
  0.6 0.0 copy-start.3
  0.7 0.0 copy-start.7
  0.7 0.0 copy-start.6
  0.7 4.6 %tree.1 = (f32[32,128]{1,0:T(8,128)}, f32[32,128]{1,0:T(8,128)}, bf16[352,384]{1,0:T(8,128)(2,1)}, bf16[384,384]{1,0:T(8,128)(2,1)}) custom-call(f32[3,2048]{1,0:T(4,128)} %points, bf16[64,2048]{1,0:T(8,128)(2,1)} %bitcast.6, bf16[64,1920]{1,0:T(8,128)(2,1)} %bitcast.15, f32[64,64]{1,0:T(8,128)} %refs_7_.1, bf16[2048,384]{1,0:T(8,128)(2,1)} %vectors.7), custom_call_target="tpu_custom_call" | custom-call | tf_op jit(solution)/shard_map/tree/pallas_call | solution.py:689
  5.3 0.5 %collective-permute-start = (bf16[384,384]{1,0:T(8,128)(2,1)}, bf16[384,384]{1,0:T(8,128)(2,1)S(1)}, u32[]{:S(2)}, u32[]{:S(2)}) collective-permute-start(bf16[384,384]{1,0:T(8,128)(2,1)} %get-tuple-element.46), channel_id=1, source_target_pairs={{0,1},{1,0},{2,3},{3,2},{4,5},{5,4},{6,7},{7,6},{8,9},{9,8},{10,11... | collective-permute-start | bytes 884744 | tf_op jit(solution)/shard_map/ppermute | solution.py:653
  5.8 6.6 %collective-permute-start.4 = (bf16[352,384]{1,0:T(8,128)(2,1)}, bf16[352,384]{1,0:T(8,128)(2,1)S(1)}, u32[]{:S(2)}, u32[]{:S(2)}) collective-permute-start(bf16[352,384]{1,0:T(8,128)(2,1)} %get-tuple-element.64), channel_id=1, source_target_pairs={{0,31},{1,2},{2,1},{3,4},{4,3},{5,6},{6,5},{7,8},{8,7},{9,10},{10,... | collective-permute-start | bytes 811016 | tf_op jit(solution)/shard_map/ppermute | solution.py:658
  12.4 0.0 copy-done
  12.4 0.0 copy-done.3
  12.4 0.0 copy-done.7
  12.4 0.0 copy-done.6
  12.4 0.0 copy-start.8
  12.4 0.0 copy-start.5
  12.4 1.3 %chunk_0.1 = (bf16[512,384]{1,0:T(8,128)(2,1)S(1)}, bf16[2048,64]{1,0:T(8,128)(2,1)S(1)}, bf16[64,2048]{1,0:T(8,128)(2,1)S(1)}, bf16[48,2048]{1,0:T(8,128)(2,1)S...) custom-call(f32[3,2048]{1,0:T(4,128)S(1)} %copy-done.3, s32[12,32]{1,0:T(8,128)S(1)} %bitcast.12, ...), custom_call_target="tpu_custom_call" | custom-call | flops 1000000000 | bytes 4000000 | tf_op jit(solution)/shard_map/chunk_0/pallas_call | solution.py:732
  13.7 0.0 collective-permute-done.inner
  13.7 0.0 copy-done.8
  13.8 0.1 collective-permute-start.1
  13.9 0.0 copy-done.5
  13.9 1.4 %chunk_1.1 = (bf16[512,384]{1,0:T(8,128)(2,1)S(1)}, bf16[768,256]{1,0:T(8,128)(2,1)S(1)}) custom-call(f32[32,128]{1,0:T(8,128)S(1)} %add_add_fusion.after, s32[3,32]{1,0:T(4,128)S(1)} %bitcast.8, bf16[2048,64]{1,0:T(8,128)(2,1)S(1)} %get-tuple-element.51.refs_0_.first_rows, bf16[48,2048]{1,0:T(8,128)(2,1)S(1)} %get-tuple-element.52.refs_1_.second_cols, ...), custom_call_target="tpu_custom_call" | custom-call | flops 1000000000 | bytes 4000000 | tf_op jit(solution)/shard_map/chunk_1/pallas_call | solution.py:768
  15.2 1.8 %collective-permute-done.1 = f32[32,128]{1,0:T(8,128)S(1)} collective-permute-done((f32[32,128]{1,0:T(8,128)S(1)}, f32[32,128]{1,0:T(8,128)S(1)}, u32[]{:S(2)}, u32[]{:S(2)}) %collective-permute-start.1) | collective-permute-done | bytes 16416 | tf_op jit(solution)/shard_map/ppermute | solution.py:663
  17.0 0.9 %collective-permute-start.2 = (f32[32,128]{1,0:T(8,128)S(1)}, f32[32,128]{1,0:T(8,128)S(1)}, u32[]{:S(2)}, u32[]{:S(2)}) collective-permute-start(f32[32,128]{1,0:T(8,128)S(1)} %add.24.after), channel_id=1, source_target_pairs={{0,17},{1,16},{2,19},{3,18},{4,21},{5,20},{6,23},{7,22},{8,25},{9,... | collective-permute-start | bytes 49160 | tf_op jit(solution)/shard_map/ppermute | solution.py:663
  17.9 0.9 %chunk_2.1 = (bf16[256,384]{1,0:T(8,128)(2,1)S(1)}, bf16[768,256]{1,0:T(8,128)(2,1)S(1)}) custom-call(f32[32,128]{1,0:T(8,128)S(1)} %add.24.after, s32[3,32]{1,0:T(4,128)S(1)} %bitcast.9, bf16[2048,64]{1,0:T(8,128)(2,1)S(1)} %get-tuple-element.51.refs_0_.first_rows, bf16[48,2048]{1,0:T(8,128)(2,1)S(1)} %get-tuple-element.52.refs_1_.second_cols, ...), custom_call_target="tpu_custom_call" | custom-call | flops 1000000000 | bytes 4000000 | tf_op jit(solution)/shard_map/chunk_2/pallas_call | solution.py:768
  18.8 2.3 %collective-permute-done.2 = f32[32,128]{1,0:T(8,128)S(1)} collective-permute-done((f32[32,128]{1,0:T(8,128)S(1)}, f32[32,128]{1,0:T(8,128)S(1)}, u32[]{:S(2)}, u32[]{:S(2)}) %collective-permute-start.2) | collective-permute-done | bytes 16416 | tf_op jit(solution)/shard_map/ppermute | solution.py:663
  21.1 0.0 copy-start.1
  21.1 0.0 copy-start.4
  21.1 0.1 collective-permute-start.3
  21.2 0.0 collective-permute-done.4.outer
  21.2 2.0 %edges.1 = (bf16[512,384]{1,0:T(8,128)(2,1)S(1)}, bf16[1024,128]{1,0:T(8,128)(2,1)S(1)}) custom-call(f32[64,128]{1,0:T(8,128)S(1)} %pad_maximum_fusion.after, bf16[384,384]{1,0:T(8,128)(2,1)S(1)} %collective-permute-done.inner, bf16[352,384]{1,0:T(8,128)(2,1)S(1)} %collective-permute-done.4.outer, bf16[2048,64]{1,0:T(8,128)(2,1)S(1)} %get-tuple-element.51.refs_0_.first_rows, ...), custom_call_target="tpu_custom_call" | custom-call | flops 1000000000 | bytes 4000000 | tf_op jit(solution)/shard_map/edges/pallas_call | solution.py:788
  23.2 1.3 %collective-permute-done.3 = f32[64,128]{1,0:T(8,128)S(1)} collective-permute-done((f32[64,128]{1,0:T(8,128)S(1)}, f32[64,128]{1,0:T(8,128)S(1)}, u32[]{:S(2)}, u32[]{:S(2)}) %collective-permute-start.3) | collective-permute-done | bytes 32800 | tf_op jit(solution)/shard_map/ppermute | solution.py:663
  24.5 0.0 collective-permute-start.5
  24.5 0.0 copy-done.1
  24.5 0.0 copy-done.4
  24.5 0.0 copy-start.2
  24.6 1.6 %chunk_3.1 = (bf16[256,384]{1,0:T(8,128)(2,1)S(1)}, bf16[1536,256]{1,0:T(8,128)(2,1)S(1)}, f32[1920,128]{1,0:T(8,128)S(1)}) custom-call(f32[64,128]{1,0:T(8,128)S(1)} %fusion.after, s32[3,32]{1,0:T(4,128)S(1)} %bitcast.10, bf16[384,384]{1,0:T(8,128)(2,1)S(1)} %collective-permute-done.inner, bf16[352,384]{1,0:T(8,128)(2,1)S(1)} %collective-permute-done.4.outer, ...), custom_call_target="tpu_custom_call" | custom-call | flops 1000000000 | bytes 4000000 | tf_op jit(solution)/shard_map/chunk_3/pallas_call | solution.py:809
  26.1 1.7 %collective-permute-done.5 = f32[64,128]{1,0:T(8,128)S(1)} collective-permute-done((f32[64,128]{1,0:T(8,128)S(1)}, f32[64,128]{1,0:T(8,128)S(1)}, u32[]{:S(2)}, u32[]{:S(2)}) %collective-permute-start.5) | collective-permute-done | bytes 32800 | tf_op jit(solution)/shard_map/ppermute | solution.py:663
  27.9 0.0 copy-done.2
  27.9 5.0 %leaves.1 = (bf16[2048,384]{1,0:T(8,128)(2,1)}, bf16[3072,128]{1,0:T(8,128)(2,1)S(1)}, bf16[3072,128]{1,0:T(8,128)(2,1)S(1)}, f32[64,64]{1,0:T(8,128)}, f32[64,64]{1,0:T(8,128)}, /*index=5*/f32[64,64]{1,0:T(8,128)}) custom-call(bf16[512,384]{1,0:T(8,128)(2,1)S(1)} %get-tuple-element.49.refs_0_, bf16[512,384]{1,0:T(8,128)(2,1)S(1)} %get-tuple-element.58.refs_1_, ...), custom_call_target="tpu_custom_call" | custom-call | tf_op jit(solution)/shard_map/leaves/pallas_call | solution.py:848
  32.9 2.9 %far.1 = bf16[64,6144]{1,0:T(8,128)(2,1)} custom-call(s32[3,32]{1,0:T(4,128)S(1)} %bitcast.11, bf16[3072,128]{1,0:T(8,128)(2,1)S(1)} %get-tuple-element.75.high, bf16[3072,128]{1,0:T(8,128)(2,1)S(1)} %get-tuple-element.76.low, bf16[768,256]{1,0:T(8,128)(2,1)S(1)} %get-tuple-element.77.refs_0_, bf16[768,256]{1,0:T(8,128)(2,1)S(1)} %get-tuple-element.78.refs_1_, ...), custom_call_target="tpu_custom_call" | custom-call | tf_op jit(solution)/shard_map/far/pallas_call | solution.py:869
  (6 shorter events, 0.0 us)
Async XLA Ops:
  0.6 11.8 %copy-start = (bf16[2048,384]{1,0:T(8,128)(2,1)S(1)}, bf16[2048,384]{1,0:T(8,128)(2,1)}, u32[]{:S(2)}) copy-start(bf16[2048,384]{1,0:T(8,128)(2,1)} %vectors.7) | copy-start | bytes 4718596
  0.6 11.8 %copy-start.3 = (f32[3,2048]{1,0:T(4,128)S(1)}, f32[3,2048]{1,0:T(4,128)}, u32[]{:S(2)}) copy-start(f32[3,2048]{1,0:T(4,128)} %points) | copy-start | bytes 73732
  0.7 11.7 %copy-start.7 = (s32[32]{0:T(128)S(1)}, s32[32]{0:T(128)}, u32[]{:S(2)}) copy-start(s32[32]{0:T(128)} %param.14) | copy-start | bytes 388
  0.7 11.7 %copy-start.6 = (s32[32,12]{0,1:T(8,128)S(1)}, s32[32,12]{0,1:T(8,128)}, u32[]{:S(2)}) copy-start(s32[32,12]{0,1:T(8,128)} %param.13) | copy-start | bytes 4612
  5.3 8.5 %collective-permute-start = (bf16[384,384]{1,0:T(8,128)(2,1)}, bf16[384,384]{1,0:T(8,128)(2,1)S(1)}, u32[]{:S(2)}, u32[]{:S(2)}) collective-permute-start(bf16[384,384]{1,0:T(8,128)(2,1)} %get-tuple-element.46), channel_id=1, source_target_pairs={{0,1},{1,0},{2,3},{3,2},{4,5},{5,4},{6,7},{7,6},{8,9},{9,8},{10,11... | collective-permute-start | bytes 884744 | tf_op jit(solution)/shard_map/ppermute | solution.py:653
  5.8 15.4 %collective-permute-start.4 = (bf16[352,384]{1,0:T(8,128)(2,1)}, bf16[352,384]{1,0:T(8,128)(2,1)S(1)}, u32[]{:S(2)}, u32[]{:S(2)}) collective-permute-start(bf16[352,384]{1,0:T(8,128)(2,1)} %get-tuple-element.64), channel_id=1, source_target_pairs={{0,31},{1,2},{2,1},{3,4},{4,3},{5,6},{6,5},{7,8},{8,7},{9,10},{10,... | collective-permute-start | bytes 811016 | tf_op jit(solution)/shard_map/ppermute | solution.py:658
  12.4 1.3 %copy-start.8 = (f32[32,128]{1,0:T(8,128)S(1)}, f32[32,128]{1,0:T(8,128)}, u32[]{:S(2)}) copy-start(f32[32,128]{1,0:T(8,128)} %get-tuple-element.45) | copy-start | bytes 49156
  12.4 1.4 %copy-start.5 = (s32[32,3]{0,1:T(4,128)S(1)}, s32[32,3]{0,1:T(4,128)}, u32[]{:S(2)}) copy-start(s32[32,3]{0,1:T(4,128)} %param.15) | copy-start | bytes 1156
  13.8 3.2 %collective-permute-start.1 = (f32[32,128]{1,0:T(8,128)S(1)}, f32[32,128]{1,0:T(8,128)S(1)}, u32[]{:S(2)}, u32[]{:S(2)}) collective-permute-start(f32[32,128]{1,0:T(8,128)S(1)} %add_add_fusion.after), channel_id=1, source_target_pairs={{0,9},{1,8},{2,11},{3,10},{4,13},{5,12},{6,15},{7,14},{8,1},{9,0},... | collective-permute-start | bytes 49160 | tf_op jit(solution)/shard_map/ppermute | solution.py:663
  17.0 4.1 %collective-permute-start.2 = (f32[32,128]{1,0:T(8,128)S(1)}, f32[32,128]{1,0:T(8,128)S(1)}, u32[]{:S(2)}, u32[]{:S(2)}) collective-permute-start(f32[32,128]{1,0:T(8,128)S(1)} %add.24.after), channel_id=1, source_target_pairs={{0,17},{1,16},{2,19},{3,18},{4,21},{5,20},{6,23},{7,22},{8,25},{9,... | collective-permute-start | bytes 49160 | tf_op jit(solution)/shard_map/ppermute | solution.py:663
  21.1 3.4 %copy-start.1 = (bf16[2048,64]{0,1:T(8,128)(2,1)S(1)}, bf16[2048,64]{0,1:T(8,128)(2,1)}, u32[]{:S(2)}) copy-start(bf16[2048,64]{0,1:T(8,128)(2,1)} %param.9) | copy-start | bytes 786436
  21.1 3.4 %copy-start.4 = (f32[32,128]{1,0:T(8,128)S(1)}, f32[32,128]{1,0:T(8,128)}, u32[]{:S(2)}) copy-start(f32[32,128]{1,0:T(8,128)} %get-tuple-element.68.top) | copy-start | bytes 49156
  21.1 3.4 %collective-permute-start.3 = (f32[64,128]{1,0:T(8,128)S(1)}, f32[64,128]{1,0:T(8,128)S(1)}, u32[]{:S(2)}, u32[]{:S(2)}) collective-permute-start(f32[64,128]{1,0:T(8,128)S(1)} %pad_maximum_fusion.after), channel_id=1, source_target_pairs={{0,3},{1,2},{2,1},{3,0},{4,7},{5,6},{6,5},{7,4},{8,11},{9,10},{10,... | collective-permute-start | bytes 98312 | tf_op jit(solution)/shard_map/ppermute | solution.py:663
  24.5 3.3 %collective-permute-start.5 = (f32[64,128]{1,0:T(8,128)S(1)}, f32[64,128]{1,0:T(8,128)S(1)}, u32[]{:S(2)}, u32[]{:S(2)}) collective-permute-start(f32[64,128]{1,0:T(8,128)S(1)} %fusion.after), channel_id=1, source_target_pairs={{0,5},{1,4},{2,7},{3,6},{4,1},{5,0},{6,3},{7,2},{8,13},{9,12},{10,... | collective-permute-start | bytes 98312 | tf_op jit(solution)/shard_map/ppermute | solution.py:663
  24.5 3.3 %copy-start.2 = (f32[64,64]{1,0:T(8,128)S(1)}, f32[64,64]{1,0:T(8,128)}, u32[]{:S(2)}) copy-start(f32[64,64]{1,0:T(8,128)} %refs_7_.1) | copy-start | bytes 49156

commit v11 on v10

--- a/solution.py
+++ b/solution.py
@@ -55,7 +55,7 @@
 
 def tree_kernel(
     points_in, basis_in, below_in, transfer_in, vectors,
-    dense, top, outer, inner, points, basis, below, transfer, passing, packed, staged, sems,
+    dense, top, outer, inner, points, basis, below, transfer, passing, packed, staged, small, sems,
 ):
     width = basis.shape[0]
     count = basis.shape[1] // width
@@ -184,9 +184,9 @@
             jnp.concatenate([high, middle, low, high, middle, high], axis=1),
         )
     total = total * (4.0 / count)
-    top[...] = fold(total[:width, :width])
+    small[0, :, :] = fold(total[:width, :width])
     halves = fold(total[width:, width:])
-    dense[...] = halves
+    small[1, :, :] = halves
     staged[...] = jnp.concatenate(split3(halves), axis=1)
     copies.append(
         pltpu.make_async_copy(
@@ -194,6 +194,9 @@
         )
     )
     copies[-1].start()
+    for n, target in enumerate((top, dense)):
+        copies.append(pltpu.make_async_copy(small.at[n], target, sems.at[11 + n]))
+        copies[-1].start()
     for copy in copies:
         copy.wait()
 
@@ -227,8 +230,8 @@
                     jnp.where(row >= k, tile[k], 0.0) if i == p else tile[k]
                 )
         for q in range(p + 1, panels):
-            for start in range(q, panels, 2):
-                group = range(start, min(start + 2, panels))
+            for start in range(q, panels, 4):
+                group = range(start, min(start + 4, panels))
                 accs = {
                     (i, k): work[8 * q + k, 8 * i : 8 * i + 8, :] for i in group for k in range(8)
                 }
@@ -695,7 +698,7 @@
             block_of(extra + half),
         ),
         in_specs=[hbm] * 5,
-        out_specs=(vmem, vmem, hbm, hbm),
+        out_specs=(hbm,) * 4,
         scratch_shapes=[
             pltpu.VMEM((3, own * width), F32),
             pltpu.VMEM((width, own * width), BF16),
@@ -704,13 +707,13 @@
             pltpu.VMEM((2, halo, columns), BF16),
             pltpu.VMEM((2, width + 32, columns), BF16),
             pltpu.VMEM((half, columns), BF16),
-            pltpu.SemaphoreType.DMA((11,)),
+            pltpu.VMEM((2, half, 2 * width), F32),
+            pltpu.SemaphoreType.DMA((13,)),
         ],
         compiler_params=room(60),
         name="tree",
     )(points, basis, inner_transfer.T, device_transfer, vectors)
     from_inner = swap_inner(to_inner)
-    from_outer = swap_outer(to_outer)
 
     sub_bits = members.bit_length() - 1
     steps = [members << bit for bit in range(groups.bit_length() - 1)]
@@ -751,7 +754,8 @@
         from_inner[extra:, n * 2 * width : (n + 1) * 2 * width].astype(F32) for n in range(3)
     ]
     pair_gram = gram = dense + (summands[0] + (summands[1] + summands[2]))
-    gram, parts[0] = lax.optimization_barrier((gram, parts[0]))
+    gram, parts[0], to_outer = lax.optimization_barrier((gram, parts[0], to_outer))
+    from_outer = swap_outer(to_outer)
     first_rows, first_cols, second_cols, second_rows, switches = shared
     jobs = [1, 2, "edges", 3]
     for n in range(max(len(steps), len(jobs))):

time: 36.2 us -> 36.4 us (level)
  waiting for transfers between devices: 7.09 us -> 8.25 us
  Pallas kernels: 19.7 us -> 19.1 us
    ppermute x1, starting transfers between devices: 6.59 us -> 4.34 us  [swap_outer(): lax.ppermute(block, AXES, [(i, (i + 1 if i % 2 else i - 1) % many) for i...]
    ppermute x4, starting transfers between devices: 1.02 us -> 2.96 us  [exchange(): return value + lax.ppermute(value, AXES, pairs)]
    ppermute x4, waiting for transfers between devices: 7.08 us -> 8.18 us  [exchange(): return value + lax.ppermute(value, AXES, pairs)]
    pallas_call x1, Pallas kernels: 4.6 us -> 4.02 us  [per_device(): pl.pallas_call(tree_kernel, out_shape=(jax.ShapeDtypeStruct((half, 2 * wi...]
  transfers between devices with their start and end apart: 6 -> 6, of which waited for: 4 -> 4; matrix products, arithmetic and copies ran while one was open for 0% -> 0% of each run, Pallas kernels for 20% -> 14%
where the time goes in v11:
time: 36.4 us; the launch traced here: 36.2 us
  Pallas kernels  19.1 us (52%)
  waiting for transfers between devices  8.25 us (23%)
  starting transfers between devices  7.82 us (21%)
  between operations  1 us (3%)
    ppermute x4, waiting for transfers between devices, exchange(): return value + lax.ppermute(value, AXES, pairs)  8.18 us
    pallas_call x1, Pallas kernels, per_device(): pl.pallas_call(functools.partial(leaves_kernel, chunks, members, groups),...  5 us
    ppermute x1, starting transfers between devices, swap_outer(): lax.ppermute(block, AXES, [(i, (i + 1 if i % 2 else i - 1) % many) for i...  4.34 us
    pallas_call x1, Pallas kernels, per_device(): pl.pallas_call(tree_kernel, out_shape=(jax.ShapeDtypeStruct((half, 2 * wi...  4.02 us
    ppermute x4, starting transfers between devices, exchange(): return value + lax.ppermute(value, AXES, pairs)  2.96 us
    pallas_call x1, Pallas kernels, per_device(): pl.pallas_call(functools.partial(far_kernel, plan), out_shape=jax.ShapeDt...  2.92 us
    pallas_call x2, Pallas kernels, per_device(): pl.pallas_call(chunk_kernel(layer_chunk, pair_chunk, halo, width), out_sh...  2.26 us
    pallas_call x1, Pallas kernels, per_device(): pl.pallas_call(edges_kernel, out_shape=(part_shape(2), jax.ShapeDtypeStru...  1.98 us
  transfers between devices with their start and end apart: 6, of which 4 were waited for; matrix products, arithmetic and copies ran while one was open for 0% of the time, Pallas kernels for 14%

profile of v11, /device:TPU:0, one launch (start us, length us, event | category | flops | bytes accessed | tf_op | source)
XLA Modules:
  0.0 36.2 jit_solution(237404482917961654)
XLA Ops:
  0.6 0.0 copy-start
  0.6 0.0 copy-start.3
  0.7 0.0 copy-start.7
  0.7 0.0 copy-start.6
  0.7 4.0 %tree.1 = (f32[32,128]{1,0:T(8,128)}, f32[32,128]{1,0:T(8,128)}, bf16[352,384]{1,0:T(8,128)(2,1)}, bf16[384,384]{1,0:T(8,128)(2,1)}) custom-call(f32[3,2048]{1,0:T(4,128)} %points, bf16[64,2048]{1,0:T(8,128)(2,1)} %bitcast.6, bf16[64,1920]{1,0:T(8,128)(2,1)} %bitcast.15, f32[64,64]{1,0:T(8,128)} %refs_7_.1, bf16[2048,384]{1,0:T(8,128)(2,1)} %vectors.7), custom_call_target="tpu_custom_call" | custom-call | tf_op jit(solution)/shard_map/tree/pallas_call | solution.py:692
  4.7 0.5 %collective-permute-start = (bf16[384,384]{1,0:T(8,128)(2,1)}, bf16[384,384]{1,0:T(8,128)(2,1)S(1)}, u32[]{:S(2)}, u32[]{:S(2)}) collective-permute-start(bf16[384,384]{1,0:T(8,128)(2,1)} %get-tuple-element.47), channel_id=1, source_target_pairs={{0,1},{1,0},{2,3},{3,2},{4,5},{5,4},{6,7},{7,6},{8,9},{9,8},{10,11... | collective-permute-start | bytes 884744 | tf_op jit(solution)/shard_map/ppermute | solution.py:656
  5.2 0.0 copy-done
  5.2 0.0 copy-done.3
  5.2 0.0 copy-done.7
  5.2 0.0 copy-done.6
  5.2 0.0 copy-start.8
  5.2 0.0 copy-start.9
  5.3 0.0 copy-start.5
  5.3 1.3 %chunk_0.1 = (bf16[512,384]{1,0:T(8,128)(2,1)S(1)}, bf16[2048,64]{1,0:T(8,128)(2,1)S(1)}, bf16[64,2048]{1,0:T(8,128)(2,1)S(1)}, bf16[48,2048]{1,0:T(8,128)(2,1)S...) custom-call(f32[3,2048]{1,0:T(4,128)S(1)} %copy-done.3, s32[12,32]{1,0:T(8,128)S(1)} %bitcast.12, ...), custom_call_target="tpu_custom_call" | custom-call | flops 1000000000 | bytes 4000000 | tf_op jit(solution)/shard_map/chunk_0/pallas_call | solution.py:735
  6.6 0.1 collective-permute-done.inner
  6.6 0.0 copy-done.8
  6.7 2.7 %collective-permute-start.1 = (f32[32,128]{1,0:T(8,128)S(1)}, f32[32,128]{1,0:T(8,128)S(1)}, u32[]{:S(2)}, u32[]{:S(2)}) collective-permute-start(f32[32,128]{1,0:T(8,128)S(1)} %add_add_fusion.after), channel_id=1, source_target_pairs={{0,9},{1,8},{2,11},{3,10},{4,13},{5,12},{6,15},{7,14},{8,1},{9,0},... | collective-permute-start | bytes 49160 | tf_op jit(solution)/shard_map/ppermute | solution.py:666
  9.4 0.0 copy-done.9
  9.4 4.3 %collective-permute-start.4 = (bf16[352,384]{1,0:T(8,128)(2,1)S(1)}, bf16[352,384]{1,0:T(8,128)(2,1)S(1)}, u32[]{:S(2)}, u32[]{:S(2)}) collective-permute-start(bf16[352,384]{1,0:T(8,128)(2,1)S(1)} %copy-done.9), channel_id=1, source_target_pairs={{0,31},{1,2},{2,1},{3,4},{4,3},{5,6},{6,5},{7,8},{8,7},{9,10},{10,... | collective-permute-start | bytes 811016 | tf_op jit(solution)/shard_map/ppermute | solution.py:661
  13.7 0.0 copy-done.5
  13.7 1.4 %chunk_1.1 = (bf16[512,384]{1,0:T(8,128)(2,1)S(1)}, bf16[768,256]{1,0:T(8,128)(2,1)S(1)}) custom-call(f32[32,128]{1,0:T(8,128)S(1)} %add_add_fusion.after, s32[3,32]{1,0:T(4,128)S(1)} %bitcast.8, bf16[2048,64]{1,0:T(8,128)(2,1)S(1)} %get-tuple-element.53.refs_0_.first_rows, bf16[48,2048]{1,0:T(8,128)(2,1)S(1)} %get-tuple-element.54.refs_1_.second_cols, ...), custom_call_target="tpu_custom_call" | custom-call | flops 1000000000 | bytes 4000000 | tf_op jit(solution)/shard_map/chunk_1/pallas_call | solution.py:772
  15.1 0.0 collective-permute-done.1
  15.1 0.1 collective-permute-start.2
  15.2 0.9 %chunk_2.1 = (bf16[256,384]{1,0:T(8,128)(2,1)S(1)}, bf16[768,256]{1,0:T(8,128)(2,1)S(1)}) custom-call(f32[32,128]{1,0:T(8,128)S(1)} %add.24.after, s32[3,32]{1,0:T(4,128)S(1)} %bitcast.9, bf16[2048,64]{1,0:T(8,128)(2,1)S(1)} %get-tuple-element.53.refs_0_.first_rows, bf16[48,2048]{1,0:T(8,128)(2,1)S(1)} %get-tuple-element.54.refs_1_.second_cols, ...), custom_call_target="tpu_custom_call" | custom-call | flops 1000000000 | bytes 4000000 | tf_op jit(solution)/shard_map/chunk_2/pallas_call | solution.py:772
  16.1 3.1 %collective-permute-done.2 = f32[32,128]{1,0:T(8,128)S(1)} collective-permute-done((f32[32,128]{1,0:T(8,128)S(1)}, f32[32,128]{1,0:T(8,128)S(1)}, u32[]{:S(2)}, u32[]{:S(2)}) %collective-permute-start.2) | collective-permute-done | bytes 16416 | tf_op jit(solution)/shard_map/ppermute | solution.py:666
  19.3 0.1 collective-permute-start.3
  19.4 3.3 %collective-permute-done.3 = f32[64,128]{1,0:T(8,128)S(1)} collective-permute-done((f32[64,128]{1,0:T(8,128)S(1)}, f32[64,128]{1,0:T(8,128)S(1)}, u32[]{:S(2)}, u32[]{:S(2)}) %collective-permute-start.3) | collective-permute-done | bytes 32800 | tf_op jit(solution)/shard_map/ppermute | solution.py:666
  22.7 0.0 copy-start.1
  22.7 0.0 copy-start.4
  22.7 0.0 collective-permute-done.4.outer
  22.7 2.0 %edges.1 = (bf16[512,384]{1,0:T(8,128)(2,1)S(1)}, bf16[1024,128]{1,0:T(8,128)(2,1)S(1)}) custom-call(f32[64,128]{1,0:T(8,128)S(1)} %pad_maximum_fusion.after, bf16[384,384]{1,0:T(8,128)(2,1)S(1)} %collective-permute-done.inner, bf16[352,384]{1,0:T(8,128)(2,1)S(1)} %collective-permute-done.4.outer, bf16[2048,64]{1,0:T(8,128)(2,1)S(1)} %get-tuple-element.53.refs_0_.first_rows, ...), custom_call_target="tpu_custom_call" | custom-call | flops 1000000000 | bytes 4000000 | tf_op jit(solution)/shard_map/edges/pallas_call | solution.py:792
  24.7 0.1 collective-permute-start.5
  24.8 0.0 copy-done.1
  24.8 0.0 copy-done.4
  24.8 0.0 copy-start.2
  24.8 1.6 %chunk_3.1 = (bf16[256,384]{1,0:T(8,128)(2,1)S(1)}, bf16[1536,256]{1,0:T(8,128)(2,1)S(1)}, f32[1920,128]{1,0:T(8,128)S(1)}) custom-call(f32[64,128]{1,0:T(8,128)S(1)} %fusion.after, s32[3,32]{1,0:T(4,128)S(1)} %bitcast.10, bf16[384,384]{1,0:T(8,128)(2,1)S(1)} %collective-permute-done.inner, bf16[352,384]{1,0:T(8,128)(2,1)S(1)} %collective-permute-done.4.outer, ...), custom_call_target="tpu_custom_call" | custom-call | flops 1000000000 | bytes 4000000 | tf_op jit(solution)/shard_map/chunk_3/pallas_call | solution.py:813
  26.4 1.7 %collective-permute-done.5 = f32[64,128]{1,0:T(8,128)S(1)} collective-permute-done((f32[64,128]{1,0:T(8,128)S(1)}, f32[64,128]{1,0:T(8,128)S(1)}, u32[]{:S(2)}, u32[]{:S(2)}) %collective-permute-start.5) | collective-permute-done | bytes 32800 | tf_op jit(solution)/shard_map/ppermute | solution.py:666
  28.1 0.0 copy-done.2
  28.1 5.0 %leaves.1 = (bf16[2048,384]{1,0:T(8,128)(2,1)}, bf16[3072,128]{1,0:T(8,128)(2,1)S(1)}, bf16[3072,128]{1,0:T(8,128)(2,1)S(1)}, f32[64,64]{1,0:T(8,128)}, f32[64,64]{1,0:T(8,128)}, /*index=5*/f32[64,64]{1,0:T(8,128)}) custom-call(bf16[512,384]{1,0:T(8,128)(2,1)S(1)} %get-tuple-element.51.refs_0_, bf16[512,384]{1,0:T(8,128)(2,1)S(1)} %get-tuple-element.60.refs_1_, ...), custom_call_target="tpu_custom_call" | custom-call | tf_op jit(solution)/shard_map/leaves/pallas_call | solution.py:852
  33.1 2.9 %far.1 = bf16[64,6144]{1,0:T(8,128)(2,1)} custom-call(s32[3,32]{1,0:T(4,128)S(1)} %bitcast.11, bf16[3072,128]{1,0:T(8,128)(2,1)S(1)} %get-tuple-element.77.high, bf16[3072,128]{1,0:T(8,128)(2,1)S(1)} %get-tuple-element.78.low, bf16[768,256]{1,0:T(8,128)(2,1)S(1)} %get-tuple-element.79.refs_0_, bf16[768,256]{1,0:T(8,128)(2,1)S(1)} %get-tuple-element.80.refs_1_, ...), custom_call_target="tpu_custom_call" | custom-call | tf_op jit(solution)/shard_map/far/pallas_call | solution.py:873
  (6 shorter events, 0.0 us)
Async XLA Ops:
  0.6 4.6 %copy-start = (bf16[2048,384]{1,0:T(8,128)(2,1)S(1)}, bf16[2048,384]{1,0:T(8,128)(2,1)}, u32[]{:S(2)}) copy-start(bf16[2048,384]{1,0:T(8,128)(2,1)} %vectors.7) | copy-start | bytes 4718596
  0.6 4.6 %copy-start.3 = (f32[3,2048]{1,0:T(4,128)S(1)}, f32[3,2048]{1,0:T(4,128)}, u32[]{:S(2)}) copy-start(f32[3,2048]{1,0:T(4,128)} %points) | copy-start | bytes 73732
  0.7 4.6 %copy-start.7 = (s32[32]{0:T(128)S(1)}, s32[32]{0:T(128)}, u32[]{:S(2)}) copy-start(s32[32]{0:T(128)} %param.14) | copy-start | bytes 388
  0.7 4.6 %copy-start.6 = (s32[32,12]{0,1:T(8,128)S(1)}, s32[32,12]{0,1:T(8,128)}, u32[]{:S(2)}) copy-start(s32[32,12]{0,1:T(8,128)} %param.13) | copy-start | bytes 4612
  4.7 1.9 %collective-permute-start = (bf16[384,384]{1,0:T(8,128)(2,1)}, bf16[384,384]{1,0:T(8,128)(2,1)S(1)}, u32[]{:S(2)}, u32[]{:S(2)}) collective-permute-start(bf16[384,384]{1,0:T(8,128)(2,1)} %get-tuple-element.47), channel_id=1, source_target_pairs={{0,1},{1,0},{2,3},{3,2},{4,5},{5,4},{6,7},{7,6},{8,9},{9,8},{10,11... | collective-permute-start | bytes 884744 | tf_op jit(solution)/shard_map/ppermute | solution.py:656
  5.2 1.4 %copy-start.8 = (f32[32,128]{1,0:T(8,128)S(1)}, f32[32,128]{1,0:T(8,128)}, u32[]{:S(2)}) copy-start(f32[32,128]{1,0:T(8,128)} %get-tuple-element.46) | copy-start | bytes 49156
  5.2 4.2 %copy-start.9 = (bf16[352,384]{1,0:T(8,128)(2,1)S(1)}, bf16[352,384]{1,0:T(8,128)(2,1)}, u32[]{:S(2)}) copy-start(bf16[352,384]{1,0:T(8,128)(2,1)} %get-tuple-element.66) | copy-start | bytes 811012
  5.3 8.5 %copy-start.5 = (s32[32,3]{0,1:T(4,128)S(1)}, s32[32,3]{0,1:T(4,128)}, u32[]{:S(2)}) copy-start(s32[32,3]{0,1:T(4,128)} %param.15) | copy-start | bytes 1156
  6.7 8.5 %collective-permute-start.1 = (f32[32,128]{1,0:T(8,128)S(1)}, f32[32,128]{1,0:T(8,128)S(1)}, u32[]{:S(2)}, u32[]{:S(2)}) collective-permute-start(f32[32,128]{1,0:T(8,128)S(1)} %add_add_fusion.after), channel_id=1, source_target_pairs={{0,9},{1,8},{2,11},{3,10},{4,13},{5,12},{6,15},{7,14},{8,1},{9,0},... | collective-permute-start | bytes 49160 | tf_op jit(solution)/shard_map/ppermute | solution.py:666
  9.4 13.3 %collective-permute-start.4 = (bf16[352,384]{1,0:T(8,128)(2,1)S(1)}, bf16[352,384]{1,0:T(8,128)(2,1)S(1)}, u32[]{:S(2)}, u32[]{:S(2)}) collective-permute-start(bf16[352,384]{1,0:T(8,128)(2,1)S(1)} %copy-done.9), channel_id=1, source_target_pairs={{0,31},{1,2},{2,1},{3,4},{4,3},{5,6},{6,5},{7,8},{8,7},{9,10},{10,... | collective-permute-start | bytes 811016 | tf_op jit(solution)/shard_map/ppermute | solution.py:661
  15.1 4.1 %collective-permute-start.2 = (f32[32,128]{1,0:T(8,128)S(1)}, f32[32,128]{1,0:T(8,128)S(1)}, u32[]{:S(2)}, u32[]{:S(2)}) collective-permute-start(f32[32,128]{1,0:T(8,128)S(1)} %add.24.after), channel_id=1, source_target_pairs={{0,17},{1,16},{2,19},{3,18},{4,21},{5,20},{6,23},{7,22},{8,25},{9,... | collective-permute-start | bytes 49160 | tf_op jit(solution)/shard_map/ppermute | solution.py:666
  19.3 3.4 %collective-permute-start.3 = (f32[64,128]{1,0:T(8,128)S(1)}, f32[64,128]{1,0:T(8,128)S(1)}, u32[]{:S(2)}, u32[]{:S(2)}) collective-permute-start(f32[64,128]{1,0:T(8,128)S(1)} %pad_maximum_fusion.after), channel_id=1, source_target_pairs={{0,3},{1,2},{2,1},{3,0},{4,7},{5,6},{6,5},{7,4},{8,11},{9,10},{10,... | collective-permute-start | bytes 98312 | tf_op jit(solution)/shard_map/ppermute | solution.py:666
  22.7 2.1 %copy-start.1 = (bf16[2048,64]{0,1:T(8,128)(2,1)S(1)}, bf16[2048,64]{0,1:T(8,128)(2,1)}, u32[]{:S(2)}) copy-start(bf16[2048,64]{0,1:T(8,128)(2,1)} %param.9) | copy-start | bytes 786436
  22.7 2.1 %copy-start.4 = (f32[32,128]{1,0:T(8,128)S(1)}, f32[32,128]{1,0:T(8,128)}, u32[]{:S(2)}) copy-start(f32[32,128]{1,0:T(8,128)} %get-tuple-element.70.top) | copy-start | bytes 49156
  24.7 3.4 %collective-permute-start.5 = (f32[64,128]{1,0:T(8,128)S(1)}, f32[64,128]{1,0:T(8,128)S(1)}, u32[]{:S(2)}, u32[]{:S(2)}) collective-permute-start(f32[64,128]{1,0:T(8,128)S(1)} %fusion.after), channel_id=1, source_target_pairs={{0,5},{1,4},{2,7},{3,6},{4,1},{5,0},{6,3},{7,2},{8,13},{9,12},{10,... | collective-permute-start | bytes 98312 | tf_op jit(solution)/shard_map/ppermute | solution.py:666
  24.8 3.3 %copy-start.2 = (f32[64,64]{1,0:T(8,128)S(1)}, f32[64,64]{1,0:T(8,128)}, u32[]{:S(2)}) copy-start(f32[64,64]{1,0:T(8,128)} %refs_7_.1) | copy-start | bytes 49156

commit v12 on v11

--- a/solution.py
+++ b/solution.py
@@ -407,8 +407,9 @@
 
 
 def edges_kernel(
-    after, inner, outer, first_rows, second_cols, switches, vectors,
-    out, halo_rows, ends, sides, place, halo_cols, sems,
+    pairs, after, far_in, inner, outer, first_rows, second_cols, switches, vectors,
+    first_cols, own_rows, top,
+    out, blocks, grams, ends, sides, place, halo_cols, far_list, second_rows, sems,
 ):
     halo = ends.shape[1]
     width = halo // LAYER
@@ -419,7 +420,7 @@
     arrived = ((inner, 1 - odd), (outer, odd))
     side_copies = [
         pltpu.make_async_copy(
-            block.at[pl.ds(halo + width, extra), :], sides.at[side], sems.at[n]
+            block.at[pl.ds(halo, extra), :], sides.at[side], sems.at[n]
         )
         for n, (block, side) in enumerate(arrived)
     ]
@@ -427,20 +428,30 @@
         pltpu.make_async_copy(block.at[pl.ds(0, halo), :], ends.at[side], sems.at[2 + n])
         for n, (block, side) in enumerate(arrived)
     ]
-    for copy in side_copies + end_copies:
+    list_copy = pltpu.make_async_copy(far_in, far_list, sems.at[4])
+    for copy in side_copies + end_copies + [list_copy]:
         copy.start()
     lanes = PAD * width
+    second_rows[lanes : lanes + own * width, :] = own_rows[...]
     place[...] = jnp.zeros(place.shape, F32)
     for copy in side_copies:
         copy.wait()
     for side, first_leaf in enumerate((-PAD, own)):
         for n in range(2):
-            values = sides[side, 16 * n : 16 * n + 16, 0:halo].astype(F32)
+            base = width + 16 * n
+            values = sides[side, base : base + 16, 0:halo].astype(F32)
             place[0:3, n * halo : (n + 1) * halo] = values[0:3, :] + values[8:11, :]
         leaf = iota((8, lanes), 1) // width + (first_leaf + PAD)
         second = features(place[...], leaf, layers // 2 + PAD // LAYER)[1]
         halo_cols[side, :, :] = second.astype(BF16)
-        halo_rows[side * lanes : (side + 1) * lanes, :] = rows_of(second)
+        at = (PAD + first_leaf) * width
+        second_rows[at : at + lanes, :] = rows_of(second)
+        for n in range(6):
+            piece = sides[side, 0:width, n * width : (n + 1) * width]
+            at = (6 * side + n) * STRIDE
+            grams[at : at + width // 2, :] = fold(mm_nt(piece, piece))
+    for n in range(12, 16):
+        grams[n * STRIDE : n * STRIDE + width // 2, :] = top[...]
     weights = [
         near_weights(
             first_rows, jnp.concatenate(columns, axis=1), switches, index, halo
@@ -458,33 +469,16 @@
     value = mm(weights[1][:, 0 : 2 * halo], vectors[(layers - 2) * halo :, :])
     value = value + mm(weights[1][:, 2 * halo :], ends[1, :, :])
     out[halo:, :] = value.astype(BF16)
-
-
-def last_chunk_kernel(layers, pairs):
-    def body(
-        after, far_in, inner, outer, first_rows, second_cols, switches, vectors,
-        first_cols, own_rows, halo_rows, basis, top,
-        out, blocks, grams, far_list, sides, second_rows, sems,
-    ):
+    list_copy.wait()
+    far_blocks(pairs, far_list, second_rows, first_cols, blocks, width, PAD, range(len(pairs)))
+
+
+def own_chunk_kernel(layers):
+    def body(after, first_rows, second_cols, switches, vectors, basis, out, grams):
         width = basis.shape[0]
         own = basis.shape[1] // width
-        total = own + 2 * PAD
-        halo = LAYER * width
         both = 2 * width
-        odd = lax.axis_index("sub") % 2
-        side_copies = [
-            pltpu.make_async_copy(block.at[pl.ds(halo, width), :], sides.at[side], sems.at[n])
-            for n, (block, side) in enumerate(((inner, 1 - odd), (outer, odd)))
-        ]
-        list_copy = pltpu.make_async_copy(far_in, far_list, sems.at[2])
-        for copy in side_copies + [list_copy]:
-            copy.start()
-        lanes = PAD * width
-        second_rows[0:lanes, :] = halo_rows[0:lanes, :]
-        second_rows[lanes : lanes + own * width, :] = own_rows[...]
-        second_rows[lanes + own * width :, :] = halo_rows[lanes:, :]
-        inner_layers(layers, vectors, first_rows, second_cols, switches, out, halo)
-
+        inner_layers(layers, vectors, first_rows, second_cols, switches, out, LAYER * width)
         lane = iota((width, both), 1)
         for n in range(own // 2):
             pair = basis[:, n * both : (n + 1) * both]
@@ -494,22 +488,8 @@
             )
             value = mm_nt(stacked, pair)
             for m in range(2):
-                at = (PAD + 2 * n + m) * STRIDE
+                at = (2 * n + m) * STRIDE
                 grams[at : at + width // 2, :] = fold(value[m * width : (m + 1) * width])
-        for spot in (0, LAYER, total - LAYER - 1, total - 1):
-            grams[spot * STRIDE : spot * STRIDE + width // 2, :] = top[...]
-        for copy in side_copies + [list_copy]:
-            copy.wait()
-        for side, spots in enumerate(
-            ((1, 2, 3, 5, 6, 7), tuple(PAD + own + m for m in (0, 1, 2, 4, 5, 6)))
-        ):
-            for n, spot in enumerate(spots):
-                piece = sides[side, 0:width, n * width : (n + 1) * width]
-                at = spot * STRIDE
-                grams[at : at + width // 2, :] = fold(mm_nt(piece, piece))
-        far_blocks(
-            pairs, far_list, second_rows, first_cols, blocks, width, PAD, range(len(pairs))
-        )
 
     return body
 
@@ -518,7 +498,8 @@
     outer_count = len(chunks) + 1
     near_parts = refs[:outer_count]
     (
-        grams,
+        own_grams,
+        halo_grams,
         upper,
         transfer,
         near,
@@ -550,27 +531,31 @@
     for copy in near_copies:
         copy.start()
 
-    spare = (LAYER, total - LAYER - 1)
+    spare = (own + 13, own + 14)
     means = (
         upper[0 : width // 2, :] * (1.0 / members),
         upper[width // 2 :, :] * (1.0 / (members * groups)),
     )
-    spot_row = iota((total, both), 0)
+    spot_row = iota((2 * PAD, both), 0)
     for i in range(width // 2):
-        rows = grams[pl.ds(i, total, stride=STRIDE), :]
+        rows = halo_grams[pl.ds(i, 2 * PAD, stride=STRIDE), :]
         for spot, mean in zip(spare, means):
-            rows = jnp.where(spot_row == spot, mean[i : i + 1, :], rows)
-        turned = rows.T
+            rows = jnp.where(spot_row == spot - own, mean[i : i + 1, :], rows)
+        turned = jnp.concatenate([own_grams[pl.ds(i, own, stride=STRIDE), :], rows], axis=0).T
         work[i, :, 0:total] = turned[0:width]
         work[i + width // 2, :, 0:total] = turned[width:]
     factor_lanes(work, width)
     from_lanes(work, factors, width, total)
-    device_factor[...] = exact(unfold(factors[0 : width // 2, :]), transfer[...])
+    at = (own + 12) * STRIDE
+    device_factor[...] = exact(unfold(factors[at : at + width // 2, :]), transfer[...])
     for target, spot in zip((group_factor, root_factor), spare):
         target[...] = unfold(factors[spot * STRIDE : spot * STRIDE + width // 2, :])
     left_lanes = iota((width // 2, both), 1) < width
-    for spot in range(total):
-        rows = factors[spot * STRIDE : spot * STRIDE + width // 2, :]
+    spots = [(PAD + t, t) for t in range(own)]
+    spots += [(spot, own + n) for n, spot in enumerate((1, 2, 3, 5, 6, 7))]
+    spots += [(PAD + own + m, own + 6 + n) for n, m in enumerate((0, 1, 2, 4, 5, 6))]
+    for spot, n in spots:
+        rows = factors[n * STRIDE : n * STRIDE + width // 2, :]
         turned = pltpu.roll(rows, width, 1)
         twice = jnp.concatenate(
             [jnp.where(left_lanes, rows, turned), jnp.where(left_lanes, turned, rows)], axis=0
@@ -757,8 +742,10 @@
     gram, parts[0], to_outer = lax.optimization_barrier((gram, parts[0], to_outer))
     from_outer = swap_outer(to_outer)
     first_rows, first_cols, second_cols, second_rows, switches = shared
-    jobs = [1, 2, "edges", 3]
+    jobs = [1, 2, 3, "edges"]
     for n in range(max(len(steps), len(jobs))):
+        if n < len(jobs) and jobs[n] == "edges":
+            gram, from_outer = lax.optimization_barrier((gram, from_outer))
         before = gram
         if n < len(steps):
             if n == len(steps) - sub_bits + 1:
@@ -788,46 +775,43 @@
             if pair_chunk:
                 plan.update((index, (len(blocks), m)) for m, index in enumerate(pair_chunk))
                 blocks.append(outs[-1])
+        elif job == 3:
+            part, own_grams = pl.pallas_call(
+                own_chunk_kernel(chunks[3]),
+                out_shape=(
+                    part_shape(len(chunks[3])),
+                    jax.ShapeDtypeStruct((own * STRIDE, 2 * width), F32),
+                ),
+                in_specs=[hbm] + [vmem] * 5,
+                out_specs=(vmem,) * 2,
+                compiler_params=room(10),
+                cost_estimate=cost,
+                name="chunk_3",
+            )(before, first_rows, second_cols, switches, vectors, basis)
+            gram, part = lax.optimization_barrier((gram, part))
+            parts.append(part)
         elif job == "edges":
-            edge_part, halo_rows = pl.pallas_call(
-                edges_kernel,
+            edge_part, edge_blocks, halo_grams = pl.pallas_call(
+                functools.partial(edges_kernel, edge_pairs),
                 out_shape=(
                     part_shape(2),
-                    jax.ShapeDtypeStruct((2 * PAD * width, 2 * width), BF16),
+                    block_shape(len(edge_pairs)),
+                    jax.ShapeDtypeStruct((2 * PAD * STRIDE, 2 * width), F32),
                 ),
-                in_specs=[hbm] * 3 + [vmem] * 4,
-                out_specs=(vmem,) * 2,
+                in_specs=[hbm] * 4 + [vmem] * 7,
+                out_specs=(vmem,) * 3,
                 scratch_shapes=[
                     pltpu.VMEM((2, halo, columns), BF16),
-                    pltpu.VMEM((2, 32, columns), BF16),
+                    pltpu.VMEM((2, width + 32, columns), BF16),
                     pltpu.VMEM((8, PAD * width), F32),
                     pltpu.VMEM((2, 48, PAD * width), BF16),
-                    pltpu.SemaphoreType.DMA((4,)),
-                ],
-                compiler_params=room(10),
-                cost_estimate=cost,
-                name="edges",
-            )(before, from_inner, from_outer, first_rows, second_cols, switches, vectors)
-            gram, edge_part = lax.optimization_barrier((gram, edge_part))
-        elif job == 3:
-            part, edge_blocks, grams = pl.pallas_call(
-                last_chunk_kernel(chunks[3], edge_pairs),
-                out_shape=(
-                    part_shape(len(chunks[3])),
-                    block_shape(len(edge_pairs)),
-                    jax.ShapeDtypeStruct((total * STRIDE, 2 * width), F32),
-                ),
-                in_specs=[hbm] * 4 + [vmem] * 9,
-                out_specs=(vmem,) * 3,
-                scratch_shapes=[
                     pltpu.SMEM(far_list.shape, jnp.int32),
-                    pltpu.VMEM((2, width, columns), BF16),
                     pltpu.VMEM((total * width, 2 * width), BF16),
-                    pltpu.SemaphoreType.DMA((3,)),
+                    pltpu.SemaphoreType.DMA((5,)),
                 ],
                 compiler_params=room(14),
                 cost_estimate=cost,
-                name="chunk_3",
+                name="edges",
             )(
                 before,
                 far_list,
@@ -839,12 +823,9 @@
                 vectors,
                 first_cols,
                 second_rows,
-                halo_rows,
-                basis,
                 top,
             )
-            gram, part = lax.optimization_barrier((gram, part))
-            parts.append(part)
+            gram, edge_part = lax.optimization_barrier((gram, edge_part))
             plan.update((index, (len(blocks), m)) for m, index in enumerate(edge_pairs))
             blocks.append(edge_blocks)
 
@@ -859,7 +840,7 @@
             square,
             square,
         ),
-        in_specs=[hbm] * (len(parts) + 1) + [vmem] * 3,
+        in_specs=[hbm] * (len(parts) + 1) + [vmem] * 4,
         out_specs=(hbm,) + (vmem,) * 5,
         scratch_shapes=[
             pltpu.VMEM((width, width, 128), F32),
@@ -868,7 +849,7 @@
         ],
         compiler_params=room(20),
         name="leaves",
-    )(*parts, edge_part, grams, gram, device_transfer)
+    )(*parts, edge_part, own_grams, halo_grams, gram, device_transfer)
 
     coupling = pl.pallas_call(
         functools.partial(far_kernel, plan),

time: 36.4 us -> 33.7 us (0.926)
  waiting for transfers between devices: 8.25 us -> 6.35 us
  Pallas kernels: 19.1 us -> 18.3 us
    ppermute x4, waiting for transfers between devices: 8.18 us -> 6.28 us  [exchange(): return value + lax.ppermute(value, AXES, pairs)]
    pallas_call x1, Pallas kernels: 5 us -> 4.3 us  [per_device(): pl.pallas_call(functools.partial(leaves_kernel, chunks, members, groups),...]
  transfers between devices with their start and end apart: 6 -> 6, of which waited for: 4 -> 4; matrix products, arithmetic and copies ran while one was open for 0% -> 0% of each run, Pallas kernels for 14% -> 21%
where the time goes in v12:
time: 33.7 us; the launch traced here: 33.5 us
  Pallas kernels  18.3 us (54%)
  starting transfers between devices  7.82 us (23%)
  waiting for transfers between devices  6.35 us (19%)
  between operations  1 us (3%)
    ppermute x4, waiting for transfers between devices, exchange(): return value + lax.ppermute(value, AXES, pairs)  6.28 us
    ppermute x1, starting transfers between devices, swap_outer(): lax.ppermute(block, AXES, [(i, (i + 1 if i % 2 else i - 1) % many) for i...  4.34 us
    pallas_call x1, Pallas kernels, per_device(): pl.pallas_call(functools.partial(leaves_kernel, chunks, members, groups),...  4.3 us
    pallas_call x1, Pallas kernels, per_device(): pl.pallas_call(tree_kernel, out_shape=(jax.ShapeDtypeStruct((half, 2 * wi...  4.02 us
    ppermute x4, starting transfers between devices, exchange(): return value + lax.ppermute(value, AXES, pairs)  2.96 us
    pallas_call x1, Pallas kernels, per_device(): pl.pallas_call(functools.partial(far_kernel, plan), out_shape=jax.ShapeDt...  2.93 us
    pallas_call x1, Pallas kernels, per_device(): pl.pallas_call(functools.partial(edges_kernel, edge_pairs), out_shape=(pa...  2.69 us
    pallas_call x2, Pallas kernels, per_device(): pl.pallas_call(chunk_kernel(layer_chunk, pair_chunk, halo, width), out_sh...  2.28 us
  transfers between devices with their start and end apart: 6, of which 4 were waited for; matrix products, arithmetic and copies ran while one was open for 0% of the time, Pallas kernels for 21%

profile of v12, /device:TPU:0, one launch (start us, length us, event | category | flops | bytes accessed | tf_op | source)
XLA Modules:
  0.0 33.5 jit_solution(16903339586233199482)
XLA Ops:
  0.6 0.0 copy-start
  0.6 0.0 copy-start.3
  0.7 0.0 copy-start.7
  0.7 0.0 copy-start.6
  0.7 4.0 %tree.1 = (f32[32,128]{1,0:T(8,128)}, f32[32,128]{1,0:T(8,128)}, bf16[352,384]{1,0:T(8,128)(2,1)}, bf16[384,384]{1,0:T(8,128)(2,1)}) custom-call(f32[3,2048]{1,0:T(4,128)} %points, bf16[64,2048]{1,0:T(8,128)(2,1)} %bitcast.6, bf16[64,1920]{1,0:T(8,128)(2,1)} %bitcast.15, f32[64,64]{1,0:T(8,128)} %refs_8_.1, bf16[2048,384]{1,0:T(8,128)(2,1)} %vectors.7), custom_call_target="tpu_custom_call" | custom-call | tf_op jit(solution)/shard_map/tree/pallas_call | solution.py:677
  4.7 0.5 %collective-permute-start = (bf16[384,384]{1,0:T(8,128)(2,1)}, bf16[384,384]{1,0:T(8,128)(2,1)S(1)}, u32[]{:S(2)}, u32[]{:S(2)}) collective-permute-start(bf16[384,384]{1,0:T(8,128)(2,1)} %get-tuple-element.49), channel_id=1, source_target_pairs={{0,1},{1,0},{2,3},{3,2},{4,5},{5,4},{6,7},{7,6},{8,9},{9,8},{10,11... | collective-permute-start | bytes 884744 | tf_op jit(solution)/shard_map/ppermute | solution.py:641
  5.2 0.0 copy-done
  5.2 0.0 copy-done.3
  5.2 0.0 copy-done.7
  5.2 0.0 copy-done.6
  5.2 0.0 copy-start.8
  5.2 0.0 copy-start.9
  5.3 0.0 copy-start.5
  5.3 1.3 %chunk_0.1 = (bf16[512,384]{1,0:T(8,128)(2,1)S(1)}, bf16[2048,64]{1,0:T(8,128)(2,1)S(1)}, bf16[64,2048]{1,0:T(8,128)(2,1)S(1)}, bf16[48,2048]{1,0:T(8,128)(2,1)S...) custom-call(f32[3,2048]{1,0:T(4,128)S(1)} %copy-done.3, s32[12,32]{1,0:T(8,128)S(1)} %bitcast.12, ...), custom_call_target="tpu_custom_call" | custom-call | flops 1000000000 | bytes 4000000 | tf_op jit(solution)/shard_map/chunk_0/pallas_call | solution.py:720
  6.6 0.1 collective-permute-done.inner
  6.6 0.0 copy-done.8
  6.7 2.7 %collective-permute-start.1 = (f32[32,128]{1,0:T(8,128)S(1)}, f32[32,128]{1,0:T(8,128)S(1)}, u32[]{:S(2)}, u32[]{:S(2)}) collective-permute-start(f32[32,128]{1,0:T(8,128)S(1)} %add_add_fusion.after), channel_id=1, source_target_pairs={{0,9},{1,8},{2,11},{3,10},{4,13},{5,12},{6,15},{7,14},{8,1},{9,0},... | collective-permute-start | bytes 49160 | tf_op jit(solution)/shard_map/ppermute | solution.py:651
  9.4 0.0 copy-done.9
  9.4 4.3 %collective-permute-start.4 = (bf16[352,384]{1,0:T(8,128)(2,1)S(1)}, bf16[352,384]{1,0:T(8,128)(2,1)S(1)}, u32[]{:S(2)}, u32[]{:S(2)}) collective-permute-start(bf16[352,384]{1,0:T(8,128)(2,1)S(1)} %copy-done.9), channel_id=1, source_target_pairs={{0,31},{1,2},{2,1},{3,4},{4,3},{5,6},{6,5},{7,8},{8,7},{9,10},{10,... | collective-permute-start | bytes 811016 | tf_op jit(solution)/shard_map/ppermute | solution.py:646
  13.7 0.0 copy-done.5
  13.7 1.4 %chunk_1.1 = (bf16[512,384]{1,0:T(8,128)(2,1)S(1)}, bf16[768,256]{1,0:T(8,128)(2,1)S(1)}) custom-call(f32[32,128]{1,0:T(8,128)S(1)} %add_add_fusion.after, s32[3,32]{1,0:T(4,128)S(1)} %bitcast.8, bf16[2048,64]{1,0:T(8,128)(2,1)S(1)} %get-tuple-element.55.refs_0_.first_rows, bf16[48,2048]{1,0:T(8,128)(2,1)S(1)} %get-tuple-element.56.refs_1_.second_cols, ...), custom_call_target="tpu_custom_call" | custom-call | flops 1000000000 | bytes 4000000 | tf_op jit(solution)/shard_map/chunk_1/pallas_call | solution.py:759
  15.1 0.0 collective-permute-done.1
  15.2 0.0 copy-start.1
  15.2 0.1 collective-permute-start.2
  15.2 0.9 %chunk_2.1 = (bf16[256,384]{1,0:T(8,128)(2,1)S(1)}, bf16[768,256]{1,0:T(8,128)(2,1)S(1)}) custom-call(f32[32,128]{1,0:T(8,128)S(1)} %add.24.after, s32[3,32]{1,0:T(4,128)S(1)} %bitcast.9, bf16[2048,64]{1,0:T(8,128)(2,1)S(1)} %get-tuple-element.55.refs_0_.first_rows, bf16[48,2048]{1,0:T(8,128)(2,1)S(1)} %get-tuple-element.56.refs_1_.second_cols, ...), custom_call_target="tpu_custom_call" | custom-call | flops 1000000000 | bytes 4000000 | tf_op jit(solution)/shard_map/chunk_2/pallas_call | solution.py:759
  16.2 3.1 %collective-permute-done.2 = f32[32,128]{1,0:T(8,128)S(1)} collective-permute-done((f32[32,128]{1,0:T(8,128)S(1)}, f32[32,128]{1,0:T(8,128)S(1)}, u32[]{:S(2)}, u32[]{:S(2)}) %collective-permute-start.2) | collective-permute-done | bytes 16416 | tf_op jit(solution)/shard_map/ppermute | solution.py:651
  19.3 0.0 copy-start.4
  19.3 0.1 collective-permute-start.3
  19.4 0.0 copy-done.1
  19.4 0.8 %chunk_3.1 = (bf16[256,384]{1,0:T(8,128)(2,1)S(1)}, f32[1280,128]{1,0:T(8,128)S(1)}) custom-call(f32[64,128]{1,0:T(8,128)S(1)} %pad_maximum_fusion.after, bf16[2048,64]{1,0:T(8,128)(2,1)S(1)} %get-tuple-element.55.refs_0_.first_rows, bf16[48,2048]{1,0:T(8,128)(2,1)S(1)} %get-tuple-element.56.refs_1_.second_cols, ...), custom_call_target="tpu_custom_call" | custom-call | flops 1000000000 | bytes 4000000 | tf_op jit(solution)/shard_map/chunk_3/pallas_call | solution.py:779
  20.2 2.5 %collective-permute-done.3 = f32[64,128]{1,0:T(8,128)S(1)} collective-permute-done((f32[64,128]{1,0:T(8,128)S(1)}, f32[64,128]{1,0:T(8,128)S(1)}, u32[]{:S(2)}, u32[]{:S(2)}) %collective-permute-start.3) | collective-permute-done | bytes 32800 | tf_op jit(solution)/shard_map/ppermute | solution.py:651
  22.7 0.0 collective-permute-done.4.outer
  22.7 0.1 collective-permute-start.5
  22.8 0.0 copy-done.4
  22.8 0.0 copy-start.2
  22.8 2.7 %edges.1 = (bf16[512,384]{1,0:T(8,128)(2,1)S(1)}, bf16[1536,256]{1,0:T(8,128)(2,1)S(1)}, f32[640,128]{1,0:T(8,128)S(1)}) custom-call(f32[64,128]{1,0:T(8,128)S(1)} %fusion.after, s32[3,32]{1,0:T(4,128)S(1)} %bitcast.10, bf16[384,384]{1,0:T(8,128)(2,1)S(1)} %collective-permute-done.inner, bf16[352,384]{1,0:T(8,128)(2,1)S(1)} %collective-permute-done.4.outer, ...), custom_call_target="tpu_custom_call" | custom-call | flops 1000000000 | bytes 4000000 | tf_op jit(solution)/shard_map/edges/pallas_call | solution.py:794
  25.5 0.6 %collective-permute-done.5 = f32[64,128]{1,0:T(8,128)S(1)} collective-permute-done((f32[64,128]{1,0:T(8,128)S(1)}, f32[64,128]{1,0:T(8,128)S(1)}, u32[]{:S(2)}, u32[]{:S(2)}) %collective-permute-start.5) | collective-permute-done | bytes 32800 | tf_op jit(solution)/shard_map/ppermute | solution.py:651
  26.2 0.0 copy-done.2
  26.2 4.3 %leaves.1 = (bf16[2048,384]{1,0:T(8,128)(2,1)}, bf16[3072,128]{1,0:T(8,128)(2,1)S(1)}, bf16[3072,128]{1,0:T(8,128)(2,1)S(1)}, f32[64,64]{1,0:T(8,128)}, f32[64,64]{1,0:T(8,128)}, /*index=5*/f32[64,64]{1,0:T(8,128)}) custom-call(bf16[512,384]{1,0:T(8,128)(2,1)S(1)} %get-tuple-element.53.refs_0_, bf16[512,384]{1,0:T(8,128)(2,1)S(1)} %get-tuple-element.62.refs_1_, ...), custom_call_target="tpu_custom_call" | custom-call | tf_op jit(solution)/shard_map/leaves/pallas_call | solution.py:833
  30.5 2.9 %far.1 = bf16[64,6144]{1,0:T(8,128)(2,1)} custom-call(s32[3,32]{1,0:T(4,128)S(1)} %bitcast.11, bf16[3072,128]{1,0:T(8,128)(2,1)S(1)} %get-tuple-element.81.high, bf16[3072,128]{1,0:T(8,128)(2,1)S(1)} %get-tuple-element.82.low, bf16[768,256]{1,0:T(8,128)(2,1)S(1)} %get-tuple-element.83.refs_0_, bf16[768,256]{1,0:T(8,128)(2,1)S(1)} %get-tuple-element.84.refs_1_, ...), custom_call_target="tpu_custom_call" | custom-call | tf_op jit(solution)/shard_map/far/pallas_call | solution.py:854
  (6 shorter events, 0.0 us)
Async XLA Ops:
  0.6 4.6 %copy-start = (bf16[2048,384]{1,0:T(8,128)(2,1)S(1)}, bf16[2048,384]{1,0:T(8,128)(2,1)}, u32[]{:S(2)}) copy-start(bf16[2048,384]{1,0:T(8,128)(2,1)} %vectors.7) | copy-start | bytes 4718596
  0.6 4.6 %copy-start.3 = (f32[3,2048]{1,0:T(4,128)S(1)}, f32[3,2048]{1,0:T(4,128)}, u32[]{:S(2)}) copy-start(f32[3,2048]{1,0:T(4,128)} %points) | copy-start | bytes 73732
  0.7 4.6 %copy-start.7 = (s32[32]{0:T(128)S(1)}, s32[32]{0:T(128)}, u32[]{:S(2)}) copy-start(s32[32]{0:T(128)} %param.14) | copy-start | bytes 388
  0.7 4.6 %copy-start.6 = (s32[32,12]{0,1:T(8,128)S(1)}, s32[32,12]{0,1:T(8,128)}, u32[]{:S(2)}) copy-start(s32[32,12]{0,1:T(8,128)} %param.13) | copy-start | bytes 4612
  4.7 1.9 %collective-permute-start = (bf16[384,384]{1,0:T(8,128)(2,1)}, bf16[384,384]{1,0:T(8,128)(2,1)S(1)}, u32[]{:S(2)}, u32[]{:S(2)}) collective-permute-start(bf16[384,384]{1,0:T(8,128)(2,1)} %get-tuple-element.49), channel_id=1, source_target_pairs={{0,1},{1,0},{2,3},{3,2},{4,5},{5,4},{6,7},{7,6},{8,9},{9,8},{10,11... | collective-permute-start | bytes 884744 | tf_op jit(solution)/shard_map/ppermute | solution.py:641
  5.2 1.4 %copy-start.8 = (f32[32,128]{1,0:T(8,128)S(1)}, f32[32,128]{1,0:T(8,128)}, u32[]{:S(2)}) copy-start(f32[32,128]{1,0:T(8,128)} %get-tuple-element.48) | copy-start | bytes 49156
  5.2 4.2 %copy-start.9 = (bf16[352,384]{1,0:T(8,128)(2,1)S(1)}, bf16[352,384]{1,0:T(8,128)(2,1)}, u32[]{:S(2)}) copy-start(bf16[352,384]{1,0:T(8,128)(2,1)} %get-tuple-element.71) | copy-start | bytes 811012
  5.3 8.5 %copy-start.5 = (s32[32,3]{0,1:T(4,128)S(1)}, s32[32,3]{0,1:T(4,128)}, u32[]{:S(2)}) copy-start(s32[32,3]{0,1:T(4,128)} %param.15) | copy-start | bytes 1156
  6.7 8.5 %collective-permute-start.1 = (f32[32,128]{1,0:T(8,128)S(1)}, f32[32,128]{1,0:T(8,128)S(1)}, u32[]{:S(2)}, u32[]{:S(2)}) collective-permute-start(f32[32,128]{1,0:T(8,128)S(1)} %add_add_fusion.after), channel_id=1, source_target_pairs={{0,9},{1,8},{2,11},{3,10},{4,13},{5,12},{6,15},{7,14},{8,1},{9,0},... | collective-permute-start | bytes 49160 | tf_op jit(solution)/shard_map/ppermute | solution.py:651
  9.4 13.3 %collective-permute-start.4 = (bf16[352,384]{1,0:T(8,128)(2,1)S(1)}, bf16[352,384]{1,0:T(8,128)(2,1)S(1)}, u32[]{:S(2)}, u32[]{:S(2)}) collective-permute-start(bf16[352,384]{1,0:T(8,128)(2,1)S(1)} %copy-done.9), channel_id=1, source_target_pairs={{0,31},{1,2},{2,1},{3,4},{4,3},{5,6},{6,5},{7,8},{8,7},{9,10},{10,... | collective-permute-start | bytes 811016 | tf_op jit(solution)/shard_map/ppermute | solution.py:646
  15.2 4.2 %copy-start.1 = (bf16[2048,64]{0,1:T(8,128)(2,1)S(1)}, bf16[2048,64]{0,1:T(8,128)(2,1)}, u32[]{:S(2)}) copy-start(bf16[2048,64]{0,1:T(8,128)(2,1)} %param.9) | copy-start | bytes 786436
  15.2 4.1 %collective-permute-start.2 = (f32[32,128]{1,0:T(8,128)S(1)}, f32[32,128]{1,0:T(8,128)S(1)}, u32[]{:S(2)}, u32[]{:S(2)}) collective-permute-start(f32[32,128]{1,0:T(8,128)S(1)} %add.24.after), channel_id=1, source_target_pairs={{0,17},{1,16},{2,19},{3,18},{4,21},{5,20},{6,23},{7,22},{8,25},{9,... | collective-permute-start | bytes 49160 | tf_op jit(solution)/shard_map/ppermute | solution.py:651
  19.3 3.5 %copy-start.4 = (f32[32,128]{1,0:T(8,128)S(1)}, f32[32,128]{1,0:T(8,128)}, u32[]{:S(2)}) copy-start(f32[32,128]{1,0:T(8,128)} %get-tuple-element.74.top) | copy-start | bytes 49156
  19.3 3.4 %collective-permute-start.3 = (f32[64,128]{1,0:T(8,128)S(1)}, f32[64,128]{1,0:T(8,128)S(1)}, u32[]{:S(2)}, u32[]{:S(2)}) collective-permute-start(f32[64,128]{1,0:T(8,128)S(1)} %pad_maximum_fusion.after), channel_id=1, source_target_pairs={{0,3},{1,2},{2,1},{3,0},{4,7},{5,6},{6,5},{7,4},{8,11},{9,10},{10,... | collective-permute-start | bytes 98312 | tf_op jit(solution)/shard_map/ppermute | solution.py:651
  22.7 3.4 %collective-permute-start.5 = (f32[64,128]{1,0:T(8,128)S(1)}, f32[64,128]{1,0:T(8,128)S(1)}, u32[]{:S(2)}, u32[]{:S(2)}) collective-permute-start(f32[64,128]{1,0:T(8,128)S(1)} %fusion.after), channel_id=1, source_target_pairs={{0,5},{1,4},{2,7},{3,6},{4,1},{5,0},{6,3},{7,2},{8,13},{9,12},{10,... | collective-permute-start | bytes 98312 | tf_op jit(solution)/shard_map/ppermute | solution.py:651
  22.8 3.3 %copy-start.2 = (f32[64,64]{1,0:T(8,128)S(1)}, f32[64,64]{1,0:T(8,128)}, u32[]{:S(2)}) copy-start(f32[64,64]{1,0:T(8,128)} %refs_8_.1) | copy-start | bytes 49156

commit v13 on v12

--- a/solution.py
+++ b/solution.py
@@ -139,9 +139,6 @@
         )
         blocks.append(mm_nt(stacked, stacked) * half_block)
     below_copy.wait()
-    for load, copy in zip(vector_loads, copies[:2]):
-        load.wait()
-        copy.start()
     halves = []
     for n, block in enumerate(blocks):
         t = below[:, n * both : (n + 1) * both]
@@ -153,6 +150,10 @@
         x = jnp.concatenate(split3(jnp.concatenate([first, second], axis=0)), axis=1)
         t = jnp.concatenate([t, u], axis=0)
         blocks.append(mm_nt(x, jnp.concatenate([t, t, t], axis=1)) * half_block)
+
+    for load, copy in zip(vector_loads, copies[:2]):
+        load.wait()
+        copy.start()
 
     transfer_copy.wait()
     end = below.shape[1]
@@ -473,8 +474,13 @@
     far_blocks(pairs, far_list, second_rows, first_cols, blocks, width, PAD, range(len(pairs)))
 
 
-def own_chunk_kernel(layers):
-    def body(after, first_rows, second_cols, switches, vectors, basis, out, grams):
+def own_chunk_kernel(layers, pairs):
+    def body(
+        after, far_in, first_rows, second_cols, switches, vectors, first_cols, second_rows, basis,
+        out, blocks, grams, far_list, sem,
+    ):
+        copy = pltpu.make_async_copy(far_in, far_list, sem)
+        copy.start()
         width = basis.shape[0]
         own = basis.shape[1] // width
         both = 2 * width
@@ -490,6 +496,9 @@
             for m in range(2):
                 at = (2 * n + m) * STRIDE
                 grams[at : at + width // 2, :] = fold(value[m * width : (m + 1) * width])
+
+        copy.wait()
+        far_blocks(pairs, far_list, second_rows, first_cols, blocks, width, 0, range(len(pairs)))
 
     return body
 
@@ -706,8 +715,8 @@
     inner_pairs = list(range(PAD // 2, (own - PAD) // 2))
     few = len(inner_pairs) // 2
     edge_pairs = [index for index in range(own // 2) if index not in inner_pairs]
-    chunks = [[1, 2], [3, 4], [5], [6]]
-    pair_chunks = [[], inner_pairs[:few], inner_pairs[few:], edge_pairs]
+    chunks = [[1, 2], [3], [4, 5], [6]]
+    pair_chunks = [[], [], inner_pairs[:few], inner_pairs[few:]]
     blocks, plan, parts = [], {}, []
 
     def part_shape(count):
@@ -776,20 +785,37 @@
                 plan.update((index, (len(blocks), m)) for m, index in enumerate(pair_chunk))
                 blocks.append(outs[-1])
         elif job == 3:
-            part, own_grams = pl.pallas_call(
-                own_chunk_kernel(chunks[3]),
+            part, own_blocks, own_grams = pl.pallas_call(
+                own_chunk_kernel(chunks[3], pair_chunks[3]),
                 out_shape=(
                     part_shape(len(chunks[3])),
+                    block_shape(len(pair_chunks[3])),
                     jax.ShapeDtypeStruct((own * STRIDE, 2 * width), F32),
                 ),
-                in_specs=[hbm] + [vmem] * 5,
-                out_specs=(vmem,) * 2,
+                in_specs=[hbm] * 2 + [vmem] * 7,
+                out_specs=(vmem,) * 3,
+                scratch_shapes=[
+                    pltpu.SMEM(far_list.shape, jnp.int32),
+                    pltpu.SemaphoreType.DMA,
+                ],
                 compiler_params=room(10),
                 cost_estimate=cost,
                 name="chunk_3",
-            )(before, first_rows, second_cols, switches, vectors, basis)
+            )(
+                before,
+                far_list,
+                first_rows,
+                second_cols,
+                switches,
+                vectors,
+                first_cols,
+                second_rows,
+                basis,
+            )
             gram, part = lax.optimization_barrier((gram, part))
             parts.append(part)
+            plan.update((index, (len(blocks), m)) for m, index in enumerate(pair_chunks[3]))
+            blocks.append(own_blocks)
         elif job == "edges":
             edge_part, edge_blocks, halo_grams = pl.pallas_call(
                 functools.partial(edges_kernel, edge_pairs),

time: 33.7 us -> 33.3 us (0.988)
  waiting for transfers between devices: 6.35 us -> 5.45 us
  Pallas kernels: 18.3 us -> 18.8 us
    ppermute x4, waiting for transfers between devices: 6.28 us -> 5.38 us  [exchange(): return value + lax.ppermute(value, AXES, pairs)]
    pallas_call x1, Pallas kernels: 0.79 us -> 1.6 us  [per_device(): pl.pallas_call(own_chunk_kernel(chunks[3], pair_chunks[3]), out_shape=(pa...]
  transfers between devices with their start and end apart: 6 -> 6, of which waited for: 4 -> 4; matrix products, arithmetic and copies ran while one was open for 0% -> 0% of each run, Pallas kernels for 21% -> 23%
where the time goes in v13:
time: 33.3 us; the launch traced here: 33.2 us
  Pallas kernels  18.8 us (56%)
  starting transfers between devices  7.89 us (24%)
  waiting for transfers between devices  5.45 us (16%)
  between operations  0.98 us (3%)
    ppermute x4, waiting for transfers between devices, exchange(): return value + lax.ppermute(value, AXES, pairs)  5.38 us
    ppermute x1, starting transfers between devices, swap_outer(): lax.ppermute(block, AXES, [(i, (i + 1 if i % 2 else i - 1) % many) for i...  4.33 us
    pallas_call x1, Pallas kernels, per_device(): pl.pallas_call(functools.partial(leaves_kernel, chunks, members, groups),...  4.3 us
    pallas_call x1, Pallas kernels, per_device(): pl.pallas_call(tree_kernel, out_shape=(jax.ShapeDtypeStruct((half, 2 * wi...  4.01 us
    ppermute x4, starting transfers between devices, exchange(): return value + lax.ppermute(value, AXES, pairs)  3.05 us
    pallas_call x1, Pallas kernels, per_device(): pl.pallas_call(functools.partial(far_kernel, plan), out_shape=jax.ShapeDt...  2.92 us
    pallas_call x1, Pallas kernels, per_device(): pl.pallas_call(functools.partial(edges_kernel, edge_pairs), out_shape=(pa...  2.65 us
    pallas_call x2, Pallas kernels, per_device(): pl.pallas_call(chunk_kernel(layer_chunk, pair_chunk, halo, width), out_sh...  1.98 us
  transfers between devices with their start and end apart: 6, of which 4 were waited for; matrix products, arithmetic and copies ran while one was open for 0% of the time, Pallas kernels for 23%

profile of v13, /device:TPU:0, one launch (start us, length us, event | category | flops | bytes accessed | tf_op | source)
XLA Modules:
  0.0 33.2 jit_solution(4537599246296433108)
XLA Ops:
  0.6 0.0 copy-start
  0.6 0.0 copy-start.3
  0.7 0.0 copy-start.7
  0.7 0.0 copy-start.6
  0.7 4.0 %tree.1 = (f32[32,128]{1,0:T(8,128)}, f32[32,128]{1,0:T(8,128)}, bf16[352,384]{1,0:T(8,128)(2,1)}, bf16[384,384]{1,0:T(8,128)(2,1)}) custom-call(f32[3,2048]{1,0:T(4,128)} %points, bf16[64,2048]{1,0:T(8,128)(2,1)} %bitcast.6, bf16[64,1920]{1,0:T(8,128)(2,1)} %bitcast.16, f32[64,64]{1,0:T(8,128)} %refs_8_.1, bf16[2048,384]{1,0:T(8,128)(2,1)} %vectors.7), custom_call_target="tpu_custom_call" | custom-call | tf_op jit(solution)/shard_map/tree/pallas_call | solution.py:686
  4.7 0.5 %collective-permute-start = (bf16[384,384]{1,0:T(8,128)(2,1)}, bf16[384,384]{1,0:T(8,128)(2,1)S(1)}, u32[]{:S(2)}, u32[]{:S(2)}) collective-permute-start(bf16[384,384]{1,0:T(8,128)(2,1)} %get-tuple-element.47), channel_id=1, source_target_pairs={{0,1},{1,0},{2,3},{3,2},{4,5},{5,4},{6,7},{7,6},{8,9},{9,8},{10,11... | collective-permute-start | bytes 884744 | tf_op jit(solution)/shard_map/ppermute | solution.py:650
  5.2 0.0 copy-done
  5.2 0.0 copy-done.3
  5.2 0.0 copy-done.7
  5.2 0.0 copy-done.6
  5.2 0.0 copy-start.8
  5.2 0.0 copy-start.9
  5.2 0.0 copy-start.5
  5.3 1.3 %chunk_0.1 = (bf16[512,384]{1,0:T(8,128)(2,1)S(1)}, bf16[2048,64]{1,0:T(8,128)(2,1)S(1)}, bf16[64,2048]{1,0:T(8,128)(2,1)S(1)}, bf16[48,2048]{1,0:T(8,128)(2,1)S...) custom-call(f32[3,2048]{1,0:T(4,128)S(1)} %copy-done.3, s32[12,32]{1,0:T(8,128)S(1)} %bitcast.13, ...), custom_call_target="tpu_custom_call" | custom-call | flops 1000000000 | bytes 4000000 | tf_op jit(solution)/shard_map/chunk_0/pallas_call | solution.py:729
  6.6 0.1 collective-permute-done.inner
  6.6 0.0 copy-done.8
  6.6 2.8 %collective-permute-start.1 = (f32[32,128]{1,0:T(8,128)S(1)}, f32[32,128]{1,0:T(8,128)S(1)}, u32[]{:S(2)}, u32[]{:S(2)}) collective-permute-start(f32[32,128]{1,0:T(8,128)S(1)} %add_add_fusion.after), channel_id=1, source_target_pairs={{0,9},{1,8},{2,11},{3,10},{4,13},{5,12},{6,15},{7,14},{8,1},{9,0},... | collective-permute-start | bytes 49160 | tf_op jit(solution)/shard_map/ppermute | solution.py:660
  9.4 0.0 copy-done.9
  9.4 4.3 %collective-permute-start.4 = (bf16[352,384]{1,0:T(8,128)(2,1)S(1)}, bf16[352,384]{1,0:T(8,128)(2,1)S(1)}, u32[]{:S(2)}, u32[]{:S(2)}) collective-permute-start(bf16[352,384]{1,0:T(8,128)(2,1)S(1)} %copy-done.9), channel_id=1, source_target_pairs={{0,31},{1,2},{2,1},{3,4},{4,3},{5,6},{6,5},{7,8},{8,7},{9,10},{10,... | collective-permute-start | bytes 811016 | tf_op jit(solution)/shard_map/ppermute | solution.py:655
  13.7 0.0 copy-done.5
  13.7 0.6 %chunk_1.1.refs_1_ = bf16[256,384]{1,0:T(8,128)(2,1)S(1)} custom-call(f32[32,128]{1,0:T(8,128)S(1)} %add_add_fusion.after, s32[3,32]{1,0:T(4,128)S(1)} %bitcast.8, bf16[2048,64]{1,0:T(8,128)(2,1)S(1)} %get-tuple-element.53.refs_0_.first_rows, bf16[48,2048]{1,0:T(8,128)(2,1)S(1)} %get-tuple-element.54.refs_1_.second_cols, ...), custom_call_target="tpu_custom_call" | custom-call | flops 1000000000 | bytes 4000000 | tf_op jit(solution)/shard_map/chunk_1/pallas_call | solution.py:768
  14.3 0.0 collective-permute-done.1
  14.4 0.0 copy-start.1
  14.4 0.1 collective-permute-start.2
  14.5 1.4 %chunk_2.1 = (bf16[512,384]{1,0:T(8,128)(2,1)S(1)}, bf16[768,256]{1,0:T(8,128)(2,1)S(1)}) custom-call(f32[32,128]{1,0:T(8,128)S(1)} %add.24.after, s32[3,32]{1,0:T(4,128)S(1)} %bitcast.9, bf16[2048,64]{1,0:T(8,128)(2,1)S(1)} %get-tuple-element.53.refs_0_.first_rows, bf16[48,2048]{1,0:T(8,128)(2,1)S(1)} %get-tuple-element.54.refs_1_.second_cols, ...), custom_call_target="tpu_custom_call" | custom-call | flops 1000000000 | bytes 4000000 | tf_op jit(solution)/shard_map/chunk_2/pallas_call | solution.py:768
  15.9 2.7 %collective-permute-done.2 = f32[32,128]{1,0:T(8,128)S(1)} collective-permute-done((f32[32,128]{1,0:T(8,128)S(1)}, f32[32,128]{1,0:T(8,128)S(1)}, u32[]{:S(2)}, u32[]{:S(2)}) %collective-permute-start.2) | collective-permute-done | bytes 16416 | tf_op jit(solution)/shard_map/ppermute | solution.py:660
  18.5 0.0 copy-start.4
  18.5 0.1 collective-permute-start.3
  18.6 0.0 copy-done.1
  18.6 1.6 %chunk_3.1 = (bf16[256,384]{1,0:T(8,128)(2,1)S(1)}, bf16[768,256]{1,0:T(8,128)(2,1)S(1)}, f32[1280,128]{1,0:T(8,128)S(1)}) custom-call(f32[64,128]{1,0:T(8,128)S(1)} %pad_maximum_fusion.after, s32[3,32]{1,0:T(4,128)S(1)} %bitcast.10, bf16[2048,64]{1,0:T(8,128)(2,1)S(1)} %get-tuple-element.53.refs_0_.first_rows, ...), custom_call_target="tpu_custom_call" | custom-call | flops 1000000000 | bytes 4000000 | tf_op jit(solution)/shard_map/chunk_3/pallas_call | solution.py:788
  20.2 1.8 %collective-permute-done.3 = f32[64,128]{1,0:T(8,128)S(1)} collective-permute-done((f32[64,128]{1,0:T(8,128)S(1)}, f32[64,128]{1,0:T(8,128)S(1)}, u32[]{:S(2)}, u32[]{:S(2)}) %collective-permute-start.3) | collective-permute-done | bytes 32800 | tf_op jit(solution)/shard_map/ppermute | solution.py:660
  22.1 0.0 collective-permute-done.4.outer
  22.1 0.1 collective-permute-start.5
  22.2 0.0 copy-done.4
  22.2 0.0 copy-start.2
  22.2 2.6 %edges.1 = (bf16[512,384]{1,0:T(8,128)(2,1)S(1)}, bf16[1536,256]{1,0:T(8,128)(2,1)S(1)}, f32[640,128]{1,0:T(8,128)S(1)}) custom-call(f32[64,128]{1,0:T(8,128)S(1)} %fusion.after, s32[3,32]{1,0:T(4,128)S(1)} %bitcast.11, bf16[384,384]{1,0:T(8,128)(2,1)S(1)} %collective-permute-done.inner, bf16[352,384]{1,0:T(8,128)(2,1)S(1)} %collective-permute-done.4.outer, ...), custom_call_target="tpu_custom_call" | custom-call | flops 1000000000 | bytes 4000000 | tf_op jit(solution)/shard_map/edges/pallas_call | solution.py:820
  24.9 0.9 %collective-permute-done.5 = f32[64,128]{1,0:T(8,128)S(1)} collective-permute-done((f32[64,128]{1,0:T(8,128)S(1)}, f32[64,128]{1,0:T(8,128)S(1)}, u32[]{:S(2)}, u32[]{:S(2)}) %collective-permute-start.5) | collective-permute-done | bytes 32800 | tf_op jit(solution)/shard_map/ppermute | solution.py:660
  25.8 0.0 copy-done.2
  25.8 4.3 %leaves.1 = (bf16[2048,384]{1,0:T(8,128)(2,1)}, bf16[3072,128]{1,0:T(8,128)(2,1)S(1)}, bf16[3072,128]{1,0:T(8,128)(2,1)S(1)}, f32[64,64]{1,0:T(8,128)}, f32[64,64]{1,0:T(8,128)}, /*index=5*/f32[64,64]{1,0:T(8,128)}) custom-call(bf16[512,384]{1,0:T(8,128)(2,1)S(1)} %get-tuple-element.51.refs_0_, bf16[256,384]{1,0:T(8,128)(2,1)S(1)} %chunk_1.1.refs_1_, ...), custom_call_target="tpu_custom_call" | custom-call | tf_op jit(solution)/shard_map/leaves/pallas_call | solution.py:859
  30.1 2.9 %far.1 = bf16[64,6144]{1,0:T(8,128)(2,1)} custom-call(s32[3,32]{1,0:T(4,128)S(1)} %bitcast.12, bf16[3072,128]{1,0:T(8,128)(2,1)S(1)} %get-tuple-element.77.high, bf16[3072,128]{1,0:T(8,128)(2,1)S(1)} %get-tuple-element.78.low, bf16[768,256]{1,0:T(8,128)(2,1)S(1)} %get-tuple-element.79.refs_0_, bf16[768,256]{1,0:T(8,128)(2,1)S(1)} %get-tuple-element.80.refs_1_, ...), custom_call_target="tpu_custom_call" | custom-call | tf_op jit(solution)/shard_map/far/pallas_call | solution.py:880
  (6 shorter events, 0.0 us)
Async XLA Ops:
  0.6 4.6 %copy-start = (bf16[2048,384]{1,0:T(8,128)(2,1)S(1)}, bf16[2048,384]{1,0:T(8,128)(2,1)}, u32[]{:S(2)}) copy-start(bf16[2048,384]{1,0:T(8,128)(2,1)} %vectors.7) | copy-start | bytes 4718596
  0.6 4.6 %copy-start.3 = (f32[3,2048]{1,0:T(4,128)S(1)}, f32[3,2048]{1,0:T(4,128)}, u32[]{:S(2)}) copy-start(f32[3,2048]{1,0:T(4,128)} %points) | copy-start | bytes 73732
  0.7 4.6 %copy-start.7 = (s32[32]{0:T(128)S(1)}, s32[32]{0:T(128)}, u32[]{:S(2)}) copy-start(s32[32]{0:T(128)} %param.14) | copy-start | bytes 388
  0.7 4.6 %copy-start.6 = (s32[32,12]{0,1:T(8,128)S(1)}, s32[32,12]{0,1:T(8,128)}, u32[]{:S(2)}) copy-start(s32[32,12]{0,1:T(8,128)} %param.13) | copy-start | bytes 4612
  4.7 1.9 %collective-permute-start = (bf16[384,384]{1,0:T(8,128)(2,1)}, bf16[384,384]{1,0:T(8,128)(2,1)S(1)}, u32[]{:S(2)}, u32[]{:S(2)}) collective-permute-start(bf16[384,384]{1,0:T(8,128)(2,1)} %get-tuple-element.47), channel_id=1, source_target_pairs={{0,1},{1,0},{2,3},{3,2},{4,5},{5,4},{6,7},{7,6},{8,9},{9,8},{10,11... | collective-permute-start | bytes 884744 | tf_op jit(solution)/shard_map/ppermute | solution.py:650
  5.2 1.4 %copy-start.8 = (f32[32,128]{1,0:T(8,128)S(1)}, f32[32,128]{1,0:T(8,128)}, u32[]{:S(2)}) copy-start(f32[32,128]{1,0:T(8,128)} %get-tuple-element.46) | copy-start | bytes 49156
  5.2 4.2 %copy-start.9 = (bf16[352,384]{1,0:T(8,128)(2,1)S(1)}, bf16[352,384]{1,0:T(8,128)(2,1)}, u32[]{:S(2)}) copy-start(bf16[352,384]{1,0:T(8,128)(2,1)} %get-tuple-element.67) | copy-start | bytes 811012
  5.2 8.5 %copy-start.5 = (s32[32,3]{0,1:T(4,128)S(1)}, s32[32,3]{0,1:T(4,128)}, u32[]{:S(2)}) copy-start(s32[32,3]{0,1:T(4,128)} %param.15) | copy-start | bytes 1156
  6.6 7.7 %collective-permute-start.1 = (f32[32,128]{1,0:T(8,128)S(1)}, f32[32,128]{1,0:T(8,128)S(1)}, u32[]{:S(2)}, u32[]{:S(2)}) collective-permute-start(f32[32,128]{1,0:T(8,128)S(1)} %add_add_fusion.after), channel_id=1, source_target_pairs={{0,9},{1,8},{2,11},{3,10},{4,13},{5,12},{6,15},{7,14},{8,1},{9,0},... | collective-permute-start | bytes 49160 | tf_op jit(solution)/shard_map/ppermute | solution.py:660
  9.4 12.7 %collective-permute-start.4 = (bf16[352,384]{1,0:T(8,128)(2,1)S(1)}, bf16[352,384]{1,0:T(8,128)(2,1)S(1)}, u32[]{:S(2)}, u32[]{:S(2)}) collective-permute-start(bf16[352,384]{1,0:T(8,128)(2,1)S(1)} %copy-done.9), channel_id=1, source_target_pairs={{0,31},{1,2},{2,1},{3,4},{4,3},{5,6},{6,5},{7,8},{8,7},{9,10},{10,... | collective-permute-start | bytes 811016 | tf_op jit(solution)/shard_map/ppermute | solution.py:655
  14.4 4.2 %copy-start.1 = (bf16[2048,64]{0,1:T(8,128)(2,1)S(1)}, bf16[2048,64]{0,1:T(8,128)(2,1)}, u32[]{:S(2)}) copy-start(bf16[2048,64]{0,1:T(8,128)(2,1)} %param.9) | copy-start | bytes 786436
  14.4 4.1 %collective-permute-start.2 = (f32[32,128]{1,0:T(8,128)S(1)}, f32[32,128]{1,0:T(8,128)S(1)}, u32[]{:S(2)}, u32[]{:S(2)}) collective-permute-start(f32[32,128]{1,0:T(8,128)S(1)} %add.24.after), channel_id=1, source_target_pairs={{0,17},{1,16},{2,19},{3,18},{4,21},{5,20},{6,23},{7,22},{8,25},{9,... | collective-permute-start | bytes 49160 | tf_op jit(solution)/shard_map/ppermute | solution.py:660
  18.5 3.7 %copy-start.4 = (f32[32,128]{1,0:T(8,128)S(1)}, f32[32,128]{1,0:T(8,128)}, u32[]{:S(2)}) copy-start(f32[32,128]{1,0:T(8,128)} %get-tuple-element.70.top) | copy-start | bytes 49156
  18.5 3.5 %collective-permute-start.3 = (f32[64,128]{1,0:T(8,128)S(1)}, f32[64,128]{1,0:T(8,128)S(1)}, u32[]{:S(2)}, u32[]{:S(2)}) collective-permute-start(f32[64,128]{1,0:T(8,128)S(1)} %pad_maximum_fusion.after), channel_id=1, source_target_pairs={{0,3},{1,2},{2,1},{3,0},{4,7},{5,6},{6,5},{7,4},{8,11},{9,10},{10,... | collective-permute-start | bytes 98312 | tf_op jit(solution)/shard_map/ppermute | solution.py:660
  22.1 3.7 %collective-permute-start.5 = (f32[64,128]{1,0:T(8,128)S(1)}, f32[64,128]{1,0:T(8,128)S(1)}, u32[]{:S(2)}, u32[]{:S(2)}) collective-permute-start(f32[64,128]{1,0:T(8,128)S(1)} %fusion.after), channel_id=1, source_target_pairs={{0,5},{1,4},{2,7},{3,6},{4,1},{5,0},{6,3},{7,2},{8,13},{9,12},{10,... | collective-permute-start | bytes 98312 | tf_op jit(solution)/shard_map/ppermute | solution.py:660
  22.2 3.5 %copy-start.2 = (f32[64,64]{1,0:T(8,128)S(1)}, f32[64,64]{1,0:T(8,128)}, u32[]{:S(2)}) copy-start(f32[64,64]{1,0:T(8,128)} %refs_8_.1) | copy-start | bytes 49156

commit v14 on v13

--- a/solution.py
+++ b/solution.py
@@ -55,7 +55,7 @@
 
 def tree_kernel(
     points_in, basis_in, below_in, transfer_in, vectors,
-    dense, top, outer, inner, points, basis, below, transfer, passing, packed, staged, small, sems,
+    dense, top, outer, inner, points, basis, below, transfer, passing, packed, small, sems,
 ):
     width = basis.shape[0]
     count = basis.shape[1] // width
@@ -188,13 +188,6 @@
     small[0, :, :] = fold(total[:width, :width])
     halves = fold(total[width:, width:])
     small[1, :, :] = halves
-    staged[...] = jnp.concatenate(split3(halves), axis=1)
-    copies.append(
-        pltpu.make_async_copy(
-            staged, inner.at[pl.ds(halo + width + 32, width // 2), :], sems.at[8]
-        )
-    )
-    copies[-1].start()
     for n, target in enumerate((top, dense)):
         copies.append(pltpu.make_async_copy(small.at[n], target, sems.at[11 + n]))
         copies[-1].start()
@@ -689,7 +682,7 @@
             jax.ShapeDtypeStruct((half, 2 * width), F32),
             jax.ShapeDtypeStruct((half, 2 * width), F32),
             block_of(extra),
-            block_of(extra + half),
+            block_of(extra),
         ),
         in_specs=[hbm] * 5,
         out_specs=(hbm,) * 4,
@@ -700,14 +693,13 @@
             pltpu.VMEM((width, width), F32),
             pltpu.VMEM((2, halo, columns), BF16),
             pltpu.VMEM((2, width + 32, columns), BF16),
-            pltpu.VMEM((half, columns), BF16),
             pltpu.VMEM((2, half, 2 * width), F32),
             pltpu.SemaphoreType.DMA((13,)),
         ],
         compiler_params=room(60),
         name="tree",
     )(points, basis, inner_transfer.T, device_transfer, vectors)
-    from_inner = swap_inner(to_inner)
+    pair_gram = gram = exchange(dense, 0)
 
     sub_bits = members.bit_length() - 1
     steps = [members << bit for bit in range(groups.bit_length() - 1)]
@@ -715,8 +707,8 @@
     inner_pairs = list(range(PAD // 2, (own - PAD) // 2))
     few = len(inner_pairs) // 2
     edge_pairs = [index for index in range(own // 2) if index not in inner_pairs]
-    chunks = [[1, 2], [3], [4, 5], [6]]
-    pair_chunks = [[], [], inner_pairs[:few], inner_pairs[few:]]
+    chunks = [[1, 2], [3, 4, 5], [6]]
+    pair_chunks = [[], inner_pairs[:few], inner_pairs[few:]]
     blocks, plan, parts = [], {}, []
 
     def part_shape(count):
@@ -725,7 +717,7 @@
     def block_shape(count):
         return jax.ShapeDtypeStruct((count * far_index.shape[1] * width, 4 * width), BF16)
 
-    late_points, dense = lax.optimization_barrier((points, dense))
+    late_points, gram = lax.optimization_barrier((points, gram))
     part, *shared = pl.pallas_call(
         first_chunk_kernel(chunks[0]),
         out_shape=(
@@ -744,14 +736,11 @@
         name="chunk_0",
     )(late_points, near_list, near_count.reshape(1, own), vectors)
     parts.append(part)
-    summands = [
-        from_inner[extra:, n * 2 * width : (n + 1) * 2 * width].astype(F32) for n in range(3)
-    ]
-    pair_gram = gram = dense + (summands[0] + (summands[1] + summands[2]))
-    gram, parts[0], to_outer = lax.optimization_barrier((gram, parts[0], to_outer))
+    gram, to_inner, to_outer = lax.optimization_barrier((gram, to_inner, to_outer))
+    from_inner = swap_inner(to_inner)
     from_outer = swap_outer(to_outer)
     first_rows, first_cols, second_cols, second_rows, switches = shared
-    jobs = [1, 2, 3, "edges"]
+    jobs = ["first", 1, 2, "edges"]
     for n in range(max(len(steps), len(jobs))):
         if n < len(jobs) and jobs[n] == "edges":
             gram, from_outer = lax.optimization_barrier((gram, from_outer))
@@ -761,7 +750,9 @@
                 gram = before = jnp.concatenate([pair_gram, gram], axis=0)
             gram = exchange(gram, steps[n])
         job = jobs[n] if n < len(jobs) else None
-        if job in (1, 2):
+        if job == "first":
+            gram, parts[0] = lax.optimization_barrier((gram, parts[0]))
+        elif job == 1:
             layer_chunk, pair_chunk = chunks[job], pair_chunks[job]
             shapes = [part_shape(len(layer_chunk))] * bool(layer_chunk)
             shapes += [block_shape(len(pair_chunk))] * bool(pair_chunk)
@@ -784,12 +775,12 @@
             if pair_chunk:
                 plan.update((index, (len(blocks), m)) for m, index in enumerate(pair_chunk))
                 blocks.append(outs[-1])
-        elif job == 3:
+        elif job == 2:
             part, own_blocks, own_grams = pl.pallas_call(
-                own_chunk_kernel(chunks[3], pair_chunks[3]),
+                own_chunk_kernel(chunks[2], pair_chunks[2]),
                 out_shape=(
-                    part_shape(len(chunks[3])),
-                    block_shape(len(pair_chunks[3])),
+                    part_shape(len(chunks[2])),
+                    block_shape(len(pair_chunks[2])),
                     jax.ShapeDtypeStruct((own * STRIDE, 2 * width), F32),
                 ),
                 in_specs=[hbm] * 2 + [vmem] * 7,
@@ -800,7 +791,7 @@
                 ],
                 compiler_params=room(10),
                 cost_estimate=cost,
-                name="chunk_3",
+                name="chunk_2",
             )(
                 before,
                 far_list,
@@ -814,7 +805,7 @@
             )
             gram, part = lax.optimization_barrier((gram, part))
             parts.append(part)
-            plan.update((index, (len(blocks), m)) for m, index in enumerate(pair_chunks[3]))
+            plan.update((index, (len(blocks), m)) for m, index in enumerate(pair_chunks[2]))
             blocks.append(own_blocks)
         elif job == "edges":
             edge_part, edge_blocks, halo_grams = pl.pallas_call(

time: 33.3 us -> 35 us (1.051)
  Pallas kernels: 18.8 us -> 19.6 us
  other arithmetic: 0.03 us -> 0.75 us
    pallas_call x1, Pallas kernels: 4.3 us -> 5.33 us  [per_device(): pl.pallas_call(functools.partial(leaves_kernel, chunks, members, groups),...]
    add x4 -> x5, other arithmetic: 0.02 us -> 0.74 us  [exchange(): return value + lax.ppermute(value, AXES, pairs)]
    ppermute x1, starting transfers between devices: 0.52 us -> 0.01 us  [swap_inner(): lax.ppermute(block, AXES, [(i, i ^ 1) for i in range(lax.axis_size(AXES))])]
    ppermute x4 -> x5, starting transfers between devices: 3.05 us -> 3.42 us  [exchange(): return value + lax.ppermute(value, AXES, pairs)]
    ppermute x4 -> x5, waiting for transfers between devices: 5.38 us -> 5.59 us  [exchange(): return value + lax.ppermute(value, AXES, pairs)]
    pallas_call x2 -> x1, Pallas kernels: 1.98 us -> 1.79 us  [per_device(): pl.pallas_call(chunk_kernel(layer_chunk, pair_chunk, halo, width), out_sh...]
  transfers between devices with their start and end apart: 6 -> 7, of which waited for: 4 -> 4; matrix products, arithmetic and copies ran while one was open for 0% -> 0% of each run, Pallas kernels for 23% -> 21%
where the time goes in v14:
time: 35 us; the launch traced here: 34.8 us
  Pallas kernels  19.6 us (56%)
  starting transfers between devices  7.73 us (22%)
  waiting for transfers between devices  5.6 us (16%)
  between operations  1.01 us (3%)
  other arithmetic  0.75 us (2%)
    ppermute x5, waiting for transfers between devices, exchange(): return value + lax.ppermute(value, AXES, pairs)  5.59 us
    pallas_call x1, Pallas kernels, per_device(): pl.pallas_call(functools.partial(leaves_kernel, chunks, members, groups),...  5.33 us
    ppermute x1, starting transfers between devices, swap_outer(): lax.ppermute(block, AXES, [(i, (i + 1 if i % 2 else i - 1) % many) for i...  4.3 us
    pallas_call x1, Pallas kernels, per_device(): pl.pallas_call(tree_kernel, out_shape=(jax.ShapeDtypeStruct((half, 2 * wi...  4 us
    ppermute x5, starting transfers between devices, exchange(): return value + lax.ppermute(value, AXES, pairs)  3.42 us
    pallas_call x1, Pallas kernels, per_device(): pl.pallas_call(functools.partial(far_kernel, plan), out_shape=jax.ShapeDt...  2.93 us
    pallas_call x1, Pallas kernels, per_device(): pl.pallas_call(functools.partial(edges_kernel, edge_pairs), out_shape=(pa...  2.68 us
    pallas_call x1, Pallas kernels, per_device(): pl.pallas_call(chunk_kernel(layer_chunk, pair_chunk, halo, width), out_sh...  1.79 us
  transfers between devices with their start and end apart: 7, of which 4 were waited for; matrix products, arithmetic and copies ran while one was open for 0% of the time, Pallas kernels for 21%

profile of v14, /device:TPU:0, one launch (start us, length us, event | category | flops | bytes accessed | tf_op | source)
XLA Modules:
  0.0 34.8 jit_solution(12985757832858743923)
XLA Ops:
  0.6 0.0 copy-start
  0.6 0.0 copy-start.3
  0.7 0.0 copy-start.7
  0.7 0.0 copy-start.6
  0.7 4.0 %tree.1 = (f32[32,128]{1,0:T(8,128)}, f32[32,128]{1,0:T(8,128)}, bf16[352,384]{1,0:T(8,128)(2,1)}, bf16[352,384]{1,0:T(8,128)(2,1)}) custom-call(f32[3,2048]{1,0:T(4,128)} %points, bf16[64,2048]{1,0:T(8,128)(2,1)} %bitcast.6, bf16[64,1920]{1,0:T(8,128)(2,1)} %bitcast.15, f32[64,64]{1,0:T(8,128)} %refs_7_.1, bf16[2048,384]{1,0:T(8,128)(2,1)} %vectors.7), custom_call_target="tpu_custom_call" | custom-call | tf_op jit(solution)/shard_map/tree/pallas_call | solution.py:679
  4.7 0.5 %collective-permute-start = (f32[32,128]{1,0:T(8,128)}, f32[32,128]{1,0:T(8,128)S(1)}, u32[]{:S(2)}, u32[]{:S(2)}) collective-permute-start(f32[32,128]{1,0:T(8,128)} %get-tuple-element.45), channel_id=1, source_target_pairs={{0,1},{1,0},{2,3},{3,2},{4,5},{5,4},{6,7},{7,6},{8,9},{9,8},{10,11... | collective-permute-start | bytes 49160 | tf_op jit(solution)/shard_map/ppermute | solution.py:653
  5.2 1.0 %collective-permute-done = f32[32,128]{1,0:T(8,128)S(1)} collective-permute-done((f32[32,128]{1,0:T(8,128)}, f32[32,128]{1,0:T(8,128)S(1)}, u32[]{:S(2)}, u32[]{:S(2)}) %collective-permute-start) | collective-permute-done | bytes 16416 | tf_op jit(solution)/shard_map/ppermute | solution.py:653
  6.2 0.7 %add.15 = f32[32,128]{1,0:T(8,128)S(1)} add(f32[32,128]{1,0:T(8,128)} %get-tuple-element.45, f32[32,128]{1,0:T(8,128)S(1)} %collective-permute-done) | non-fusion elementwise | flops 4096 | bytes 49152 | tf_op jit(solution)/shard_map/add | solution.py:653
  7.0 2.7 %collective-permute-start.1 = (f32[32,128]{1,0:T(8,128)S(1)}, f32[32,128]{1,0:T(8,128)S(1)}, u32[]{:S(2)}, u32[]{:S(2)}) collective-permute-start(f32[32,128]{1,0:T(8,128)S(1)} %add.15), channel_id=1, source_target_pairs={{0,9},{1,8},{2,11},{3,10},{4,13},{5,12},{6,15},{7,14},{8,1},{9,0},... | collective-permute-start | bytes 49160 | tf_op jit(solution)/shard_map/ppermute | solution.py:653
  9.7 4.3 %collective-permute-start.4 = (bf16[352,384]{1,0:T(8,128)(2,1)}, bf16[352,384]{1,0:T(8,128)(2,1)S(1)}, u32[]{:S(2)}, u32[]{:S(2)}) collective-permute-start(bf16[352,384]{1,0:T(8,128)(2,1)} %get-tuple-element.66), channel_id=1, source_target_pairs={{0,31},{1,2},{2,1},{3,4},{4,3},{5,6},{6,5},{7,8},{8,7},{9,10},{10,... | collective-permute-start | bytes 811016 | tf_op jit(solution)/shard_map/ppermute | solution.py:648
  14.0 0.0 collective-permute-start.6
  14.0 0.0 copy-done
  14.0 0.0 copy-done.3
  14.0 0.0 copy-done.7
  14.0 0.0 copy-done.6
  14.0 0.0 copy-start.5
  14.0 1.3 %chunk_0.1 = (bf16[512,384]{1,0:T(8,128)(2,1)S(1)}, bf16[2048,64]{1,0:T(8,128)(2,1)S(1)}, bf16[64,2048]{1,0:T(8,128)(2,1)S(1)}, bf16[48,2048]{1,0:T(8,128)(2,1)S...) custom-call(f32[3,2048]{1,0:T(4,128)S(1)} %copy-done.3, s32[12,32]{1,0:T(8,128)S(1)} %bitcast.12, ...), custom_call_target="tpu_custom_call" | custom-call | flops 1000000000 | bytes 4000000 | tf_op jit(solution)/shard_map/chunk_0/pallas_call | solution.py:721
  15.3 0.0 collective-permute-done.1
  15.3 0.1 collective-permute-start.2
  15.4 0.0 copy-done.5
  15.4 0.0 copy-start.1
  15.4 1.8 %chunk_1.1 = (bf16[768,384]{1,0:T(8,128)(2,1)S(1)}, bf16[768,256]{1,0:T(8,128)(2,1)S(1)}) custom-call(f32[32,128]{1,0:T(8,128)S(1)} %add.16.after, s32[3,32]{1,0:T(4,128)S(1)} %bitcast.8, bf16[2048,64]{1,0:T(8,128)(2,1)S(1)} %get-tuple-element.54.refs_0_.first_rows, bf16[48,2048]{1,0:T(8,128)(2,1)S(1)} %get-tuple-element.55.refs_1_.second_cols, ...), custom_call_target="tpu_custom_call" | custom-call | flops 1000000000 | bytes 4000000 | tf_op jit(solution)/shard_map/chunk_1/pallas_call | solution.py:759
  17.2 2.2 %collective-permute-done.2 = f32[32,128]{1,0:T(8,128)S(1)} collective-permute-done((f32[32,128]{1,0:T(8,128)S(1)}, f32[32,128]{1,0:T(8,128)S(1)}, u32[]{:S(2)}, u32[]{:S(2)}) %collective-permute-start.2) | collective-permute-done | bytes 16416 | tf_op jit(solution)/shard_map/ppermute | solution.py:653
  19.5 0.0 copy-start.4
  19.5 0.1 collective-permute-start.3
  19.6 0.0 copy-done.1
  19.6 1.6 %chunk_2.1 = (bf16[256,384]{1,0:T(8,128)(2,1)S(1)}, bf16[768,256]{1,0:T(8,128)(2,1)S(1)}, f32[1280,128]{1,0:T(8,128)S(1)}) custom-call(f32[64,128]{1,0:T(8,128)S(1)} %pad_maximum_fusion.after, s32[3,32]{1,0:T(4,128)S(1)} %bitcast.9, bf16[2048,64]{1,0:T(8,128)(2,1)S(1)} %get-tuple-element.54.refs_0_.first_rows, ...), custom_call_target="tpu_custom_call" | custom-call | flops 1000000000 | bytes 4000000 | tf_op jit(solution)/shard_map/chunk_2/pallas_call | solution.py:779
  21.2 1.7 %collective-permute-done.3 = f32[64,128]{1,0:T(8,128)S(1)} collective-permute-done((f32[64,128]{1,0:T(8,128)S(1)}, f32[64,128]{1,0:T(8,128)S(1)}, u32[]{:S(2)}, u32[]{:S(2)}) %collective-permute-start.3) | collective-permute-done | bytes 32800 | tf_op jit(solution)/shard_map/ppermute | solution.py:653
  22.9 0.0 collective-permute-done.4.outer
  22.9 0.1 collective-permute-start.5
  23.0 0.0 collective-permute-done.6.inner
  23.0 0.0 copy-done.4
  23.0 0.0 copy-start.2
  23.0 2.7 %edges.1 = (bf16[512,384]{1,0:T(8,128)(2,1)S(1)}, bf16[1536,256]{1,0:T(8,128)(2,1)S(1)}, f32[640,128]{1,0:T(8,128)S(1)}) custom-call(f32[64,128]{1,0:T(8,128)S(1)} %fusion.after, s32[3,32]{1,0:T(4,128)S(1)} %bitcast.10, bf16[352,384]{1,0:T(8,128)(2,1)S(1)} %collective-permute-done.6.inner, bf16[352,384]{1,0:T(8,128)(2,1)S(1)} %collective-permute-done.4.outer, ...), custom_call_target="tpu_custom_call" | custom-call | flops 1000000000 | bytes 4000000 | tf_op jit(solution)/shard_map/edges/pallas_call | solution.py:811
  25.7 0.6 %collective-permute-done.5 = f32[64,128]{1,0:T(8,128)S(1)} collective-permute-done((f32[64,128]{1,0:T(8,128)S(1)}, f32[64,128]{1,0:T(8,128)S(1)}, u32[]{:S(2)}, u32[]{:S(2)}) %collective-permute-start.5) | collective-permute-done | bytes 32800 | tf_op jit(solution)/shard_map/ppermute | solution.py:653
  26.3 0.0 copy-done.2
  26.3 5.3 %leaves.1 = (bf16[2048,384]{1,0:T(8,128)(2,1)}, bf16[3072,128]{1,0:T(8,128)(2,1)S(1)}, bf16[3072,128]{1,0:T(8,128)(2,1)S(1)}, f32[64,64]{1,0:T(8,128)}, f32[64,64]{1,0:T(8,128)}, /*index=5*/f32[64,64]{1,0:T(8,128)}) custom-call(bf16[512,384]{1,0:T(8,128)(2,1)S(1)} %get-tuple-element.52.refs_0_, bf16[768,384]{1,0:T(8,128)(2,1)S(1)} %get-tuple-element.61.refs_1_, ...), custom_call_target="tpu_custom_call" | custom-call | tf_op jit(solution)/shard_map/leaves/pallas_call | solution.py:850
  31.7 2.9 %far.1 = bf16[64,6144]{1,0:T(8,128)(2,1)} custom-call(s32[3,32]{1,0:T(4,128)S(1)} %bitcast.11, bf16[3072,128]{1,0:T(8,128)(2,1)S(1)} %get-tuple-element.77.high, bf16[3072,128]{1,0:T(8,128)(2,1)S(1)} %get-tuple-element.78.low, bf16[768,256]{1,0:T(8,128)(2,1)S(1)} %get-tuple-element.79.refs_0_, bf16[768,256]{1,0:T(8,128)(2,1)S(1)} %get-tuple-element.80.refs_1_, ...), custom_call_target="tpu_custom_call" | custom-call | tf_op jit(solution)/shard_map/far/pallas_call | solution.py:871
  (5 shorter events, 0.0 us)
Async XLA Ops:
  0.6 13.3 %copy-start = (bf16[2048,384]{1,0:T(8,128)(2,1)S(1)}, bf16[2048,384]{1,0:T(8,128)(2,1)}, u32[]{:S(2)}) copy-start(bf16[2048,384]{1,0:T(8,128)(2,1)} %vectors.7) | copy-start | bytes 4718596
  0.6 13.3 %copy-start.3 = (f32[3,2048]{1,0:T(4,128)S(1)}, f32[3,2048]{1,0:T(4,128)}, u32[]{:S(2)}) copy-start(f32[3,2048]{1,0:T(4,128)} %points) | copy-start | bytes 73732
  0.7 13.3 %copy-start.7 = (s32[32]{0:T(128)S(1)}, s32[32]{0:T(128)}, u32[]{:S(2)}) copy-start(s32[32]{0:T(128)} %param.14) | copy-start | bytes 388
  0.7 13.3 %copy-start.6 = (s32[32,12]{0,1:T(8,128)S(1)}, s32[32,12]{0,1:T(8,128)}, u32[]{:S(2)}) copy-start(s32[32,12]{0,1:T(8,128)} %param.13) | copy-start | bytes 4612
  4.7 1.6 %collective-permute-start = (f32[32,128]{1,0:T(8,128)}, f32[32,128]{1,0:T(8,128)S(1)}, u32[]{:S(2)}, u32[]{:S(2)}) collective-permute-start(f32[32,128]{1,0:T(8,128)} %get-tuple-element.45), channel_id=1, source_target_pairs={{0,1},{1,0},{2,3},{3,2},{4,5},{5,4},{6,7},{7,6},{8,9},{9,8},{10,11... | collective-permute-start | bytes 49160 | tf_op jit(solution)/shard_map/ppermute | solution.py:653
  7.0 8.4 %collective-permute-start.1 = (f32[32,128]{1,0:T(8,128)S(1)}, f32[32,128]{1,0:T(8,128)S(1)}, u32[]{:S(2)}, u32[]{:S(2)}) collective-permute-start(f32[32,128]{1,0:T(8,128)S(1)} %add.15), channel_id=1, source_target_pairs={{0,9},{1,8},{2,11},{3,10},{4,13},{5,12},{6,15},{7,14},{8,1},{9,0},... | collective-permute-start | bytes 49160 | tf_op jit(solution)/shard_map/ppermute | solution.py:653
  9.7 13.2 %collective-permute-start.4 = (bf16[352,384]{1,0:T(8,128)(2,1)}, bf16[352,384]{1,0:T(8,128)(2,1)S(1)}, u32[]{:S(2)}, u32[]{:S(2)}) collective-permute-start(bf16[352,384]{1,0:T(8,128)(2,1)} %get-tuple-element.66), channel_id=1, source_target_pairs={{0,31},{1,2},{2,1},{3,4},{4,3},{5,6},{6,5},{7,8},{8,7},{9,10},{10,... | collective-permute-start | bytes 811016 | tf_op jit(solution)/shard_map/ppermute | solution.py:648
  14.0 9.0 %collective-permute-start.6 = (bf16[352,384]{1,0:T(8,128)(2,1)}, bf16[352,384]{1,0:T(8,128)(2,1)S(1)}, u32[]{:S(2)}, u32[]{:S(2)}) collective-permute-start(bf16[352,384]{1,0:T(8,128)(2,1)} %get-tuple-element.68), channel_id=1, source_target_pairs={{0,1},{1,0},{2,3},{3,2},{4,5},{5,4},{6,7},{7,6},{8,9},{9,8},{10,11... | collective-permute-start | bytes 811016 | tf_op jit(solution)/shard_map/ppermute | solution.py:643
  14.0 1.4 %copy-start.5 = (s32[32,3]{0,1:T(4,128)S(1)}, s32[32,3]{0,1:T(4,128)}, u32[]{:S(2)}) copy-start(s32[32,3]{0,1:T(4,128)} %param.15) | copy-start | bytes 1156
  15.3 4.1 %collective-permute-start.2 = (f32[32,128]{1,0:T(8,128)S(1)}, f32[32,128]{1,0:T(8,128)S(1)}, u32[]{:S(2)}, u32[]{:S(2)}) collective-permute-start(f32[32,128]{1,0:T(8,128)S(1)} %add.16.after), channel_id=1, source_target_pairs={{0,17},{1,16},{2,19},{3,18},{4,21},{5,20},{6,23},{7,22},{8,25},{9,... | collective-permute-start | bytes 49160 | tf_op jit(solution)/shard_map/ppermute | solution.py:653
  15.4 4.1 %copy-start.1 = (bf16[2048,64]{0,1:T(8,128)(2,1)S(1)}, bf16[2048,64]{0,1:T(8,128)(2,1)}, u32[]{:S(2)}) copy-start(bf16[2048,64]{0,1:T(8,128)(2,1)} %param.9) | copy-start | bytes 786436
  19.5 3.5 %copy-start.4 = (f32[32,128]{1,0:T(8,128)S(1)}, f32[32,128]{1,0:T(8,128)}, u32[]{:S(2)}) copy-start(f32[32,128]{1,0:T(8,128)} %get-tuple-element.70.top) | copy-start | bytes 49156
  19.5 3.4 %collective-permute-start.3 = (f32[64,128]{1,0:T(8,128)S(1)}, f32[64,128]{1,0:T(8,128)S(1)}, u32[]{:S(2)}, u32[]{:S(2)}) collective-permute-start(f32[64,128]{1,0:T(8,128)S(1)} %pad_maximum_fusion.after), channel_id=1, source_target_pairs={{0,3},{1,2},{2,1},{3,0},{4,7},{5,6},{6,5},{7,4},{8,11},{9,10},{10,... | collective-permute-start | bytes 98312 | tf_op jit(solution)/shard_map/ppermute | solution.py:653
  22.9 3.4 %collective-permute-start.5 = (f32[64,128]{1,0:T(8,128)S(1)}, f32[64,128]{1,0:T(8,128)S(1)}, u32[]{:S(2)}, u32[]{:S(2)}) collective-permute-start(f32[64,128]{1,0:T(8,128)S(1)} %fusion.after), channel_id=1, source_target_pairs={{0,5},{1,4},{2,7},{3,6},{4,1},{5,0},{6,3},{7,2},{8,13},{9,12},{10,... | collective-permute-start | bytes 98312 | tf_op jit(solution)/shard_map/ppermute | solution.py:653
  23.0 3.3 %copy-start.2 = (f32[64,64]{1,0:T(8,128)S(1)}, f32[64,64]{1,0:T(8,128)}, u32[]{:S(2)}) copy-start(f32[64,64]{1,0:T(8,128)} %refs_7_.1) | copy-start | bytes 49156

commit v15 on v13

--- a/solution.py
+++ b/solution.py
@@ -790,7 +790,7 @@
                 out_shape=(
                     part_shape(len(chunks[3])),
                     block_shape(len(pair_chunks[3])),
-                    jax.ShapeDtypeStruct((own * STRIDE, 2 * width), F32),
+                    jax.ShapeDtypeStruct(((own + 1) * STRIDE, 2 * width), F32),
                 ),
                 in_specs=[hbm] * 2 + [vmem] * 7,
                 out_specs=(vmem,) * 3,
@@ -822,7 +822,7 @@
                 out_shape=(
                     part_shape(2),
                     block_shape(len(edge_pairs)),
-                    jax.ShapeDtypeStruct((2 * PAD * STRIDE, 2 * width), F32),
+                    jax.ShapeDtypeStruct(((2 * PAD + 1) * STRIDE, 2 * width), F32),
                 ),
                 in_specs=[hbm] * 4 + [vmem] * 7,
                 out_specs=(vmem,) * 3,
@@ -870,7 +870,7 @@
         out_specs=(hbm,) + (vmem,) * 5,
         scratch_shapes=[
             pltpu.VMEM((width, width, 128), F32),
-            pltpu.VMEM((total * STRIDE, 2 * width), F32),
+            pltpu.VMEM(((total + 1) * STRIDE, 2 * width), F32),
             pltpu.SemaphoreType.DMA((2 + len(parts),)),
         ],
         compiler_params=room(20),

time: 33.3 us -> 33.4 us (level)
  no operation moved by 1% of the time
where the time goes in v15:
time: 33.4 us; the launch traced here: 33.2 us
  Pallas kernels  18.8 us (56%)
  starting transfers between devices  7.89 us (24%)
  waiting for transfers between devices  5.45 us (16%)
  between operations  0.98 us (3%)
    ppermute x4, waiting for transfers between devices, exchange(): return value + lax.ppermute(value, AXES, pairs)  5.38 us
    ppermute x1, starting transfers between devices, swap_outer(): lax.ppermute(block, AXES, [(i, (i + 1 if i % 2 else i - 1) % many) for i...  4.33 us
    pallas_call x1, Pallas kernels, per_device(): pl.pallas_call(functools.partial(leaves_kernel, chunks, members, groups),...  4.33 us
    pallas_call x1, Pallas kernels, per_device(): pl.pallas_call(tree_kernel, out_shape=(jax.ShapeDtypeStruct((half, 2 * wi...  4.01 us
    ppermute x4, starting transfers between devices, exchange(): return value + lax.ppermute(value, AXES, pairs)  3.05 us
    pallas_call x1, Pallas kernels, per_device(): pl.pallas_call(functools.partial(far_kernel, plan), out_shape=jax.ShapeDt...  2.95 us
    pallas_call x1, Pallas kernels, per_device(): pl.pallas_call(functools.partial(edges_kernel, edge_pairs), out_shape=(pa...  2.65 us
    pallas_call x2, Pallas kernels, per_device(): pl.pallas_call(chunk_kernel(layer_chunk, pair_chunk, halo, width), out_sh...  1.98 us
  transfers between devices with their start and end apart: 6, of which 4 were waited for; matrix products, arithmetic and copies ran while one was open for 0% of the time, Pallas kernels for 23%

profile of v15, /device:TPU:0, one launch (start us, length us, event | category | flops | bytes accessed | tf_op | source)
XLA Modules:
  0.0 33.2 jit_solution(13207732465215620311)
XLA Ops:
  0.6 0.0 copy-start
  0.6 0.0 copy-start.3
  0.7 0.0 copy-start.7
  0.7 0.0 copy-start.6
  0.7 4.0 %tree.1 = (f32[32,128]{1,0:T(8,128)}, f32[32,128]{1,0:T(8,128)}, bf16[352,384]{1,0:T(8,128)(2,1)}, bf16[384,384]{1,0:T(8,128)(2,1)}) custom-call(f32[3,2048]{1,0:T(4,128)} %points, bf16[64,2048]{1,0:T(8,128)(2,1)} %bitcast.6, bf16[64,1920]{1,0:T(8,128)(2,1)} %bitcast.16, f32[64,64]{1,0:T(8,128)} %refs_8_.1, bf16[2048,384]{1,0:T(8,128)(2,1)} %vectors.7), custom_call_target="tpu_custom_call" | custom-call | tf_op jit(solution)/shard_map/tree/pallas_call | solution.py:686
  4.7 0.5 %collective-permute-start = (bf16[384,384]{1,0:T(8,128)(2,1)}, bf16[384,384]{1,0:T(8,128)(2,1)S(1)}, u32[]{:S(2)}, u32[]{:S(2)}) collective-permute-start(bf16[384,384]{1,0:T(8,128)(2,1)} %get-tuple-element.47), channel_id=1, source_target_pairs={{0,1},{1,0},{2,3},{3,2},{4,5},{5,4},{6,7},{7,6},{8,9},{9,8},{10,11... | collective-permute-start | bytes 884744 | tf_op jit(solution)/shard_map/ppermute | solution.py:650
  5.2 0.0 copy-done
  5.2 0.0 copy-done.3
  5.2 0.0 copy-done.7
  5.2 0.0 copy-done.6
  5.2 0.0 copy-start.8
  5.2 0.0 copy-start.9
  5.2 0.0 copy-start.5
  5.3 1.3 %chunk_0.1 = (bf16[512,384]{1,0:T(8,128)(2,1)S(1)}, bf16[2048,64]{1,0:T(8,128)(2,1)S(1)}, bf16[64,2048]{1,0:T(8,128)(2,1)S(1)}, bf16[48,2048]{1,0:T(8,128)(2,1)S...) custom-call(f32[3,2048]{1,0:T(4,128)S(1)} %copy-done.3, s32[12,32]{1,0:T(8,128)S(1)} %bitcast.13, ...), custom_call_target="tpu_custom_call" | custom-call | flops 1000000000 | bytes 4000000 | tf_op jit(solution)/shard_map/chunk_0/pallas_call | solution.py:729
  6.6 0.1 collective-permute-done.inner
  6.6 0.0 copy-done.8
  6.6 2.8 %collective-permute-start.1 = (f32[32,128]{1,0:T(8,128)S(1)}, f32[32,128]{1,0:T(8,128)S(1)}, u32[]{:S(2)}, u32[]{:S(2)}) collective-permute-start(f32[32,128]{1,0:T(8,128)S(1)} %add_add_fusion.after), channel_id=1, source_target_pairs={{0,9},{1,8},{2,11},{3,10},{4,13},{5,12},{6,15},{7,14},{8,1},{9,0},... | collective-permute-start | bytes 49160 | tf_op jit(solution)/shard_map/ppermute | solution.py:660
  9.4 0.0 copy-done.9
  9.4 4.3 %collective-permute-start.4 = (bf16[352,384]{1,0:T(8,128)(2,1)S(1)}, bf16[352,384]{1,0:T(8,128)(2,1)S(1)}, u32[]{:S(2)}, u32[]{:S(2)}) collective-permute-start(bf16[352,384]{1,0:T(8,128)(2,1)S(1)} %copy-done.9), channel_id=1, source_target_pairs={{0,31},{1,2},{2,1},{3,4},{4,3},{5,6},{6,5},{7,8},{8,7},{9,10},{10,... | collective-permute-start | bytes 811016 | tf_op jit(solution)/shard_map/ppermute | solution.py:655
  13.7 0.0 copy-done.5
  13.7 0.6 %chunk_1.1.refs_1_ = bf16[256,384]{1,0:T(8,128)(2,1)S(1)} custom-call(f32[32,128]{1,0:T(8,128)S(1)} %add_add_fusion.after, s32[3,32]{1,0:T(4,128)S(1)} %bitcast.8, bf16[2048,64]{1,0:T(8,128)(2,1)S(1)} %get-tuple-element.53.refs_0_.first_rows, bf16[48,2048]{1,0:T(8,128)(2,1)S(1)} %get-tuple-element.54.refs_1_.second_cols, ...), custom_call_target="tpu_custom_call" | custom-call | flops 1000000000 | bytes 4000000 | tf_op jit(solution)/shard_map/chunk_1/pallas_call | solution.py:768
  14.3 0.0 collective-permute-done.1
  14.4 0.0 copy-start.1
  14.4 0.1 collective-permute-start.2
  14.5 1.4 %chunk_2.1 = (bf16[512,384]{1,0:T(8,128)(2,1)S(1)}, bf16[768,256]{1,0:T(8,128)(2,1)S(1)}) custom-call(f32[32,128]{1,0:T(8,128)S(1)} %add.24.after, s32[3,32]{1,0:T(4,128)S(1)} %bitcast.9, bf16[2048,64]{1,0:T(8,128)(2,1)S(1)} %get-tuple-element.53.refs_0_.first_rows, bf16[48,2048]{1,0:T(8,128)(2,1)S(1)} %get-tuple-element.54.refs_1_.second_cols, ...), custom_call_target="tpu_custom_call" | custom-call | flops 1000000000 | bytes 4000000 | tf_op jit(solution)/shard_map/chunk_2/pallas_call | solution.py:768
  15.9 2.7 %collective-permute-done.2 = f32[32,128]{1,0:T(8,128)S(1)} collective-permute-done((f32[32,128]{1,0:T(8,128)S(1)}, f32[32,128]{1,0:T(8,128)S(1)}, u32[]{:S(2)}, u32[]{:S(2)}) %collective-permute-start.2) | collective-permute-done | bytes 16416 | tf_op jit(solution)/shard_map/ppermute | solution.py:660
  18.5 0.0 copy-start.4
  18.5 0.1 collective-permute-start.3
  18.6 0.0 copy-done.1
  18.6 1.6 %chunk_3.1 = (bf16[256,384]{1,0:T(8,128)(2,1)S(1)}, bf16[768,256]{1,0:T(8,128)(2,1)S(1)}, f32[1320,128]{1,0:T(8,128)S(1)}) custom-call(f32[64,128]{1,0:T(8,128)S(1)} %pad_maximum_fusion.after, s32[3,32]{1,0:T(4,128)S(1)} %bitcast.10, bf16[2048,64]{1,0:T(8,128)(2,1)S(1)} %get-tuple-element.53.refs_0_.first_rows, ...), custom_call_target="tpu_custom_call" | custom-call | flops 1000000000 | bytes 4000000 | tf_op jit(solution)/shard_map/chunk_3/pallas_call | solution.py:788
  20.2 1.8 %collective-permute-done.3 = f32[64,128]{1,0:T(8,128)S(1)} collective-permute-done((f32[64,128]{1,0:T(8,128)S(1)}, f32[64,128]{1,0:T(8,128)S(1)}, u32[]{:S(2)}, u32[]{:S(2)}) %collective-permute-start.3) | collective-permute-done | bytes 32800 | tf_op jit(solution)/shard_map/ppermute | solution.py:660
  22.1 0.0 collective-permute-done.4.outer
  22.1 0.1 collective-permute-start.5
  22.2 0.0 copy-done.4
  22.2 0.0 copy-start.2
  22.2 2.6 %edges.1 = (bf16[512,384]{1,0:T(8,128)(2,1)S(1)}, bf16[1536,256]{1,0:T(8,128)(2,1)S(1)}, f32[680,128]{1,0:T(8,128)S(1)}) custom-call(f32[64,128]{1,0:T(8,128)S(1)} %fusion.after, s32[3,32]{1,0:T(4,128)S(1)} %bitcast.11, bf16[384,384]{1,0:T(8,128)(2,1)S(1)} %collective-permute-done.inner, bf16[352,384]{1,0:T(8,128)(2,1)S(1)} %collective-permute-done.4.outer, ...), custom_call_target="tpu_custom_call" | custom-call | flops 1000000000 | bytes 4000000 | tf_op jit(solution)/shard_map/edges/pallas_call | solution.py:820
  24.9 0.9 %collective-permute-done.5 = f32[64,128]{1,0:T(8,128)S(1)} collective-permute-done((f32[64,128]{1,0:T(8,128)S(1)}, f32[64,128]{1,0:T(8,128)S(1)}, u32[]{:S(2)}, u32[]{:S(2)}) %collective-permute-start.5) | collective-permute-done | bytes 32800 | tf_op jit(solution)/shard_map/ppermute | solution.py:660
  25.8 0.0 copy-done.2
  25.8 4.3 %leaves.1 = (bf16[2048,384]{1,0:T(8,128)(2,1)}, bf16[3072,128]{1,0:T(8,128)(2,1)S(1)}, bf16[3072,128]{1,0:T(8,128)(2,1)S(1)}, f32[64,64]{1,0:T(8,128)}, f32[64,64]{1,0:T(8,128)}, /*index=5*/f32[64,64]{1,0:T(8,128)}) custom-call(bf16[512,384]{1,0:T(8,128)(2,1)S(1)} %get-tuple-element.51.refs_0_, bf16[256,384]{1,0:T(8,128)(2,1)S(1)} %chunk_1.1.refs_1_, ...), custom_call_target="tpu_custom_call" | custom-call | tf_op jit(solution)/shard_map/leaves/pallas_call | solution.py:859
  30.1 2.9 %far.1 = bf16[64,6144]{1,0:T(8,128)(2,1)} custom-call(s32[3,32]{1,0:T(4,128)S(1)} %bitcast.12, bf16[3072,128]{1,0:T(8,128)(2,1)S(1)} %get-tuple-element.77.high, bf16[3072,128]{1,0:T(8,128)(2,1)S(1)} %get-tuple-element.78.low, bf16[768,256]{1,0:T(8,128)(2,1)S(1)} %get-tuple-element.79.refs_0_, bf16[768,256]{1,0:T(8,128)(2,1)S(1)} %get-tuple-element.80.refs_1_, ...), custom_call_target="tpu_custom_call" | custom-call | tf_op jit(solution)/shard_map/far/pallas_call | solution.py:880
  (6 shorter events, 0.0 us)
Async XLA Ops:
  0.6 4.6 %copy-start = (bf16[2048,384]{1,0:T(8,128)(2,1)S(1)}, bf16[2048,384]{1,0:T(8,128)(2,1)}, u32[]{:S(2)}) copy-start(bf16[2048,384]{1,0:T(8,128)(2,1)} %vectors.7) | copy-start | bytes 4718596
  0.6 4.6 %copy-start.3 = (f32[3,2048]{1,0:T(4,128)S(1)}, f32[3,2048]{1,0:T(4,128)}, u32[]{:S(2)}) copy-start(f32[3,2048]{1,0:T(4,128)} %points) | copy-start | bytes 73732
  0.7 4.6 %copy-start.7 = (s32[32]{0:T(128)S(1)}, s32[32]{0:T(128)}, u32[]{:S(2)}) copy-start(s32[32]{0:T(128)} %param.14) | copy-start | bytes 388
  0.7 4.6 %copy-start.6 = (s32[32,12]{0,1:T(8,128)S(1)}, s32[32,12]{0,1:T(8,128)}, u32[]{:S(2)}) copy-start(s32[32,12]{0,1:T(8,128)} %param.13) | copy-start | bytes 4612
  4.7 1.9 %collective-permute-start = (bf16[384,384]{1,0:T(8,128)(2,1)}, bf16[384,384]{1,0:T(8,128)(2,1)S(1)}, u32[]{:S(2)}, u32[]{:S(2)}) collective-permute-start(bf16[384,384]{1,0:T(8,128)(2,1)} %get-tuple-element.47), channel_id=1, source_target_pairs={{0,1},{1,0},{2,3},{3,2},{4,5},{5,4},{6,7},{7,6},{8,9},{9,8},{10,11... | collective-permute-start | bytes 884744 | tf_op jit(solution)/shard_map/ppermute | solution.py:650
  5.2 1.4 %copy-start.8 = (f32[32,128]{1,0:T(8,128)S(1)}, f32[32,128]{1,0:T(8,128)}, u32[]{:S(2)}) copy-start(f32[32,128]{1,0:T(8,128)} %get-tuple-element.46) | copy-start | bytes 49156
  5.2 4.2 %copy-start.9 = (bf16[352,384]{1,0:T(8,128)(2,1)S(1)}, bf16[352,384]{1,0:T(8,128)(2,1)}, u32[]{:S(2)}) copy-start(bf16[352,384]{1,0:T(8,128)(2,1)} %get-tuple-element.67) | copy-start | bytes 811012
  5.2 8.5 %copy-start.5 = (s32[32,3]{0,1:T(4,128)S(1)}, s32[32,3]{0,1:T(4,128)}, u32[]{:S(2)}) copy-start(s32[32,3]{0,1:T(4,128)} %param.15) | copy-start | bytes 1156
  6.6 7.7 %collective-permute-start.1 = (f32[32,128]{1,0:T(8,128)S(1)}, f32[32,128]{1,0:T(8,128)S(1)}, u32[]{:S(2)}, u32[]{:S(2)}) collective-permute-start(f32[32,128]{1,0:T(8,128)S(1)} %add_add_fusion.after), channel_id=1, source_target_pairs={{0,9},{1,8},{2,11},{3,10},{4,13},{5,12},{6,15},{7,14},{8,1},{9,0},... | collective-permute-start | bytes 49160 | tf_op jit(solution)/shard_map/ppermute | solution.py:660
  9.4 12.7 %collective-permute-start.4 = (bf16[352,384]{1,0:T(8,128)(2,1)S(1)}, bf16[352,384]{1,0:T(8,128)(2,1)S(1)}, u32[]{:S(2)}, u32[]{:S(2)}) collective-permute-start(bf16[352,384]{1,0:T(8,128)(2,1)S(1)} %copy-done.9), channel_id=1, source_target_pairs={{0,31},{1,2},{2,1},{3,4},{4,3},{5,6},{6,5},{7,8},{8,7},{9,10},{10,... | collective-permute-start | bytes 811016 | tf_op jit(solution)/shard_map/ppermute | solution.py:655
  14.4 4.2 %copy-start.1 = (bf16[2048,64]{0,1:T(8,128)(2,1)S(1)}, bf16[2048,64]{0,1:T(8,128)(2,1)}, u32[]{:S(2)}) copy-start(bf16[2048,64]{0,1:T(8,128)(2,1)} %param.9) | copy-start | bytes 786436
  14.4 4.1 %collective-permute-start.2 = (f32[32,128]{1,0:T(8,128)S(1)}, f32[32,128]{1,0:T(8,128)S(1)}, u32[]{:S(2)}, u32[]{:S(2)}) collective-permute-start(f32[32,128]{1,0:T(8,128)S(1)} %add.24.after), channel_id=1, source_target_pairs={{0,17},{1,16},{2,19},{3,18},{4,21},{5,20},{6,23},{7,22},{8,25},{9,... | collective-permute-start | bytes 49160 | tf_op jit(solution)/shard_map/ppermute | solution.py:660
  18.5 3.7 %copy-start.4 = (f32[32,128]{1,0:T(8,128)S(1)}, f32[32,128]{1,0:T(8,128)}, u32[]{:S(2)}) copy-start(f32[32,128]{1,0:T(8,128)} %get-tuple-element.70.top) | copy-start | bytes 49156
  18.5 3.5 %collective-permute-start.3 = (f32[64,128]{1,0:T(8,128)S(1)}, f32[64,128]{1,0:T(8,128)S(1)}, u32[]{:S(2)}, u32[]{:S(2)}) collective-permute-start(f32[64,128]{1,0:T(8,128)S(1)} %pad_maximum_fusion.after), channel_id=1, source_target_pairs={{0,3},{1,2},{2,1},{3,0},{4,7},{5,6},{6,5},{7,4},{8,11},{9,10},{10,... | collective-permute-start | bytes 98312 | tf_op jit(solution)/shard_map/ppermute | solution.py:660
  22.1 3.7 %collective-permute-start.5 = (f32[64,128]{1,0:T(8,128)S(1)}, f32[64,128]{1,0:T(8,128)S(1)}, u32[]{:S(2)}, u32[]{:S(2)}) collective-permute-start(f32[64,128]{1,0:T(8,128)S(1)} %fusion.after), channel_id=1, source_target_pairs={{0,5},{1,4},{2,7},{3,6},{4,1},{5,0},{6,3},{7,2},{8,13},{9,12},{10,... | collective-permute-start | bytes 98312 | tf_op jit(solution)/shard_map/ppermute | solution.py:660
  22.2 3.5 %copy-start.2 = (f32[64,64]{1,0:T(8,128)S(1)}, f32[64,64]{1,0:T(8,128)}, u32[]{:S(2)}) copy-start(f32[64,64]{1,0:T(8,128)} %refs_8_.1) | copy-start | bytes 49156
